TPU v7x, 512 devices: a whole 4x4x16 slice. The times are simulated.
512 devices in a mesh: seq: 16 (over z), etp: 8 (over x, core), exp: 4 (over y).
Axes of the slice: x: 4, y: 4, z: 16, core: 2. Of those that a mesh axis runs over, the one named last changes fastest.
Arguments:
- tokens: bfloat16 [2048, 6144], P('seq', 'etp'), may hold values from -6 to 6
- cotangent: bfloat16 [2048, 6144], P('seq', 'etp'), may hold values from -6 to 6
- experts: int32 [2048, 2], P('seq'), may hold values from 0 to 7, as said below
- route_weight: int32 [2048, 2], P('seq'), may hold values from 4096 to 61440, as said below
- gate_weight: bfloat16 [4, 6144, 8192], P('exp', 'etp', 'seq'), may hold values from -0.078125 to 0.078125
- up_weight: bfloat16 [4, 6144, 8192], P('exp', 'etp', 'seq'), may hold values from -0.078125 to 0.078125
- down_weight: bfloat16 [4, 8192, 6144], P('exp', 'seq', 'etp'), may hold values from -0.0625 to 0.0625
Outputs:
- input_grad: bfloat16 [2048, 6144], P('seq', ('etp', 'exp'))
Inputs may be any that keep to these rules, and one draw needn't show every extreme that they name: `experts`: the two entries of a row differ. In each aligned block of 128 rows (the tokens of one index of seq) no expert is named by more than 64 rows. `route_weight`: the two entries of a row sum to 65536.
All inputs are finite; a program needn't handle non-finite values.
Results may differ from a plain program's by a relative error of at most 0.0057.
Values may be sent and summed in bfloat16 or wider, within the bound.
No kernel may reach another device: no remote copies, remote signals or barrier semaphores. Data moves between devices by JAX's collectives and lax.ppermute only.
A program may use at most 64 MiB of HBM per device.

v0:
```python
import jax
import jax.numpy as jnp
from jax import lax
from jax.sharding import PartitionSpec as P

unit_scale = 1.0 / 65536.0


def swiglu_back(gate_sum, up_sum, back_sum):
    sigmoid_gate = jax.nn.sigmoid(gate_sum)
    silu_gate = gate_sum * sigmoid_gate
    grad_up = (back_sum * silu_gate).astype(jnp.bfloat16)
    grad_gate = (back_sum * up_sum * sigmoid_gate * (1.0 + gate_sum * (1.0 - sigmoid_gate))).astype(
        jnp.bfloat16
    )
    return (grad_gate, grad_up)


def slot_tables(experts, route_weight, expert_id, capacity):
    named_hit = experts == expert_id
    chosen = jnp.any(named_hit, axis=1)
    route_share = (
        jnp.sum(jnp.where(named_hit, route_weight, 0), axis=1).astype(jnp.float32) * unit_scale
    )
    slot_order = jnp.cumsum(chosen.astype(jnp.int32)) - 1
    slot_ids = lax.broadcasted_iota(jnp.int32, (capacity, experts.shape[0]), 0)
    slot_table = jnp.where((slot_order[None, :] == slot_ids) & chosen[None, :], 1.0, 0.0).astype(
        jnp.float32
    )
    return (slot_table, route_share)


def per_device(tokens, cotangent, experts, route_weight, gate_weight, up_weight, down_weight):
    capacity = tokens.shape[0] // 2
    expert_id = lax.axis_index("exp")
    slot_table, route_share = slot_tables(experts, route_weight, expert_id, capacity)
    select_half = slot_table.astype(jnp.bfloat16)
    picked = jnp.dot(select_half, tokens, preferred_element_type=jnp.float32).astype(jnp.bfloat16)
    scaled = (route_share[:, None] * cotangent.astype(jnp.float32)).astype(jnp.bfloat16)
    picked_grad = jnp.dot(select_half, scaled, preferred_element_type=jnp.float32).astype(
        jnp.bfloat16
    )
    gate_local = gate_weight[0]
    up_local = up_weight[0]
    down_local = down_weight[0]
    hidden_cols = gate_local.shape[1]
    paired_weights = jnp.concatenate([gate_local, up_local], axis=1)
    contract_last = (((1,), (1,)), ((), ()))
    rows_in, rows_grad = (
        lax.all_gather(picked, "seq", axis=0, tiled=True),
        lax.all_gather(picked_grad, "seq", axis=0, tiled=True),
    )
    joined_part = jnp.dot(rows_in, paired_weights, preferred_element_type=jnp.float32)
    back_part = lax.dot_general(
        rows_grad, down_local, contract_last, preferred_element_type=jnp.float32
    )
    gate_part = joined_part[:, :hidden_cols]
    up_part = joined_part[:, hidden_cols:]
    gate_sum, up_sum, back_sum = lax.psum((gate_part, up_part, back_part), "etp")
    grad_gate, grad_up = swiglu_back(gate_sum, up_sum, back_sum)
    result = lax.dot_general(
        grad_gate, gate_local, contract_last, preferred_element_type=jnp.float32
    )
    returned = lax.psum_scatter(
        result
        + lax.dot_general(grad_up, up_local, contract_last, preferred_element_type=jnp.float32),
        "seq",
        scatter_dimension=0,
        tiled=True,
    )
    combined = jnp.dot(slot_table.T, returned, precision=lax.Precision.HIGHEST)
    summed = lax.psum_scatter(combined, "exp", scatter_dimension=1, tiled=True)
    return summed.astype(jnp.bfloat16)


def solution(mesh):
    placed = (
        P("seq", "etp"),
        P("seq", "etp"),
        P("seq", None),
        P("seq", None),
        P("exp", "etp", "seq"),
        P("exp", "etp", "seq"),
        P("exp", "seq", "etp"),
    )
    return jax.shard_map(
        per_device, mesh=mesh, in_specs=placed, out_specs=P("seq", ("etp", "exp")), check_vma=False
    )
```

profile of v0, /device:TPU:1, one launch (start us, length us, event | category | flops | bytes accessed | tf_op | source)
XLA Modules:
  0.0 378.4 jit_solution(14420929790684923129)
XLA Ops:
  6.5 0.8 fusion.35
  7.3 0.1 copy.9
  7.4 0.2 reduce-window.8
  7.6 0.1 add_reduce_fusion
  7.7 1.7 convolution_convert_fusion
  9.5 0.0 all-gather.3.cloned.1.call-start
  9.5 0.7 select_reduce_fusion
  10.2 1.8 convolution_convert_fusion.1
  12.0 0.0 all-gather.3.cloned.1.call-update
  12.1 0.0 all-reduce.3.cloned.1.call-start
  12.1 65.4 %all-gather.5.cloned.1.call-done = bf16[1024,768]{1,0:T(8,128)(2,1)} async-done(((bf16[64,768]{1,0:T(8,128)(2,1)}), bf16[1024,768]{1,0:T(8,128)(2,1)}) %all-gather.5.cloned.1.call-update) | async-done | bytes 1572880 | tf_op jit(solution)/shard_map/all_gather | solution.py:50
  77.5 3.6 fusion
  81.2 2.5 fusion.36
  83.6 65.3 %all-gather.3.cloned.1.call-done = bf16[1024,768]{1,0:T(8,128)(2,1)} async-done(((bf16[64,768]{1,0:T(8,128)(2,1)}), bf16[1024,768]{1,0:T(8,128)(2,1)}) %all-gather.3.cloned.1.call-update) | async-done | bytes 1572880 | tf_op jit(solution)/shard_map/all_gather | solution.py:51
  148.9 3.7 fusion.5
  152.7 0.0 reduce-scatter.3.cloned.1.call-start
  152.7 106.4 %all-reduce.3.cloned.1.call-done = (f32[1024,512]{1,0:T(8,128)}, f32[1024,512]{1,0:T(8,128)}, f32[1024,512]{1,0:T(8,128)}) async-done(((f32[1024,512]{1,0:T(8,128)}, f32[1024,512]{1,0:T(8,128)}, f32[1024,512]{1,0:T(8,128)}), (f32[1024,512]{1,0:T(8,128)}, f32[1024,512]{1,0:T(8,128)}, f32[1024,512]{1,0:T(8,128)})) %all-reduce.3.cloned.1.call-update) | async-done | bytes 6291472 | tf_op jit(solution)/shard_map/psum | solution.py:59
  259.1 4.5 %fusion.4 = f32[1024,768]{1,0:T(8,128)S(1)} fusion(f32[1024,512]{1,0:T(8,128)} %get-tuple-element.5, f32[1024,512]{1,0:T(8,128)} %get-tuple-element.6, f32[1024,512]{1,0:T(8,128)} %get-tuple-element.7, bf16[1,768,512]{2,1,0:T(8,128)(2,1)S(1)} %copy-done.3), kind=kOutput, calls=%fused_computation.10 | convolution fusion | flops 810549248 | bytes 10223616 | tf_op jit(solution)/shard_map/dot_general | solution.py:61
  263.7 3.0 convolution_add_fusion
  266.7 0.0 reduce-scatter.5.cloned.1.call-start
  266.7 67.8 %reduce-scatter.3.cloned.1.call-done = f32[64,768]{1,0:T(8,128)} async-done(((f32[1024,768]{1,0:T(8,128)}), f32[64,768]{1,0:T(8,128)}) %reduce-scatter.3.cloned.1.call-update) | async-done | bytes 196624 | tf_op jit(solution)/shard_map/reduce_scatter | solution.py:64
  334.5 2.5 fusion.8
  337.0 33.3 %reduce-scatter.5.cloned.1.call-done = f32[128,192]{0,1:T(8,128)} async-done(((f32[128,768]{0,1:T(8,128)}), f32[128,192]{0,1:T(8,128)}) %reduce-scatter.5.cloned.1.call-update) | async-done | bytes 98320 | tf_op jit(solution)/shard_map/reduce_scatter | solution.py:72
  370.3 1.5 convert_element_type.56
  (17 shorter events, 0.1 us)
Async XLA Ops:
  6.5 142.4 %copy-start = (bf16[1,512,768]{2,1,0:T(8,128)(2,1)S(1)}, bf16[1,512,768]{2,1,0:T(8,128)(2,1)}, u32[]{:S(2)}) copy-start(bf16[1,512,768]{2,1,0:T(8,128)(2,1)} %param.13) | copy-start | bytes 2359300
  6.5 71.0 %all-gather.5.cloned.1.call-start = ((), (), s32[]{:S(2)}) async-start(), calls=%async_computation.3 | async-start | bytes 1671168 | tf_op jit(solution)/shard_map/all_gather | solution.py:50
  9.5 139.5 %all-gather.3.cloned.1.call-start = ((), (), s32[]{:S(2)}) async-start(), calls=%async_computation.2 | async-start | bytes 1671168 | tf_op jit(solution)/shard_map/all_gather | solution.py:51
  12.1 247.0 %all-reduce.3.cloned.1.call-start = ((), (), s32[]{:S(2)}) async-start(), calls=%async_computation.6 | async-start | bytes 12582912 | tf_op jit(solution)/shard_map/psum | solution.py:59
  152.7 106.5 %copy-start.3 = (bf16[1,768,512]{2,1,0:T(8,128)(2,1)S(1)}, bf16[1,768,512]{2,1,0:T(8,128)(2,1)}, u32[]{:S(2)}) copy-start(bf16[1,768,512]{2,1,0:T(8,128)(2,1)} %param.11) | copy-start | bytes 2359300
  152.7 181.8 %reduce-scatter.3.cloned.1.call-start = ((), (), s32[]{:S(2)}) async-start(), calls=%async_computation.4 | async-start | bytes 3342336 | tf_op jit(solution)/shard_map/reduce_scatter | solution.py:64
  259.1 4.5 %copy-start.1 = (f32[1024,512]{1,0:T(8,128)S(1)}, f32[1024,512]{1,0:T(8,128)}, u32[]{:S(2)}) copy-start(f32[1024,512]{1,0:T(8,128)} %get-tuple-element.5) | copy-start | bytes 6291460
  259.1 4.5 %copy-start.2 = (f32[1024,512]{1,0:T(8,128)S(1)}, f32[1024,512]{1,0:T(8,128)}, u32[]{:S(2)}) copy-start(f32[1024,512]{1,0:T(8,128)} %get-tuple-element.6) | copy-start | bytes 6291460
  259.1 4.5 %copy-start.4 = (bf16[1,768,512]{2,1,0:T(8,128)(2,1)S(1)}, bf16[1,768,512]{2,1,0:T(8,128)(2,1)}, u32[]{:S(2)}) copy-start(bf16[1,768,512]{2,1,0:T(8,128)(2,1)} %param.12) | copy-start | bytes 2359300
  266.7 103.7 %reduce-scatter.5.cloned.1.call-start = ((), (), s32[]{:S(2)}) async-start(), calls=%async_computation.5 | async-start | bytes 491520 | tf_op jit(solution)/shard_map/reduce_scatter | solution.py:72
Sparse Core Ops, SparseCore 0:
  9.6 67.9 all-gather.4
  79.6 69.2 all-gather.2
  152.8 106.2 all-reduce.2
  266.8 67.6 reduce-scatter.2
  337.2 33.0 reduce-scatter.4
where the time goes:
time: 380 us; the launch traced here: 378 us
  waiting for transfers between devices  338 us (89%)
  matrix products  20.8 us (5%)
  between operations  13.2 us (3%)
    psum x1, waiting for transfers between devices, per_device(): lax.psum((gate_part, up_part, back_part), 'etp')  106 us
    reduce_scatter x1, waiting for transfers between devices, per_device(): lax.psum_scatter(result + lax.dot_general(grad_up, up_local, contract_las...  67.8 us
    all_gather x1, waiting for transfers between devices, per_device(): lax.all_gather(picked, 'seq', axis=0, tiled=True)  65.4 us
    all_gather x1, waiting for transfers between devices, per_device(): lax.all_gather(picked_grad, 'seq', axis=0, tiled=True)  65.3 us
    reduce_scatter x1, waiting for transfers between devices, per_device(): summed = lax.psum_scatter(combined, 'exp', scatter_dimension=1, tiled=True)  33.3 us
  transfers between devices with their start and end apart: 5, of which 5 were waited for; matrix products, arithmetic and copies ran while one was open for 2% of the time, Pallas kernels for 0%

commit v1 on v0

v1 whole, which is shorter than its diff:
```python
import jax
import jax.numpy as jnp
from jax import lax
from jax.experimental import pallas as pl
from jax.experimental.pallas import tpu as pltpu
from jax.sharding import Mesh
from jax.sharding import PartitionSpec as P

unit_scale = 1.0 / 65536.0
window = 4
table_rows = 16
bf16 = jnp.bfloat16
f32 = jnp.float32
contract_last = (((1,), (1,)), ((), ()))
contract_first = (((0,), (0,)), ((), ()))
swap_cores = [(0, 1), (1, 0)]
vmem_bytes = 48 * 1024 * 1024


def kernel_call(body, out_shape, n_in, scalars=0):
    vmem = pl.BlockSpec(memory_space=pltpu.VMEM)
    smem = pl.BlockSpec(memory_space=pltpu.SMEM)
    return pl.pallas_call(
        body,
        out_shape=out_shape,
        in_specs=[smem] * scalars + [vmem] * n_in,
        out_specs=vmem,
        compiler_params=pltpu.CompilerParams(vmem_limit_bytes=vmem_bytes),
    )


def slot_map(experts):
    count = experts.shape[0]
    ids = lax.broadcasted_iota(jnp.int32, (window, count), 0)
    named = (experts[:, 0][None, :] == ids) | (experts[:, 1][None, :] == ids)
    before = lax.broadcasted_iota(jnp.int32, (count, count), 0) <= lax.broadcasted_iota(
        jnp.int32, (count, count), 1
    )
    order = jnp.dot(named.astype(bf16), before.astype(bf16), preferred_element_type=f32)
    return jnp.where(named, order - 1.0, -1.0)


def pick_kernel(pay_ref, out_ref):
    blocks, _, cols = pay_ref.shape
    count = pay_ref.shape[1] - table_rows
    part = out_ref.shape[4]
    slot_ids = lax.broadcasted_iota(jnp.int32, (2 * part, count), 0).astype(f32)
    for b in range(blocks):
        table = pay_ref[b, count:, :count].astype(f32)
        select = jnp.concatenate(
            [jnp.where(table[e : e + 1] == slot_ids, 1.0, 0.0) for e in range(window)], axis=0
        ).astype(bf16)
        rows = jnp.dot(select, pay_ref[b, :count, :], preferred_element_type=f32).astype(bf16)
        for e in range(window):
            for core in range(2):
                begin = (2 * e + core) * part
                piece = rows[begin : begin + part]
                for pair in range(2):
                    out_ref[core, e, pair, b] = piece


def joined_kernel(core_ref, x_ref, gate_ref, up_ref, gate_far_ref, up_far_ref, out_ref):
    core = core_ref[0]
    quarter = x_ref.shape[-1]
    hidden = gate_ref.shape[1]
    blocks, _, part, _ = out_ref.shape
    for pair in range(2):
        for m, (near, far) in enumerate(((gate_ref, gate_far_ref), (up_ref, up_far_ref))):
            total = None
            for side, weight in ((core, near), (1 - core, far)):
                for q in range(window):
                    term = jnp.dot(
                        x_ref[side, q, pair],
                        weight[q * quarter : (q + 1) * quarter, :],
                        preferred_element_type=f32,
                    )
                    total = term if total is None else total + term
            out_ref[:, pair, :, m * hidden : (m + 1) * hidden] = total.astype(bf16).reshape(
                blocks, part, hidden
            )


def result_kernel(core_ref, g_ref, gate_ref, up_ref, gate_far_ref, up_far_ref, out_ref):
    core = core_ref[0]
    hidden = gate_ref.shape[1]
    quarter = out_ref.shape[-1]
    blocks, _, part, _ = g_ref.shape
    for pair in range(2):
        grad_gate = g_ref[:, pair, :, :hidden].reshape(blocks * part, hidden)
        grad_up = g_ref[:, pair, :, hidden:].reshape(blocks * part, hidden)
        for side, gate, up in ((core, gate_ref, up_ref), (1 - core, gate_far_ref, up_far_ref)):
            for q in range(window):
                span = slice(q * quarter, (q + 1) * quarter)
                rows = lax.dot_general(
                    grad_gate, gate[span, :], contract_last, preferred_element_type=f32
                ) + lax.dot_general(
                    grad_up, up[span, :], contract_last, preferred_element_type=f32
                )
                out_ref[side, q, pair] = rows.astype(bf16)


def combine_kernel(pay_ref, rows_ref, out_ref):
    blocks, count, cols = out_ref.shape
    part = rows_ref.shape[4]
    slot_ids = lax.broadcasted_iota(jnp.int32, (part, count), 0).astype(f32)
    for b in range(blocks):
        table = pay_ref[b, count:, :count].astype(f32)
        pieces, values = [], []
        for core in range(2):
            for e in range(window):
                hit = jnp.where(table[e : e + 1] == slot_ids + float(core * part), 1.0, 0.0)
                for pair in range(2):
                    pieces.append(hit)
                    values.append(rows_ref[core, e, pair, b])
        select = jnp.concatenate(pieces, axis=0).astype(bf16)
        dense = lax.dot_general(
            select, jnp.concatenate(values, axis=0), contract_first, preferred_element_type=f32
        )
        out_ref[b] = dense.astype(bf16)


def per_device(tokens, cotangent, experts, route_weight, gate_weight, up_weight, down_weight):
    core, expert_id = lax.axis_index("c"), lax.axis_index("y")
    n_high, n_x = lax.axis_size("zh"), lax.axis_size("x")
    group = ("c", "y", "zl")
    count, feats = tokens.shape
    quarter = feats // window
    part = count // 4
    gate, up, down = gate_weight[0], up_weight[0], down_weight[0]
    hidden = gate.shape[1]
    core_id = core.reshape(1).astype(jnp.int32)

    cot_far = lax.ppermute(cotangent, "c", swap_cores)

    table = slot_map(experts)
    own_quarter = lax.dynamic_slice_in_dim(tokens, expert_id * quarter, quarter, axis=1)
    table_pad = jnp.pad(table.astype(bf16), ((0, table_rows - window), (0, quarter - count)))
    pay = jnp.concatenate([own_quarter, table_pad], axis=0)
    pay = lax.all_to_all(
        jnp.broadcast_to(pay[None], (n_high, *pay.shape)), "zh", 0, 0, tiled=True
    )

    share = (
        jnp.sum(jnp.where(experts == expert_id, route_weight, 0), axis=1).astype(f32) * unit_scale
    )
    own_slots = lax.dynamic_slice_in_dim(table, expert_id, 1, axis=0)
    slot_ids = lax.broadcasted_iota(jnp.int32, (part, count), 0) + core * part
    select_half = jnp.where(own_slots == slot_ids.astype(f32), 1.0, 0.0).astype(bf16)
    both = jnp.concatenate([cotangent, cot_far], axis=1)
    scaled = (share[:, None] * both.astype(f32)).astype(bf16)
    picked = jnp.dot(select_half, scaled, preferred_element_type=f32).astype(bf16)
    rows_grad = lax.all_gather(picked, ("zh", "zl"), axis=0, tiled=True)

    gate_far = lax.ppermute(gate, "c", swap_cores)
    up_far = lax.ppermute(up, "c", swap_cores)
    down_far = lax.ppermute(down, "c", swap_cores)

    picks = kernel_call(
        pick_kernel, jax.ShapeDtypeStruct((2, window, 2, n_high, part, quarter), bf16), 1
    )(pay)
    rows_in = lax.all_to_all(
        picks.reshape(4 * window, n_high * part, quarter), group, 0, 0, tiled=True
    ).reshape(2, window, 2, n_high * part, quarter)
    joined = kernel_call(
        joined_kernel, jax.ShapeDtypeStruct((n_high, 2, part, 2 * hidden), bf16), 5, 1
    )(core_id, rows_in, gate, up, gate_far, up_far)
    rows = 2 * n_high * part
    joined = lax.all_to_all(joined.reshape(rows, 2 * hidden), "x", 0, 0, tiled=True)

    back = lax.dot_general(
        rows_grad[:, :feats], down, contract_last, preferred_element_type=f32
    ) + lax.dot_general(rows_grad[:, feats:], down_far, contract_last, preferred_element_type=f32)
    back = lax.all_to_all(back.astype(bf16), "x", 0, 0, tiled=True)

    joined_sum = jnp.sum(joined.reshape(n_x, rows // n_x, 2 * hidden).astype(f32), axis=0)
    back_sum = jnp.sum(back.reshape(n_x, rows // n_x, hidden).astype(f32), axis=0)
    gate_sum, up_sum = joined_sum[:, :hidden], joined_sum[:, hidden:]
    sigmoid_gate = jax.nn.sigmoid(gate_sum)
    grad_up = (back_sum * (gate_sum * sigmoid_gate)).astype(bf16)
    grad_gate = (
        back_sum * up_sum * sigmoid_gate * (1.0 + gate_sum * (1.0 - sigmoid_gate))
    ).astype(bf16)
    grads = jnp.concatenate([grad_gate, grad_up], axis=1)
    grads = lax.all_to_all(
        jnp.broadcast_to(grads[None], (n_x, *grads.shape)), "x", 0, 0, tiled=True
    )

    result = kernel_call(
        result_kernel, jax.ShapeDtypeStruct((2, window, 2, n_high * part, quarter), bf16), 5, 1
    )(core_id, grads.reshape(n_high, 2, part, 2 * hidden), gate, up, gate_far, up_far)
    result = lax.all_to_all(
        result.reshape(4 * window, n_high * part, quarter), group, 0, 0, tiled=True
    )
    dense = kernel_call(
        combine_kernel, jax.ShapeDtypeStruct((n_high, count, quarter), bf16), 2
    )(pay, result.reshape(2, window, 2, n_high, part, quarter))
    dense = lax.all_to_all(dense, "zh", 0, 0, tiled=True)
    return jnp.sum(dense.astype(f32), axis=0).astype(bf16)


def solution(mesh):
    split = Mesh(
        mesh.devices.reshape(mesh.shape["seq"] // 2, 2, mesh.shape["etp"] // 2, 2, -1),
        ("zh", "zl", "x", "c", "y"),
    )
    seq, etp = ("zh", "zl"), ("x", "c")
    placed = (
        P(seq, etp),
        P(seq, etp),
        P(seq, None),
        P(seq, None),
        P("y", etp, seq),
        P("y", etp, seq),
        P("y", seq, etp),
    )
    return jax.shard_map(
        per_device, mesh=split, in_specs=placed, out_specs=P(seq, ("x", "c", "y")), check_vma=False
    )
```

time: 380 us -> 267 us (0.70)
  the two profiles are of different devices: /device:TPU:1 before, /device:TPU:2 now
where the time goes in v1:
time: 267 us; the launch traced here: 266 us
  blocking collectives  125 us (47%)
  waiting for transfers between devices  72.9 us (27%)
  starting transfers between devices  23.3 us (9%)
  between operations  13.6 us (5%)
  local copies, waits for them, and re-layouts  13.2 us (5%)
  Pallas kernels  11.3 us (4%)
  matrix products  5.68 us (2%)
    all_gather x1, waiting for transfers between devices, per_device(): rows_grad = lax.all_gather(picked, ('zh', 'zl'), axis=0, tiled=True)  58.8 us
    all_to_all x1, blocking collectives, per_device(): lax.all_to_all(jnp.broadcast_to(pay[None], (n_high, *pay.shape)), 'zh', 0...  50.6 us
    all_to_all x1, blocking collectives, per_device(): dense = lax.all_to_all(dense, 'zh', 0, 0, tiled=True)  34.3 us
    all_to_all x1, blocking collectives, per_device(): lax.all_to_all(result.reshape(4 * window, n_high * part, quarter), group,...  26.6 us
    all_to_all x1, blocking collectives, per_device(): lax.all_to_all(jnp.broadcast_to(grads[None], (n_x, *grads.shape)), 'x', 0...  13.4 us
    all_to_all x1, waiting for transfers between devices, per_device(): lax.all_to_all(joined.reshape(rows, 2 * hidden), 'x', 0, 0, tiled=True)  13.1 us
  transfers between devices with their start and end apart: 8, of which 3 were waited for; matrix products, arithmetic and copies ran while one was open for 4% of the time, Pallas kernels for 2%

profile of v1, /device:TPU:2, one launch (start us, length us, event | category | flops | bytes accessed | tf_op | source)
XLA Modules:
  0.0 266.0 jit_solution(17736917678951603167)
XLA Ops:
  6.5 0.8 slice_bitcast_fusion.1
  7.7 50.6 %all_to_all.43.pay_ref = bf16[8,144,192]{2,1,0:T(8,128)(2,1)S(1)} all-to-all(bf16[8,144,192]{2,1,0:T(8,128)(2,1)S(1)} %broadcast_in_dim.27), channel_id=1, replica_groups=mesh['zh'=8,'zl'=2,'x'=4,'c'=2,'y'=4] {'zh'}, dimensions={0} | all-to-all | bytes 884736 | tf_op jit(solution)/shard_map/all_to_all | solution.py:139
  58.6 2.3 copy.8
  61.0 4.8 %all-to-all-start.2 = ((bf16[16,256,192]{1,2,0:T(8,128)(2,1)}), bf16[16,256,192]{1,2,0:T(8,128)(2,1)}, u32[]{:S(2)}, u32[]{:S(2)}) async-start(bf16[16,256,192]{1,2,0:T(8,128)(2,1)} %copy.8), calls=%async_computation.2 | async-start | bytes 3145728 | tf_op jit(solution)/shard_map/all_to_all | solution.py:161
  65.8 2.3 collective-permute-start
  68.2 1.0 collective-permute-done
  69.1 0.9 convolution_convert_fusion
  70.1 2.3 collective-permute-start.1
  72.4 2.1 collective-permute-start.2
  74.5 2.3 collective-permute-start.3
  76.7 58.8 %all-gather.2.cloned.1.call-done = bf16[512,1536]{1,0:T(8,128)(2,1)} async-done(((bf16[32,1536]{1,0:T(8,128)(2,1)}), bf16[512,1536]{1,0:T(8,128)(2,1)}) %all-gather.2.cloned.1.call-update) | async-done | bytes 1572880 | tf_op jit(solution)/shard_map/all_gather | solution.py:152
  135.5 2.1 fusion.3
  137.7 2.5 fusion
  140.2 4.8 %all-to-all-start.1 = ((bf16[4,128,512]{2,1,0:T(8,128)(2,1)}), bf16[4,128,512]{2,1,0:T(8,128)(2,1)S(1)}, u32[]{:S(2)}, u32[]{:S(2)}) async-start(bf16[4,128,512]{2,1,0:T(8,128)(2,1)} %bitcast.31), calls=%async_computation.1 | async-start | bytes 1048576 | tf_op jit(solution)/shard_map/all_to_all | solution.py:173
  145.0 3.7 %copy.9 = bf16[16,256,192]{2,1,0:T(8,128)(2,1)} copy(bf16[16,256,192]{1,2,0:T(8,128)(2,1)} %all-to-all-done.2) | data formatting | bytes 3145728 | tf_op jit(solution)/shard_map/all_to_all | solution.py:161
  148.8 5.3 %shard_map.74 = bf16[8,2,32,1024]{3,2,1,0:T(8,128)(2,1)} custom-call(s32[1]{0:T(128)} %bitcast.2.core_ref, bf16[2,4,2,256,192]{4,3,2,1,0:T(8,128)(2,1)} %bitcast.29, bf16[768,512]{1,0:T(8,128)(2,1)S(1)} %bitcast.24, bf16[768,512]{1,0:T(8,128)(2,1)S(1)} %bitcast.27, bf16[768,512]{1,0:T(8,128)(2,1)} %collective-permute-done.2.gate_far_ref, ...), custom_call_target="tpu_custom_call" | custom-call | tf_op jit(solution)/shard_map/pallas_call | solution.py:164
  154.0 4.8 %all-to-all-start.3 = ((bf16[4,128,1024]{2,1,0:T(8,128)(2,1)}), bf16[4,128,1024]{2,1,0:T(8,128)(2,1)S(1)}, u32[]{:S(2)}, u32[]{:S(2)}) async-start(bf16[4,128,1024]{2,1,0:T(8,128)(2,1)} %bitcast.10), calls=%async_computation.3 | async-start | bytes 2097152 | tf_op jit(solution)/shard_map/all_to_all | solution.py:168
  158.9 13.1 %all-to-all-done.3 = bf16[4,128,1024]{2,1,0:T(8,128)(2,1)S(1)} async-done(((bf16[4,128,1024]{2,1,0:T(8,128)(2,1)}), bf16[4,128,1024]{2,1,0:T(8,128)(2,1)S(1)}, u32[]{:S(2)}, u32[]{:S(2)}) %all-to-all-start.3) | async-done | bytes 1048608 | tf_op jit(solution)/shard_map/all_to_all | solution.py:168
  172.5 13.4 %all_to_all.44 = bf16[4,128,1024]{2,1,0:T(8,128)(2,1)S(1)} all-to-all(bf16[4,128,1024]{2,1,0:T(8,128)(2,1)S(1)} %broadcast_in_dim.31), channel_id=1, replica_groups=mesh['zh'=8,'zl'=2,'x'=4,'c'=2,'y'=4] {'x'}, dimensions={0} | all-to-all | bytes 2097152 | tf_op jit(solution)/shard_map/all_to_all | solution.py:184
  186.0 5.1 %shard_map.75 = bf16[2,4,2,256,192]{4,3,2,1,0:T(8,128)(2,1)} custom-call(s32[1]{0:T(128)} %bitcast.2.core_ref, bf16[8,2,32,1024]{3,2,1,0:T(8,128)(2,1)S(1)} %bitcast.22, bf16[768,512]{1,0:T(8,128)(2,1)S(1)} %bitcast.25, bf16[768,512]{1,0:T(8,128)(2,1)S(1)} %bitcast.28, bf16[768,512]{1,0:T(8,128)(2,1)} %collective-permute-done.2.gate_far_ref, ...), custom_call_target="tpu_custom_call" | custom-call | tf_op jit(solution)/shard_map/pallas_call | solution.py:188
  191.0 3.1 %copy.10 = bf16[16,256,192]{1,2,0:T(8,128)(2,1)S(1)} copy(bf16[16,256,192]{2,1,0:T(8,128)(2,1)} %bitcast.30) | data formatting | bytes 3145728 | tf_op jit(solution)/shard_map/reshape | solution.py:192
  194.1 26.6 %all_to_all.45 = bf16[16,256,192]{1,2,0:T(8,128)(2,1)} all-to-all(bf16[16,256,192]{1,2,0:T(8,128)(2,1)S(1)} %copy.10), channel_id=1, replica_groups=mesh['zh'=8,'zl'=2,'x'=4,'c'=2,'y'=4] {'c','y','zl'}, dimensions={0} | all-to-all | bytes 3145728 | tf_op jit(solution)/shard_map/all_to_all | solution.py:191
  220.7 2.7 %copy.11 = bf16[16,256,192]{2,1,0:T(8,128)(2,1)S(1)} copy(bf16[16,256,192]{1,2,0:T(8,128)(2,1)} %all_to_all.45) | data formatting | bytes 3145728 | tf_op jit(solution)/shard_map/all_to_all | solution.py:191
  224.2 34.3 %all_to_all.46 = bf16[8,128,192]{1,2,0:T(8,128)(2,1)S(1)} all-to-all(bf16[8,128,192]{1,2,0:T(8,128)(2,1)S(1)} %copy.12), channel_id=1, replica_groups=mesh['zh'=8,'zl'=2,'x'=4,'c'=2,'y'=4] {'zh'}, dimensions={0} | all-to-all | bytes 786432 | tf_op jit(solution)/shard_map/all_to_all | solution.py:197
  (40 shorter events, 2.9 us)
Async XLA Ops:
  6.5 1.0 copy-start
  60.9 4.8 %copy-start.7 = (bf16[128,768]{1,0:T(8,128)(2,1)S(1)}, bf16[128,768]{1,0:T(8,128)(2,1)}, u32[]{:S(2)}) copy-start(bf16[128,768]{1,0:T(8,128)(2,1)} %param.8) | copy-start | bytes 589828
  60.9 7.2 %copy-start.5 = (s32[128,2]{0,1:T(2,128)S(1)}, s32[128,2]{0,1:T(2,128)}, u32[]{:S(2)}) copy-start(s32[128,2]{0,1:T(2,128)} %param.9) | copy-start | bytes 3076
  60.9 7.2 %copy-start.6 = (s32[128,2]{0,1:T(2,128)S(1)}, s32[128,2]{0,1:T(2,128)}, u32[]{:S(2)}) copy-start(s32[128,2]{0,1:T(2,128)} %param.10) | copy-start | bytes 3076
  60.9 11.4 %copy-start.1 = (bf16[1,768,512]{2,1,0:T(8,128)(2,1)S(1)}, bf16[1,768,512]{2,1,0:T(8,128)(2,1)}, u32[]{:S(2)}) copy-start(bf16[1,768,512]{2,1,0:T(8,128)(2,1)} %param.11) | copy-start | bytes 2359300
  61.0 13.5 %copy-start.2 = (bf16[1,768,512]{2,1,0:T(8,128)(2,1)S(1)}, bf16[1,768,512]{2,1,0:T(8,128)(2,1)}, u32[]{:S(2)}) copy-start(bf16[1,768,512]{2,1,0:T(8,128)(2,1)} %param.12) | copy-start | bytes 2359300
  61.0 79.2 %all-to-all-start.2 = ((bf16[16,256,192]{1,2,0:T(8,128)(2,1)}), bf16[16,256,192]{1,2,0:T(8,128)(2,1)}, u32[]{:S(2)}, u32[]{:S(2)}) async-start(bf16[16,256,192]{1,2,0:T(8,128)(2,1)} %copy.8), calls=%async_computation.2 | async-start | bytes 3145728 | tf_op jit(solution)/shard_map/all_to_all | solution.py:161
  65.7 69.8 %all-gather.2.cloned.1.call-start = ((), (), s32[]{:S(2)}) async-start(), calls=%async_computation.7 | async-start | bytes 1671168 | tf_op jit(solution)/shard_map/all_gather | solution.py:152
  65.8 3.3 %collective-permute-start = (bf16[128,768]{1,0:T(8,128)(2,1)S(1)}, bf16[128,768]{1,0:T(8,128)(2,1)S(1)}, u32[]{:S(2)}, u32[]{:S(2)}) collective-permute-start(bf16[128,768]{1,0:T(8,128)(2,1)S(1)} %copy-done.7), channel_id=1, source_target_pairs={{0,4},{4,0},{1,5},{5,1},{2,6},{6,2},{3,7},{7,3},{8,12},{12,8},{9,1... | collective-permute-start | bytes 589832 | tf_op jit(solution)/shard_map/ppermute | solution.py:133
  70.1 67.5 %collective-permute-start.1 = (bf16[512,768]{1,0:T(8,128)(2,1)}, bf16[512,768]{1,0:T(8,128)(2,1)}, u32[]{:S(2)}, u32[]{:S(2)}) collective-permute-start(bf16[512,768]{1,0:T(8,128)(2,1)} %bitcast.32), channel_id=1, source_target_pairs={{0,4},{4,0},{1,5},{5,1},{2,6},{6,2},{3,7},{7,3},{8,12},{12,8},{9,1... | collective-permute-start | bytes 2359304 | tf_op jit(solution)/shard_map/ppermute | solution.py:156
  72.4 76.4 %collective-permute-start.2 = (bf16[768,512]{1,0:T(8,128)(2,1)S(1)}, bf16[768,512]{1,0:T(8,128)(2,1)}, u32[]{:S(2)}, u32[]{:S(2)}) collective-permute-start(bf16[768,512]{1,0:T(8,128)(2,1)S(1)} %bitcast.23), channel_id=1, source_target_pairs={{0,4},{4,0},{1,5},{5,1},{2,6},{6,2},{3,7},{7,3},{8,12},{12,8},{9,1... | collective-permute-start | bytes 2359304 | tf_op jit(solution)/shard_map/ppermute | solution.py:154
  74.5 74.3 %collective-permute-start.3 = (bf16[768,512]{1,0:T(8,128)(2,1)S(1)}, bf16[768,512]{1,0:T(8,128)(2,1)}, u32[]{:S(2)}, u32[]{:S(2)}) collective-permute-start(bf16[768,512]{1,0:T(8,128)(2,1)S(1)} %bitcast.26), channel_id=1, source_target_pairs={{0,4},{4,0},{1,5},{5,1},{2,6},{6,2},{3,7},{7,3},{8,12},{12,8},{9,1... | collective-permute-start | bytes 2359304 | tf_op jit(solution)/shard_map/ppermute | solution.py:155
  135.5 2.1 copy-start.4
  140.2 13.9 %all-to-all-start.1 = ((bf16[4,128,512]{2,1,0:T(8,128)(2,1)}), bf16[4,128,512]{2,1,0:T(8,128)(2,1)S(1)}, u32[]{:S(2)}, u32[]{:S(2)}) async-start(bf16[4,128,512]{2,1,0:T(8,128)(2,1)} %bitcast.31), calls=%async_computation.1 | async-start | bytes 1048576 | tf_op jit(solution)/shard_map/all_to_all | solution.py:173
  154.0 18.0 %all-to-all-start.3 = ((bf16[4,128,1024]{2,1,0:T(8,128)(2,1)}), bf16[4,128,1024]{2,1,0:T(8,128)(2,1)S(1)}, u32[]{:S(2)}, u32[]{:S(2)}) async-start(bf16[4,128,1024]{2,1,0:T(8,128)(2,1)} %bitcast.10), calls=%async_computation.3 | async-start | bytes 2097152 | tf_op jit(solution)/shard_map/all_to_all | solution.py:168
  172.4 13.6 %copy-start.3 = (bf16[1,768,512]{2,1,0:T(8,128)(2,1)S(1)}, bf16[1,768,512]{2,1,0:T(8,128)(2,1)}, u32[]{:S(2)}) copy-start(bf16[1,768,512]{2,1,0:T(8,128)(2,1)} %param.12) | copy-start | bytes 2359300
Sparse Core Ops, SparseCore 0:
  70.2 65.2 all-gather.1

commit v2 on v1

v2 whole, which is shorter than its diff:
```python
import functools

import jax
import jax.numpy as jnp
from jax import lax
from jax.experimental import pallas as pl
from jax.experimental.pallas import tpu as pltpu
from jax.sharding import Mesh
from jax.sharding import PartitionSpec as P

unit_scale = 1.0 / 65536.0
window = 4
table_rows = 16
block_step = 1024
bf16 = jnp.bfloat16
f32 = jnp.float32
contract_last = (((1,), (1,)), ((), ()))
swap_cores = [(0, 1), (1, 0)]
group = ("c", "zl", "y")
vmem_bytes = 48 * 1024 * 1024


def kernel_call(body, out_shape, n_in, scalars=0):
    vmem = pl.BlockSpec(memory_space=pltpu.VMEM)
    smem = pl.BlockSpec(memory_space=pltpu.SMEM)
    return pl.pallas_call(
        body,
        out_shape=out_shape,
        in_specs=[smem] * scalars + [vmem] * n_in,
        out_specs=jax.tree.map(lambda _: vmem, out_shape),
        compiler_params=pltpu.CompilerParams(vmem_limit_bytes=vmem_bytes),
    )


def slot_map(experts):
    count = experts.shape[0]
    ids = lax.broadcasted_iota(jnp.int32, (window, count), 0)
    named = (experts[:, 0][None, :] == ids) | (experts[:, 1][None, :] == ids)
    before = lax.broadcasted_iota(jnp.int32, (count, count), 0) <= lax.broadcasted_iota(
        jnp.int32, (count, count), 1
    )
    order = jnp.dot(named.astype(bf16), before.astype(bf16), preferred_element_type=f32)
    return jnp.where(named, order - 1.0, -1.0)


def selects(pay_ref, first, blocks, part):
    count = pay_ref.shape[2]
    top = pay_ref.shape[1] - table_rows
    table = jnp.concatenate(
        [
            pay_ref[first + i, top:, :].astype(f32)[:window] + float(i * block_step)
            for i in range(blocks)
        ],
        axis=1,
    )
    row = lax.broadcasted_iota(jnp.int32, (blocks * part, blocks * count), 0)
    slot = (row // part * block_step + row % part).astype(f32)
    return [
        [
            jnp.where(table[e : e + 1] == slot + float(core * part), 1.0, 0.0).astype(bf16)
            for core in range(2)
        ]
        for e in range(window)
    ]


def pick_kernel(pay_ref, out_ref):
    n_blocks, rows, count = pay_ref.shape
    top = rows - table_rows
    part = out_ref.shape[-1] // n_blocks
    blocks = 128 // part
    for first in range(0, n_blocks, blocks):
        dense = jnp.concatenate([pay_ref[first + i, :top, :] for i in range(blocks)], axis=1)
        span = slice(first * part, (first + blocks) * part)
        for e, select in enumerate(selects(pay_ref, first, blocks, part)):
            for core in range(2):
                picked = lax.dot_general(
                    dense, select[core], contract_last, preferred_element_type=f32
                ).astype(bf16)
                out_ref[core, 0, e, :, span] = picked
                out_ref[core, 1, e, :, span] = picked


def pair_kernel(n_x, gate_ref, up_ref, out_ref, flip_ref):
    share = gate_ref.shape[1] // n_x
    for i in range(2 * n_x):
        ref, begin = (gate_ref, up_ref)[i % 2], i // 2 * share
        piece = ref[:, begin : begin + share]
        out_ref[:, i * share : (i + 1) * share] = piece
        flip_ref[i * share : (i + 1) * share, :] = piece.T


def joined_kernel(core_ref, x_ref, near_ref, far_ref, out_ref):
    core = core_ref[0]
    width = x_ref.shape[-1]
    for pair in range(2):
        total = jnp.dot(near_ref[...], x_ref[core, pair], preferred_element_type=f32)
        total += jnp.dot(far_ref[...], x_ref[1 - core, pair], preferred_element_type=f32)
        out_ref[:, pair * width : (pair + 1) * width] = total.astype(bf16)


def back_kernel(rows_ref, near_ref, far_ref, out_ref):
    blocks, _, part, feats = rows_ref.shape
    width = blocks * part
    half = feats // 2
    for pair in range(2):
        rows = rows_ref[:, pair].reshape(width, feats)
        total = lax.dot_general(
            near_ref[...], rows[:, :half], contract_last, preferred_element_type=f32
        )
        total += lax.dot_general(
            far_ref[...], rows[:, half:], contract_last, preferred_element_type=f32
        )
        out_ref[:, pair * width : (pair + 1) * width] = total.astype(bf16)


def grad_kernel(joined_ref, back_ref, out_ref):
    n_x, hidden, _ = back_ref.shape
    gate_sum, up_sum, back_sum = (
        sum(ref[i, begin : begin + hidden, :].astype(f32) for i in range(n_x))
        for ref, begin in ((joined_ref, 0), (joined_ref, hidden), (back_ref, 0))
    )
    sigmoid_gate = jax.nn.sigmoid(gate_sum)
    grad_up = (back_sum * (gate_sum * sigmoid_gate)).astype(bf16)
    grad_gate = (
        back_sum * up_sum * sigmoid_gate * (1.0 + gate_sum * (1.0 - sigmoid_gate))
    ).astype(bf16)
    for i in range(n_x):
        out_ref[i, :hidden, :] = grad_gate
        out_ref[i, hidden:, :] = grad_up


def result_kernel(core_ref, g_ref, near_ref, far_ref, out_ref):
    core = core_ref[0]
    width = out_ref.shape[-1]
    for side, weight in ((core, near_ref), (1 - core, far_ref)):
        rows = jnp.dot(weight[...], g_ref[...], preferred_element_type=f32).astype(bf16)
        for pair in range(2):
            out_ref[side, pair] = rows[:, pair * width : (pair + 1) * width]


def combine_kernel(pay_ref, rows_ref, out_ref):
    n_blocks, quarter, count = out_ref.shape
    part = rows_ref.shape[-1] // n_blocks
    blocks = 128 // part
    for first in range(0, n_blocks, blocks):
        span = slice(first * part, (first + blocks) * part)
        total = None
        for e, select in enumerate(selects(pay_ref, first, blocks, part)):
            values = jnp.concatenate(
                [rows_ref[core, pair, e, :, span] for core in range(2) for pair in range(2)],
                axis=1,
            )
            chosen = jnp.concatenate([select[core] for core in range(2) for _ in range(2)], axis=0)
            term = jnp.dot(values, chosen, preferred_element_type=f32)
            total = term if total is None else total + term
        for i in range(blocks):
            out_ref[first + i] = total[:, i * count : (i + 1) * count].astype(bf16)


def token_path(args):
    pay, gate, up, down, core_id = args
    n_high, n_x = lax.axis_size("zh"), lax.axis_size("x")
    count = pay.shape[1]
    quarter = pay.shape[0] - table_rows
    feats, hidden = gate.shape
    width = n_high * count // 4
    pay = lax.all_to_all(
        jnp.broadcast_to(pay[None], (n_high, *pay.shape)), "zh", 0, 0, tiled=True
    )
    paired, paired_t = kernel_call(
        functools.partial(pair_kernel, n_x),
        (
            jax.ShapeDtypeStruct((feats, 2 * hidden), bf16),
            jax.ShapeDtypeStruct((2 * hidden, feats), bf16),
        ),
        2,
    )(gate, up)
    paired_far = lax.ppermute(paired, "c", swap_cores)
    paired_t_far = lax.ppermute(paired_t, "c", swap_cores)
    down_far = lax.ppermute(down, "c", swap_cores)
    picks = kernel_call(
        pick_kernel, jax.ShapeDtypeStruct((2, 2, window, quarter, width), bf16), 1
    )(pay)
    rows_in = lax.all_to_all(
        picks.reshape(4 * window, quarter, width), group, 0, 0, tiled=True
    ).reshape(2, 2, feats, width)
    joined = kernel_call(
        joined_kernel, jax.ShapeDtypeStruct((2 * hidden, 2 * width), bf16), 3, 1
    )(core_id, rows_in, paired_t, paired_t_far)
    return pay, joined, paired, paired_far, down_far


def per_device(tokens, cotangent, experts, route_weight, gate_weight, up_weight, down_weight):
    core, expert_id = lax.axis_index("c"), lax.axis_index("y")
    n_high, n_x = lax.axis_size("zh"), lax.axis_size("x")
    n_group = 4 * window
    count, feats = tokens.shape
    quarter = feats // window
    part = count // 4
    width = n_high * part
    gate, up, down = gate_weight[0], up_weight[0], down_weight[0]
    hidden = gate.shape[1]
    share_h = hidden // n_x
    core_id = core.reshape(1).astype(jnp.int32)

    cot_far = lax.ppermute(cotangent, "c", swap_cores)
    table = slot_map(experts)
    share = (
        jnp.sum(jnp.where(experts == expert_id, route_weight, 0), axis=1).astype(f32) * unit_scale
    )
    own_slots = lax.dynamic_slice_in_dim(table, expert_id, 1, axis=0)
    slot_ids = lax.broadcasted_iota(jnp.int32, (part, count), 0) + core * part
    select_half = jnp.where(own_slots == slot_ids.astype(f32), 1.0, 0.0).astype(bf16)
    both = jnp.concatenate([cotangent, cot_far], axis=1)
    scaled = (share[:, None] * both.astype(f32)).astype(bf16)
    picked = jnp.dot(select_half, scaled, preferred_element_type=f32).astype(bf16)
    rows_grad = lax.all_gather(picked, ("zh", "zl"), axis=0, tiled=True)

    own_quarter = lax.dynamic_slice_in_dim(tokens, expert_id * quarter, quarter, axis=1)
    table_pad = jnp.pad(table.astype(bf16), ((0, table_rows - window), (0, 0)))
    pay = jnp.concatenate([own_quarter.T, table_pad], axis=0)
    pay, joined, paired, paired_far, down_far = lax.cond(
        route_weight[0, 0] > 0, token_path, token_path, (pay, gate, up, down, core_id)
    )
    joined = lax.all_to_all(
        joined.reshape(n_x, 2 * share_h, 2 * width), "x", 0, 0, tiled=True
    )

    back = kernel_call(back_kernel, jax.ShapeDtypeStruct((hidden, 2 * width), bf16), 3)(
        rows_grad.reshape(n_high, 2, part, 2 * feats), down, down_far
    )
    back = lax.all_to_all(back.reshape(n_x, share_h, 2 * width), "x", 0, 0, tiled=True)

    grads = kernel_call(
        grad_kernel, jax.ShapeDtypeStruct((n_x, 2 * share_h, 2 * width), bf16), 2
    )(joined, back)
    grads = lax.all_to_all(grads, "x", 0, 0, tiled=True).reshape(2 * hidden, 2 * width)

    result = kernel_call(
        result_kernel, jax.ShapeDtypeStruct((2, 2, feats, width), bf16), 3, 1
    )(core_id, grads, paired, paired_far)
    result = lax.all_to_all(
        result.reshape(n_group, quarter, width), group, 0, 0, tiled=True
    )
    dense = kernel_call(
        combine_kernel, jax.ShapeDtypeStruct((n_high, quarter, count), bf16), 2
    )(pay, result.reshape(2, 2, window, quarter, width))
    dense = lax.all_to_all(dense, "zh", 0, 0, tiled=True)
    return jnp.sum(dense.astype(f32), axis=0).astype(bf16).T


def solution(mesh):
    split = Mesh(
        mesh.devices.reshape(mesh.shape["seq"] // 2, 2, mesh.shape["etp"] // 2, 2, -1),
        ("zh", "zl", "x", "c", "y"),
    )
    seq, etp = ("zh", "zl"), ("x", "c")
    placed = (
        P(seq, etp),
        P(seq, etp),
        P(seq, None),
        P(seq, None),
        P("y", etp, seq),
        P("y", etp, seq),
        P("y", seq, etp),
    )
    return jax.shard_map(
        per_device, mesh=split, in_specs=placed, out_specs=P(seq, ("x", "c", "y")), check_vma=False
    )
```

time: 267 us -> 220 us (0.82)
  the two profiles are of different devices: /device:TPU:2 before, /device:TPU:1 now
where the time goes in v2:
time: 220 us; the launch traced here: 219 us
  blocking collectives  124 us (56%)
  waiting for transfers between devices  28.2 us (13%)
  starting transfers between devices  26 us (12%)
  Pallas kernels  16.4 us (7%)
  between operations  14.1 us (6%)
  local copies, waits for them, and re-layouts  7.15 us (3%)
    all_to_all x1, blocking collectives, token_path(): lax.all_to_all(jnp.broadcast_to(pay[None], (n_high, *pay.shape)), 'zh', 0...  41 us
    all_to_all x1, blocking collectives, per_device(): dense = lax.all_to_all(dense, 'zh', 0, 0, tiled=True)  29.4 us
    all_to_all x1, blocking collectives, per_device(): lax.all_to_all(result.reshape(n_group, quarter, width), group, 0, 0, tile...  28 us
    all_to_all x1, waiting for transfers between devices, token_path(): lax.all_to_all(picks.reshape(4 * window, quarter, width), group, 0, 0, ti...  17.3 us
    all_to_all x1, blocking collectives, per_device(): lax.all_to_all(grads, 'x', 0, 0, tiled=True).reshape(2 * hidden, 2 * width)  15 us
    all_to_all x1, waiting for transfers between devices, per_device(): lax.all_to_all(joined.reshape(n_x, 2 * share_h, 2 * width), 'x', 0, 0, ti...  10.9 us
    all_to_all x1, blocking collectives, per_device(): lax.all_to_all(back.reshape(n_x, share_h, 2 * width), 'x', 0, 0, tiled=True)  10.3 us
    ppermute x1, starting transfers between devices, per_device(): cot_far = lax.ppermute(cotangent, 'c', swap_cores)  8.91 us
  transfers between devices with their start and end apart: 7, of which 2 were waited for; matrix products, arithmetic and copies ran while one was open for 1% of the time, Pallas kernels for 5%

profile of v2, /device:TPU:1, one launch (start us, length us, event | category | flops | bytes accessed | tf_op | source)
XLA Modules:
  0.0 219.0 jit_solution(3602455667390223392)
XLA Ops:
  6.5 8.9 %collective-permute-start.6 = (bf16[128,768]{1,0:T(8,128)(2,1)}, bf16[128,768]{1,0:T(8,128)(2,1)S(1)}, u32[]{:S(2)}, u32[]{:S(2)}) collective-permute-start(bf16[128,768]{1,0:T(8,128)(2,1)} %param.10), channel_id=1, source_target_pairs={{0,4},{4,0},{1,5},{5,1},{2,6},{6,2},{3,7},{7,3},{8,12},{12,8},{9,1... | collective-permute-start | bytes 589832 | tf_op jit(solution)/shard_map/ppermute | solution.py:207
  17.1 1.9 convolution_convert_fusion
  19.0 1.2 slice.9
  21.1 82.1 %conditional.1 = (bf16[8,208,128]{2,1,0:T(8,128)(2,1)}, bf16[1024,512]{1,0:T(8,128)(2,1)S(1)}, bf16[768,1024]{1,0:T(8,128)(2,1)}, bf16[768,1024]{1,0:T(8,128)(2,1)}, bf16[512,768]{1,0:T(8,128)(2,1)}) conditional(s32[]{:T(128)} %bitcast.4, (bf16[208,128]{1,0:T(8,128)(2,1)S(1)}, bf16[768,512]{1,0:T(8,128)(2,1)}, bf16[768,512]{1,0:T(8,128)(2,1)}, ...), branch_computations={%region_0.1_spmd, %region_1.2_spmd} | conditional | bytes 34361592 | solution.py:223
  21.2 41.0 %all_to_all.42.pay_ref = bf16[8,208,128]{2,1,0:T(8,128)(2,1)} all-to-all(bf16[8,208,128]{2,1,0:T(8,128)(2,1)S(1)} %broadcast_in_dim.18), channel_id=1, replica_groups=mesh['zh'=8,'zl'=2,'x'=4,'c'=2,'y'=4] {'zh'}, dimensions={0} | all-to-all | bytes 851968 | tf_op jit(solution)/shard_map/cond/branch_1_fun/all_to_all | solution.py:168
  62.1 3.2 %branch_1_fun.3 = bf16[2,2,4,192,256]{4,3,2,1,0:T(8,128)(2,1)} custom-call(bf16[8,208,128]{2,1,0:T(8,128)(2,1)} %all_to_all.42.pay_ref), custom_call_target="tpu_custom_call" | custom-call | tf_op jit(solution)/shard_map/cond/branch_1_fun/pallas_call | solution.py:182
  65.3 6.8 %all-to-all-start.3 = ((bf16[16,192,256]{2,1,0:T(8,128)(2,1)}), bf16[16,192,256]{2,1,0:T(8,128)(2,1)S(1)}, u32[]{:S(2)}, u32[]{:S(2)}) async-start(bf16[16,192,256]{2,1,0:T(8,128)(2,1)} %bitcast.2), calls=%async_computation.3 | async-start | bytes 3145728 | tf_op jit(solution)/shard_map/cond/branch_1_fun/all_to_all | solution.py:185
  72.1 3.1 %branch_1_fun.4 = (bf16[768,1024]{1,0:T(8,128)(2,1)}, bf16[1024,768]{1,0:T(8,128)(2,1)S(1)}) custom-call(bf16[768,512]{1,0:T(8,128)(2,1)} %get-tuple-element.34.gate_ref, bf16[768,512]{1,0:T(8,128)(2,1)} %get-tuple-element.35.up_ref), custom_call_target="tpu_custom_call" | custom-call | tf_op jit(solution)/shard_map/cond/branch_1_fun/pallas_call | solution.py:171
  75.1 2.0 collective-permute-start.3
  77.1 2.3 %collective-permute-start.4 = (bf16[768,1024]{1,0:T(8,128)(2,1)}, bf16[768,1024]{1,0:T(8,128)(2,1)}, u32[]{:S(2)}, u32[]{:S(2)}) collective-permute-start(bf16[768,1024]{1,0:T(8,128)(2,1)} %get-tuple-element.60), channel_id=1, source_target_pairs={{0,4},{4,0},{1,5},{5,1},{2,6},{6,2},{3,7},{7,3},{8,12},{12,8},{9,1... | collective-permute-start | bytes 4718600 | tf_op jit(solution)/shard_map/cond/branch_1_fun/ppermute | solution.py:179
  79.5 2.0 collective-permute-start.5
  82.6 17.3 %all-to-all-done.3 = bf16[16,192,256]{2,1,0:T(8,128)(2,1)S(1)} async-done(((bf16[16,192,256]{2,1,0:T(8,128)(2,1)}), bf16[16,192,256]{2,1,0:T(8,128)(2,1)S(1)}, u32[]{:S(2)}, u32[]{:S(2)}) %all-to-all-start.3) | async-done | bytes 1572896 | tf_op jit(solution)/shard_map/cond/branch_1_fun/all_to_all | solution.py:185
  99.9 1.4 copy-done.5
  101.3 1.8 branch_1_fun.5
  104.1 4.0 %all-to-all-start.4 = ((bf16[4,256,512]{2,1,0:T(8,128)(2,1)}), bf16[4,256,512]{2,1,0:T(8,128)(2,1)S(1)}, u32[]{:S(2)}, u32[]{:S(2)}) async-start(bf16[4,256,512]{2,1,0:T(8,128)(2,1)} %bitcast.30), calls=%async_computation.4 | async-start | bytes 2097152 | tf_op jit(solution)/shard_map/all_to_all | solution.py:226
  108.2 1.4 copy-done.1
  109.6 2.4 %shard_map.73 = bf16[512,512]{1,0:T(8,128)(2,1)S(1)} custom-call(bf16[8,2,32,1536]{3,2,1,0:T(8,128)(2,1)S(1)} %bitcast.29, bf16[512,768]{1,0:T(8,128)(2,1)} %bitcast.11.near_ref, bf16[512,768]{1,0:T(8,128)(2,1)} %get-tuple-element.46.far_ref), custom_call_target="tpu_custom_call" | custom-call | tf_op jit(solution)/shard_map/pallas_call | solution.py:230
  112.0 10.9 %all-to-all-done.4.joined_ref = bf16[4,256,512]{2,1,0:T(8,128)(2,1)S(1)} async-done(((bf16[4,256,512]{2,1,0:T(8,128)(2,1)}), bf16[4,256,512]{2,1,0:T(8,128)(2,1)S(1)}, u32[]{:S(2)}, u32[]{:S(2)}) %all-to-all-start.4) | async-done | bytes 1048608 | tf_op jit(solution)/shard_map/all_to_all | solution.py:226
  122.9 10.3 %all_to_all.43.back_ref = bf16[4,128,512]{2,1,0:T(8,128)(2,1)S(1)} all-to-all(bf16[4,128,512]{2,1,0:T(8,128)(2,1)S(1)} %bitcast.28), channel_id=1, replica_groups=mesh['zh'=8,'zl'=2,'x'=4,'c'=2,'y'=4] {'x'}, dimensions={0} | all-to-all | bytes 1048576 | tf_op jit(solution)/shard_map/all_to_all | solution.py:233
  133.4 15.0 %all_to_all.44 = bf16[4,256,512]{2,1,0:T(8,128)(2,1)S(1)} all-to-all(bf16[4,256,512]{2,1,0:T(8,128)(2,1)S(1)} %shard_map.74), channel_id=1, replica_groups=mesh['zh'=8,'zl'=2,'x'=4,'c'=2,'y'=4] {'x'}, dimensions={0} | all-to-all | bytes 2097152 | tf_op jit(solution)/shard_map/all_to_all | solution.py:238
  148.4 3.7 %shard_map.75 = bf16[2,2,768,256]{3,2,1,0:T(8,128)(2,1)S(1)} custom-call(s32[1]{0:T(128)} %bitcast.10.core_ref, bf16[1024,512]{1,0:T(8,128)(2,1)S(1)} %bitcast.27, bf16[768,1024]{1,0:T(8,128)(2,1)} %get-tuple-element.47.near_ref, bf16[768,1024]{1,0:T(8,128)(2,1)} %get-tuple-element.48.far_ref), custom_call_target="tpu_custom_call" | custom-call | tf_op jit(solution)/shard_map/pallas_call | solution.py:240
  152.1 28.0 %all_to_all.45 = bf16[16,192,256]{2,1,0:T(8,128)(2,1)S(1)} all-to-all(bf16[16,192,256]{2,1,0:T(8,128)(2,1)S(1)} %bitcast.26), channel_id=1, replica_groups=mesh['zh'=8,'zl'=2,'x'=4,'c'=2,'y'=4] {'c','zl','y'}, dimensions={0} | all-to-all | bytes 3145728 | tf_op jit(solution)/shard_map/all_to_all | solution.py:243
  180.1 2.0 shard_map.76
  182.1 29.4 %all_to_all.46 = bf16[8,192,128]{2,1,0:T(8,128)(2,1)S(1)} all-to-all(bf16[8,192,128]{2,1,0:T(8,128)(2,1)S(1)} %shard_map.76), channel_id=1, replica_groups=mesh['zh'=8,'zl'=2,'x'=4,'c'=2,'y'=4] {'zh'}, dimensions={0} | all-to-all | bytes 786432 | tf_op jit(solution)/shard_map/all_to_all | solution.py:249
  (27 shorter events, 5.0 us)
Async XLA Ops:
  6.5 13.6 %copy-start = (bf16[128,768]{1,0:T(8,128)(2,1)S(1)}, bf16[128,768]{1,0:T(8,128)(2,1)}, u32[]{:S(2)}) copy-start(bf16[128,768]{1,0:T(8,128)(2,1)} %param.9) | copy-start | bytes 589828
  6.5 101.6 %all-gather.2.cloned.1.call-start = ((), (), s32[]{:S(2)}) async-start(), calls=%async_computation.9 | async-start | bytes 1671168 | tf_op jit(solution)/shard_map/all_gather | solution.py:218
  6.5 10.6 %collective-permute-start.6 = (bf16[128,768]{1,0:T(8,128)(2,1)}, bf16[128,768]{1,0:T(8,128)(2,1)S(1)}, u32[]{:S(2)}, u32[]{:S(2)}) collective-permute-start(bf16[128,768]{1,0:T(8,128)(2,1)} %param.10), channel_id=1, source_target_pairs={{0,4},{4,0},{1,5},{5,1},{2,6},{6,2},{3,7},{7,3},{8,12},{12,8},{9,1... | collective-permute-start | bytes 589832 | tf_op jit(solution)/shard_map/ppermute | solution.py:207
  65.3 34.6 %all-to-all-start.3 = ((bf16[16,192,256]{2,1,0:T(8,128)(2,1)}), bf16[16,192,256]{2,1,0:T(8,128)(2,1)S(1)}, u32[]{:S(2)}, u32[]{:S(2)}) async-start(bf16[16,192,256]{2,1,0:T(8,128)(2,1)} %bitcast.2), calls=%async_computation.3 | async-start | bytes 3145728 | tf_op jit(solution)/shard_map/cond/branch_1_fun/all_to_all | solution.py:185
  75.1 6.4 %collective-permute-start.3 = (bf16[1024,768]{1,0:T(8,128)(2,1)S(1)}, bf16[1024,768]{1,0:T(8,128)(2,1)S(1)}, u32[]{:S(2)}, u32[]{:S(2)}) collective-permute-start(bf16[1024,768]{1,0:T(8,128)(2,1)S(1)} %get-tuple-element.36.near_ref), channel_id=1, source_target_pairs={{0,4},{4,0},{1,5},{5,1},{2,6},{6,2},{3,7},{7,3},{8,12},{12,8},{9,1... | collective-permute-start | bytes 4718600 | tf_op jit(solution)/shard_map/cond/branch_1_fun/ppermute | solution.py:180
  77.1 26.0 %collective-permute-start.4 = (bf16[768,1024]{1,0:T(8,128)(2,1)}, bf16[768,1024]{1,0:T(8,128)(2,1)}, u32[]{:S(2)}, u32[]{:S(2)}) collective-permute-start(bf16[768,1024]{1,0:T(8,128)(2,1)} %get-tuple-element.60), channel_id=1, source_target_pairs={{0,4},{4,0},{1,5},{5,1},{2,6},{6,2},{3,7},{7,3},{8,12},{12,8},{9,1... | collective-permute-start | bytes 4718600 | tf_op jit(solution)/shard_map/cond/branch_1_fun/ppermute | solution.py:179
  79.5 23.6 %collective-permute-start.5 = (bf16[512,768]{1,0:T(8,128)(2,1)}, bf16[512,768]{1,0:T(8,128)(2,1)}, u32[]{:S(2)}, u32[]{:S(2)}) collective-permute-start(bf16[512,768]{1,0:T(8,128)(2,1)} %get-tuple-element.38), channel_id=1, source_target_pairs={{0,4},{4,0},{1,5},{5,1},{2,6},{6,2},{3,7},{7,3},{8,12},{12,8},{9,1... | collective-permute-start | bytes 2359304 | tf_op jit(solution)/shard_map/cond/branch_1_fun/ppermute | solution.py:181
  81.5 1.1 copy-start.4
  99.9 1.4 copy-start.5
  103.1 1.0 copy-start.6
  104.1 18.7 %all-to-all-start.4 = ((bf16[4,256,512]{2,1,0:T(8,128)(2,1)}), bf16[4,256,512]{2,1,0:T(8,128)(2,1)S(1)}, u32[]{:S(2)}, u32[]{:S(2)}) async-start(bf16[4,256,512]{2,1,0:T(8,128)(2,1)} %bitcast.30), calls=%async_computation.4 | async-start | bytes 2097152 | tf_op jit(solution)/shard_map/all_to_all | solution.py:226
  108.2 1.4 copy-start.1
Sparse Core Ops, SparseCore 0:
  19.1 72.9 all-gather.1

commit v3 on v0

v3 whole, which is shorter than its diff:
```python
import jax
import jax.numpy as jnp
from jax import lax
from jax.experimental import pallas as pl
from jax.experimental.pallas import tpu as pltpu
from jax.sharding import Mesh
from jax.sharding import PartitionSpec as P

unit_scale = 1.0 / 65536.0
window = 4
block_step = 1024
bf16 = jnp.bfloat16
f32 = jnp.float32
contract_last = (((1,), (1,)), ((), ()))
swap_cores = [(0, 1), (1, 0)]
group = ("c", "zl", "y")
vmem_bytes = 48 * 1024 * 1024


def kernel_call(body, out_shape, n_in, scalars=0):
    vmem = pl.BlockSpec(memory_space=pltpu.VMEM)
    smem = pl.BlockSpec(memory_space=pltpu.SMEM)
    return pl.pallas_call(
        body,
        out_shape=out_shape,
        in_specs=[smem] * scalars + [vmem] * n_in,
        out_specs=jax.tree.map(lambda _: vmem, out_shape),
        compiler_params=pltpu.CompilerParams(vmem_limit_bytes=vmem_bytes),
    )


def prep_kernel(
    place_ref, experts_ref, weight_ref, tok_ref, cot_ref, tok_far_ref, cot_far_ref, out_ref
):
    core, expert_id = place_ref[0], place_ref[1]
    part = out_ref.shape[0]
    count, feats = tok_ref.shape
    first, second = experts_ref[0:1, :], experts_ref[1:2, :]
    ids = lax.broadcasted_iota(jnp.int32, (window, count), 0)
    named = (first == ids) | (second == ids)
    before = lax.broadcasted_iota(jnp.int32, (count, count), 0) <= lax.broadcasted_iota(
        jnp.int32, (count, count), 1
    )
    order = jnp.dot(
        jnp.where(named, 1.0, 0.0).astype(bf16),
        jnp.where(before, 1.0, 0.0).astype(bf16),
        preferred_element_type=f32,
    )
    table = jnp.where(named, order - 1.0, -1.0)
    own = jnp.sum(jnp.where(ids == expert_id, table, 0.0), axis=0, keepdims=True)
    share = (
        jnp.where(first == expert_id, weight_ref[0:1, :], 0)
        + jnp.where(second == expert_id, weight_ref[1:2, :], 0)
    ).astype(f32) * unit_scale
    slot = (lax.broadcasted_iota(jnp.int32, (part, count), 0) + core * part).astype(f32)
    hit = own == slot
    select = jnp.where(hit, 1.0, 0.0).astype(bf16)
    slot_share = jnp.sum(jnp.where(hit, share, 0.0), axis=1, keepdims=True)
    for i, ref in enumerate((tok_ref, tok_far_ref, cot_ref, cot_far_ref)):
        picked = jnp.dot(select, ref[...], preferred_element_type=f32)
        if i >= 2:
            picked = slot_share * picked
        out_ref[:, i * feats : (i + 1) * feats] = picked.astype(bf16)
    out_ref[:, 4 * feats :] = jnp.concatenate(
        [table, jnp.zeros((part - window, count), f32)], axis=0
    ).astype(bf16)


def flip_kernel(in_ref, out_ref):
    out_ref[...] = in_ref[...].T


def products_kernel(
    rows_ref, gate_ref, up_ref, down_ref, gate_far_ref, up_far_ref, down_far_ref, out_ref
):
    feats, hidden = gate_ref.shape
    n_x, share, _ = out_ref.shape
    for m, (begin, near, far) in enumerate(
        ((0, gate_ref, gate_far_ref), (0, up_ref, up_far_ref), (2, down_ref, down_far_ref))
    ):
        total = jnp.dot(
            rows_ref[:, begin * feats : (begin + 1) * feats],
            near[...],
            preferred_element_type=f32,
        )
        total += jnp.dot(
            rows_ref[:, (begin + 1) * feats : (begin + 2) * feats],
            far[...],
            preferred_element_type=f32,
        )
        out_ref[:, :, m * hidden : (m + 1) * hidden] = total.astype(bf16).reshape(
            n_x, share, hidden
        )


def grad_kernel(sums_ref, out_ref):
    n_x, _, width = sums_ref.shape
    hidden = width // 3
    gate_sum, up_sum, back_sum = (
        sum(sums_ref[i, :, m * hidden : (m + 1) * hidden].astype(f32) for i in range(n_x))
        for m in range(3)
    )
    sigmoid_gate = jax.nn.sigmoid(gate_sum)
    grad_up = (back_sum * (gate_sum * sigmoid_gate)).astype(bf16)
    grad_gate = (
        back_sum * up_sum * sigmoid_gate * (1.0 + gate_sum * (1.0 - sigmoid_gate))
    ).astype(bf16)
    for i in range(n_x):
        out_ref[i, :, :hidden] = grad_gate
        out_ref[i, :, hidden:] = grad_up


def result_kernel(core_ref, g_ref, gate_ref, up_ref, gate_far_ref, up_far_ref, out_ref):
    core = core_ref[0]
    blocks, _, part, both = g_ref.shape
    hidden = both // 2
    for pair in range(2):
        grads = g_ref[:, pair].reshape(blocks * part, both)
        for side, gate, up in ((core, gate_ref, up_ref), (1 - core, gate_far_ref, up_far_ref)):
            rows = lax.dot_general(
                gate[...], grads[:, :hidden], contract_last, preferred_element_type=f32
            )
            rows += lax.dot_general(
                up[...], grads[:, hidden:], contract_last, preferred_element_type=f32
            )
            out_ref[side, pair] = rows.astype(bf16)


def combine_kernel(pair_ref, table_ref, rows_ref, out_ref):
    pair_id = pair_ref[0]
    n_blocks, quarter, count = out_ref.shape
    part = rows_ref.shape[-1] // n_blocks
    blocks = 128 // part
    row = lax.broadcasted_iota(jnp.int32, (blocks * part, blocks * count), 0)
    slot = (row // part * block_step + row % part).astype(f32)
    for first in range(0, n_blocks, blocks):
        span = slice(first * part, (first + blocks) * part)
        table = jnp.concatenate(
            [
                table_ref[first + i, pair_id].astype(f32)[:window] + float(i * block_step)
                for i in range(blocks)
            ],
            axis=1,
        )
        total = None
        for e in range(window):
            values, chosen = [], []
            for core in range(2):
                select = jnp.where(
                    table[e : e + 1] == slot + float(core * part), 1.0, 0.0
                ).astype(bf16)
                for pair in range(2):
                    values.append(rows_ref[core, pair, e, :, span])
                    chosen.append(select)
            term = jnp.dot(
                jnp.concatenate(values, axis=1),
                jnp.concatenate(chosen, axis=0),
                preferred_element_type=f32,
            )
            total = term if total is None else total + term
        for i in range(blocks):
            out_ref[first + i] = total[:, i * count : (i + 1) * count].astype(bf16)


def per_device(tokens, cotangent, experts, route_weight, gate_weight, up_weight, down_weight):
    core, expert_id = lax.axis_index("c"), lax.axis_index("y")
    n_high, n_x = lax.axis_size("zh"), lax.axis_size("x")
    n_group = 4 * window
    count, feats = tokens.shape
    quarter = feats // window
    part = count // 4
    width = n_high * part
    gate, up, down = gate_weight[0], up_weight[0], down_weight[0]
    hidden = gate.shape[1]
    core_id = core.reshape(1).astype(jnp.int32)
    pair_id = lax.axis_index("zl").reshape(1).astype(jnp.int32)
    place = jnp.stack([core, expert_id]).astype(jnp.int32)

    tok_far = lax.ppermute(tokens, "c", swap_cores)
    cot_far = lax.ppermute(cotangent, "c", swap_cores)
    picked = kernel_call(
        prep_kernel, jax.ShapeDtypeStruct((part, 4 * feats + count), bf16), 6, 1
    )(place, experts.T, route_weight.T, tokens, cotangent, tok_far, cot_far)
    rows = lax.all_gather(picked, ("zh", "zl"), axis=0, tiled=True)

    down_t = kernel_call(flip_kernel, jax.ShapeDtypeStruct((feats, hidden), bf16), 1)(down)
    gate_far, up_far, down_far = (lax.ppermute(w, "c", swap_cores) for w in (gate, up, down_t))

    sums = kernel_call(
        products_kernel, jax.ShapeDtypeStruct((n_x, 2 * width // n_x, 3 * hidden), bf16), 7
    )(rows, gate, up, down_t, gate_far, up_far, down_far)
    sums = lax.all_to_all(sums, "x", 0, 0, tiled=True)
    grads = kernel_call(
        grad_kernel, jax.ShapeDtypeStruct((n_x, 2 * width // n_x, 2 * hidden), bf16), 1
    )(sums)
    grads = lax.all_to_all(grads, "x", 0, 0, tiled=True)

    result = kernel_call(
        result_kernel, jax.ShapeDtypeStruct((2, 2, feats, width), bf16), 5, 1
    )(core_id, grads.reshape(n_high, 2, part, 2 * hidden), gate, up, gate_far, up_far)
    result = lax.all_to_all(result.reshape(n_group, quarter, width), group, 0, 0, tiled=True)
    dense = kernel_call(
        combine_kernel, jax.ShapeDtypeStruct((n_high, quarter, count), bf16), 2, 1
    )(
        pair_id,
        rows[:, 4 * feats :].reshape(n_high, 2, part, count),
        result.reshape(2, 2, window, quarter, width),
    )
    dense = lax.all_to_all(dense, "zh", 0, 0, tiled=True)
    return jnp.sum(dense.astype(f32), axis=0).astype(bf16).T


def solution(mesh):
    split = Mesh(
        mesh.devices.reshape(mesh.shape["seq"] // 2, 2, mesh.shape["etp"] // 2, 2, -1),
        ("zh", "zl", "x", "c", "y"),
    )
    seq, etp = ("zh", "zl"), ("x", "c")
    placed = (
        P(seq, etp),
        P(seq, etp),
        P(seq, None),
        P(seq, None),
        P("y", etp, seq),
        P("y", etp, seq),
        P("y", seq, etp),
    )
    return jax.shard_map(
        per_device, mesh=split, in_specs=placed, out_specs=P(seq, ("x", "c", "y")), check_vma=False
    )
```

time: 380 us -> 215 us (0.57)
  waiting for transfers between devices: 338 us -> 79.7 us
  blocking collectives: 0 us -> 64.1 us
  starting transfers between devices: 0.17 us -> 34.9 us
  matrix products: 20.8 us -> 0 us
  Pallas kernels: 0 us -> 11.9 us
  local copies, waits for them, and re-layouts: 2.61 us -> 9.33 us
    psum x1 -> x0, waiting for transfers between devices: 106 us -> none  [per_device(): lax.psum((gate_part, up_part, back_part), 'etp')]
    reduce_scatter x2 -> x0, waiting for transfers between devices: 101 us -> none  [the longest x1 67.8 us: per_device(): lax.psum_scatter(result + lax.dot_general(grad_up, up_local, contract_las...]
    all_gather x2 -> x1, waiting for transfers between devices: 131 us -> 55.9 us  [per_device(): rows = lax.all_gather(picked, ('zh', 'zl'), axis=0, tiled=True)]
    all_to_all x0 -> x3, blocking collectives: none -> 64.1 us  [the longest x1 32.4 us: per_device(): dense = lax.all_to_all(dense, 'zh', 0, 0, tiled=True)]
    all_to_all x0 -> x1, waiting for transfers between devices: none -> 21 us  [per_device(): lax.all_to_all(result.reshape(n_group, quarter, width), group, 0, 0, tile...]
    dot_general x7 -> x0, matrix products: 20.8 us -> none  [the longest x1 4.51 us: per_device(): lax.dot_general(grad_gate, gate_local, contract_last, preferred_element_t...]
    all_to_all x0 -> x1, starting transfers between devices: none -> 17.7 us  [per_device(): lax.all_to_all(result.reshape(n_group, quarter, width), group, 0, 0, tile...]
    ppermute x0 -> x5, starting transfers between devices: none -> 17.2 us  [the longest x1 8.91 us: per_device(): tok_far = lax.ppermute(tokens, 'c', swap_cores)]
  transfers between devices with their start and end apart: 5 -> 7, of which waited for: 5 -> 4; matrix products, arithmetic and copies ran while one was open for 2% -> 0% of each run, Pallas kernels for 0% -> 0%
where the time goes in v3:
time: 215 us; the launch traced here: 214 us
  waiting for transfers between devices  79.7 us (37%)
  blocking collectives  64.1 us (30%)
  starting transfers between devices  34.9 us (16%)
  between operations  13.5 us (6%)
  Pallas kernels  11.9 us (6%)
  local copies, waits for them, and re-layouts  9.33 us (4%)
    all_gather x1, waiting for transfers between devices, per_device(): rows = lax.all_gather(picked, ('zh', 'zl'), axis=0, tiled=True)  55.9 us
    all_to_all x1, blocking collectives, per_device(): dense = lax.all_to_all(dense, 'zh', 0, 0, tiled=True)  32.4 us
    all_to_all x1, waiting for transfers between devices, per_device(): lax.all_to_all(result.reshape(n_group, quarter, width), group, 0, 0, tile...  21 us
    all_to_all x1, starting transfers between devices, per_device(): lax.all_to_all(result.reshape(n_group, quarter, width), group, 0, 0, tile...  17.7 us
    all_to_all x1, blocking collectives, per_device(): sums = lax.all_to_all(sums, 'x', 0, 0, tiled=True)  16.5 us
    all_to_all x1, blocking collectives, per_device(): grads = lax.all_to_all(grads, 'x', 0, 0, tiled=True)  15.2 us
    ppermute x1, starting transfers between devices, per_device(): tok_far = lax.ppermute(tokens, 'c', swap_cores)  8.91 us
    unnamed x24, local copies, waits for them, and re-layouts  8.42 us
  transfers between devices with their start and end apart: 7, of which 4 were waited for; matrix products, arithmetic and copies ran while one was open for 0% of the time, Pallas kernels for 0%

profile of v3, /device:TPU:1, one launch (start us, length us, event | category | flops | bytes accessed | tf_op | source)
XLA Modules:
  0.0 214.3 jit_solution(10130450558765227364)
XLA Ops:
  6.5 8.9 %collective-permute-start = (bf16[128,768]{1,0:T(8,128)(2,1)}, bf16[128,768]{1,0:T(8,128)(2,1)S(1)}, u32[]{:S(2)}, u32[]{:S(2)}) collective-permute-start(bf16[128,768]{1,0:T(8,128)(2,1)} %tok_ref.1), channel_id=1, source_target_pairs={{0,4},{4,0},{1,5},{5,1},{2,6},{6,2},{3,7},{7,3},{8,12},{12,8},{9,1... | collective-permute-start | bytes 589832 | tf_op jit(solution)/shard_map/ppermute | solution.py:179
  15.5 1.9 collective-permute-start.1
  17.5 1.5 collective-permute-done.1.cot_far_ref
  19.0 0.9 copy-done.8
  19.9 0.9 copy-done.9
  22.2 1.6 shard_map.73
  23.8 2.0 collective-permute-start.2
  25.9 2.3 %collective-permute-start.3 = (bf16[768,512]{1,0:T(8,128)(2,1)}, bf16[768,512]{1,0:T(8,128)(2,1)S(1)}, u32[]{:S(2)}, u32[]{:S(2)}) collective-permute-start(bf16[768,512]{1,0:T(8,128)(2,1)} %bitcast.18), channel_id=1, source_target_pairs={{0,4},{4,0},{1,5},{5,1},{2,6},{6,2},{3,7},{7,3},{8,12},{12,8},{9,1... | collective-permute-start | bytes 2359304 | tf_op jit(solution)/shard_map/ppermute | solution.py:187
  28.2 1.1 copy-done.7
  29.6 2.0 collective-permute-start.4
  32.6 1.2 collective-permute-done.4.down_far_ref
  33.8 0.9 copy-done.5
  34.7 55.9 %all-gather.2.cloned.1.call-done.rows_ref = bf16[512,3200]{1,0:T(8,128)(2,1)} async-done(((bf16[32,3200]{1,0:T(8,128)(2,1)}), bf16[512,3200]{1,0:T(8,128)(2,1)}) %all-gather.2.cloned.1.call-update) | async-done | bytes 3276816 | tf_op jit(solution)/shard_map/all_gather | solution.py:184
  90.6 1.1 copy-done.3
  91.7 1.1 copy-done.6
  92.9 5.7 %shard_map.75 = bf16[4,128,1536]{2,1,0:T(8,128)(2,1)} custom-call(bf16[512,3200]{1,0:T(8,128)(2,1)} %all-gather.2.cloned.1.call-done.rows_ref, bf16[768,512]{1,0:T(8,128)(2,1)S(1)} %bitcast.16, bf16[768,512]{1,0:T(8,128)(2,1)S(1)} %bitcast.19, bf16[768,512]{1,0:T(8,128)(2,1)S(1)} %shard_map.74.down_ref, ...), custom_call_target="tpu_custom_call" | custom-call | tf_op jit(solution)/shard_map/pallas_call | solution.py:189
  98.6 16.5 %all_to_all.20.sums_ref = bf16[4,128,1536]{2,1,0:T(8,128)(2,1)S(1)} all-to-all(bf16[4,128,1536]{2,1,0:T(8,128)(2,1)} %shard_map.75), channel_id=1, replica_groups=mesh['zh'=8,'zl'=2,'x'=4,'c'=2,'y'=4] {'x'}, dimensions={0} | all-to-all | bytes 3145728 | tf_op jit(solution)/shard_map/all_to_all | solution.py:192
  115.4 15.2 %all_to_all.21 = bf16[4,128,1024]{2,1,0:T(8,128)(2,1)S(1)} all-to-all(bf16[4,128,1024]{2,1,0:T(8,128)(2,1)S(1)} %shard_map.76), channel_id=1, replica_groups=mesh['zh'=8,'zl'=2,'x'=4,'c'=2,'y'=4] {'x'}, dimensions={0} | all-to-all | bytes 2097152 | tf_op jit(solution)/shard_map/all_to_all | solution.py:196
  130.6 3.1 %shard_map.77 = bf16[2,2,768,256]{3,2,1,0:T(8,128)(2,1)} custom-call(s32[1]{0:T(128)} %bitcast.1.core_ref, bf16[8,2,32,1024]{3,2,1,0:T(8,128)(2,1)S(1)} %bitcast.14, bf16[768,512]{1,0:T(8,128)(2,1)S(1)} %bitcast.17, bf16[768,512]{1,0:T(8,128)(2,1)S(1)} %bitcast.20, bf16[768,512]{1,0:T(8,128)(2,1)S(1)} %collective-permute-done.2.gate_far_ref, ...), custom_call_target="tpu_custom_call" | custom-call | tf_op jit(solution)/shard_map/pallas_call | solution.py:198
  133.7 17.7 %all-to-all-start.2 = ((bf16[16,192,256]{2,1,0:T(8,128)(2,1)}), bf16[16,192,256]{2,1,0:T(8,128)(2,1)S(1)}, u32[]{:S(2)}, u32[]{:S(2)}) async-start(bf16[16,192,256]{2,1,0:T(8,128)(2,1)} %bitcast.10), calls=%async_computation.2 | async-start | bytes 3145728 | tf_op jit(solution)/shard_map/all_to_all | solution.py:201
  151.4 0.9 slice.4
  152.3 21.0 %all-to-all-done.2 = bf16[16,192,256]{2,1,0:T(8,128)(2,1)S(1)} async-done(((bf16[16,192,256]{2,1,0:T(8,128)(2,1)}), bf16[16,192,256]{2,1,0:T(8,128)(2,1)S(1)}, u32[]{:S(2)}, u32[]{:S(2)}) %all-to-all-start.2) | async-done | bytes 1572896 | tf_op jit(solution)/shard_map/all_to_all | solution.py:201
  173.3 1.0 shard_map.78
  174.4 32.4 %all_to_all.22 = bf16[8,192,128]{2,1,0:T(8,128)(2,1)S(1)} all-to-all(bf16[8,192,128]{2,1,0:T(8,128)(2,1)S(1)} %shard_map.78), channel_id=1, replica_groups=mesh['zh'=8,'zl'=2,'x'=4,'c'=2,'y'=4] {'zh'}, dimensions={0} | all-to-all | bytes 786432 | tf_op jit(solution)/shard_map/all_to_all | solution.py:209
  (27 shorter events, 3.6 us)
Async XLA Ops:
  6.5 84.1 %copy-start = (bf16[1,768,512]{2,1,0:T(8,128)(2,1)S(1)}, bf16[1,768,512]{2,1,0:T(8,128)(2,1)}, u32[]{:S(2)}) copy-start(bf16[1,768,512]{2,1,0:T(8,128)(2,1)} %param.11) | copy-start | bytes 2359300
  6.5 84.1 %copy-start.1 = (bf16[1,768,512]{2,1,0:T(8,128)(2,1)S(1)}, bf16[1,768,512]{2,1,0:T(8,128)(2,1)}, u32[]{:S(2)}) copy-start(bf16[1,768,512]{2,1,0:T(8,128)(2,1)} %param.12) | copy-start | bytes 2359300
  6.5 84.1 %all-gather.2.cloned.1.call-start = ((), (), s32[]{:S(2)}) async-start(), calls=%async_computation.4 | async-start | bytes 3481600 | tf_op jit(solution)/shard_map/all_gather | solution.py:184
  6.5 10.9 %collective-permute-start = (bf16[128,768]{1,0:T(8,128)(2,1)}, bf16[128,768]{1,0:T(8,128)(2,1)S(1)}, u32[]{:S(2)}, u32[]{:S(2)}) collective-permute-start(bf16[128,768]{1,0:T(8,128)(2,1)} %tok_ref.1), channel_id=1, source_target_pairs={{0,4},{4,0},{1,5},{5,1},{2,6},{6,2},{3,7},{7,3},{8,12},{12,8},{9,1... | collective-permute-start | bytes 589832 | tf_op jit(solution)/shard_map/ppermute | solution.py:179
  15.5 3.5 %collective-permute-start.1 = (bf16[128,768]{1,0:T(8,128)(2,1)}, bf16[128,768]{1,0:T(8,128)(2,1)S(1)}, u32[]{:S(2)}, u32[]{:S(2)}) collective-permute-start(bf16[128,768]{1,0:T(8,128)(2,1)} %cot_ref.1), channel_id=1, source_target_pairs={{0,4},{4,0},{1,5},{5,1},{2,6},{6,2},{3,7},{7,3},{8,12},{12,8},{9,1... | collective-permute-start | bytes 589832 | tf_op jit(solution)/shard_map/ppermute | solution.py:180
  19.0 0.9 copy-start.8
  19.9 0.9 copy-start.9
  20.9 0.7 copy-start.10
  21.5 0.7 copy-start.11
  23.8 7.8 %collective-permute-start.2 = (bf16[768,512]{1,0:T(8,128)(2,1)}, bf16[768,512]{1,0:T(8,128)(2,1)S(1)}, u32[]{:S(2)}, u32[]{:S(2)}) collective-permute-start(bf16[768,512]{1,0:T(8,128)(2,1)} %bitcast.15), channel_id=1, source_target_pairs={{0,4},{4,0},{1,5},{5,1},{2,6},{6,2},{3,7},{7,3},{8,12},{12,8},{9,1... | collective-permute-start | bytes 2359304 | tf_op jit(solution)/shard_map/ppermute | solution.py:187
  25.9 5.8 %collective-permute-start.3 = (bf16[768,512]{1,0:T(8,128)(2,1)}, bf16[768,512]{1,0:T(8,128)(2,1)S(1)}, u32[]{:S(2)}, u32[]{:S(2)}) collective-permute-start(bf16[768,512]{1,0:T(8,128)(2,1)} %bitcast.18), channel_id=1, source_target_pairs={{0,4},{4,0},{1,5},{5,1},{2,6},{6,2},{3,7},{7,3},{8,12},{12,8},{9,1... | collective-permute-start | bytes 2359304 | tf_op jit(solution)/shard_map/ppermute | solution.py:187
  28.2 1.1 copy-start.7
  29.6 4.2 %collective-permute-start.4 = (bf16[768,512]{1,0:T(8,128)(2,1)S(1)}, bf16[768,512]{1,0:T(8,128)(2,1)S(1)}, u32[]{:S(2)}, u32[]{:S(2)}) collective-permute-start(bf16[768,512]{1,0:T(8,128)(2,1)S(1)} %shard_map.74.down_ref), channel_id=1, source_target_pairs={{0,4},{4,0},{1,5},{5,1},{2,6},{6,2},{3,7},{7,3},{8,12},{12,8},{9,1... | collective-permute-start | bytes 2359304 | tf_op jit(solution)/shard_map/ppermute | solution.py:187
  31.7 0.9 copy-start.2
  33.8 0.9 copy-start.5
  90.6 1.1 copy-start.3
  91.7 1.1 copy-start.6
  115.4 15.2 %copy-start.4 = (bf16[768,512]{1,0:T(8,128)(2,1)S(1)}, bf16[768,512]{1,0:T(8,128)(2,1)}, u32[]{:S(2)}) copy-start(bf16[768,512]{1,0:T(8,128)(2,1)} %copy-done.2) | copy-start | bytes 2359300
  133.7 39.7 %all-to-all-start.2 = ((bf16[16,192,256]{2,1,0:T(8,128)(2,1)}), bf16[16,192,256]{2,1,0:T(8,128)(2,1)S(1)}, u32[]{:S(2)}, u32[]{:S(2)}) async-start(bf16[16,192,256]{2,1,0:T(8,128)(2,1)} %bitcast.10), calls=%async_computation.2 | async-start | bytes 3145728 | tf_op jit(solution)/shard_map/all_to_all | solution.py:201
Sparse Core Ops, SparseCore 0:
  24.0 66.6 all-gather.1

commit v4 on v0

v4 whole, which is shorter than its diff:
```python
import jax
import jax.numpy as jnp
from jax import lax
from jax.experimental import pallas as pl
from jax.experimental.pallas import tpu as pltpu
from jax.sharding import Mesh
from jax.sharding import PartitionSpec as P

unit_scale = 1.0 / 65536.0
window = 4
table_rows = 16
bf16 = jnp.bfloat16
f32 = jnp.float32
contract_last = (((1,), (1,)), ((), ()))
contract_first = (((0,), (0,)), ((), ()))
vmem_bytes = 56 * 1024 * 1024
blocks_at = ((0, 0), (0, 1), (-1, 0), (1, 0), (-1, 1), (1, 1), (2, 0), (2, 1))


def kernel_call(body, out_shape, spaces, scratch=()):
    return pl.pallas_call(
        body,
        out_shape=out_shape,
        in_specs=[pl.BlockSpec(memory_space=space) for space in spaces],
        out_specs=jax.tree.map(lambda _: pl.BlockSpec(memory_space=pltpu.VMEM), out_shape),
        scratch_shapes=list(scratch),
        compiler_params=pltpu.CompilerParams(vmem_limit_bytes=vmem_bytes),
    )


def prep_kernel(expert_ref, experts_ref, weight_ref, tok_ref, cot_ref, out_ref, table_ref):
    expert_id = expert_ref[0]
    n_dest, both, feats = out_ref.shape
    part = both // 2
    count = tok_ref.shape[0]
    first, second = experts_ref[0:1, :], experts_ref[1:2, :]
    ids = lax.broadcasted_iota(jnp.int32, (window, count), 0)
    named = (first == ids) | (second == ids)
    before = lax.broadcasted_iota(jnp.int32, (count, count), 0) <= lax.broadcasted_iota(
        jnp.int32, (count, count), 1
    )
    order = jnp.dot(
        jnp.where(named, 1.0, 0.0).astype(bf16),
        jnp.where(before, 1.0, 0.0).astype(bf16),
        preferred_element_type=f32,
    )
    table = jnp.where(named, order - 1.0, -1.0)
    own = jnp.sum(jnp.where(ids == expert_id, table, 0.0), axis=0, keepdims=True)
    share = (
        jnp.where(first == expert_id, weight_ref[0:1, :], 0)
        + jnp.where(second == expert_id, weight_ref[1:2, :], 0)
    ).astype(f32) * unit_scale
    slot = lax.broadcasted_iota(jnp.int32, (n_dest * part, count), 0).astype(f32)
    hit = own == slot
    select = jnp.where(hit, 1.0, 0.0).astype(bf16)
    slot_share = jnp.sum(jnp.where(hit, share, 0.0), axis=1, keepdims=True)
    tok = jnp.dot(select, tok_ref[...], preferred_element_type=f32)
    cot = slot_share * jnp.dot(select, cot_ref[...], preferred_element_type=f32)
    for d in range(n_dest):
        span = slice(d * part, (d + 1) * part)
        out_ref[d] = jnp.concatenate([tok[span], cot[span]], axis=0).astype(bf16)
    padded = jnp.concatenate(
        [table, jnp.zeros((table_rows - window, count), f32)], axis=0
    ).astype(bf16)
    for i in range(table_ref.shape[0]):
        table_ref[i] = padded


def weights_kernel(gate_ref, up_ref, down_ref, low_ref, high_ref):
    half = low_ref.shape[1]
    for i, ref in enumerate((low_ref, high_ref)):
        span = slice(i * half, (i + 1) * half)
        ref[0] = gate_ref[span, :]
        ref[1] = up_ref[span, :]
        ref[2] = down_ref[:, span].T


def block_kernel(place_ref, *refs):
    n_w = 2 * len(blocks_at)
    rows_hbm, weights_hbm = refs[0], refs[1 : 1 + n_w]
    out_ref, rows_ref, weights_ref, total_ref, sems = refs[1 + n_w :]
    x, core = place_ref[0], place_ref[1]
    n_z, n_s, both, feats = rows_ref.shape
    n_x = n_s // 2
    _, _, half, hidden = weights_ref.shape[1:]
    copies = [pltpu.make_async_copy(rows_hbm, rows_ref, sems.at[n_w])]
    copies += [
        pltpu.make_async_copy(w, weights_ref.at[i // 2, i % 2], sems.at[i])
        for i, w in enumerate(weights_hbm)
    ]
    for copy in copies:
        copy.start()
    copies[0].wait()

    def source(dx, dc):
        return lax.rem(x + dx + n_x, n_x) * 2 + (1 - core if dc else core)

    for b, (dx, dc) in enumerate(blocks_at):
        copies[1 + 2 * b].wait()
        copies[2 + 2 * b].wait()
        rows = rows_ref[:, source(dx, dc)].reshape(n_z * both, feats)
        for m in range(3):
            span = slice(m * hidden, (m + 1) * hidden)
            term = jnp.dot(rows[:, :half], weights_ref[b, 0, m], preferred_element_type=f32)
            term += jnp.dot(rows[:, half:], weights_ref[b, 1, m], preferred_element_type=f32)
            if b == 0:
                total_ref[:, span] = term
            else:
                total_ref[:, span] += term

    part = both // 2
    gate_sum, up_sum, back_sum = (
        total_ref[:, m * hidden : (m + 1) * hidden]
        .reshape(n_z, both, hidden)[:, begin : begin + part]
        .reshape(n_z * part, hidden)
        for m, begin in ((0, 0), (1, 0), (2, part))
    )
    sigmoid_gate = jax.nn.sigmoid(gate_sum)
    grad_up = (back_sum * (gate_sum * sigmoid_gate)).astype(bf16)
    grad_gate = (
        back_sum * up_sum * sigmoid_gate * (1.0 + gate_sum * (1.0 - sigmoid_gate))
    ).astype(bf16)

    slots = n_z * part
    quarter = feats // window
    for b, (dx, dc) in enumerate(blocks_at):
        s = source(dx, dc)
        for y in range(window):
            side, begin = y * quarter // half, y * quarter % half
            span = slice(begin, begin + quarter)
            rows = lax.dot_general(
                grad_gate, weights_ref[b, side, 0, span], contract_last, preferred_element_type=f32
            ) + lax.dot_general(
                grad_up, weights_ref[b, side, 1, span], contract_last, preferred_element_type=f32
            )
            out_ref[s, y, :slots, :] = rows[:, :128].astype(bf16)
            out_ref[s, y, slots:, :] = jnp.concatenate(
                [rows[: slots // 2, 128:], rows[slots // 2 :, 128:]], axis=1
            ).astype(bf16)


def combine_kernel(table_ref, rows_ref, out_ref):
    n_z, quarter, count = out_ref.shape
    n_d = rows_ref.shape[0]
    part = 64 // n_d
    slots = n_z * part
    rest = quarter - 128
    slot = lax.broadcasted_iota(jnp.int32, (n_d * part, count), 0).astype(f32)
    sources = [(d, e) for e in range(window) for d in range(n_d)]
    for p in range(n_z // 4):
        begin = 2 * part * p
        tails = [
            rows_ref[d, e, slots + begin : slots + begin + 2 * part, :].astype(f32)
            for d, e in sources
        ]
        for upper in range(2):
            at = upper * slots // 2 + begin
            heads = [rows_ref[d, e, at : at + 2 * part, :].astype(f32) for d, e in sources]
            for j in range(2):
                z = upper * n_z // 2 + 2 * p + j
                span = slice(j * part, (j + 1) * part)
                values = jnp.concatenate(
                    [
                        jnp.concatenate([v[span] for v in heads], axis=0),
                        jnp.concatenate([v[span] for v in tails], axis=0),
                    ],
                    axis=1,
                ).astype(bf16)
                table = table_ref[z].astype(f32)
                select = jnp.concatenate(
                    [jnp.where(table[e : e + 1] == slot, 1.0, 0.0) for e in range(window)], axis=0
                ).astype(bf16)
                dense = lax.dot_general(
                    values, select, contract_first, preferred_element_type=f32
                ).astype(bf16)
                out_ref[z, :128, :] = dense[:128]
                out_ref[z, 128:, :] = dense[128 + upper * rest : 128 + (upper + 1) * rest]


def gather_weights(low, high):
    n_x = lax.axis_size("x")
    ahead = [(i, (i + 1) % n_x) for i in range(n_x)]
    behind = [(i, (i - 1) % n_x) for i in range(n_x)]

    def swap(value):
        return lax.ppermute(value, "c", [(0, 1), (1, 0)])

    low_before = lax.ppermute(low, "x", ahead)
    high_after = lax.ppermute(high, "x", behind)
    high_before = lax.ppermute(high, "x", ahead)
    low_after = lax.ppermute(low, "x", behind)
    low_across = lax.ppermute(low_before, "x", ahead)
    high_across = lax.ppermute(high_after, "x", behind)
    near = [(low, high), (low_before, high_before), (low_after, high_after), (low_across, high_across)]
    far = [(swap(a), swap(b)) for a, b in near]
    return [near[0], far[0], near[1], near[2], far[1], far[2], near[3], far[3]]


def per_device(tokens, cotangent, experts, route_weight, gate_weight, up_weight, down_weight):
    n_z = lax.axis_size("zh") * lax.axis_size("zl")
    n_s = lax.axis_size("x") * lax.axis_size("c")
    count, feats = tokens.shape
    quarter = feats // window
    part = count // 2 // n_s
    gate, up, down = gate_weight[0], up_weight[0], down_weight[0]
    hidden = gate.shape[1]
    expert_id = lax.axis_index("y").reshape(1).astype(jnp.int32)
    place = jnp.stack([lax.axis_index("x"), lax.axis_index("c")]).astype(jnp.int32)
    smem, vmem, anywhere = pltpu.SMEM, pltpu.VMEM, pl.ANY

    pieces, tables = kernel_call(
        prep_kernel,
        (
            jax.ShapeDtypeStruct((n_s, 2 * part, feats), bf16),
            jax.ShapeDtypeStruct((n_z, table_rows, count), bf16),
        ),
        [smem] + [vmem] * 4,
    )(expert_id, experts.T, route_weight.T, tokens, cotangent)
    pieces = lax.all_to_all(pieces, ("x", "c"), 0, 0, tiled=True)
    rows = lax.all_gather(
        pieces.reshape(n_s * 2 * part, feats), ("zh", "zl"), axis=0, tiled=True
    ).reshape(n_z, n_s, 2 * part, feats)

    tables, gate, up, down, pieces = lax.optimization_barrier((tables, gate, up, down, pieces))
    low, high = kernel_call(
        weights_kernel,
        (jax.ShapeDtypeStruct((3, feats // 2, hidden), bf16),) * 2,
        [vmem] * 3,
    )(gate, up, down)
    weights = gather_weights(low, high)
    tables = lax.all_to_all(tables, ("zh", "zl"), 0, 0, tiled=True)

    result = kernel_call(
        block_kernel,
        jax.ShapeDtypeStruct((n_s, window, quarter, n_z * part), bf16),
        [smem] + [anywhere] * (1 + 2 * len(blocks_at)),
        [
            pltpu.VMEM((n_z, n_s, 2 * part, feats), bf16),
            pltpu.VMEM((len(blocks_at), 2, 3, feats // 2, hidden), bf16),
            pltpu.VMEM((n_z * 2 * part, 3 * hidden), f32),
            pltpu.SemaphoreType.DMA((2 * len(blocks_at) + 1,)),
        ],
    )(place, rows, *[half for block in weights for half in block])
    result = lax.all_to_all(
        result.reshape(n_s * window, quarter, n_z * part), ("x", "c", "y"), 0, 0, tiled=True
    ).reshape(n_s, window, quarter, n_z * part)
    dense = kernel_call(
        combine_kernel, jax.ShapeDtypeStruct((n_z, quarter, count), bf16), [vmem] * 2
    )(tables, result)
    dense = lax.all_to_all(dense, ("zh", "zl"), 0, 0, tiled=True)
    return jnp.sum(dense.astype(f32), axis=0).astype(bf16).T


def solution(mesh):
    split = Mesh(
        mesh.devices.reshape(mesh.shape["seq"] // 2, 2, mesh.shape["etp"] // 2, 2, -1),
        ("zh", "zl", "x", "c", "y"),
    )
    seq, etp = ("zh", "zl"), ("x", "c")
    placed = (
        P(seq, etp),
        P(seq, etp),
        P(seq, None),
        P(seq, None),
        P("y", etp, seq),
        P("y", etp, seq),
        P("y", seq, etp),
    )
    return jax.shard_map(
        per_device, mesh=split, in_specs=placed, out_specs=P(seq, ("x", "c", "y")), check_vma=False
    )
```

time: 380 us -> 236 us (0.62)
  the two profiles are of different devices: /device:TPU:1 before, /device:TPU:64 now
where the time goes in v4:
time: 236 us; the launch traced here: 235 us
  blocking collectives  92.5 us (39%)
  waiting for transfers between devices  53.9 us (23%)
  starting transfers between devices  49.3 us (21%)
  Pallas kernels  24.2 us (10%)
  between operations  13.6 us (6%)
    all_to_all x1, blocking collectives, per_device(): dense = lax.all_to_all(dense, ('zh', 'zl'), 0, 0, tiled=True)  53.2 us
    all_to_all x1, blocking collectives, per_device(): lax.all_to_all(result.reshape(n_s * window, quarter, n_z * part), ('x', '...  28.1 us
    ppermute x1, waiting for transfers between devices, gather_weights(): low_across = lax.ppermute(low_before, 'x', ahead)  17.2 us
    ppermute x1, waiting for transfers between devices, gather_weights(): low_after = lax.ppermute(low, 'x', behind)  17 us
    ppermute x8, starting transfers between devices, swap(): return lax.ppermute(value, 'c', [(0, 1), (1, 0)])  16.3 us
    pallas_call x1, Pallas kernels, per_device(): kernel_call(block_kernel, jax.ShapeDtypeStruct((n_s, window, quarter, n_z...  15.8 us
    ppermute x1, waiting for transfers between devices, gather_weights(): high_after = lax.ppermute(high, 'x', behind)  15.7 us
    all_to_all x1, starting transfers between devices, per_device(): tables = lax.all_to_all(tables, ('zh', 'zl'), 0, 0, tiled=True)  14.8 us
  transfers between devices with their start and end apart: 16, of which 5 were waited for; matrix products, arithmetic and copies ran while one was open for 0% of the time, Pallas kernels for 8%

profile of v4, /device:TPU:64, one launch (start us, length us, event | category | flops | bytes accessed | tf_op | source)
XLA Modules:
  0.0 234.9 jit_solution(7535394142749901797)
XLA Ops:
  6.5 2.1 shard_map.73
  8.6 11.2 %all_to_all.20 = bf16[8,16,768]{2,1,0:T(8,128)(2,1)} all-to-all(bf16[8,16,768]{2,1,0:T(8,128)(2,1)} %get-tuple-element.14), channel_id=1, replica_groups=mesh['zh'=8,'zl'=2,'x'=4,'c'=2,'y'=4] {'x','c'}, dimensions={0} | all-to-all | bytes 393216 | tf_op jit(solution)/shard_map/all_to_all | solution.py:219
  19.9 3.3 %shard_map.74 = (bf16[3,384,512]{2,1,0:T(8,128)(2,1)}, bf16[3,384,512]{2,1,0:T(8,128)(2,1)}) custom-call(bf16[768,512]{1,0:T(8,128)(2,1)} %bitcast.17, bf16[768,512]{1,0:T(8,128)(2,1)} %bitcast.18, bf16[512,768]{1,0:T(8,128)(2,1)} %bitcast.19), custom_call_target="tpu_custom_call" | custom-call | tf_op jit(solution)/shard_map/pallas_call | solution.py:225
  23.1 3.1 %collective-permute-start.4 = (bf16[3,384,512]{2,1,0:T(8,128)(2,1)}, bf16[3,384,512]{2,1,0:T(8,128)(2,1)S(1)}, u32[]{:S(2)}, u32[]{:S(2)}) collective-permute-start(bf16[3,384,512]{2,1,0:T(8,128)(2,1)} %get-tuple-element.19.refs_1_), channel_id=1, source_target_pairs={{0,24},{8,0},{16,8},{24,16},{1,25},{9,1},{17,9},{25,17},{2,26},{10... | collective-permute-start | bytes 3538952 | tf_op jit(solution)/shard_map/ppermute | solution.py:191
  26.2 2.8 %collective-permute-start.2 = (bf16[3,384,512]{2,1,0:T(8,128)(2,1)}, bf16[3,384,512]{2,1,0:T(8,128)(2,1)S(1)}, u32[]{:S(2)}, u32[]{:S(2)}) collective-permute-start(bf16[3,384,512]{2,1,0:T(8,128)(2,1)} %get-tuple-element.19.refs_1_), channel_id=1, source_target_pairs={{0,8},{8,16},{16,24},{24,0},{1,9},{9,17},{17,25},{25,1},{2,10},{10... | collective-permute-start | bytes 3538952 | tf_op jit(solution)/shard_map/ppermute | solution.py:188
  29.0 1.9 collective-permute-start
  30.9 4.3 %collective-permute-start.5 = (bf16[3,384,512]{2,1,0:T(8,128)(2,1)}, bf16[3,384,512]{2,1,0:T(8,128)(2,1)}, u32[]{:S(2)}, u32[]{:S(2)}) collective-permute-start(bf16[3,384,512]{2,1,0:T(8,128)(2,1)} %get-tuple-element.20.refs_2_), channel_id=1, source_target_pairs={{0,24},{8,0},{16,8},{24,16},{1,25},{9,1},{17,9},{25,17},{2,26},{10... | collective-permute-start | bytes 3538952 | tf_op jit(solution)/shard_map/ppermute | solution.py:189
  35.2 1.9 collective-permute-start.3
  37.1 17.0 %collective-permute-done.4.refs_7_ = bf16[3,384,512]{2,1,0:T(8,128)(2,1)S(1)} collective-permute-done((bf16[3,384,512]{2,1,0:T(8,128)(2,1)}, bf16[3,384,512]{2,1,0:T(8,128)(2,1)S(1)}, u32[]{:S(2)}, u32[]{:S(2)}) %collective-permute-start.4) | collective-permute-done | bytes 1179680 | tf_op jit(solution)/shard_map/ppermute | solution.py:191
  56.0 2.4 %collective-permute-done.2.refs_5_ = bf16[3,384,512]{2,1,0:T(8,128)(2,1)S(1)} collective-permute-done((bf16[3,384,512]{2,1,0:T(8,128)(2,1)}, bf16[3,384,512]{2,1,0:T(8,128)(2,1)S(1)}, u32[]{:S(2)}, u32[]{:S(2)}) %collective-permute-start.2) | collective-permute-done | bytes 1179680 | tf_op jit(solution)/shard_map/ppermute | solution.py:188
  60.4 1.9 collective-permute-start.10
  62.3 15.7 %collective-permute-done.5.refs_8_ = bf16[3,384,512]{2,1,0:T(8,128)(2,1)} collective-permute-done((bf16[3,384,512]{2,1,0:T(8,128)(2,1)}, bf16[3,384,512]{2,1,0:T(8,128)(2,1)}, u32[]{:S(2)}, u32[]{:S(2)}) %collective-permute-start.5) | collective-permute-done | bytes 1179680 | tf_op jit(solution)/shard_map/ppermute | solution.py:189
  78.0 4.3 %collective-permute-start.11 = (bf16[3,384,512]{2,1,0:T(8,128)(2,1)}, bf16[3,384,512]{2,1,0:T(8,128)(2,1)}, u32[]{:S(2)}, u32[]{:S(2)}) collective-permute-start(bf16[3,384,512]{2,1,0:T(8,128)(2,1)} %collective-permute-done.5.refs_8_), channel_id=1, source_target_pairs={{0,24},{8,0},{16,8},{24,16},{1,25},{9,1},{17,9},{25,17},{2,26},{10... | collective-permute-start | bytes 3538952 | tf_op jit(solution)/shard_map/ppermute | solution.py:193
  83.8 1.9 collective-permute-start.6
  85.8 2.4 %collective-permute-start.9 = (bf16[3,384,512]{2,1,0:T(8,128)(2,1)}, bf16[3,384,512]{2,1,0:T(8,128)(2,1)}, u32[]{:S(2)}, u32[]{:S(2)}) collective-permute-start(bf16[3,384,512]{2,1,0:T(8,128)(2,1)} %collective-permute-done.5.refs_8_), channel_id=1, source_target_pairs={{0,4},{4,0},{1,5},{5,1},{2,6},{6,2},{3,7},{7,3},{8,12},{12,8},{9,1... | collective-permute-start | bytes 3538952 | tf_op jit(solution)/shard_map/ppermute | solution.py:186
  88.2 1.9 collective-permute-start.7
  90.1 17.2 %collective-permute-done.10.refs_13_ = bf16[3,384,512]{2,1,0:T(8,128)(2,1)} collective-permute-done((bf16[3,384,512]{2,1,0:T(8,128)(2,1)S(1)}, bf16[3,384,512]{2,1,0:T(8,128)(2,1)}, u32[]{:S(2)}, u32[]{:S(2)}) %collective-permute-start.10) | collective-permute-done | bytes 1179680 | tf_op jit(solution)/shard_map/ppermute | solution.py:192
  107.3 1.9 collective-permute-start.12
  109.3 2.4 %collective-permute-start.13 = (bf16[3,384,512]{2,1,0:T(8,128)(2,1)}, bf16[3,384,512]{2,1,0:T(8,128)(2,1)}, u32[]{:S(2)}, u32[]{:S(2)}) collective-permute-start(bf16[3,384,512]{2,1,0:T(8,128)(2,1)} %collective-permute-done.11.refs_14_), channel_id=1, source_target_pairs={{0,4},{4,0},{1,5},{5,1},{2,6},{6,2},{3,7},{7,3},{8,12},{12,8},{9,1... | collective-permute-start | bytes 3538952 | tf_op jit(solution)/shard_map/ppermute | solution.py:186
  111.7 14.8 %all-to-all-start.1 = ((bf16[16,16,128]{2,1,0:T(8,128)(2,1)}), bf16[16,16,128]{2,1,0:T(8,128)(2,1)}, u32[]{:S(2)}, u32[]{:S(2)}) async-start(bf16[16,16,128]{2,1,0:T(8,128)(2,1)} %get-tuple-element.15), calls=%async_computation.1 | async-start | bytes 131072 | tf_op jit(solution)/shard_map/all_to_all | solution.py:231
  127.2 15.8 %shard_map.75 = bf16[8,4,192,128]{3,2,1,0:T(8,128)(2,1)} custom-call(s32[2]{0:T(128)} %pad_add_fusion.place_ref, bf16[16,8,16,768]{3,2,1,0:T(8,128)(2,1)} %bitcast.15, bf16[3,384,512]{2,1,0:T(8,128)(2,1)} %get-tuple-element.19.refs_1_, bf16[3,384,512]{2,1,0:T(8,128)(2,1)} %get-tuple-element.20.refs_2_, bf16[3,384,512]{2,1,0:T(8,128)(2,1)} %copy-done.2, ...), custom_call_target="tpu_custom_call" | custom-call | tf_op jit(solution)/shard_map/pallas_call | solution.py:233
  142.9 28.1 %all_to_all.21 = bf16[32,192,128]{2,1,0:T(8,128)(2,1)} all-to-all(bf16[32,192,128]{2,1,0:T(8,128)(2,1)} %bitcast.13), channel_id=1, replica_groups=mesh['zh'=8,'zl'=2,'x'=4,'c'=2,'y'=4] {'x','c','y'}, dimensions={0} | all-to-all | bytes 3145728 | tf_op jit(solution)/shard_map/all_to_all | solution.py:244
  171.0 3.1 %shard_map.76 = bf16[16,192,128]{2,1,0:T(8,128)(2,1)} custom-call(bf16[16,16,128]{2,1,0:T(8,128)(2,1)} %all-to-all-done.1.table_ref, bf16[8,4,192,128]{3,2,1,0:T(8,128)(2,1)} %bitcast.14), custom_call_target="tpu_custom_call" | custom-call | tf_op jit(solution)/shard_map/pallas_call | solution.py:247
  174.1 53.2 %all_to_all.22 = bf16[16,192,128]{2,1,0:T(8,128)(2,1)S(1)} all-to-all(bf16[16,192,128]{2,1,0:T(8,128)(2,1)} %shard_map.76), channel_id=1, replica_groups=mesh['zh'=8,'zl'=2,'x'=4,'c'=2,'y'=4] {'zh','zl'}, dimensions={0} | all-to-all | bytes 1572864 | tf_op jit(solution)/shard_map/all_to_all | solution.py:250
  (28 shorter events, 6.7 us)
Async XLA Ops:
  6.5 120.6 %all-gather.2.cloned.1.call-start = ((), (), s32[]{:S(2)}) async-start(), calls=%async_computation.4 | async-start | bytes 3342336 | tf_op jit(solution)/shard_map/all_gather | solution.py:220
  23.1 31.0 %collective-permute-start.4 = (bf16[3,384,512]{2,1,0:T(8,128)(2,1)}, bf16[3,384,512]{2,1,0:T(8,128)(2,1)S(1)}, u32[]{:S(2)}, u32[]{:S(2)}) collective-permute-start(bf16[3,384,512]{2,1,0:T(8,128)(2,1)} %get-tuple-element.19.refs_1_), channel_id=1, source_target_pairs={{0,24},{8,0},{16,8},{24,16},{1,25},{9,1},{17,9},{25,17},{2,26},{10... | collective-permute-start | bytes 3538952 | tf_op jit(solution)/shard_map/ppermute | solution.py:191
  26.2 32.2 %collective-permute-start.2 = (bf16[3,384,512]{2,1,0:T(8,128)(2,1)}, bf16[3,384,512]{2,1,0:T(8,128)(2,1)S(1)}, u32[]{:S(2)}, u32[]{:S(2)}) collective-permute-start(bf16[3,384,512]{2,1,0:T(8,128)(2,1)} %get-tuple-element.19.refs_1_), channel_id=1, source_target_pairs={{0,8},{8,16},{16,24},{24,0},{1,9},{9,17},{17,25},{25,1},{2,10},{10... | collective-permute-start | bytes 3538952 | tf_op jit(solution)/shard_map/ppermute | solution.py:188
  29.0 31.4 %collective-permute-start = (bf16[3,384,512]{2,1,0:T(8,128)(2,1)}, bf16[3,384,512]{2,1,0:T(8,128)(2,1)S(1)}, u32[]{:S(2)}, u32[]{:S(2)}) collective-permute-start(bf16[3,384,512]{2,1,0:T(8,128)(2,1)} %get-tuple-element.19.refs_1_), channel_id=1, source_target_pairs={{0,4},{4,0},{1,5},{5,1},{2,6},{6,2},{3,7},{7,3},{8,12},{12,8},{9,1... | collective-permute-start | bytes 3538952 | tf_op jit(solution)/shard_map/ppermute | solution.py:186
  30.9 47.1 %collective-permute-start.5 = (bf16[3,384,512]{2,1,0:T(8,128)(2,1)}, bf16[3,384,512]{2,1,0:T(8,128)(2,1)}, u32[]{:S(2)}, u32[]{:S(2)}) collective-permute-start(bf16[3,384,512]{2,1,0:T(8,128)(2,1)} %get-tuple-element.20.refs_2_), channel_id=1, source_target_pairs={{0,24},{8,0},{16,8},{24,16},{1,25},{9,1},{17,9},{25,17},{2,26},{10... | collective-permute-start | bytes 3538952 | tf_op jit(solution)/shard_map/ppermute | solution.py:189
  35.2 48.6 %collective-permute-start.3 = (bf16[3,384,512]{2,1,0:T(8,128)(2,1)}, bf16[3,384,512]{2,1,0:T(8,128)(2,1)}, u32[]{:S(2)}, u32[]{:S(2)}) collective-permute-start(bf16[3,384,512]{2,1,0:T(8,128)(2,1)} %get-tuple-element.20.refs_2_), channel_id=1, source_target_pairs={{0,8},{8,16},{16,24},{24,0},{1,9},{9,17},{17,25},{25,1},{2,10},{10... | collective-permute-start | bytes 3538952 | tf_op jit(solution)/shard_map/ppermute | solution.py:190
  54.1 73.0 %copy-start = (bf16[3,384,512]{2,1,0:T(8,128)(2,1)}, bf16[3,384,512]{2,1,0:T(8,128)(2,1)S(1)}, u32[]{:S(2)}) copy-start(bf16[3,384,512]{2,1,0:T(8,128)(2,1)S(1)} %collective-permute-done.4.refs_7_) | copy-start | bytes 3538948
  54.1 31.6 %collective-permute-start.1 = (bf16[3,384,512]{2,1,0:T(8,128)(2,1)}, bf16[3,384,512]{2,1,0:T(8,128)(2,1)S(1)}, u32[]{:S(2)}, u32[]{:S(2)}) collective-permute-start(bf16[3,384,512]{2,1,0:T(8,128)(2,1)} %get-tuple-element.20.refs_2_), channel_id=1, source_target_pairs={{0,4},{4,0},{1,5},{5,1},{2,6},{6,2},{3,7},{7,3},{8,12},{12,8},{9,1... | collective-permute-start | bytes 3538952 | tf_op jit(solution)/shard_map/ppermute | solution.py:186
  58.4 68.7 %copy-start.1 = (bf16[3,384,512]{2,1,0:T(8,128)(2,1)}, bf16[3,384,512]{2,1,0:T(8,128)(2,1)S(1)}, u32[]{:S(2)}) copy-start(bf16[3,384,512]{2,1,0:T(8,128)(2,1)S(1)} %collective-permute-done.2.refs_5_) | copy-start | bytes 3538948
  58.4 29.7 %collective-permute-start.8 = (bf16[3,384,512]{2,1,0:T(8,128)(2,1)S(1)}, bf16[3,384,512]{2,1,0:T(8,128)(2,1)S(1)}, u32[]{:S(2)}, u32[]{:S(2)}) collective-permute-start(bf16[3,384,512]{2,1,0:T(8,128)(2,1)S(1)} %collective-permute-done.4.refs_7_), channel_id=1, source_target_pairs={{0,4},{4,0},{1,5},{5,1},{2,6},{6,2},{3,7},{7,3},{8,12},{12,8},{9,1... | collective-permute-start | bytes 3538952 | tf_op jit(solution)/shard_map/ppermute | solution.py:186
  60.4 66.8 %copy-start.2 = (bf16[3,384,512]{2,1,0:T(8,128)(2,1)}, bf16[3,384,512]{2,1,0:T(8,128)(2,1)S(1)}, u32[]{:S(2)}) copy-start(bf16[3,384,512]{2,1,0:T(8,128)(2,1)S(1)} %collective-permute-done.refs_3_) | copy-start | bytes 3538948
  60.4 47.0 %collective-permute-start.10 = (bf16[3,384,512]{2,1,0:T(8,128)(2,1)S(1)}, bf16[3,384,512]{2,1,0:T(8,128)(2,1)}, u32[]{:S(2)}, u32[]{:S(2)}) collective-permute-start(bf16[3,384,512]{2,1,0:T(8,128)(2,1)S(1)} %collective-permute-done.2.refs_5_), channel_id=1, source_target_pairs={{0,8},{8,16},{16,24},{24,0},{1,9},{9,17},{17,25},{25,1},{2,10},{10... | collective-permute-start | bytes 3538952 | tf_op jit(solution)/shard_map/ppermute | solution.py:192
  78.0 31.2 %collective-permute-start.11 = (bf16[3,384,512]{2,1,0:T(8,128)(2,1)}, bf16[3,384,512]{2,1,0:T(8,128)(2,1)}, u32[]{:S(2)}, u32[]{:S(2)}) collective-permute-start(bf16[3,384,512]{2,1,0:T(8,128)(2,1)} %collective-permute-done.5.refs_8_), channel_id=1, source_target_pairs={{0,24},{8,0},{16,8},{24,16},{1,25},{9,1},{17,9},{25,17},{2,26},{10... | collective-permute-start | bytes 3538952 | tf_op jit(solution)/shard_map/ppermute | solution.py:193
  83.8 43.2 %collective-permute-start.6 = (bf16[3,384,512]{2,1,0:T(8,128)(2,1)S(1)}, bf16[3,384,512]{2,1,0:T(8,128)(2,1)}, u32[]{:S(2)}, u32[]{:S(2)}) collective-permute-start(bf16[3,384,512]{2,1,0:T(8,128)(2,1)S(1)} %collective-permute-done.2.refs_5_), channel_id=1, source_target_pairs={{0,4},{4,0},{1,5},{5,1},{2,6},{6,2},{3,7},{7,3},{8,12},{12,8},{9,1... | collective-permute-start | bytes 3538952 | tf_op jit(solution)/shard_map/ppermute | solution.py:186
  85.7 21.6 %copy-start.3 = (bf16[3,384,512]{2,1,0:T(8,128)(2,1)}, bf16[3,384,512]{2,1,0:T(8,128)(2,1)S(1)}, u32[]{:S(2)}) copy-start(bf16[3,384,512]{2,1,0:T(8,128)(2,1)S(1)} %collective-permute-done.1.refs_4_) | copy-start | bytes 3538948
  85.8 41.3 %collective-permute-start.9 = (bf16[3,384,512]{2,1,0:T(8,128)(2,1)}, bf16[3,384,512]{2,1,0:T(8,128)(2,1)}, u32[]{:S(2)}, u32[]{:S(2)}) collective-permute-start(bf16[3,384,512]{2,1,0:T(8,128)(2,1)} %collective-permute-done.5.refs_8_), channel_id=1, source_target_pairs={{0,4},{4,0},{1,5},{5,1},{2,6},{6,2},{3,7},{7,3},{8,12},{12,8},{9,1... | collective-permute-start | bytes 3538952 | tf_op jit(solution)/shard_map/ppermute | solution.py:186
  88.2 21.1 %copy-start.4 = (bf16[3,384,512]{2,1,0:T(8,128)(2,1)}, bf16[3,384,512]{2,1,0:T(8,128)(2,1)S(1)}, u32[]{:S(2)}) copy-start(bf16[3,384,512]{2,1,0:T(8,128)(2,1)S(1)} %collective-permute-done.8.refs_11_) | copy-start | bytes 3538948
  88.2 38.9 %collective-permute-start.7 = (bf16[3,384,512]{2,1,0:T(8,128)(2,1)}, bf16[3,384,512]{2,1,0:T(8,128)(2,1)}, u32[]{:S(2)}, u32[]{:S(2)}) collective-permute-start(bf16[3,384,512]{2,1,0:T(8,128)(2,1)} %collective-permute-done.3.refs_6_), channel_id=1, source_target_pairs={{0,4},{4,0},{1,5},{5,1},{2,6},{6,2},{3,7},{7,3},{8,12},{12,8},{9,1... | collective-permute-start | bytes 3538952 | tf_op jit(solution)/shard_map/ppermute | solution.py:186
  107.3 19.7 %collective-permute-start.12 = (bf16[3,384,512]{2,1,0:T(8,128)(2,1)}, bf16[3,384,512]{2,1,0:T(8,128)(2,1)}, u32[]{:S(2)}, u32[]{:S(2)}) collective-permute-start(bf16[3,384,512]{2,1,0:T(8,128)(2,1)} %collective-permute-done.10.refs_13_), channel_id=1, source_target_pairs={{0,4},{4,0},{1,5},{5,1},{2,6},{6,2},{3,7},{7,3},{8,12},{12,8},{9,1... | collective-permute-start | bytes 3538952 | tf_op jit(solution)/shard_map/ppermute | solution.py:186
  109.3 17.8 %collective-permute-start.13 = (bf16[3,384,512]{2,1,0:T(8,128)(2,1)}, bf16[3,384,512]{2,1,0:T(8,128)(2,1)}, u32[]{:S(2)}, u32[]{:S(2)}) collective-permute-start(bf16[3,384,512]{2,1,0:T(8,128)(2,1)} %collective-permute-done.11.refs_14_), channel_id=1, source_target_pairs={{0,4},{4,0},{1,5},{5,1},{2,6},{6,2},{3,7},{7,3},{8,12},{12,8},{9,1... | collective-permute-start | bytes 3538952 | tf_op jit(solution)/shard_map/ppermute | solution.py:186
  111.7 31.2 %all-to-all-start.1 = ((bf16[16,16,128]{2,1,0:T(8,128)(2,1)}), bf16[16,16,128]{2,1,0:T(8,128)(2,1)}, u32[]{:S(2)}, u32[]{:S(2)}) async-start(bf16[16,16,128]{2,1,0:T(8,128)(2,1)} %get-tuple-element.15), calls=%async_computation.1 | async-start | bytes 131072 | tf_op jit(solution)/shard_map/all_to_all | solution.py:231
Sparse Core Ops, SparseCore 0:
  20.0 76.9 all-gather.1

commit v5 on v4

--- a/solution.py
+++ b/solution.py
@@ -83,6 +83,8 @@
     n_z, n_s, both, feats = rows_ref.shape
     n_x = n_s // 2
     _, _, half, hidden = weights_ref.shape[1:]
+    part = both // 2
+    slots = n_z * part
     copies = [pltpu.make_async_copy(rows_hbm, rows_ref, sems.at[n_w])]
     copies += [
         pltpu.make_async_copy(w, weights_ref.at[i // 2, i % 2], sems.at[i])
@@ -98,8 +100,12 @@
     for b, (dx, dc) in enumerate(blocks_at):
         copies[1 + 2 * b].wait()
         copies[2 + 2 * b].wait()
-        rows = rows_ref[:, source(dx, dc)].reshape(n_z * both, feats)
-        for m in range(3):
+        loaded = rows_ref[:, source(dx, dc)].astype(f32)
+        tok, cot = (
+            loaded[:, begin : begin + part].reshape(slots, feats).astype(bf16)
+            for begin in (0, part)
+        )
+        for m, rows in enumerate((tok, tok, cot)):
             span = slice(m * hidden, (m + 1) * hidden)
             term = jnp.dot(rows[:, :half], weights_ref[b, 0, m], preferred_element_type=f32)
             term += jnp.dot(rows[:, half:], weights_ref[b, 1, m], preferred_element_type=f32)
@@ -108,12 +114,17 @@
             else:
                 total_ref[:, span] += term
 
-    part = both // 2
     gate_sum, up_sum, back_sum = (
-        total_ref[:, m * hidden : (m + 1) * hidden]
-        .reshape(n_z, both, hidden)[:, begin : begin + part]
-        .reshape(n_z * part, hidden)
-        for m, begin in ((0, 0), (1, 0), (2, part))
+        jnp.concatenate(
+            [
+                total_ref[:, m * hidden : (m + 1) * hidden]
+                .reshape(n_z // 2, 2, part, hidden)[:, pair]
+                .reshape(slots // 2, hidden)
+                for pair in range(2)
+            ],
+            axis=0,
+        )
+        for m in range(3)
     )
     sigmoid_gate = jax.nn.sigmoid(gate_sum)
     grad_up = (back_sum * (gate_sum * sigmoid_gate)).astype(bf16)
@@ -121,7 +132,6 @@
         back_sum * up_sum * sigmoid_gate * (1.0 + gate_sum * (1.0 - sigmoid_gate))
     ).astype(bf16)
 
-    slots = n_z * part
     quarter = feats // window
     for b, (dx, dc) in enumerate(blocks_at):
         s = source(dx, dc)
@@ -133,31 +143,35 @@
             ) + lax.dot_general(
                 grad_up, weights_ref[b, side, 1, span], contract_last, preferred_element_type=f32
             )
-            out_ref[s, y, :slots, :] = rows[:, :128].astype(bf16)
-            out_ref[s, y, slots:, :] = jnp.concatenate(
-                [rows[: slots // 2, 128:], rows[slots // 2 :, 128:]], axis=1
-            ).astype(bf16)
+            for pair in range(2):
+                mine = rows[pair * slots // 2 : (pair + 1) * slots // 2]
+                out_ref[s, y, pair, : slots // 2, :] = mine[:, :128].astype(bf16)
+                out_ref[s, y, pair, slots // 2 :, :] = jnp.concatenate(
+                    [mine[: slots // 4, 128:], mine[slots // 4 :, 128:]], axis=1
+                ).astype(bf16)
 
 
 def combine_kernel(table_ref, rows_ref, out_ref):
-    n_z, quarter, count = out_ref.shape
+    n_blocks, quarter, count = out_ref.shape
     n_d = rows_ref.shape[0]
     part = 64 // n_d
-    slots = n_z * part
+    slots = n_blocks * part
     rest = quarter - 128
     slot = lax.broadcasted_iota(jnp.int32, (n_d * part, count), 0).astype(f32)
-    sources = [(d, e) for e in range(window) for d in range(n_d)]
-    for p in range(n_z // 4):
+    sources = [(d, e, pair) for pair in range(2) for e in range(window) for d in range(n_d)]
+    for p in range(n_blocks // 4):
         begin = 2 * part * p
         tails = [
-            rows_ref[d, e, slots + begin : slots + begin + 2 * part, :].astype(f32)
-            for d, e in sources
+            rows_ref[(*source, slice(slots + begin, slots + begin + 2 * part))].astype(f32)
+            for source in sources
         ]
         for upper in range(2):
             at = upper * slots // 2 + begin
-            heads = [rows_ref[d, e, at : at + 2 * part, :].astype(f32) for d, e in sources]
+            heads = [
+                rows_ref[(*source, slice(at, at + 2 * part))].astype(f32) for source in sources
+            ]
             for j in range(2):
-                z = upper * n_z // 2 + 2 * p + j
+                block = upper * n_blocks // 2 + 2 * p + j
                 span = slice(j * part, (j + 1) * part)
                 values = jnp.concatenate(
                     [
@@ -166,18 +180,19 @@
                     ],
                     axis=1,
                 ).astype(bf16)
-                table = table_ref[z].astype(f32)
+                table = table_ref[block].astype(f32)
                 select = jnp.concatenate(
-                    [jnp.where(table[e : e + 1] == slot, 1.0, 0.0) for e in range(window)], axis=0
+                    [jnp.where(table[e : e + 1] == slot, 1.0, 0.0) for e in range(window)] * 2,
+                    axis=0,
                 ).astype(bf16)
                 dense = lax.dot_general(
                     values, select, contract_first, preferred_element_type=f32
                 ).astype(bf16)
-                out_ref[z, :128, :] = dense[:128]
-                out_ref[z, 128:, :] = dense[128 + upper * rest : 128 + (upper + 1) * rest]
-
-
-def gather_weights(low, high):
+                out_ref[block, :128, :] = dense[:128]
+                out_ref[block, 128:, :] = dense[128 + upper * rest : 128 + (upper + 1) * rest]
+
+
+def gather_weights(low, high, tables):
     n_x = lax.axis_size("x")
     ahead = [(i, (i + 1) % n_x) for i in range(n_x)]
     behind = [(i, (i - 1) % n_x) for i in range(n_x)]
@@ -187,17 +202,23 @@
 
     low_before = lax.ppermute(low, "x", ahead)
     high_after = lax.ppermute(high, "x", behind)
-    high_before = lax.ppermute(high, "x", ahead)
-    low_after = lax.ppermute(low, "x", behind)
+    far = (swap(low), swap(high))
+    low_later, high_later, tables, far = lax.optimization_barrier((low, high, tables, far))
+    high_before = lax.ppermute(high_later, "x", ahead)
+    low_after = lax.ppermute(low_later, "x", behind)
+    tables = lax.all_to_all(tables, "zh", 0, 0, tiled=True)
+    low_before, high_after, tables = lax.optimization_barrier((low_before, high_after, tables))
     low_across = lax.ppermute(low_before, "x", ahead)
     high_across = lax.ppermute(high_after, "x", behind)
-    near = [(low, high), (low_before, high_before), (low_after, high_after), (low_across, high_across)]
-    far = [(swap(a), swap(b)) for a, b in near]
-    return [near[0], far[0], near[1], near[2], far[1], far[2], near[3], far[3]]
+    near = [(low_before, high_before), (low_after, high_after), (low_across, high_across)]
+    swapped = [(swap(a), swap(b)) for a, b in near]
+    blocks = [(low, high), far, near[0], near[1], swapped[0], swapped[1], near[2], swapped[2]]
+    return blocks, tables
 
 
 def per_device(tokens, cotangent, experts, route_weight, gate_weight, up_weight, down_weight):
-    n_z = lax.axis_size("zh") * lax.axis_size("zl")
+    n_high = lax.axis_size("zh")
+    n_z = n_high * lax.axis_size("zl")
     n_s = lax.axis_size("x") * lax.axis_size("c")
     count, feats = tokens.shape
     quarter = feats // window
@@ -212,7 +233,7 @@
         prep_kernel,
         (
             jax.ShapeDtypeStruct((n_s, 2 * part, feats), bf16),
-            jax.ShapeDtypeStruct((n_z, table_rows, count), bf16),
+            jax.ShapeDtypeStruct((n_high, table_rows, count), bf16),
         ),
         [smem] + [vmem] * 4,
     )(expert_id, experts.T, route_weight.T, tokens, cotangent)
@@ -227,27 +248,27 @@
         (jax.ShapeDtypeStruct((3, feats // 2, hidden), bf16),) * 2,
         [vmem] * 3,
     )(gate, up, down)
-    weights = gather_weights(low, high)
-    tables = lax.all_to_all(tables, ("zh", "zl"), 0, 0, tiled=True)
+    weights, tables = gather_weights(low, high, tables)
 
     result = kernel_call(
         block_kernel,
-        jax.ShapeDtypeStruct((n_s, window, quarter, n_z * part), bf16),
+        jax.ShapeDtypeStruct((n_s, window, 2, quarter // 2, n_z * part), bf16),
         [smem] + [anywhere] * (1 + 2 * len(blocks_at)),
         [
             pltpu.VMEM((n_z, n_s, 2 * part, feats), bf16),
             pltpu.VMEM((len(blocks_at), 2, 3, feats // 2, hidden), bf16),
-            pltpu.VMEM((n_z * 2 * part, 3 * hidden), f32),
+            pltpu.VMEM((n_z * part, 3 * hidden), f32),
             pltpu.SemaphoreType.DMA((2 * len(blocks_at) + 1,)),
         ],
     )(place, rows, *[half for block in weights for half in block])
+    shape = result.shape
     result = lax.all_to_all(
-        result.reshape(n_s * window, quarter, n_z * part), ("x", "c", "y"), 0, 0, tiled=True
-    ).reshape(n_s, window, quarter, n_z * part)
+        result.reshape(n_s * window * 2, *shape[3:]), ("x", "c", "y", "zl"), 0, 0, tiled=True
+    ).reshape(shape)
     dense = kernel_call(
-        combine_kernel, jax.ShapeDtypeStruct((n_z, quarter, count), bf16), [vmem] * 2
+        combine_kernel, jax.ShapeDtypeStruct((n_high, quarter, count), bf16), [vmem] * 2
     )(tables, result)
-    dense = lax.all_to_all(dense, ("zh", "zl"), 0, 0, tiled=True)
+    dense = lax.all_to_all(dense, "zh", 0, 0, tiled=True)
     return jnp.sum(dense.astype(f32), axis=0).astype(bf16).T
 
 

time: 236 us -> 218 us (0.924)
  the two profiles are of different devices: /device:TPU:64 before, /device:TPU:1 now
where the time goes in v5:
time: 218 us; the launch traced here: 217 us
  blocking collectives  83.1 us (38%)
  starting transfers between devices  53.4 us (24%)
  waiting for transfers between devices  42.1 us (19%)
  Pallas kernels  22.5 us (10%)
  between operations  13.6 us (6%)
    all_to_all x1, blocking collectives, per_device(): dense = lax.all_to_all(dense, 'zh', 0, 0, tiled=True)  37.4 us
    all_to_all x1, blocking collectives, per_device(): lax.all_to_all(result.reshape(n_s * window * 2, *shape[3:]), ('x', 'c', '...  28.9 us
    ppermute x8, starting transfers between devices, swap(): return lax.ppermute(value, 'c', [(0, 1), (1, 0)])  23.2 us
    ppermute x1, waiting for transfers between devices, gather_weights(): low_across = lax.ppermute(low_before, 'x', ahead)  19.1 us
    all_to_all x1, blocking collectives, per_device(): pieces = lax.all_to_all(pieces, ('x', 'c'), 0, 0, tiled=True)  16.8 us
    pallas_call x1, Pallas kernels, per_device(): kernel_call(block_kernel, jax.ShapeDtypeStruct((n_s, window, 2, quarter /...  14.2 us
    ppermute x1, waiting for transfers between devices, gather_weights(): high_before = lax.ppermute(high_later, 'x', ahead)  12.3 us
    all_to_all x1, starting transfers between devices, gather_weights(): tables = lax.all_to_all(tables, 'zh', 0, 0, tiled=True)  9.85 us
  transfers between devices with their start and end apart: 16, of which 6 were waited for; matrix products, arithmetic and copies ran while one was open for 0% of the time, Pallas kernels for 2%

profile of v5, /device:TPU:1, one launch (start us, length us, event | category | flops | bytes accessed | tf_op | source)
XLA Modules:
  0.0 216.9 jit_solution(11476196663837974435)
XLA Ops:
  6.5 2.1 shard_map.73
  8.6 16.8 %all_to_all.20 = bf16[8,16,768]{2,1,0:T(8,128)(2,1)} all-to-all(bf16[8,16,768]{2,1,0:T(8,128)(2,1)} %get-tuple-element.22), channel_id=1, replica_groups=mesh['zh'=8,'zl'=2,'x'=4,'c'=2,'y'=4] {'x','c'}, dimensions={0} | all-to-all | bytes 393216 | tf_op jit(solution)/shard_map/all_to_all | solution.py:240
  25.4 3.3 %shard_map.74 = (bf16[3,384,512]{2,1,0:T(8,128)(2,1)}, bf16[3,384,512]{2,1,0:T(8,128)(2,1)}) custom-call(bf16[768,512]{1,0:T(8,128)(2,1)} %bitcast.17, bf16[768,512]{1,0:T(8,128)(2,1)} %bitcast.18, bf16[512,768]{1,0:T(8,128)(2,1)} %bitcast.19), custom_call_target="tpu_custom_call" | custom-call | tf_op jit(solution)/shard_map/pallas_call | solution.py:246
  28.7 2.8 %collective-permute-start.2 = (bf16[3,384,512]{2,1,0:T(8,128)(2,1)}, bf16[3,384,512]{2,1,0:T(8,128)(2,1)S(1)}, u32[]{:S(2)}, u32[]{:S(2)}) collective-permute-start(bf16[3,384,512]{2,1,0:T(8,128)(2,1)} %get-tuple-element.35.refs_1_), channel_id=1, source_target_pairs={{0,4},{4,0},{1,5},{5,1},{2,6},{6,2},{3,7},{7,3},{8,12},{12,8},{9,1... | collective-permute-start | bytes 3538952 | tf_op jit(solution)/shard_map/ppermute | solution.py:201
  31.5 1.9 collective-permute-start.3
  33.5 2.2 %collective-permute-start = (bf16[3,384,512]{2,1,0:T(8,128)(2,1)}, bf16[3,384,512]{2,1,0:T(8,128)(2,1)S(1)}, u32[]{:S(2)}, u32[]{:S(2)}) collective-permute-start(bf16[3,384,512]{2,1,0:T(8,128)(2,1)} %get-tuple-element.35.refs_1_), channel_id=1, source_target_pairs={{0,8},{8,16},{16,24},{24,0},{1,9},{9,17},{17,25},{25,1},{2,10},{10... | collective-permute-start | bytes 3538952 | tf_op jit(solution)/shard_map/ppermute | solution.py:203
  35.7 4.3 %collective-permute-start.1 = (bf16[3,384,512]{2,1,0:T(8,128)(2,1)}, bf16[3,384,512]{2,1,0:T(8,128)(2,1)}, u32[]{:S(2)}, u32[]{:S(2)}) collective-permute-start(bf16[3,384,512]{2,1,0:T(8,128)(2,1)} %get-tuple-element.34.refs_2_), channel_id=1, source_target_pairs={{0,24},{8,0},{16,8},{24,16},{1,25},{9,1},{17,9},{25,17},{2,26},{10... | collective-permute-start | bytes 3538952 | tf_op jit(solution)/shard_map/ppermute | solution.py:204
  40.0 9.9 %all-to-all-start.1 = ((bf16[8,16,128]{2,1,0:T(8,128)(2,1)}), bf16[8,16,128]{2,1,0:T(8,128)(2,1)}, u32[]{:S(2)}, u32[]{:S(2)}) async-start(bf16[8,16,128]{2,1,0:T(8,128)(2,1)} %get-tuple-element.29), calls=%async_computation.1 | async-start | bytes 65536 | tf_op jit(solution)/shard_map/all_to_all | solution.py:209
  51.8 4.6 %collective-permute-start.5 = (bf16[3,384,512]{2,1,0:T(8,128)(2,1)}, bf16[3,384,512]{2,1,0:T(8,128)(2,1)}, u32[]{:S(2)}, u32[]{:S(2)}) collective-permute-start(bf16[3,384,512]{2,1,0:T(8,128)(2,1)} %get-tuple-element.35.refs_1_), channel_id=1, source_target_pairs={{0,24},{8,0},{16,8},{24,16},{1,25},{9,1},{17,9},{25,17},{2,26},{10... | collective-permute-start | bytes 3538952 | tf_op jit(solution)/shard_map/ppermute | solution.py:208
  56.4 7.5 %collective-permute-done.refs_5_ = bf16[3,384,512]{2,1,0:T(8,128)(2,1)S(1)} collective-permute-done((bf16[3,384,512]{2,1,0:T(8,128)(2,1)}, bf16[3,384,512]{2,1,0:T(8,128)(2,1)S(1)}, u32[]{:S(2)}, u32[]{:S(2)}) %collective-permute-start) | collective-permute-done | bytes 1179680 | tf_op jit(solution)/shard_map/ppermute | solution.py:203
  64.8 2.0 collective-permute-start.10
  66.8 4.7 %collective-permute-start.6 = (bf16[3,384,512]{2,1,0:T(8,128)(2,1)S(1)}, bf16[3,384,512]{2,1,0:T(8,128)(2,1)S(1)}, u32[]{:S(2)}, u32[]{:S(2)}) collective-permute-start(bf16[3,384,512]{2,1,0:T(8,128)(2,1)S(1)} %collective-permute-done.refs_5_), channel_id=1, source_target_pairs={{0,4},{4,0},{1,5},{5,1},{2,6},{6,2},{3,7},{7,3},{8,12},{12,8},{9,1... | collective-permute-start | bytes 3538952 | tf_op jit(solution)/shard_map/ppermute | solution.py:201
  71.6 5.3 %collective-permute-start.11 = (bf16[3,384,512]{2,1,0:T(8,128)(2,1)}, bf16[3,384,512]{2,1,0:T(8,128)(2,1)}, u32[]{:S(2)}, u32[]{:S(2)}) collective-permute-start(bf16[3,384,512]{2,1,0:T(8,128)(2,1)} %collective-permute-done.1.refs_8_), channel_id=1, source_target_pairs={{0,24},{8,0},{16,8},{24,16},{1,25},{9,1},{17,9},{25,17},{2,26},{10... | collective-permute-start | bytes 3538952 | tf_op jit(solution)/shard_map/ppermute | solution.py:212
  76.9 12.3 %collective-permute-done.4.refs_6_ = bf16[3,384,512]{2,1,0:T(8,128)(2,1)} collective-permute-done((bf16[3,384,512]{2,1,0:T(8,128)(2,1)}, bf16[3,384,512]{2,1,0:T(8,128)(2,1)}, u32[]{:S(2)}, u32[]{:S(2)}) %collective-permute-start.4) | collective-permute-done | bytes 1179680 | tf_op jit(solution)/shard_map/ppermute | solution.py:207
  89.2 4.2 %collective-permute-start.9 = (bf16[3,384,512]{2,1,0:T(8,128)(2,1)}, bf16[3,384,512]{2,1,0:T(8,128)(2,1)}, u32[]{:S(2)}, u32[]{:S(2)}) collective-permute-start(bf16[3,384,512]{2,1,0:T(8,128)(2,1)} %collective-permute-done.1.refs_8_), channel_id=1, source_target_pairs={{0,4},{4,0},{1,5},{5,1},{2,6},{6,2},{3,7},{7,3},{8,12},{12,8},{9,1... | collective-permute-start | bytes 3538952 | tf_op jit(solution)/shard_map/ppermute | solution.py:201
  93.4 1.9 collective-permute-start.7
  95.3 19.1 %collective-permute-done.10.refs_13_ = bf16[3,384,512]{2,1,0:T(8,128)(2,1)} collective-permute-done((bf16[3,384,512]{2,1,0:T(8,128)(2,1)S(1)}, bf16[3,384,512]{2,1,0:T(8,128)(2,1)}, u32[]{:S(2)}, u32[]{:S(2)}) %collective-permute-start.10) | collective-permute-done | bytes 1179680 | tf_op jit(solution)/shard_map/ppermute | solution.py:211
  114.5 3.2 %collective-permute-start.8 = (bf16[3,384,512]{2,1,0:T(8,128)(2,1)}, bf16[3,384,512]{2,1,0:T(8,128)(2,1)}, u32[]{:S(2)}, u32[]{:S(2)}) collective-permute-start(bf16[3,384,512]{2,1,0:T(8,128)(2,1)} %collective-permute-done.5.refs_7_), channel_id=1, source_target_pairs={{0,4},{4,0},{1,5},{5,1},{2,6},{6,2},{3,7},{7,3},{8,12},{12,8},{9,1... | collective-permute-start | bytes 3538952 | tf_op jit(solution)/shard_map/ppermute | solution.py:201
  120.7 2.4 %collective-permute-start.13 = (bf16[3,384,512]{2,1,0:T(8,128)(2,1)}, bf16[3,384,512]{2,1,0:T(8,128)(2,1)}, u32[]{:S(2)}, u32[]{:S(2)}) collective-permute-start(bf16[3,384,512]{2,1,0:T(8,128)(2,1)} %collective-permute-done.11.refs_14_), channel_id=1, source_target_pairs={{0,4},{4,0},{1,5},{5,1},{2,6},{6,2},{3,7},{7,3},{8,12},{12,8},{9,1... | collective-permute-start | bytes 3538952 | tf_op jit(solution)/shard_map/ppermute | solution.py:201
  123.8 2.1 collective-permute-done.13.refs_16_
  125.9 14.2 %shard_map.75 = bf16[8,4,2,96,128]{4,3,2,1,0:T(8,128)(2,1)} custom-call(s32[2]{0:T(128)} %pad_add_fusion.place_ref, bf16[16,8,16,768]{3,2,1,0:T(8,128)(2,1)} %bitcast.15, bf16[3,384,512]{2,1,0:T(8,128)(2,1)} %get-tuple-element.35.refs_1_, bf16[3,384,512]{2,1,0:T(8,128)(2,1)} %get-tuple-element.34.refs_2_, bf16[3,384,512]{2,1,0:T(8,128)(2,1)} %copy-done, ...), custom_call_target="tpu_custom_call" | custom-call | tf_op jit(solution)/shard_map/pallas_call | solution.py:253
  140.1 28.9 %all_to_all.21 = bf16[64,96,128]{2,1,0:T(8,128)(2,1)} all-to-all(bf16[64,96,128]{2,1,0:T(8,128)(2,1)} %bitcast.13), channel_id=1, replica_groups=mesh['zh'=8,'zl'=2,'x'=4,'c'=2,'y'=4] {'x','c','y','zl'}, dimensions={0} | all-to-all | bytes 3145728 | tf_op jit(solution)/shard_map/all_to_all | solution.py:265
  169.0 3.0 %shard_map.76 = bf16[8,192,128]{2,1,0:T(8,128)(2,1)} custom-call(bf16[8,16,128]{2,1,0:T(8,128)(2,1)} %all-to-all-done.1.table_ref, bf16[8,4,2,96,128]{4,3,2,1,0:T(8,128)(2,1)} %bitcast.14), custom_call_target="tpu_custom_call" | custom-call | tf_op jit(solution)/shard_map/pallas_call | solution.py:268
  172.0 37.4 %all_to_all.22 = bf16[8,192,128]{2,1,0:T(8,128)(2,1)S(1)} all-to-all(bf16[8,192,128]{2,1,0:T(8,128)(2,1)} %shard_map.76), channel_id=1, replica_groups=mesh['zh'=8,'zl'=2,'x'=4,'c'=2,'y'=4] {'zh'}, dimensions={0} | all-to-all | bytes 786432 | tf_op jit(solution)/shard_map/all_to_all | solution.py:271
  (26 shorter events, 7.2 us)
Async XLA Ops:
  6.5 119.4 %all-gather.2.cloned.1.call-start = ((), (), s32[]{:S(2)}) async-start(), calls=%async_computation.4 | async-start | bytes 3342336 | tf_op jit(solution)/shard_map/all_gather | solution.py:241
  28.7 11.3 %collective-permute-start.2 = (bf16[3,384,512]{2,1,0:T(8,128)(2,1)}, bf16[3,384,512]{2,1,0:T(8,128)(2,1)S(1)}, u32[]{:S(2)}, u32[]{:S(2)}) collective-permute-start(bf16[3,384,512]{2,1,0:T(8,128)(2,1)} %get-tuple-element.35.refs_1_), channel_id=1, source_target_pairs={{0,4},{4,0},{1,5},{5,1},{2,6},{6,2},{3,7},{7,3},{8,12},{12,8},{9,1... | collective-permute-start | bytes 3538952 | tf_op jit(solution)/shard_map/ppermute | solution.py:201
  31.5 8.5 %collective-permute-start.3 = (bf16[3,384,512]{2,1,0:T(8,128)(2,1)}, bf16[3,384,512]{2,1,0:T(8,128)(2,1)S(1)}, u32[]{:S(2)}, u32[]{:S(2)}) collective-permute-start(bf16[3,384,512]{2,1,0:T(8,128)(2,1)} %get-tuple-element.34.refs_2_), channel_id=1, source_target_pairs={{0,4},{4,0},{1,5},{5,1},{2,6},{6,2},{3,7},{7,3},{8,12},{12,8},{9,1... | collective-permute-start | bytes 3538952 | tf_op jit(solution)/shard_map/ppermute | solution.py:201
  33.5 30.4 %collective-permute-start = (bf16[3,384,512]{2,1,0:T(8,128)(2,1)}, bf16[3,384,512]{2,1,0:T(8,128)(2,1)S(1)}, u32[]{:S(2)}, u32[]{:S(2)}) collective-permute-start(bf16[3,384,512]{2,1,0:T(8,128)(2,1)} %get-tuple-element.35.refs_1_), channel_id=1, source_target_pairs={{0,8},{8,16},{16,24},{24,0},{1,9},{9,17},{17,25},{25,1},{2,10},{10... | collective-permute-start | bytes 3538952 | tf_op jit(solution)/shard_map/ppermute | solution.py:203
  35.7 29.1 %collective-permute-start.1 = (bf16[3,384,512]{2,1,0:T(8,128)(2,1)}, bf16[3,384,512]{2,1,0:T(8,128)(2,1)}, u32[]{:S(2)}, u32[]{:S(2)}) collective-permute-start(bf16[3,384,512]{2,1,0:T(8,128)(2,1)} %get-tuple-element.34.refs_2_), channel_id=1, source_target_pairs={{0,24},{8,0},{16,8},{24,16},{1,25},{9,1},{17,9},{25,17},{2,26},{10... | collective-permute-start | bytes 3538952 | tf_op jit(solution)/shard_map/ppermute | solution.py:204
  40.0 85.9 %copy-start = (bf16[3,384,512]{2,1,0:T(8,128)(2,1)}, bf16[3,384,512]{2,1,0:T(8,128)(2,1)S(1)}, u32[]{:S(2)}) copy-start(bf16[3,384,512]{2,1,0:T(8,128)(2,1)S(1)} %collective-permute-done.2.refs_3_) | copy-start | bytes 3538948
  40.0 85.9 %copy-start.1 = (bf16[3,384,512]{2,1,0:T(8,128)(2,1)}, bf16[3,384,512]{2,1,0:T(8,128)(2,1)S(1)}, u32[]{:S(2)}) copy-start(bf16[3,384,512]{2,1,0:T(8,128)(2,1)S(1)} %collective-permute-done.3.refs_4_) | copy-start | bytes 3538948
  40.0 24.8 %all-to-all-start.1 = ((bf16[8,16,128]{2,1,0:T(8,128)(2,1)}), bf16[8,16,128]{2,1,0:T(8,128)(2,1)}, u32[]{:S(2)}, u32[]{:S(2)}) async-start(bf16[8,16,128]{2,1,0:T(8,128)(2,1)} %get-tuple-element.29), calls=%async_computation.1 | async-start | bytes 65536 | tf_op jit(solution)/shard_map/all_to_all | solution.py:209
  49.9 39.3 %collective-permute-start.4 = (bf16[3,384,512]{2,1,0:T(8,128)(2,1)}, bf16[3,384,512]{2,1,0:T(8,128)(2,1)}, u32[]{:S(2)}, u32[]{:S(2)}) collective-permute-start(bf16[3,384,512]{2,1,0:T(8,128)(2,1)} %get-tuple-element.34.refs_2_), channel_id=1, source_target_pairs={{0,8},{8,16},{16,24},{24,0},{1,9},{9,17},{17,25},{25,1},{2,10},{10... | collective-permute-start | bytes 3538952 | tf_op jit(solution)/shard_map/ppermute | solution.py:207
  51.8 41.6 %collective-permute-start.5 = (bf16[3,384,512]{2,1,0:T(8,128)(2,1)}, bf16[3,384,512]{2,1,0:T(8,128)(2,1)}, u32[]{:S(2)}, u32[]{:S(2)}) collective-permute-start(bf16[3,384,512]{2,1,0:T(8,128)(2,1)} %get-tuple-element.35.refs_1_), channel_id=1, source_target_pairs={{0,24},{8,0},{16,8},{24,16},{1,25},{9,1},{17,9},{25,17},{2,26},{10... | collective-permute-start | bytes 3538952 | tf_op jit(solution)/shard_map/ppermute | solution.py:208
  63.9 62.0 %copy-start.2 = (bf16[3,384,512]{2,1,0:T(8,128)(2,1)}, bf16[3,384,512]{2,1,0:T(8,128)(2,1)S(1)}, u32[]{:S(2)}) copy-start(bf16[3,384,512]{2,1,0:T(8,128)(2,1)S(1)} %collective-permute-done.refs_5_) | copy-start | bytes 3538948
  64.8 49.7 %collective-permute-start.10 = (bf16[3,384,512]{2,1,0:T(8,128)(2,1)S(1)}, bf16[3,384,512]{2,1,0:T(8,128)(2,1)}, u32[]{:S(2)}, u32[]{:S(2)}) collective-permute-start(bf16[3,384,512]{2,1,0:T(8,128)(2,1)S(1)} %collective-permute-done.refs_5_), channel_id=1, source_target_pairs={{0,8},{8,16},{16,24},{24,0},{1,9},{9,17},{17,25},{25,1},{2,10},{10... | collective-permute-start | bytes 3538952 | tf_op jit(solution)/shard_map/ppermute | solution.py:211
  66.8 50.9 %collective-permute-start.6 = (bf16[3,384,512]{2,1,0:T(8,128)(2,1)S(1)}, bf16[3,384,512]{2,1,0:T(8,128)(2,1)S(1)}, u32[]{:S(2)}, u32[]{:S(2)}) collective-permute-start(bf16[3,384,512]{2,1,0:T(8,128)(2,1)S(1)} %collective-permute-done.refs_5_), channel_id=1, source_target_pairs={{0,4},{4,0},{1,5},{5,1},{2,6},{6,2},{3,7},{7,3},{8,12},{12,8},{9,1... | collective-permute-start | bytes 3538952 | tf_op jit(solution)/shard_map/ppermute | solution.py:201
  71.6 49.1 %collective-permute-start.11 = (bf16[3,384,512]{2,1,0:T(8,128)(2,1)}, bf16[3,384,512]{2,1,0:T(8,128)(2,1)}, u32[]{:S(2)}, u32[]{:S(2)}) collective-permute-start(bf16[3,384,512]{2,1,0:T(8,128)(2,1)} %collective-permute-done.1.refs_8_), channel_id=1, source_target_pairs={{0,24},{8,0},{16,8},{24,16},{1,25},{9,1},{17,9},{25,17},{2,26},{10... | collective-permute-start | bytes 3538952 | tf_op jit(solution)/shard_map/ppermute | solution.py:212
  89.2 34.5 %collective-permute-start.9 = (bf16[3,384,512]{2,1,0:T(8,128)(2,1)}, bf16[3,384,512]{2,1,0:T(8,128)(2,1)}, u32[]{:S(2)}, u32[]{:S(2)}) collective-permute-start(bf16[3,384,512]{2,1,0:T(8,128)(2,1)} %collective-permute-done.1.refs_8_), channel_id=1, source_target_pairs={{0,4},{4,0},{1,5},{5,1},{2,6},{6,2},{3,7},{7,3},{8,12},{12,8},{9,1... | collective-permute-start | bytes 3538952 | tf_op jit(solution)/shard_map/ppermute | solution.py:201
  93.4 30.3 %collective-permute-start.7 = (bf16[3,384,512]{2,1,0:T(8,128)(2,1)}, bf16[3,384,512]{2,1,0:T(8,128)(2,1)}, u32[]{:S(2)}, u32[]{:S(2)}) collective-permute-start(bf16[3,384,512]{2,1,0:T(8,128)(2,1)} %collective-permute-done.4.refs_6_), channel_id=1, source_target_pairs={{0,4},{4,0},{1,5},{5,1},{2,6},{6,2},{3,7},{7,3},{8,12},{12,8},{9,1... | collective-permute-start | bytes 3538952 | tf_op jit(solution)/shard_map/ppermute | solution.py:201
  114.5 9.2 %collective-permute-start.8 = (bf16[3,384,512]{2,1,0:T(8,128)(2,1)}, bf16[3,384,512]{2,1,0:T(8,128)(2,1)}, u32[]{:S(2)}, u32[]{:S(2)}) collective-permute-start(bf16[3,384,512]{2,1,0:T(8,128)(2,1)} %collective-permute-done.5.refs_7_), channel_id=1, source_target_pairs={{0,4},{4,0},{1,5},{5,1},{2,6},{6,2},{3,7},{7,3},{8,12},{12,8},{9,1... | collective-permute-start | bytes 3538952 | tf_op jit(solution)/shard_map/ppermute | solution.py:201
  117.7 1.0 copy-start.3
  118.8 5.1 %collective-permute-start.12 = (bf16[3,384,512]{2,1,0:T(8,128)(2,1)}, bf16[3,384,512]{2,1,0:T(8,128)(2,1)}, u32[]{:S(2)}, u32[]{:S(2)}) collective-permute-start(bf16[3,384,512]{2,1,0:T(8,128)(2,1)} %collective-permute-done.10.refs_13_), channel_id=1, source_target_pairs={{0,4},{4,0},{1,5},{5,1},{2,6},{6,2},{3,7},{7,3},{8,12},{12,8},{9,1... | collective-permute-start | bytes 3538952 | tf_op jit(solution)/shard_map/ppermute | solution.py:201
  120.7 5.2 %collective-permute-start.13 = (bf16[3,384,512]{2,1,0:T(8,128)(2,1)}, bf16[3,384,512]{2,1,0:T(8,128)(2,1)}, u32[]{:S(2)}, u32[]{:S(2)}) collective-permute-start(bf16[3,384,512]{2,1,0:T(8,128)(2,1)} %collective-permute-done.11.refs_14_), channel_id=1, source_target_pairs={{0,4},{4,0},{1,5},{5,1},{2,6},{6,2},{3,7},{7,3},{8,12},{12,8},{9,1... | collective-permute-start | bytes 3538952 | tf_op jit(solution)/shard_map/ppermute | solution.py:201
Sparse Core Ops, SparseCore 0:
  25.5 66.4 all-gather.1

commit v6 on v5

--- a/solution.py
+++ b/solution.py
@@ -192,24 +192,25 @@
                 out_ref[block, 128:, :] = dense[128 + upper * rest : 128 + (upper + 1) * rest]
 
 
+def swap(value):
+    return lax.ppermute(value, "c", [(0, 1), (1, 0)])
+
+
 def gather_weights(low, high, tables):
     n_x = lax.axis_size("x")
     ahead = [(i, (i + 1) % n_x) for i in range(n_x)]
     behind = [(i, (i - 1) % n_x) for i in range(n_x)]
-
-    def swap(value):
-        return lax.ppermute(value, "c", [(0, 1), (1, 0)])
-
     low_before = lax.ppermute(low, "x", ahead)
     high_after = lax.ppermute(high, "x", behind)
     far = (swap(low), swap(high))
-    low_later, high_later, tables, far = lax.optimization_barrier((low, high, tables, far))
+    low_later, high_later, far = lax.optimization_barrier((low, high, far))
     high_before = lax.ppermute(high_later, "x", ahead)
     low_after = lax.ppermute(low_later, "x", behind)
-    tables = lax.all_to_all(tables, "zh", 0, 0, tiled=True)
-    low_before, high_after, tables = lax.optimization_barrier((low_before, high_after, tables))
     low_across = lax.ppermute(low_before, "x", ahead)
     high_across = lax.ppermute(high_after, "x", behind)
+    tables, low_before, high_after = lax.optimization_barrier((tables, low_before, high_after))
+    tables = lax.all_to_all(tables, "zh", 0, 0, tiled=True)
+    tables, high_before, low_after = lax.optimization_barrier((tables, high_before, low_after))
     near = [(low_before, high_before), (low_after, high_after), (low_across, high_across)]
     swapped = [(swap(a), swap(b)) for a, b in near]
     blocks = [(low, high), far, near[0], near[1], swapped[0], swapped[1], near[2], swapped[2]]
@@ -237,17 +238,18 @@
         ),
         [smem] + [vmem] * 4,
     )(expert_id, experts.T, route_weight.T, tokens, cotangent)
+    gate, up, down, pieces = lax.optimization_barrier((gate, up, down, pieces))
     pieces = lax.all_to_all(pieces, ("x", "c"), 0, 0, tiled=True)
-    rows = lax.all_gather(
-        pieces.reshape(n_s * 2 * part, feats), ("zh", "zl"), axis=0, tiled=True
-    ).reshape(n_z, n_s, 2 * part, feats)
-
-    tables, gate, up, down, pieces = lax.optimization_barrier((tables, gate, up, down, pieces))
     low, high = kernel_call(
         weights_kernel,
         (jax.ShapeDtypeStruct((3, feats // 2, hidden), bf16),) * 2,
         [vmem] * 3,
     )(gate, up, down)
+    pieces, low, high, tables = lax.optimization_barrier((pieces, low, high, tables))
+    rows = lax.all_gather(
+        pieces.reshape(n_s * 2 * part, feats), ("zh", "zl"), axis=0, tiled=True
+    ).reshape(n_z, n_s, 2 * part, feats)
+
     weights, tables = gather_weights(low, high, tables)
 
     result = kernel_call(

time: 218 us -> 214 us (0.982)
  blocking collectives: 83.1 us -> 66.9 us
  starting transfers between devices: 53.4 us -> 65.8 us
    all_to_all x1 -> x0, blocking collectives: 16.8 us -> none  [per_device(): pieces = lax.all_to_all(pieces, ('x', 'c'), 0, 0, tiled=True)]
    ppermute x1, waiting for transfers between devices: 12.3 us -> 1.88 us  [gather_weights(): high_before = lax.ppermute(high_later, 'x', ahead)]
    all_to_all x0 -> x1, starting transfers between devices: none -> 10.2 us  [per_device(): pieces = lax.all_to_all(pieces, ('x', 'c'), 0, 0, tiled=True)]
    ppermute x1, waiting for transfers between devices: 7.52 us -> 17.3 us  [gather_weights(): low_before = lax.ppermute(low, 'x', ahead)]
    ppermute x1, waiting for transfers between devices: 19.1 us -> 11.5 us  [gather_weights(): low_across = lax.ppermute(low_before, 'x', ahead)]
    all_to_all x1, waiting for transfers between devices: 0.01 us -> 5.97 us  [gather_weights(): tables = lax.all_to_all(tables, 'zh', 0, 0, tiled=True)]
    all_to_all x0 -> x1, waiting for transfers between devices: none -> 2.63 us  [per_device(): pieces = lax.all_to_all(pieces, ('x', 'c'), 0, 0, tiled=True)]
  transfers between devices with their start and end apart: 16 -> 17, of which waited for: 6 -> 8; matrix products, arithmetic and copies ran while one was open for 0% -> 0% of each run, Pallas kernels for 2% -> 2%
where the time goes in v6:
time: 214 us; the launch traced here: 213 us
  blocking collectives  66.9 us (31%)
  starting transfers between devices  65.8 us (31%)
  waiting for transfers between devices  42.5 us (20%)
  Pallas kernels  22.5 us (11%)
  between operations  13.6 us (6%)
    all_to_all x1, blocking collectives, per_device(): dense = lax.all_to_all(dense, 'zh', 0, 0, tiled=True)  38 us
    all_to_all x1, blocking collectives, per_device(): lax.all_to_all(result.reshape(n_s * window * 2, *shape[3:]), ('x', 'c', '...  28.9 us
    ppermute x8, starting transfers between devices, swap(): return lax.ppermute(value, 'c', [(0, 1), (1, 0)])  24.8 us
    ppermute x1, waiting for transfers between devices, gather_weights(): low_before = lax.ppermute(low, 'x', ahead)  17.3 us
    pallas_call x1, Pallas kernels, per_device(): kernel_call(block_kernel, jax.ShapeDtypeStruct((n_s, window, 2, quarter /...  14.2 us
    ppermute x1, waiting for transfers between devices, gather_weights(): low_across = lax.ppermute(low_before, 'x', ahead)  11.5 us
    all_to_all x1, starting transfers between devices, gather_weights(): tables = lax.all_to_all(tables, 'zh', 0, 0, tiled=True)  10.4 us
    all_to_all x1, starting transfers between devices, per_device(): pieces = lax.all_to_all(pieces, ('x', 'c'), 0, 0, tiled=True)  10.2 us
  transfers between devices with their start and end apart: 17, of which 8 were waited for; matrix products, arithmetic and copies ran while one was open for 0% of the time, Pallas kernels for 2%

profile of v6, /device:TPU:1, one launch (start us, length us, event | category | flops | bytes accessed | tf_op | source)
XLA Modules:
  0.0 213.2 jit_solution(10638522942001299950)
XLA Ops:
  6.5 2.1 shard_map.73
  8.6 10.2 %all-to-all-start = ((bf16[8,16,768]{2,1,0:T(8,128)(2,1)}), bf16[8,16,768]{2,1,0:T(8,128)(2,1)S(1)}, u32[]{:S(2)}, u32[]{:S(2)}) async-start(bf16[8,16,768]{2,1,0:T(8,128)(2,1)} %get-tuple-element.28), calls=%async_computation | async-start | bytes 393216 | tf_op jit(solution)/shard_map/all_to_all | solution.py:242
  18.8 3.3 %shard_map.74 = (bf16[3,384,512]{2,1,0:T(8,128)(2,1)}, bf16[3,384,512]{2,1,0:T(8,128)(2,1)}) custom-call(bf16[768,512]{1,0:T(8,128)(2,1)} %bitcast.17, bf16[768,512]{1,0:T(8,128)(2,1)} %bitcast.18, bf16[512,768]{1,0:T(8,128)(2,1)} %bitcast.19), custom_call_target="tpu_custom_call" | custom-call | tf_op jit(solution)/shard_map/pallas_call | solution.py:243
  22.1 2.6 %all-to-all-done = bf16[8,16,768]{2,1,0:T(8,128)(2,1)S(1)} async-done(((bf16[8,16,768]{2,1,0:T(8,128)(2,1)}), bf16[8,16,768]{2,1,0:T(8,128)(2,1)S(1)}, u32[]{:S(2)}, u32[]{:S(2)}) %all-to-all-start) | async-done | bytes 196640 | tf_op jit(solution)/shard_map/all_to_all | solution.py:242
  25.4 2.9 %collective-permute-start.2 = (bf16[3,384,512]{2,1,0:T(8,128)(2,1)}, bf16[3,384,512]{2,1,0:T(8,128)(2,1)S(1)}, u32[]{:S(2)}, u32[]{:S(2)}) collective-permute-start(bf16[3,384,512]{2,1,0:T(8,128)(2,1)} %get-tuple-element.40.refs_1_), channel_id=1, source_target_pairs={{0,4},{4,0},{1,5},{5,1},{2,6},{6,2},{3,7},{7,3},{8,12},{12,8},{9,1... | collective-permute-start | bytes 3538952 | tf_op jit(solution)/shard_map/ppermute | solution.py:196
  30.2 2.2 %collective-permute-start = (bf16[3,384,512]{2,1,0:T(8,128)(2,1)}, bf16[3,384,512]{2,1,0:T(8,128)(2,1)S(1)}, u32[]{:S(2)}, u32[]{:S(2)}) collective-permute-start(bf16[3,384,512]{2,1,0:T(8,128)(2,1)} %get-tuple-element.40.refs_1_), channel_id=1, source_target_pairs={{0,8},{8,16},{16,24},{24,0},{1,9},{9,17},{17,25},{25,1},{2,10},{10... | collective-permute-start | bytes 3538952 | tf_op jit(solution)/shard_map/ppermute | solution.py:203
  32.4 4.3 %collective-permute-start.1 = (bf16[3,384,512]{2,1,0:T(8,128)(2,1)}, bf16[3,384,512]{2,1,0:T(8,128)(2,1)}, u32[]{:S(2)}, u32[]{:S(2)}) collective-permute-start(bf16[3,384,512]{2,1,0:T(8,128)(2,1)} %get-tuple-element.39.refs_2_), channel_id=1, source_target_pairs={{0,24},{8,0},{16,8},{24,16},{1,25},{9,1},{17,9},{25,17},{2,26},{10... | collective-permute-start | bytes 3538952 | tf_op jit(solution)/shard_map/ppermute | solution.py:204
  38.7 4.6 %collective-permute-start.5 = (bf16[3,384,512]{2,1,0:T(8,128)(2,1)}, bf16[3,384,512]{2,1,0:T(8,128)(2,1)}, u32[]{:S(2)}, u32[]{:S(2)}) collective-permute-start(bf16[3,384,512]{2,1,0:T(8,128)(2,1)} %get-tuple-element.40.refs_1_), channel_id=1, source_target_pairs={{0,24},{8,0},{16,8},{24,16},{1,25},{9,1},{17,9},{25,17},{2,26},{10... | collective-permute-start | bytes 3538952 | tf_op jit(solution)/shard_map/ppermute | solution.py:208
  43.2 17.3 %collective-permute-done.refs_5_ = bf16[3,384,512]{2,1,0:T(8,128)(2,1)S(1)} collective-permute-done((bf16[3,384,512]{2,1,0:T(8,128)(2,1)}, bf16[3,384,512]{2,1,0:T(8,128)(2,1)S(1)}, u32[]{:S(2)}, u32[]{:S(2)}) %collective-permute-start) | collective-permute-done | bytes 1179680 | tf_op jit(solution)/shard_map/ppermute | solution.py:203
  61.5 2.0 collective-permute-start.10
  63.6 4.7 %collective-permute-start.6 = (bf16[3,384,512]{2,1,0:T(8,128)(2,1)S(1)}, bf16[3,384,512]{2,1,0:T(8,128)(2,1)}, u32[]{:S(2)}, u32[]{:S(2)}) collective-permute-start(bf16[3,384,512]{2,1,0:T(8,128)(2,1)S(1)} %collective-permute-done.refs_5_), channel_id=1, source_target_pairs={{0,4},{4,0},{1,5},{5,1},{2,6},{6,2},{3,7},{7,3},{8,12},{12,8},{9,1... | collective-permute-start | bytes 3538952 | tf_op jit(solution)/shard_map/ppermute | solution.py:196
  68.3 5.3 %collective-permute-start.11 = (bf16[3,384,512]{2,1,0:T(8,128)(2,1)}, bf16[3,384,512]{2,1,0:T(8,128)(2,1)}, u32[]{:S(2)}, u32[]{:S(2)}) collective-permute-start(bf16[3,384,512]{2,1,0:T(8,128)(2,1)} %collective-permute-done.1.refs_8_), channel_id=1, source_target_pairs={{0,24},{8,0},{16,8},{24,16},{1,25},{9,1},{17,9},{25,17},{2,26},{10... | collective-permute-start | bytes 3538952 | tf_op jit(solution)/shard_map/ppermute | solution.py:210
  73.6 10.4 %all-to-all-start.1 = ((bf16[8,16,128]{2,1,0:T(8,128)(2,1)}), bf16[8,16,128]{2,1,0:T(8,128)(2,1)}, u32[]{:S(2)}, u32[]{:S(2)}) async-start(bf16[8,16,128]{2,1,0:T(8,128)(2,1)} %get-tuple-element.38), calls=%async_computation.1 | async-start | bytes 65536 | tf_op jit(solution)/shard_map/all_to_all | solution.py:212
  85.9 4.2 %collective-permute-start.9 = (bf16[3,384,512]{2,1,0:T(8,128)(2,1)}, bf16[3,384,512]{2,1,0:T(8,128)(2,1)}, u32[]{:S(2)}, u32[]{:S(2)}) collective-permute-start(bf16[3,384,512]{2,1,0:T(8,128)(2,1)} %collective-permute-done.1.refs_8_), channel_id=1, source_target_pairs={{0,4},{4,0},{1,5},{5,1},{2,6},{6,2},{3,7},{7,3},{8,12},{12,8},{9,1... | collective-permute-start | bytes 3538952 | tf_op jit(solution)/shard_map/ppermute | solution.py:196
  90.1 6.0 %all-to-all-done.1.table_ref = bf16[8,16,128]{2,1,0:T(8,128)(2,1)} async-done(((bf16[8,16,128]{2,1,0:T(8,128)(2,1)}), bf16[8,16,128]{2,1,0:T(8,128)(2,1)}, u32[]{:S(2)}, u32[]{:S(2)}) %all-to-all-start.1) | async-done | bytes 32800 | tf_op jit(solution)/shard_map/all_to_all | solution.py:212
  96.1 3.6 %collective-permute-start.7 = (bf16[3,384,512]{2,1,0:T(8,128)(2,1)}, bf16[3,384,512]{2,1,0:T(8,128)(2,1)}, u32[]{:S(2)}, u32[]{:S(2)}) collective-permute-start(bf16[3,384,512]{2,1,0:T(8,128)(2,1)} %collective-permute-done.4.refs_6_), channel_id=1, source_target_pairs={{0,4},{4,0},{1,5},{5,1},{2,6},{6,2},{3,7},{7,3},{8,12},{12,8},{9,1... | collective-permute-start | bytes 3538952 | tf_op jit(solution)/shard_map/ppermute | solution.py:196
  99.7 11.5 %collective-permute-done.10.refs_13_ = bf16[3,384,512]{2,1,0:T(8,128)(2,1)} collective-permute-done((bf16[3,384,512]{2,1,0:T(8,128)(2,1)S(1)}, bf16[3,384,512]{2,1,0:T(8,128)(2,1)}, u32[]{:S(2)}, u32[]{:S(2)}) %collective-permute-start.10) | collective-permute-done | bytes 1179680 | tf_op jit(solution)/shard_map/ppermute | solution.py:209
  111.2 3.2 %collective-permute-start.12 = (bf16[3,384,512]{2,1,0:T(8,128)(2,1)}, bf16[3,384,512]{2,1,0:T(8,128)(2,1)}, u32[]{:S(2)}, u32[]{:S(2)}) collective-permute-start(bf16[3,384,512]{2,1,0:T(8,128)(2,1)} %collective-permute-done.10.refs_13_), channel_id=1, source_target_pairs={{0,4},{4,0},{1,5},{5,1},{2,6},{6,2},{3,7},{7,3},{8,12},{12,8},{9,1... | collective-permute-start | bytes 3538952 | tf_op jit(solution)/shard_map/ppermute | solution.py:196
  116.4 2.4 %collective-permute-start.13 = (bf16[3,384,512]{2,1,0:T(8,128)(2,1)}, bf16[3,384,512]{2,1,0:T(8,128)(2,1)}, u32[]{:S(2)}, u32[]{:S(2)}) collective-permute-start(bf16[3,384,512]{2,1,0:T(8,128)(2,1)} %collective-permute-done.11.refs_14_), channel_id=1, source_target_pairs={{0,4},{4,0},{1,5},{5,1},{2,6},{6,2},{3,7},{7,3},{8,12},{12,8},{9,1... | collective-permute-start | bytes 3538952 | tf_op jit(solution)/shard_map/ppermute | solution.py:196
  119.5 2.1 collective-permute-done.13.refs_16_
  121.6 14.2 %shard_map.75 = bf16[8,4,2,96,128]{4,3,2,1,0:T(8,128)(2,1)} custom-call(s32[2]{0:T(128)} %pad_add_fusion.place_ref, bf16[16,8,16,768]{3,2,1,0:T(8,128)(2,1)} %bitcast.15, bf16[3,384,512]{2,1,0:T(8,128)(2,1)} %get-tuple-element.40.refs_1_, bf16[3,384,512]{2,1,0:T(8,128)(2,1)} %get-tuple-element.39.refs_2_, bf16[3,384,512]{2,1,0:T(8,128)(2,1)} %copy-done, ...), custom_call_target="tpu_custom_call" | custom-call | tf_op jit(solution)/shard_map/pallas_call | solution.py:255
  135.8 28.9 %all_to_all.20 = bf16[64,96,128]{2,1,0:T(8,128)(2,1)} all-to-all(bf16[64,96,128]{2,1,0:T(8,128)(2,1)} %bitcast.13), channel_id=1, replica_groups=mesh['zh'=8,'zl'=2,'x'=4,'c'=2,'y'=4] {'x','c','y','zl'}, dimensions={0} | all-to-all | bytes 3145728 | tf_op jit(solution)/shard_map/all_to_all | solution.py:267
  164.7 3.0 %shard_map.76 = bf16[8,192,128]{2,1,0:T(8,128)(2,1)} custom-call(bf16[8,16,128]{2,1,0:T(8,128)(2,1)} %all-to-all-done.1.table_ref, bf16[8,4,2,96,128]{4,3,2,1,0:T(8,128)(2,1)} %bitcast.14), custom_call_target="tpu_custom_call" | custom-call | tf_op jit(solution)/shard_map/pallas_call | solution.py:270
  167.7 38.0 %all_to_all.21 = bf16[8,192,128]{2,1,0:T(8,128)(2,1)S(1)} all-to-all(bf16[8,192,128]{2,1,0:T(8,128)(2,1)} %shard_map.76), channel_id=1, replica_groups=mesh['zh'=8,'zl'=2,'x'=4,'c'=2,'y'=4] {'zh'}, dimensions={0} | all-to-all | bytes 786432 | tf_op jit(solution)/shard_map/all_to_all | solution.py:273
  (27 shorter events, 10.7 us)
Async XLA Ops:
  8.6 16.1 %all-to-all-start = ((bf16[8,16,768]{2,1,0:T(8,128)(2,1)}), bf16[8,16,768]{2,1,0:T(8,128)(2,1)S(1)}, u32[]{:S(2)}, u32[]{:S(2)}) async-start(bf16[8,16,768]{2,1,0:T(8,128)(2,1)} %get-tuple-element.28), calls=%async_computation | async-start | bytes 393216 | tf_op jit(solution)/shard_map/all_to_all | solution.py:242
  18.8 102.8 %all-gather.2.cloned.1.call-start = ((), (), s32[]{:S(2)}) async-start(), calls=%async_computation.4 | async-start | bytes 3342336 | tf_op jit(solution)/shard_map/all_gather | solution.py:249
  24.7 0.7 copy-start.3
  25.4 11.3 %collective-permute-start.2 = (bf16[3,384,512]{2,1,0:T(8,128)(2,1)}, bf16[3,384,512]{2,1,0:T(8,128)(2,1)S(1)}, u32[]{:S(2)}, u32[]{:S(2)}) collective-permute-start(bf16[3,384,512]{2,1,0:T(8,128)(2,1)} %get-tuple-element.40.refs_1_), channel_id=1, source_target_pairs={{0,4},{4,0},{1,5},{5,1},{2,6},{6,2},{3,7},{7,3},{8,12},{12,8},{9,1... | collective-permute-start | bytes 3538952 | tf_op jit(solution)/shard_map/ppermute | solution.py:196
  28.3 8.5 %collective-permute-start.3 = (bf16[3,384,512]{2,1,0:T(8,128)(2,1)}, bf16[3,384,512]{2,1,0:T(8,128)(2,1)S(1)}, u32[]{:S(2)}, u32[]{:S(2)}) collective-permute-start(bf16[3,384,512]{2,1,0:T(8,128)(2,1)} %get-tuple-element.39.refs_2_), channel_id=1, source_target_pairs={{0,4},{4,0},{1,5},{5,1},{2,6},{6,2},{3,7},{7,3},{8,12},{12,8},{9,1... | collective-permute-start | bytes 3538952 | tf_op jit(solution)/shard_map/ppermute | solution.py:196
  30.2 30.3 %collective-permute-start = (bf16[3,384,512]{2,1,0:T(8,128)(2,1)}, bf16[3,384,512]{2,1,0:T(8,128)(2,1)S(1)}, u32[]{:S(2)}, u32[]{:S(2)}) collective-permute-start(bf16[3,384,512]{2,1,0:T(8,128)(2,1)} %get-tuple-element.40.refs_1_), channel_id=1, source_target_pairs={{0,8},{8,16},{16,24},{24,0},{1,9},{9,17},{17,25},{25,1},{2,10},{10... | collective-permute-start | bytes 3538952 | tf_op jit(solution)/shard_map/ppermute | solution.py:203
  32.4 29.1 %collective-permute-start.1 = (bf16[3,384,512]{2,1,0:T(8,128)(2,1)}, bf16[3,384,512]{2,1,0:T(8,128)(2,1)}, u32[]{:S(2)}, u32[]{:S(2)}) collective-permute-start(bf16[3,384,512]{2,1,0:T(8,128)(2,1)} %get-tuple-element.39.refs_2_), channel_id=1, source_target_pairs={{0,24},{8,0},{16,8},{24,16},{1,25},{9,1},{17,9},{25,17},{2,26},{10... | collective-permute-start | bytes 3538952 | tf_op jit(solution)/shard_map/ppermute | solution.py:204
  36.7 84.9 %copy-start = (bf16[3,384,512]{2,1,0:T(8,128)(2,1)}, bf16[3,384,512]{2,1,0:T(8,128)(2,1)S(1)}, u32[]{:S(2)}) copy-start(bf16[3,384,512]{2,1,0:T(8,128)(2,1)S(1)} %collective-permute-done.2.refs_3_) | copy-start | bytes 3538948
  36.7 84.9 %copy-start.1 = (bf16[3,384,512]{2,1,0:T(8,128)(2,1)}, bf16[3,384,512]{2,1,0:T(8,128)(2,1)S(1)}, u32[]{:S(2)}) copy-start(bf16[3,384,512]{2,1,0:T(8,128)(2,1)S(1)} %collective-permute-done.3.refs_4_) | copy-start | bytes 3538948
  36.7 49.2 %collective-permute-start.4 = (bf16[3,384,512]{2,1,0:T(8,128)(2,1)}, bf16[3,384,512]{2,1,0:T(8,128)(2,1)}, u32[]{:S(2)}, u32[]{:S(2)}) collective-permute-start(bf16[3,384,512]{2,1,0:T(8,128)(2,1)} %get-tuple-element.39.refs_2_), channel_id=1, source_target_pairs={{0,8},{8,16},{16,24},{24,0},{1,9},{9,17},{17,25},{25,1},{2,10},{10... | collective-permute-start | bytes 3538952 | tf_op jit(solution)/shard_map/ppermute | solution.py:207
  38.7 57.4 %collective-permute-start.5 = (bf16[3,384,512]{2,1,0:T(8,128)(2,1)}, bf16[3,384,512]{2,1,0:T(8,128)(2,1)}, u32[]{:S(2)}, u32[]{:S(2)}) collective-permute-start(bf16[3,384,512]{2,1,0:T(8,128)(2,1)} %get-tuple-element.40.refs_1_), channel_id=1, source_target_pairs={{0,24},{8,0},{16,8},{24,16},{1,25},{9,1},{17,9},{25,17},{2,26},{10... | collective-permute-start | bytes 3538952 | tf_op jit(solution)/shard_map/ppermute | solution.py:208
  60.5 61.1 %copy-start.2 = (bf16[3,384,512]{2,1,0:T(8,128)(2,1)}, bf16[3,384,512]{2,1,0:T(8,128)(2,1)S(1)}, u32[]{:S(2)}) copy-start(bf16[3,384,512]{2,1,0:T(8,128)(2,1)S(1)} %collective-permute-done.refs_5_) | copy-start | bytes 3538948
  61.5 49.7 %collective-permute-start.10 = (bf16[3,384,512]{2,1,0:T(8,128)(2,1)S(1)}, bf16[3,384,512]{2,1,0:T(8,128)(2,1)}, u32[]{:S(2)}, u32[]{:S(2)}) collective-permute-start(bf16[3,384,512]{2,1,0:T(8,128)(2,1)S(1)} %collective-permute-done.refs_5_), channel_id=1, source_target_pairs={{0,8},{8,16},{16,24},{24,0},{1,9},{9,17},{17,25},{25,1},{2,10},{10... | collective-permute-start | bytes 3538952 | tf_op jit(solution)/shard_map/ppermute | solution.py:209
  63.6 50.9 %collective-permute-start.6 = (bf16[3,384,512]{2,1,0:T(8,128)(2,1)S(1)}, bf16[3,384,512]{2,1,0:T(8,128)(2,1)}, u32[]{:S(2)}, u32[]{:S(2)}) collective-permute-start(bf16[3,384,512]{2,1,0:T(8,128)(2,1)S(1)} %collective-permute-done.refs_5_), channel_id=1, source_target_pairs={{0,4},{4,0},{1,5},{5,1},{2,6},{6,2},{3,7},{7,3},{8,12},{12,8},{9,1... | collective-permute-start | bytes 3538952 | tf_op jit(solution)/shard_map/ppermute | solution.py:196
  68.3 48.1 %collective-permute-start.11 = (bf16[3,384,512]{2,1,0:T(8,128)(2,1)}, bf16[3,384,512]{2,1,0:T(8,128)(2,1)}, u32[]{:S(2)}, u32[]{:S(2)}) collective-permute-start(bf16[3,384,512]{2,1,0:T(8,128)(2,1)} %collective-permute-done.1.refs_8_), channel_id=1, source_target_pairs={{0,24},{8,0},{16,8},{24,16},{1,25},{9,1},{17,9},{25,17},{2,26},{10... | collective-permute-start | bytes 3538952 | tf_op jit(solution)/shard_map/ppermute | solution.py:210
  73.6 22.5 %all-to-all-start.1 = ((bf16[8,16,128]{2,1,0:T(8,128)(2,1)}), bf16[8,16,128]{2,1,0:T(8,128)(2,1)}, u32[]{:S(2)}, u32[]{:S(2)}) async-start(bf16[8,16,128]{2,1,0:T(8,128)(2,1)} %get-tuple-element.38), calls=%async_computation.1 | async-start | bytes 65536 | tf_op jit(solution)/shard_map/all_to_all | solution.py:212
  85.9 33.5 %collective-permute-start.9 = (bf16[3,384,512]{2,1,0:T(8,128)(2,1)}, bf16[3,384,512]{2,1,0:T(8,128)(2,1)}, u32[]{:S(2)}, u32[]{:S(2)}) collective-permute-start(bf16[3,384,512]{2,1,0:T(8,128)(2,1)} %collective-permute-done.1.refs_8_), channel_id=1, source_target_pairs={{0,4},{4,0},{1,5},{5,1},{2,6},{6,2},{3,7},{7,3},{8,12},{12,8},{9,1... | collective-permute-start | bytes 3538952 | tf_op jit(solution)/shard_map/ppermute | solution.py:196
  96.1 23.4 %collective-permute-start.7 = (bf16[3,384,512]{2,1,0:T(8,128)(2,1)}, bf16[3,384,512]{2,1,0:T(8,128)(2,1)}, u32[]{:S(2)}, u32[]{:S(2)}) collective-permute-start(bf16[3,384,512]{2,1,0:T(8,128)(2,1)} %collective-permute-done.4.refs_6_), channel_id=1, source_target_pairs={{0,4},{4,0},{1,5},{5,1},{2,6},{6,2},{3,7},{7,3},{8,12},{12,8},{9,1... | collective-permute-start | bytes 3538952 | tf_op jit(solution)/shard_map/ppermute | solution.py:196
  111.2 8.2 %collective-permute-start.12 = (bf16[3,384,512]{2,1,0:T(8,128)(2,1)}, bf16[3,384,512]{2,1,0:T(8,128)(2,1)}, u32[]{:S(2)}, u32[]{:S(2)}) collective-permute-start(bf16[3,384,512]{2,1,0:T(8,128)(2,1)} %collective-permute-done.10.refs_13_), channel_id=1, source_target_pairs={{0,4},{4,0},{1,5},{5,1},{2,6},{6,2},{3,7},{7,3},{8,12},{12,8},{9,1... | collective-permute-start | bytes 3538952 | tf_op jit(solution)/shard_map/ppermute | solution.py:196
  114.5 5.1 %collective-permute-start.8 = (bf16[3,384,512]{2,1,0:T(8,128)(2,1)}, bf16[3,384,512]{2,1,0:T(8,128)(2,1)}, u32[]{:S(2)}, u32[]{:S(2)}) collective-permute-start(bf16[3,384,512]{2,1,0:T(8,128)(2,1)} %collective-permute-done.5.refs_7_), channel_id=1, source_target_pairs={{0,4},{4,0},{1,5},{5,1},{2,6},{6,2},{3,7},{7,3},{8,12},{12,8},{9,1... | collective-permute-start | bytes 3538952 | tf_op jit(solution)/shard_map/ppermute | solution.py:196
  116.4 5.2 %collective-permute-start.13 = (bf16[3,384,512]{2,1,0:T(8,128)(2,1)}, bf16[3,384,512]{2,1,0:T(8,128)(2,1)}, u32[]{:S(2)}, u32[]{:S(2)}) collective-permute-start(bf16[3,384,512]{2,1,0:T(8,128)(2,1)} %collective-permute-done.11.refs_14_), channel_id=1, source_target_pairs={{0,4},{4,0},{1,5},{5,1},{2,6},{6,2},{3,7},{7,3},{8,12},{12,8},{9,1... | collective-permute-start | bytes 3538952 | tf_op jit(solution)/shard_map/ppermute | solution.py:196
Sparse Core Ops, SparseCore 0:
  25.5 66.9 all-gather.1

commit v7 on v6

--- a/solution.py
+++ b/solution.py
@@ -28,9 +28,19 @@
     )
 
 
-def prep_kernel(expert_ref, experts_ref, weight_ref, tok_ref, cot_ref, out_ref, table_ref):
-    expert_id = expert_ref[0]
-    n_dest, both, feats = out_ref.shape
+def prep_kernel(
+    place_ref,
+    experts_ref,
+    weight_ref,
+    tok_ref,
+    cot_ref,
+    tok_out_ref,
+    keep_ref,
+    send_ref,
+    table_ref,
+):
+    expert_id, core = place_ref[0], place_ref[1]
+    n_dest, both, half = tok_out_ref.shape
     part = both // 2
     count = tok_ref.shape[0]
     first, second = experts_ref[0:1, :], experts_ref[1:2, :]
@@ -57,8 +67,19 @@
     tok = jnp.dot(select, tok_ref[...], preferred_element_type=f32)
     cot = slot_share * jnp.dot(select, cot_ref[...], preferred_element_type=f32)
     for d in range(n_dest):
-        span = slice(d * part, (d + 1) * part)
-        out_ref[d] = jnp.concatenate([tok[span], cot[span]], axis=0).astype(bf16)
+        rows = tok[d * part : (d + 1) * part]
+        tok_out_ref[d] = jnp.concatenate([rows[:, :half], rows[:, half:]], axis=0).astype(bf16)
+    sets = [
+        jnp.concatenate(
+            [cot[d * part : (d + 1) * part] for d in range(side, n_dest, 2)], axis=0
+        )
+        for side in range(2)
+    ]
+    mine = jnp.where(core == 0, sets[0], sets[1]).astype(bf16)
+    other = jnp.where(core == 0, sets[1], sets[0]).astype(bf16)
+    for h in range(2):
+        keep_ref[h] = mine[:, h * half : (h + 1) * half]
+        send_ref[h] = other[:, h * half : (h + 1) * half]
     padded = jnp.concatenate(
         [table, jnp.zeros((table_rows - window, count), f32)], axis=0
     ).astype(bf16)
@@ -66,65 +87,99 @@
         table_ref[i] = padded
 
 
-def weights_kernel(gate_ref, up_ref, down_ref, low_ref, high_ref):
+def weights_kernel(gate_ref, up_ref, down_ref, low_ref, high_ref, flip_ref):
     half = low_ref.shape[1]
     for i, ref in enumerate((low_ref, high_ref)):
         span = slice(i * half, (i + 1) * half)
         ref[0] = gate_ref[span, :]
         ref[1] = up_ref[span, :]
-        ref[2] = down_ref[:, span].T
-
-
-def block_kernel(place_ref, *refs):
-    n_w = 2 * len(blocks_at)
-    rows_hbm, weights_hbm = refs[0], refs[1 : 1 + n_w]
-    out_ref, rows_ref, weights_ref, total_ref, sems = refs[1 + n_w :]
+        flip_ref[span, :] = down_ref[:, span].T
+
+
+def source(place_ref, n_x, dx, dc):
     x, core = place_ref[0], place_ref[1]
-    n_z, n_s, both, feats = rows_ref.shape
-    n_x = n_s // 2
-    _, _, half, hidden = weights_ref.shape[1:]
-    part = both // 2
-    slots = n_z * part
-    copies = [pltpu.make_async_copy(rows_hbm, rows_ref, sems.at[n_w])]
-    copies += [
+    return lax.rem(x + dx + n_x, n_x) * 2 + (1 - core if dc else core)
+
+
+def back_kernel(rows_hbm, down_ref, down_far_ref, out_ref, rows_ref, sem):
+    n_x, slots, hidden = out_ref.shape
+    n_z, _, sub, half = rows_ref.shape
+    per_z = 2 * sub
+    copy = pltpu.make_async_copy(rows_hbm.at[:, pl.ds(8, 8)], rows_ref, sem)
+    copy.start()
+    copy.wait()
+    total = None
+    for side, weight in enumerate((down_ref, down_far_ref)):
+        for h in range(2):
+            at = 4 * side + 2 * h
+            rows = rows_ref[:, at : at + 2].reshape(n_z * per_z, half)
+            term = jnp.dot(
+                rows, weight[h * half : (h + 1) * half, :], preferred_element_type=f32
+            )
+            total = term if total is None else total + term
+    total = total.reshape(n_z, n_x, slots // n_z, hidden)
+    for i in range(n_x):
+        out_ref[i] = total[:, i].reshape(slots, hidden).astype(bf16)
+
+
+def start_weights(weights_hbm, weights_ref, sems):
+    copies = [
         pltpu.make_async_copy(w, weights_ref.at[i // 2, i % 2], sems.at[i])
         for i, w in enumerate(weights_hbm)
     ]
     for copy in copies:
         copy.start()
-    copies[0].wait()
-
-    def source(dx, dc):
-        return lax.rem(x + dx + n_x, n_x) * 2 + (1 - core if dc else core)
-
+    return copies
+
+
+def products_kernel(place_ref, *refs):
+    n_w = 2 * len(blocks_at)
+    rows_hbm, weights_hbm = refs[0], refs[1 : 1 + n_w]
+    total_ref, rows_ref, weights_ref, sems = refs[1 + n_w :]
+    n_z, n_s, both, half = rows_ref.shape
+    part = both // 2
+    hidden = weights_ref.shape[-1]
+    rows_copy = pltpu.make_async_copy(rows_hbm.at[:, pl.ds(0, n_s)], rows_ref, sems.at[n_w])
+    rows_copy.start()
+    copies = start_weights(weights_hbm, weights_ref, sems)
+    rows_copy.wait()
     for b, (dx, dc) in enumerate(blocks_at):
-        copies[1 + 2 * b].wait()
-        copies[2 + 2 * b].wait()
-        loaded = rows_ref[:, source(dx, dc)].astype(f32)
-        tok, cot = (
-            loaded[:, begin : begin + part].reshape(slots, feats).astype(bf16)
+        copies[2 * b].wait()
+        copies[2 * b + 1].wait()
+        loaded = rows_ref[:, source(place_ref, n_s // 2, dx, dc)].astype(f32)
+        low, high = (
+            loaded[:, begin : begin + part].reshape(n_z * part, half).astype(bf16)
             for begin in (0, part)
         )
-        for m, rows in enumerate((tok, tok, cot)):
+        for m in range(2):
             span = slice(m * hidden, (m + 1) * hidden)
-            term = jnp.dot(rows[:, :half], weights_ref[b, 0, m], preferred_element_type=f32)
-            term += jnp.dot(rows[:, half:], weights_ref[b, 1, m], preferred_element_type=f32)
+            term = jnp.dot(low, weights_ref[b, 0, m], preferred_element_type=f32)
+            term += jnp.dot(high, weights_ref[b, 1, m], preferred_element_type=f32)
             if b == 0:
                 total_ref[:, span] = term
             else:
                 total_ref[:, span] += term
 
+
+def result_kernel(place_ref, *refs):
+    n_w = 2 * len(blocks_at)
+    sums_ref, back_ref, weights_hbm = refs[0], refs[1], refs[2 : 2 + n_w]
+    out_ref, weights_ref, sems = refs[2 + n_w :]
+    n_x, slots, hidden = back_ref.shape
+    half = weights_ref.shape[3]
+    n_z = slots // 8
+    copies = start_weights(weights_hbm, weights_ref, sems)
+
+    back = sum(back_ref[i].astype(f32) for i in range(n_x))
     gate_sum, up_sum, back_sum = (
         jnp.concatenate(
             [
-                total_ref[:, m * hidden : (m + 1) * hidden]
-                .reshape(n_z // 2, 2, part, hidden)[:, pair]
-                .reshape(slots // 2, hidden)
+                value.reshape(n_z // 2, 2, 8, hidden)[:, pair].reshape(slots // 2, hidden)
                 for pair in range(2)
             ],
             axis=0,
         )
-        for m in range(3)
+        for value in (sums_ref[:, :hidden], sums_ref[:, hidden:], back)
     )
     sigmoid_gate = jax.nn.sigmoid(gate_sum)
     grad_up = (back_sum * (gate_sum * sigmoid_gate)).astype(bf16)
@@ -132,9 +187,11 @@
         back_sum * up_sum * sigmoid_gate * (1.0 + gate_sum * (1.0 - sigmoid_gate))
     ).astype(bf16)
 
-    quarter = feats // window
+    quarter = 2 * half // window
     for b, (dx, dc) in enumerate(blocks_at):
-        s = source(dx, dc)
+        s = source(place_ref, n_x, dx, dc)
+        copies[2 * b].wait()
+        copies[2 * b + 1].wait()
         for y in range(window):
             side, begin = y * quarter // half, y * quarter % half
             span = slice(begin, begin + quarter)
@@ -220,49 +277,78 @@
 def per_device(tokens, cotangent, experts, route_weight, gate_weight, up_weight, down_weight):
     n_high = lax.axis_size("zh")
     n_z = n_high * lax.axis_size("zl")
-    n_s = lax.axis_size("x") * lax.axis_size("c")
+    n_x = lax.axis_size("x")
+    n_s = n_x * lax.axis_size("c")
     count, feats = tokens.shape
     quarter = feats // window
     part = count // 2 // n_s
     gate, up, down = gate_weight[0], up_weight[0], down_weight[0]
     hidden = gate.shape[1]
-    expert_id = lax.axis_index("y").reshape(1).astype(jnp.int32)
-    place = jnp.stack([lax.axis_index("x"), lax.axis_index("c")]).astype(jnp.int32)
+    x, core = lax.axis_index("x"), lax.axis_index("c")
+    prep_place = jnp.stack([lax.axis_index("y"), core]).astype(jnp.int32)
+    place = jnp.stack([x, core]).astype(jnp.int32)
     smem, vmem, anywhere = pltpu.SMEM, pltpu.VMEM, pl.ANY
-
-    pieces, tables = kernel_call(
+    half = feats // 2
+
+    pieces, keep, send, tables = kernel_call(
         prep_kernel,
         (
-            jax.ShapeDtypeStruct((n_s, 2 * part, feats), bf16),
+            jax.ShapeDtypeStruct((n_s, 2 * part, half), bf16),
+            jax.ShapeDtypeStruct((2, n_s * part // 2, half), bf16),
+            jax.ShapeDtypeStruct((2, n_s * part // 2, half), bf16),
             jax.ShapeDtypeStruct((n_high, table_rows, count), bf16),
         ),
         [smem] + [vmem] * 4,
-    )(expert_id, experts.T, route_weight.T, tokens, cotangent)
+    )(prep_place, experts.T, route_weight.T, tokens, cotangent)
     gate, up, down, pieces = lax.optimization_barrier((gate, up, down, pieces))
     pieces = lax.all_to_all(pieces, ("x", "c"), 0, 0, tiled=True)
-    low, high = kernel_call(
+    cot_far = swap(send)
+    low, high, down_t = kernel_call(
         weights_kernel,
-        (jax.ShapeDtypeStruct((3, feats // 2, hidden), bf16),) * 2,
+        (
+            jax.ShapeDtypeStruct((2, half, hidden), bf16),
+            jax.ShapeDtypeStruct((2, half, hidden), bf16),
+            jax.ShapeDtypeStruct((feats, hidden), bf16),
+        ),
         [vmem] * 3,
     )(gate, up, down)
-    pieces, low, high, tables = lax.optimization_barrier((pieces, low, high, tables))
-    rows = lax.all_gather(
-        pieces.reshape(n_s * 2 * part, feats), ("zh", "zl"), axis=0, tiled=True
-    ).reshape(n_z, n_s, 2 * part, feats)
-
+    pieces, low, high, down_t, tables = lax.optimization_barrier(
+        (pieces, low, high, down_t, tables)
+    )
+    own = jnp.concatenate([v.reshape(-1, half) for v in (pieces, keep, cot_far)], axis=0)
+    rows = lax.all_gather(own, ("zh", "zl"), axis=0, tiled=True).reshape(
+        n_z, 2 * n_s, 2 * part, half
+    )
     weights, tables = gather_weights(low, high, tables)
-
+    weights = [value for block in weights for value in block]
+    down_far = swap(down_t)
+
+    back = kernel_call(
+        back_kernel,
+        jax.ShapeDtypeStruct((n_x, n_z * part, hidden), bf16),
+        [anywhere, vmem, vmem],
+        [pltpu.VMEM((n_z, n_s, 2 * part, half), bf16), pltpu.SemaphoreType.DMA],
+    )(rows, down_t, down_far)
+    back = lax.all_to_all(back, "x", 0, 0, tiled=True)
+    sums = kernel_call(
+        products_kernel,
+        jax.ShapeDtypeStruct((n_z * part, 2 * hidden), f32),
+        [smem] + [anywhere] * (1 + len(weights)),
+        [
+            pltpu.VMEM((n_z, n_s, 2 * part, half), bf16),
+            pltpu.VMEM((len(blocks_at), 2, 2, half, hidden), bf16),
+            pltpu.SemaphoreType.DMA((len(weights) + 1,)),
+        ],
+    )(place, rows, *weights)
     result = kernel_call(
-        block_kernel,
+        result_kernel,
         jax.ShapeDtypeStruct((n_s, window, 2, quarter // 2, n_z * part), bf16),
-        [smem] + [anywhere] * (1 + 2 * len(blocks_at)),
+        [smem, vmem, vmem] + [anywhere] * len(weights),
         [
-            pltpu.VMEM((n_z, n_s, 2 * part, feats), bf16),
-            pltpu.VMEM((len(blocks_at), 2, 3, feats // 2, hidden), bf16),
-            pltpu.VMEM((n_z * part, 3 * hidden), f32),
-            pltpu.SemaphoreType.DMA((2 * len(blocks_at) + 1,)),
+            pltpu.VMEM((len(blocks_at), 2, 2, half, hidden), bf16),
+            pltpu.SemaphoreType.DMA((len(weights),)),
         ],
-    )(place, rows, *[half for block in weights for half in block])
+    )(place, sums, back, *weights)
     shape = result.shape
     result = lax.all_to_all(
         result.reshape(n_s * window * 2, *shape[3:]), ("x", "c", "y", "zl"), 0, 0, tiled=True

time: 214 us -> 208 us (0.972)
  waiting for transfers between devices: 42.5 us -> 24.7 us
  starting transfers between devices: 65.8 us -> 73.3 us
  Pallas kernels: 22.5 us -> 29.9 us
  blocking collectives: 66.9 us -> 62.1 us
    ppermute x1, waiting for transfers between devices: 11.5 us -> 0.01 us  [gather_weights(): low_across = lax.ppermute(low_before, 'x', ahead)]
    ppermute x1, waiting for transfers between devices: 17.3 us -> 5.9 us  [gather_weights(): low_before = lax.ppermute(low, 'x', ahead)]
    pallas_call x3 -> x5, Pallas kernels: 19.5 us -> 27 us  [the longest x1 9.69 us: per_device(): kernel_call(result_kernel, jax.ShapeDtypeStruct((n_s, window, 2, quarter...]
    all_to_all x1, blocking collectives: 38 us -> 31 us  [per_device(): dense = lax.all_to_all(dense, 'zh', 0, 0, tiled=True)]
    ppermute x1, waiting for transfers between devices: 1.88 us -> 7.54 us  [gather_weights(): high_before = lax.ppermute(high_later, 'x', ahead)]
    ppermute x8 -> x10, starting transfers between devices: 24.8 us -> 29.4 us  [swap(): return lax.ppermute(value, 'c', [(0, 1), (1, 0)])]
    all_to_all x0 -> x1, starting transfers between devices: none -> 3.48 us  [per_device(): back = lax.all_to_all(back, 'x', 0, 0, tiled=True)]
    all_to_all x1, waiting for transfers between devices: 2.63 us -> 0.01 us  [per_device(): pieces = lax.all_to_all(pieces, ('x', 'c'), 0, 0, tiled=True)]
  transfers between devices with their start and end apart: 17 -> 20, of which waited for: 8 -> 5; matrix products, arithmetic and copies ran while one was open for 0% -> 0% of each run, Pallas kernels for 2% -> 7%
where the time goes in v7:
time: 208 us; the launch traced here: 207 us
  starting transfers between devices  73.3 us (35%)
  blocking collectives  62.1 us (30%)
  Pallas kernels  29.9 us (14%)
  waiting for transfers between devices  24.7 us (12%)
  between operations  13.7 us (7%)
  other arithmetic  2.55 us (1%)
    all_to_all x1, blocking collectives, per_device(): lax.all_to_all(result.reshape(n_s * window * 2, *shape[3:]), ('x', 'c', '...  31.1 us
    all_to_all x1, blocking collectives, per_device(): dense = lax.all_to_all(dense, 'zh', 0, 0, tiled=True)  31 us
    ppermute x10, starting transfers between devices, swap(): return lax.ppermute(value, 'c', [(0, 1), (1, 0)])  29.4 us
    all_to_all x1, starting transfers between devices, gather_weights(): tables = lax.all_to_all(tables, 'zh', 0, 0, tiled=True)  10.5 us
    all_to_all x1, starting transfers between devices, per_device(): pieces = lax.all_to_all(pieces, ('x', 'c'), 0, 0, tiled=True)  10.3 us
    pallas_call x1, Pallas kernels, per_device(): kernel_call(result_kernel, jax.ShapeDtypeStruct((n_s, window, 2, quarter...  9.69 us
    all_to_all x1, waiting for transfers between devices, gather_weights(): tables = lax.all_to_all(tables, 'zh', 0, 0, tiled=True)  7.94 us
    ppermute x1, waiting for transfers between devices, gather_weights(): high_before = lax.ppermute(high_later, 'x', ahead)  7.54 us
  transfers between devices with their start and end apart: 20, of which 5 were waited for; matrix products, arithmetic and copies ran while one was open for 0% of the time, Pallas kernels for 7%

profile of v7, /device:TPU:1, one launch (start us, length us, event | category | flops | bytes accessed | tf_op | source)
XLA Modules:
  0.0 207.1 jit_solution(8654789447100097348)
XLA Ops:
  9.2 10.3 %all-to-all-start = ((bf16[8,16,384]{2,1,0:T(8,128)(2,1)}), bf16[8,16,384]{2,1,0:T(8,128)(2,1)S(1)}, u32[]{:S(2)}, u32[]{:S(2)}) async-start(bf16[8,16,384]{2,1,0:T(8,128)(2,1)} %get-tuple-element.32), calls=%async_computation | async-start | bytes 196608 | tf_op jit(solution)/shard_map/all_to_all | solution.py:304
  21.5 3.3 %shard_map.74 = (bf16[2,384,512]{2,1,0:T(8,128)(2,1)}, bf16[2,384,512]{2,1,0:T(8,128)(2,1)}, bf16[768,512]{1,0:T(8,128)(2,1)}) custom-call(bf16[768,512]{1,0:T(8,128)(2,1)} %bitcast.19, bf16[768,512]{1,0:T(8,128)(2,1)} %bitcast.20, bf16[512,768]{1,0:T(8,128)(2,1)} %bitcast.21), custom_call_target="tpu_custom_call" | custom-call | tf_op jit(solution)/shard_map/pallas_call | solution.py:306
  25.5 2.4 %collective-permute-start.2 = (bf16[2,384,512]{2,1,0:T(8,128)(2,1)}, bf16[2,384,512]{2,1,0:T(8,128)(2,1)S(1)}, u32[]{:S(2)}, u32[]{:S(2)}) collective-permute-start(bf16[2,384,512]{2,1,0:T(8,128)(2,1)} %get-tuple-element.45.refs_1_.refs_2_), channel_id=1, source_target_pairs={{0,4},{4,0},{1,5},{5,1},{2,6},{6,2},{3,7},{7,3},{8,12},{12,8},{9,1... | collective-permute-start | bytes 2359304 | tf_op jit(solution)/shard_map/ppermute | solution.py:253
  29.9 3.5 %collective-permute-start = (bf16[2,384,512]{2,1,0:T(8,128)(2,1)}, bf16[2,384,512]{2,1,0:T(8,128)(2,1)S(1)}, u32[]{:S(2)}, u32[]{:S(2)}) collective-permute-start(bf16[2,384,512]{2,1,0:T(8,128)(2,1)} %get-tuple-element.45.refs_1_.refs_2_), channel_id=1, source_target_pairs={{0,8},{8,16},{16,24},{24,0},{1,9},{9,17},{17,25},{25,1},{2,10},{10... | collective-permute-start | bytes 2359304 | tf_op jit(solution)/shard_map/ppermute | solution.py:260
  33.4 3.2 %collective-permute-start.1 = (bf16[2,384,512]{2,1,0:T(8,128)(2,1)}, bf16[2,384,512]{2,1,0:T(8,128)(2,1)S(1)}, u32[]{:S(2)}, u32[]{:S(2)}) collective-permute-start(bf16[2,384,512]{2,1,0:T(8,128)(2,1)} %get-tuple-element.44.refs_2_.refs_3_), channel_id=1, source_target_pairs={{0,24},{8,0},{16,8},{24,16},{1,25},{9,1},{17,9},{25,17},{2,26},{10... | collective-permute-start | bytes 2359304 | tf_op jit(solution)/shard_map/ppermute | solution.py:261
  38.7 4.4 %collective-permute-start.5 = (bf16[2,384,512]{2,1,0:T(8,128)(2,1)}, bf16[2,384,512]{2,1,0:T(8,128)(2,1)}, u32[]{:S(2)}, u32[]{:S(2)}) collective-permute-start(bf16[2,384,512]{2,1,0:T(8,128)(2,1)} %get-tuple-element.45.refs_1_.refs_2_), channel_id=1, source_target_pairs={{0,24},{8,0},{16,8},{24,16},{1,25},{9,1},{17,9},{25,17},{2,26},{10... | collective-permute-start | bytes 2359304 | tf_op jit(solution)/shard_map/ppermute | solution.py:265
  43.1 3.3 %collective-permute-start.15 = (bf16[768,512]{1,0:T(8,128)(2,1)}, bf16[768,512]{1,0:T(8,128)(2,1)}, u32[]{:S(2)}, u32[]{:S(2)}) collective-permute-start(bf16[768,512]{1,0:T(8,128)(2,1)} %get-tuple-element.56.down_ref), channel_id=1, source_target_pairs={{0,4},{4,0},{1,5},{5,1},{2,6},{6,2},{3,7},{7,3},{8,12},{12,8},{9,1... | collective-permute-start | bytes 2359304 | tf_op jit(solution)/shard_map/ppermute | solution.py:253
  46.4 5.9 %collective-permute-done.refs_5_.refs_6_ = bf16[2,384,512]{2,1,0:T(8,128)(2,1)S(1)} collective-permute-done((bf16[2,384,512]{2,1,0:T(8,128)(2,1)}, bf16[2,384,512]{2,1,0:T(8,128)(2,1)S(1)}, u32[]{:S(2)}, u32[]{:S(2)}) %collective-permute-start) | collective-permute-done | bytes 786464 | tf_op jit(solution)/shard_map/ppermute | solution.py:260
  54.3 3.1 %collective-permute-start.11 = (bf16[2,384,512]{2,1,0:T(8,128)(2,1)S(1)}, bf16[2,384,512]{2,1,0:T(8,128)(2,1)}, u32[]{:S(2)}, u32[]{:S(2)}) collective-permute-start(bf16[2,384,512]{2,1,0:T(8,128)(2,1)S(1)} %collective-permute-done.refs_5_.refs_6_), channel_id=1, source_target_pairs={{0,8},{8,16},{16,24},{24,0},{1,9},{9,17},{17,25},{25,1},{2,10},{10... | collective-permute-start | bytes 2359304 | tf_op jit(solution)/shard_map/ppermute | solution.py:266
  57.4 4.3 %collective-permute-start.7 = (bf16[2,384,512]{2,1,0:T(8,128)(2,1)S(1)}, bf16[2,384,512]{2,1,0:T(8,128)(2,1)}, u32[]{:S(2)}, u32[]{:S(2)}) collective-permute-start(bf16[2,384,512]{2,1,0:T(8,128)(2,1)S(1)} %collective-permute-done.refs_5_.refs_6_), channel_id=1, source_target_pairs={{0,4},{4,0},{1,5},{5,1},{2,6},{6,2},{3,7},{7,3},{8,12},{12,8},{9,1... | collective-permute-start | bytes 2359304 | tf_op jit(solution)/shard_map/ppermute | solution.py:253
  61.6 7.5 %collective-permute-done.4.refs_6_.refs_7_ = bf16[2,384,512]{2,1,0:T(8,128)(2,1)} collective-permute-done((bf16[2,384,512]{2,1,0:T(8,128)(2,1)}, bf16[2,384,512]{2,1,0:T(8,128)(2,1)}, u32[]{:S(2)}, u32[]{:S(2)}) %collective-permute-start.4) | collective-permute-done | bytes 786464 | tf_op jit(solution)/shard_map/ppermute | solution.py:264
  69.2 3.5 %collective-permute-start.12 = (bf16[2,384,512]{2,1,0:T(8,128)(2,1)S(1)}, bf16[2,384,512]{2,1,0:T(8,128)(2,1)}, u32[]{:S(2)}, u32[]{:S(2)}) collective-permute-start(bf16[2,384,512]{2,1,0:T(8,128)(2,1)S(1)} %collective-permute-done.1.refs_8_.refs_9_), channel_id=1, source_target_pairs={{0,24},{8,0},{16,8},{24,16},{1,25},{9,1},{17,9},{25,17},{2,26},{10... | collective-permute-start | bytes 2359304 | tf_op jit(solution)/shard_map/ppermute | solution.py:267
  72.7 10.5 %all-to-all-start.1 = ((bf16[8,16,128]{2,1,0:T(8,128)(2,1)}), bf16[8,16,128]{2,1,0:T(8,128)(2,1)S(1)}, u32[]{:S(2)}, u32[]{:S(2)}) async-start(bf16[8,16,128]{2,1,0:T(8,128)(2,1)} %get-tuple-element.43), calls=%async_computation.1 | async-start | bytes 65536 | tf_op jit(solution)/shard_map/all_to_all | solution.py:269
  83.1 4.0 %collective-permute-start.10 = (bf16[2,384,512]{2,1,0:T(8,128)(2,1)S(1)}, bf16[2,384,512]{2,1,0:T(8,128)(2,1)}, u32[]{:S(2)}, u32[]{:S(2)}) collective-permute-start(bf16[2,384,512]{2,1,0:T(8,128)(2,1)S(1)} %collective-permute-done.1.refs_8_.refs_9_), channel_id=1, source_target_pairs={{0,4},{4,0},{1,5},{5,1},{2,6},{6,2},{3,7},{7,3},{8,12},{12,8},{9,1... | collective-permute-start | bytes 2359304 | tf_op jit(solution)/shard_map/ppermute | solution.py:253
  87.1 7.9 %all-to-all-done.1.table_ref = bf16[8,16,128]{2,1,0:T(8,128)(2,1)S(1)} async-done(((bf16[8,16,128]{2,1,0:T(8,128)(2,1)}), bf16[8,16,128]{2,1,0:T(8,128)(2,1)S(1)}, u32[]{:S(2)}, u32[]{:S(2)}) %all-to-all-start.1) | async-done | bytes 32800 | tf_op jit(solution)/shard_map/all_to_all | solution.py:269
  95.1 5.2 %collective-permute-start.8 = (bf16[2,384,512]{2,1,0:T(8,128)(2,1)}, bf16[2,384,512]{2,1,0:T(8,128)(2,1)}, u32[]{:S(2)}, u32[]{:S(2)}) collective-permute-start(bf16[2,384,512]{2,1,0:T(8,128)(2,1)} %collective-permute-done.4.refs_6_.refs_7_), channel_id=1, source_target_pairs={{0,4},{4,0},{1,5},{5,1},{2,6},{6,2},{3,7},{7,3},{8,12},{12,8},{9,1... | collective-permute-start | bytes 2359304 | tf_op jit(solution)/shard_map/ppermute | solution.py:253
  102.2 2.4 %collective-permute-start.9 = (bf16[2,384,512]{2,1,0:T(8,128)(2,1)}, bf16[2,384,512]{2,1,0:T(8,128)(2,1)}, u32[]{:S(2)}, u32[]{:S(2)}) collective-permute-start(bf16[2,384,512]{2,1,0:T(8,128)(2,1)} %collective-permute-done.5.refs_7_.refs_8_), channel_id=1, source_target_pairs={{0,4},{4,0},{1,5},{5,1},{2,6},{6,2},{3,7},{7,3},{8,12},{12,8},{9,1... | collective-permute-start | bytes 2359304 | tf_op jit(solution)/shard_map/ppermute | solution.py:253
  106.6 4.8 %shard_map.76 = bf16[4,128,512]{2,1,0:T(8,128)(2,1)} custom-call(bf16[16,16,16,384]{3,2,1,0:T(8,128)(2,1)} %bitcast.15, bf16[768,512]{1,0:T(8,128)(2,1)} %get-tuple-element.56.down_ref, bf16[768,512]{1,0:T(8,128)(2,1)} %collective-permute-done.15.down_far_ref), custom_call_target="tpu_custom_call" | custom-call | tf_op jit(solution)/shard_map/pallas_call | solution.py:326
  111.5 3.5 %all-to-all-start.2 = ((bf16[4,128,512]{2,1,0:T(8,128)(2,1)}), bf16[4,128,512]{2,1,0:T(8,128)(2,1)S(1)}, u32[]{:S(2)}, u32[]{:S(2)}) async-start(bf16[4,128,512]{2,1,0:T(8,128)(2,1)} %shard_map.76), calls=%async_computation.2 | async-start | bytes 1048576 | tf_op jit(solution)/shard_map/all_to_all | solution.py:332
  115.6 7.1 %shard_map.75.refs_0_ = f32[128,1024]{1,0:T(8,128)} custom-call(s32[2]{0:T(128)} %pad_add_fusion.1.place_ref, bf16[16,16,16,384]{3,2,1,0:T(8,128)(2,1)} %bitcast.16, bf16[2,384,512]{2,1,0:T(8,128)(2,1)} %get-tuple-element.45.refs_1_.refs_2_, bf16[2,384,512]{2,1,0:T(8,128)(2,1)} %get-tuple-element.44.refs_2_.refs_3_, bf16[2,384,512]{2,1,0:T(8,128)(2,1)} %copy-done, ...), custom_call_target="tpu_custom_call" | custom-call | tf_op jit(solution)/shard_map/pallas_call | solution.py:333
  124.8 9.7 %shard_map.77 = bf16[8,4,2,96,128]{4,3,2,1,0:T(8,128)(2,1)} custom-call(s32[2]{0:T(128)} %pad_add_fusion.1.place_ref, f32[128,1024]{1,0:T(8,128)} %shard_map.75.refs_0_, bf16[4,128,512]{2,1,0:T(8,128)(2,1)} %copy-done.4, bf16[2,384,512]{2,1,0:T(8,128)(2,1)} %get-tuple-element.45.refs_1_.refs_2_, bf16[2,384,512]{2,1,0:T(8,128)(2,1)} %get-tuple-element.44.refs_2_.refs_3_, ...), custom_call_target="tpu_custom_call" | custom-call | tf_op jit(solution)/shard_map/pallas_call | solution.py:343
  134.5 31.1 %all_to_all.25 = bf16[64,96,128]{2,1,0:T(8,128)(2,1)} all-to-all(bf16[64,96,128]{2,1,0:T(8,128)(2,1)} %bitcast.17), channel_id=1, replica_groups=mesh['zh'=8,'zl'=2,'x'=4,'c'=2,'y'=4] {'x','c','y','zl'}, dimensions={0} | all-to-all | bytes 3145728 | tf_op jit(solution)/shard_map/all_to_all | solution.py:353
  165.6 2.9 %shard_map.78 = bf16[8,192,128]{2,1,0:T(8,128)(2,1)} custom-call(bf16[8,16,128]{2,1,0:T(8,128)(2,1)} %copy-done.5, bf16[8,4,2,96,128]{4,3,2,1,0:T(8,128)(2,1)} %bitcast.18), custom_call_target="tpu_custom_call" | custom-call | tf_op jit(solution)/shard_map/pallas_call | solution.py:356
  168.6 31.0 %all_to_all.26 = bf16[8,192,128]{2,1,0:T(8,128)(2,1)S(1)} all-to-all(bf16[8,192,128]{2,1,0:T(8,128)(2,1)} %shard_map.78), channel_id=1, replica_groups=mesh['zh'=8,'zl'=2,'x'=4,'c'=2,'y'=4] {'zh'}, dimensions={0} | all-to-all | bytes 786432 | tf_op jit(solution)/shard_map/all_to_all | solution.py:359
  (43 shorter events, 18.8 us)
Async XLA Ops:
  9.2 15.6 %all-to-all-start = ((bf16[8,16,384]{2,1,0:T(8,128)(2,1)}), bf16[8,16,384]{2,1,0:T(8,128)(2,1)S(1)}, u32[]{:S(2)}, u32[]{:S(2)}) async-start(bf16[8,16,384]{2,1,0:T(8,128)(2,1)} %get-tuple-element.32), calls=%async_computation | async-start | bytes 196608 | tf_op jit(solution)/shard_map/all_to_all | solution.py:304
  19.4 87.2 %all-gather.2.cloned.1.call-start = ((), (), s32[]{:S(2)}) async-start(), calls=%async_computation.5 | async-start | bytes 3342336 | tf_op jit(solution)/shard_map/all_gather | solution.py:319
  19.4 5.4 %collective-permute-start.6 = (bf16[2,32,384]{2,1,0:T(8,128)(2,1)}, bf16[2,32,384]{2,1,0:T(8,128)(2,1)S(1)}, u32[]{:S(2)}, u32[]{:S(2)}) collective-permute-start(bf16[2,32,384]{2,1,0:T(8,128)(2,1)} %get-tuple-element.49), channel_id=1, source_target_pairs={{0,4},{4,0},{1,5},{5,1},{2,6},{6,2},{3,7},{7,3},{8,12},{12,8},{9,1... | collective-permute-start | bytes 147464 | tf_op jit(solution)/shard_map/ppermute | solution.py:253
  25.5 11.0 %collective-permute-start.2 = (bf16[2,384,512]{2,1,0:T(8,128)(2,1)}, bf16[2,384,512]{2,1,0:T(8,128)(2,1)S(1)}, u32[]{:S(2)}, u32[]{:S(2)}) collective-permute-start(bf16[2,384,512]{2,1,0:T(8,128)(2,1)} %get-tuple-element.45.refs_1_.refs_2_), channel_id=1, source_target_pairs={{0,4},{4,0},{1,5},{5,1},{2,6},{6,2},{3,7},{7,3},{8,12},{12,8},{9,1... | collective-permute-start | bytes 2359304 | tf_op jit(solution)/shard_map/ppermute | solution.py:253
  27.9 8.7 %collective-permute-start.3 = (bf16[2,384,512]{2,1,0:T(8,128)(2,1)}, bf16[2,384,512]{2,1,0:T(8,128)(2,1)S(1)}, u32[]{:S(2)}, u32[]{:S(2)}) collective-permute-start(bf16[2,384,512]{2,1,0:T(8,128)(2,1)} %get-tuple-element.44.refs_2_.refs_3_), channel_id=1, source_target_pairs={{0,4},{4,0},{1,5},{5,1},{2,6},{6,2},{3,7},{7,3},{8,12},{12,8},{9,1... | collective-permute-start | bytes 2359304 | tf_op jit(solution)/shard_map/ppermute | solution.py:253
  29.9 22.4 %collective-permute-start = (bf16[2,384,512]{2,1,0:T(8,128)(2,1)}, bf16[2,384,512]{2,1,0:T(8,128)(2,1)S(1)}, u32[]{:S(2)}, u32[]{:S(2)}) collective-permute-start(bf16[2,384,512]{2,1,0:T(8,128)(2,1)} %get-tuple-element.45.refs_1_.refs_2_), channel_id=1, source_target_pairs={{0,8},{8,16},{16,24},{24,0},{1,9},{9,17},{17,25},{25,1},{2,10},{10... | collective-permute-start | bytes 2359304 | tf_op jit(solution)/shard_map/ppermute | solution.py:260
  33.4 20.9 %collective-permute-start.1 = (bf16[2,384,512]{2,1,0:T(8,128)(2,1)}, bf16[2,384,512]{2,1,0:T(8,128)(2,1)S(1)}, u32[]{:S(2)}, u32[]{:S(2)}) collective-permute-start(bf16[2,384,512]{2,1,0:T(8,128)(2,1)} %get-tuple-element.44.refs_2_.refs_3_), channel_id=1, source_target_pairs={{0,24},{8,0},{16,8},{24,16},{1,25},{9,1},{17,9},{25,17},{2,26},{10... | collective-permute-start | bytes 2359304 | tf_op jit(solution)/shard_map/ppermute | solution.py:261
  36.6 74.9 %copy-start = (bf16[2,384,512]{2,1,0:T(8,128)(2,1)}, bf16[2,384,512]{2,1,0:T(8,128)(2,1)S(1)}, u32[]{:S(2)}) copy-start(bf16[2,384,512]{2,1,0:T(8,128)(2,1)S(1)} %collective-permute-done.2.refs_3_.refs_4_) | copy-start | bytes 2359300
  36.6 74.9 %copy-start.1 = (bf16[2,384,512]{2,1,0:T(8,128)(2,1)}, bf16[2,384,512]{2,1,0:T(8,128)(2,1)S(1)}, u32[]{:S(2)}) copy-start(bf16[2,384,512]{2,1,0:T(8,128)(2,1)S(1)} %collective-permute-done.3.refs_4_.refs_5_) | copy-start | bytes 2359300
  36.6 32.6 %collective-permute-start.4 = (bf16[2,384,512]{2,1,0:T(8,128)(2,1)}, bf16[2,384,512]{2,1,0:T(8,128)(2,1)}, u32[]{:S(2)}, u32[]{:S(2)}) collective-permute-start(bf16[2,384,512]{2,1,0:T(8,128)(2,1)} %get-tuple-element.44.refs_2_.refs_3_), channel_id=1, source_target_pairs={{0,8},{8,16},{16,24},{24,0},{1,9},{9,17},{17,25},{25,1},{2,10},{10... | collective-permute-start | bytes 2359304 | tf_op jit(solution)/shard_map/ppermute | solution.py:264
  38.7 44.4 %collective-permute-start.5 = (bf16[2,384,512]{2,1,0:T(8,128)(2,1)}, bf16[2,384,512]{2,1,0:T(8,128)(2,1)}, u32[]{:S(2)}, u32[]{:S(2)}) collective-permute-start(bf16[2,384,512]{2,1,0:T(8,128)(2,1)} %get-tuple-element.45.refs_1_.refs_2_), channel_id=1, source_target_pairs={{0,24},{8,0},{16,8},{24,16},{1,25},{9,1},{17,9},{25,17},{2,26},{10... | collective-permute-start | bytes 2359304 | tf_op jit(solution)/shard_map/ppermute | solution.py:265
  43.1 52.0 %collective-permute-start.15 = (bf16[768,512]{1,0:T(8,128)(2,1)}, bf16[768,512]{1,0:T(8,128)(2,1)}, u32[]{:S(2)}, u32[]{:S(2)}) collective-permute-start(bf16[768,512]{1,0:T(8,128)(2,1)} %get-tuple-element.56.down_ref), channel_id=1, source_target_pairs={{0,4},{4,0},{1,5},{5,1},{2,6},{6,2},{3,7},{7,3},{8,12},{12,8},{9,1... | collective-permute-start | bytes 2359304 | tf_op jit(solution)/shard_map/ppermute | solution.py:253
  52.3 59.1 %copy-start.2 = (bf16[2,384,512]{2,1,0:T(8,128)(2,1)}, bf16[2,384,512]{2,1,0:T(8,128)(2,1)S(1)}, u32[]{:S(2)}) copy-start(bf16[2,384,512]{2,1,0:T(8,128)(2,1)S(1)} %collective-permute-done.refs_5_.refs_6_) | copy-start | bytes 2359300
  54.3 57.2 %copy-start.3 = (bf16[2,384,512]{2,1,0:T(8,128)(2,1)}, bf16[2,384,512]{2,1,0:T(8,128)(2,1)S(1)}, u32[]{:S(2)}) copy-start(bf16[2,384,512]{2,1,0:T(8,128)(2,1)S(1)} %collective-permute-done.1.refs_8_.refs_9_) | copy-start | bytes 2359300
  54.3 46.0 %collective-permute-start.11 = (bf16[2,384,512]{2,1,0:T(8,128)(2,1)S(1)}, bf16[2,384,512]{2,1,0:T(8,128)(2,1)}, u32[]{:S(2)}, u32[]{:S(2)}) collective-permute-start(bf16[2,384,512]{2,1,0:T(8,128)(2,1)S(1)} %collective-permute-done.refs_5_.refs_6_), channel_id=1, source_target_pairs={{0,8},{8,16},{16,24},{24,0},{1,9},{9,17},{17,25},{25,1},{2,10},{10... | collective-permute-start | bytes 2359304 | tf_op jit(solution)/shard_map/ppermute | solution.py:266
  57.4 44.8 %collective-permute-start.7 = (bf16[2,384,512]{2,1,0:T(8,128)(2,1)S(1)}, bf16[2,384,512]{2,1,0:T(8,128)(2,1)}, u32[]{:S(2)}, u32[]{:S(2)}) collective-permute-start(bf16[2,384,512]{2,1,0:T(8,128)(2,1)S(1)} %collective-permute-done.refs_5_.refs_6_), channel_id=1, source_target_pairs={{0,4},{4,0},{1,5},{5,1},{2,6},{6,2},{3,7},{7,3},{8,12},{12,8},{9,1... | collective-permute-start | bytes 2359304 | tf_op jit(solution)/shard_map/ppermute | solution.py:253
  69.2 35.5 %collective-permute-start.12 = (bf16[2,384,512]{2,1,0:T(8,128)(2,1)S(1)}, bf16[2,384,512]{2,1,0:T(8,128)(2,1)}, u32[]{:S(2)}, u32[]{:S(2)}) collective-permute-start(bf16[2,384,512]{2,1,0:T(8,128)(2,1)S(1)} %collective-permute-done.1.refs_8_.refs_9_), channel_id=1, source_target_pairs={{0,24},{8,0},{16,8},{24,16},{1,25},{9,1},{17,9},{25,17},{2,26},{10... | collective-permute-start | bytes 2359304 | tf_op jit(solution)/shard_map/ppermute | solution.py:267
  72.7 22.4 %all-to-all-start.1 = ((bf16[8,16,128]{2,1,0:T(8,128)(2,1)}), bf16[8,16,128]{2,1,0:T(8,128)(2,1)S(1)}, u32[]{:S(2)}, u32[]{:S(2)}) async-start(bf16[8,16,128]{2,1,0:T(8,128)(2,1)} %get-tuple-element.43), calls=%async_computation.1 | async-start | bytes 65536 | tf_op jit(solution)/shard_map/all_to_all | solution.py:269
  83.1 32.4 %collective-permute-start.10 = (bf16[2,384,512]{2,1,0:T(8,128)(2,1)S(1)}, bf16[2,384,512]{2,1,0:T(8,128)(2,1)}, u32[]{:S(2)}, u32[]{:S(2)}) collective-permute-start(bf16[2,384,512]{2,1,0:T(8,128)(2,1)S(1)} %collective-permute-done.1.refs_8_.refs_9_), channel_id=1, source_target_pairs={{0,4},{4,0},{1,5},{5,1},{2,6},{6,2},{3,7},{7,3},{8,12},{12,8},{9,1... | collective-permute-start | bytes 2359304 | tf_op jit(solution)/shard_map/ppermute | solution.py:253
  95.1 20.5 %collective-permute-start.8 = (bf16[2,384,512]{2,1,0:T(8,128)(2,1)}, bf16[2,384,512]{2,1,0:T(8,128)(2,1)}, u32[]{:S(2)}, u32[]{:S(2)}) collective-permute-start(bf16[2,384,512]{2,1,0:T(8,128)(2,1)} %collective-permute-done.4.refs_6_.refs_7_), channel_id=1, source_target_pairs={{0,4},{4,0},{1,5},{5,1},{2,6},{6,2},{3,7},{7,3},{8,12},{12,8},{9,1... | collective-permute-start | bytes 2359304 | tf_op jit(solution)/shard_map/ppermute | solution.py:253
  100.3 15.3 %collective-permute-start.13 = (bf16[2,384,512]{2,1,0:T(8,128)(2,1)}, bf16[2,384,512]{2,1,0:T(8,128)(2,1)}, u32[]{:S(2)}, u32[]{:S(2)}) collective-permute-start(bf16[2,384,512]{2,1,0:T(8,128)(2,1)} %collective-permute-done.11.refs_13_.refs_14_), channel_id=1, source_target_pairs={{0,4},{4,0},{1,5},{5,1},{2,6},{6,2},{3,7},{7,3},{8,12},{12,8},{9,1... | collective-permute-start | bytes 2359304 | tf_op jit(solution)/shard_map/ppermute | solution.py:253
  102.2 13.4 %collective-permute-start.9 = (bf16[2,384,512]{2,1,0:T(8,128)(2,1)}, bf16[2,384,512]{2,1,0:T(8,128)(2,1)}, u32[]{:S(2)}, u32[]{:S(2)}) collective-permute-start(bf16[2,384,512]{2,1,0:T(8,128)(2,1)} %collective-permute-done.5.refs_7_.refs_8_), channel_id=1, source_target_pairs={{0,4},{4,0},{1,5},{5,1},{2,6},{6,2},{3,7},{7,3},{8,12},{12,8},{9,1... | collective-permute-start | bytes 2359304 | tf_op jit(solution)/shard_map/ppermute | solution.py:253
  104.6 11.0 %collective-permute-start.14 = (bf16[2,384,512]{2,1,0:T(8,128)(2,1)}, bf16[2,384,512]{2,1,0:T(8,128)(2,1)}, u32[]{:S(2)}, u32[]{:S(2)}) collective-permute-start(bf16[2,384,512]{2,1,0:T(8,128)(2,1)} %collective-permute-done.12.refs_14_.refs_15_), channel_id=1, source_target_pairs={{0,4},{4,0},{1,5},{5,1},{2,6},{6,2},{3,7},{7,3},{8,12},{12,8},{9,1... | collective-permute-start | bytes 2359304 | tf_op jit(solution)/shard_map/ppermute | solution.py:253
  111.5 12.5 %all-to-all-start.2 = ((bf16[4,128,512]{2,1,0:T(8,128)(2,1)}), bf16[4,128,512]{2,1,0:T(8,128)(2,1)S(1)}, u32[]{:S(2)}, u32[]{:S(2)}) async-start(bf16[4,128,512]{2,1,0:T(8,128)(2,1)} %shard_map.76), calls=%async_computation.2 | async-start | bytes 1048576 | tf_op jit(solution)/shard_map/all_to_all | solution.py:332
  (3 other events, 32.9 us)
Sparse Core Ops, SparseCore 0:
  25.7 68.1 all-gather.1

commit v8 on v7

--- a/solution.py
+++ b/solution.py
@@ -14,22 +14,26 @@
 contract_last = (((1,), (1,)), ((), ()))
 contract_first = (((0,), (0,)), ((), ()))
 vmem_bytes = 56 * 1024 * 1024
+small_vmem_bytes = 16 * 1024 * 1024
 blocks_at = ((0, 0), (0, 1), (-1, 0), (1, 0), (-1, 1), (1, 1), (2, 0), (2, 1))
 
 
-def kernel_call(body, out_shape, spaces, scratch=()):
+def kernel_call(
+    body, out_shape, spaces, scratch=(), out_space=pltpu.VMEM, vmem_limit=vmem_bytes
+):
     return pl.pallas_call(
         body,
         out_shape=out_shape,
         in_specs=[pl.BlockSpec(memory_space=space) for space in spaces],
-        out_specs=jax.tree.map(lambda _: pl.BlockSpec(memory_space=pltpu.VMEM), out_shape),
+        out_specs=jax.tree.map(lambda _: pl.BlockSpec(memory_space=out_space), out_shape),
         scratch_shapes=list(scratch),
-        compiler_params=pltpu.CompilerParams(vmem_limit_bytes=vmem_bytes),
+        compiler_params=pltpu.CompilerParams(vmem_limit_bytes=vmem_limit),
     )
 
 
 def prep_kernel(
-    place_ref,
+    expert_ref,
+    core_ref,
     experts_ref,
     weight_ref,
     tok_ref,
@@ -39,7 +43,7 @@
     send_ref,
     table_ref,
 ):
-    expert_id, core = place_ref[0], place_ref[1]
+    expert_id, core = expert_ref[0], core_ref[0]
     n_dest, both, half = tok_out_ref.shape
     part = both // 2
     count = tok_ref.shape[0]
@@ -80,11 +84,10 @@
     for h in range(2):
         keep_ref[h] = mine[:, h * half : (h + 1) * half]
         send_ref[h] = other[:, h * half : (h + 1) * half]
-    padded = jnp.concatenate(
-        [table, jnp.zeros((table_rows - window, count), f32)], axis=0
+    padded = jnp.concatenate([table, jnp.zeros((table_rows - window, count), f32)], axis=0)
+    table_ref[...] = jnp.concatenate(
+        [padded, jnp.zeros((table_rows, half - count), f32)], axis=1
     ).astype(bf16)
-    for i in range(table_ref.shape[0]):
-        table_ref[i] = padded
 
 
 def weights_kernel(gate_ref, up_ref, down_ref, low_ref, high_ref, flip_ref):
@@ -96,25 +99,34 @@
         flip_ref[span, :] = down_ref[:, span].T
 
 
-def source(place_ref, n_x, dx, dc):
-    x, core = place_ref[0], place_ref[1]
+def source(x_ref, core_ref, n_x, dx, dc):
+    x, core = x_ref[0], core_ref[0]
     return lax.rem(x + dx + n_x, n_x) * 2 + (1 - core if dc else core)
 
 
-def back_kernel(rows_hbm, down_ref, down_far_ref, out_ref, rows_ref, sem):
+def back_kernel(rows_hbm, near_hbm, far_hbm, out_ref, rows_ref, near_ref, far_ref, sems):
     n_x, slots, hidden = out_ref.shape
-    n_z, _, sub, half = rows_ref.shape
+    n_z, sub, half = rows_ref.shape[1:2] + rows_ref.shape[3:]
     per_z = 2 * sub
-    copy = pltpu.make_async_copy(rows_hbm.at[:, pl.ds(8, 8)], rows_ref, sem)
-    copy.start()
-    copy.wait()
+    copies = []
+    for side, (weight_hbm, weight_ref) in enumerate(((near_hbm, near_ref), (far_hbm, far_ref))):
+        at = 8 + 4 * side
+        copies.append(
+            pltpu.make_async_copy(
+                rows_hbm.at[:, pl.ds(at, 4)], rows_ref.at[side], sems.at[2 * side]
+            )
+        )
+        copies.append(pltpu.make_async_copy(weight_hbm, weight_ref, sems.at[2 * side + 1]))
+    for copy in copies:
+        copy.start()
     total = None
-    for side, weight in enumerate((down_ref, down_far_ref)):
+    for side, weight_ref in enumerate((near_ref, far_ref)):
+        copies[2 * side].wait()
+        copies[2 * side + 1].wait()
         for h in range(2):
-            at = 4 * side + 2 * h
-            rows = rows_ref[:, at : at + 2].reshape(n_z * per_z, half)
+            rows = rows_ref[side, :, 2 * h : 2 * h + 2].reshape(n_z * per_z, half)
             term = jnp.dot(
-                rows, weight[h * half : (h + 1) * half, :], preferred_element_type=f32
+                rows, weight_ref[h * half : (h + 1) * half, :], preferred_element_type=f32
             )
             total = term if total is None else total + term
     total = total.reshape(n_z, n_x, slots // n_z, hidden)
@@ -132,7 +144,7 @@
     return copies
 
 
-def products_kernel(place_ref, *refs):
+def products_kernel(x_ref, core_ref, *refs):
     n_w = 2 * len(blocks_at)
     rows_hbm, weights_hbm = refs[0], refs[1 : 1 + n_w]
     total_ref, rows_ref, weights_ref, sems = refs[1 + n_w :]
@@ -146,7 +158,7 @@
     for b, (dx, dc) in enumerate(blocks_at):
         copies[2 * b].wait()
         copies[2 * b + 1].wait()
-        loaded = rows_ref[:, source(place_ref, n_s // 2, dx, dc)].astype(f32)
+        loaded = rows_ref[:, source(x_ref, core_ref, n_s // 2, dx, dc)].astype(f32)
         low, high = (
             loaded[:, begin : begin + part].reshape(n_z * part, half).astype(bf16)
             for begin in (0, part)
@@ -161,14 +173,20 @@
                 total_ref[:, span] += term
 
 
-def result_kernel(place_ref, *refs):
+def result_kernel(x_ref, core_ref, *refs):
     n_w = 2 * len(blocks_at)
-    sums_ref, back_ref, weights_hbm = refs[0], refs[1], refs[2 : 2 + n_w]
-    out_ref, weights_ref, sems = refs[2 + n_w :]
+    sums_hbm, back_hbm, weights_hbm = refs[0], refs[1], refs[2 : 2 + n_w]
+    out_hbm, sums_ref, back_ref, weights_ref, out_ref, sems, out_sems = refs[2 + n_w :]
     n_x, slots, hidden = back_ref.shape
     half = weights_ref.shape[3]
     n_z = slots // 8
+    sums_copy = pltpu.make_async_copy(sums_hbm, sums_ref, sems.at[n_w])
+    back_copy = pltpu.make_async_copy(back_hbm, back_ref, sems.at[n_w + 1])
+    sums_copy.start()
+    back_copy.start()
     copies = start_weights(weights_hbm, weights_ref, sems)
+    sums_copy.wait()
+    back_copy.wait()
 
     back = sum(back_ref[i].astype(f32) for i in range(n_x))
     gate_sum, up_sum, back_sum = (
@@ -188,8 +206,9 @@
     ).astype(bf16)
 
     quarter = 2 * half // window
+    sent = []
     for b, (dx, dc) in enumerate(blocks_at):
-        s = source(place_ref, n_x, dx, dc)
+        s = source(x_ref, core_ref, n_x, dx, dc)
         copies[2 * b].wait()
         copies[2 * b + 1].wait()
         for y in range(window):
@@ -206,6 +225,10 @@
                 out_ref[s, y, pair, slots // 2 :, :] = jnp.concatenate(
                     [mine[: slots // 4, 128:], mine[slots // 4 :, 128:]], axis=1
                 ).astype(bf16)
+        sent.append(pltpu.make_async_copy(out_ref.at[s], out_hbm.at[s], out_sems.at[b]))
+        sent[-1].start()
+    for copy in sent:
+        copy.wait()
 
 
 def combine_kernel(table_ref, rows_ref, out_ref):
@@ -253,7 +276,7 @@
     return lax.ppermute(value, "c", [(0, 1), (1, 0)])
 
 
-def gather_weights(low, high, tables):
+def gather_weights(low, high):
     n_x = lax.axis_size("x")
     ahead = [(i, (i + 1) % n_x) for i in range(n_x)]
     behind = [(i, (i - 1) % n_x) for i in range(n_x)]
@@ -265,13 +288,10 @@
     low_after = lax.ppermute(low_later, "x", behind)
     low_across = lax.ppermute(low_before, "x", ahead)
     high_across = lax.ppermute(high_after, "x", behind)
-    tables, low_before, high_after = lax.optimization_barrier((tables, low_before, high_after))
-    tables = lax.all_to_all(tables, "zh", 0, 0, tiled=True)
-    tables, high_before, low_after = lax.optimization_barrier((tables, high_before, low_after))
     near = [(low_before, high_before), (low_after, high_after), (low_across, high_across)]
     swapped = [(swap(a), swap(b)) for a, b in near]
     blocks = [(low, high), far, near[0], near[1], swapped[0], swapped[1], near[2], swapped[2]]
-    return blocks, tables
+    return blocks
 
 
 def per_device(tokens, cotangent, experts, route_weight, gate_weight, up_weight, down_weight):
@@ -284,25 +304,30 @@
     part = count // 2 // n_s
     gate, up, down = gate_weight[0], up_weight[0], down_weight[0]
     hidden = gate.shape[1]
-    x, core = lax.axis_index("x"), lax.axis_index("c")
-    prep_place = jnp.stack([lax.axis_index("y"), core]).astype(jnp.int32)
-    place = jnp.stack([x, core]).astype(jnp.int32)
+    x, core, expert_id = (
+        lax.axis_index(name).reshape(1).astype(jnp.int32) for name in ("x", "c", "y")
+    )
     smem, vmem, anywhere = pltpu.SMEM, pltpu.VMEM, pl.ANY
     half = feats // 2
-
-    pieces, keep, send, tables = kernel_call(
+    groups = 2 * n_s + 1
+
+    pieces, keep, send, table = kernel_call(
         prep_kernel,
         (
             jax.ShapeDtypeStruct((n_s, 2 * part, half), bf16),
             jax.ShapeDtypeStruct((2, n_s * part // 2, half), bf16),
             jax.ShapeDtypeStruct((2, n_s * part // 2, half), bf16),
-            jax.ShapeDtypeStruct((n_high, table_rows, count), bf16),
+            jax.ShapeDtypeStruct((table_rows, half), bf16),
         ),
-        [smem] + [vmem] * 4,
-    )(prep_place, experts.T, route_weight.T, tokens, cotangent)
-    gate, up, down, pieces = lax.optimization_barrier((gate, up, down, pieces))
+        [smem] * 2 + [vmem] * 4,
+    )(expert_id, core, experts.T, route_weight.T, tokens, cotangent)
     pieces = lax.all_to_all(pieces, ("x", "c"), 0, 0, tiled=True)
-    cot_far = swap(send)
+    own = jnp.concatenate([v.reshape(-1, half) for v in (pieces, keep, swap(send), table)], axis=0)
+    gate, up, down, own = lax.optimization_barrier((gate, up, down, own))
+    rows = lax.all_gather(own, ("zh", "zl"), axis=0, tiled=True).reshape(
+        n_z, groups, 2 * part, half
+    )
+
     low, high, down_t = kernel_call(
         weights_kernel,
         (
@@ -312,49 +337,61 @@
         ),
         [vmem] * 3,
     )(gate, up, down)
-    pieces, low, high, down_t, tables = lax.optimization_barrier(
-        (pieces, low, high, down_t, tables)
-    )
-    own = jnp.concatenate([v.reshape(-1, half) for v in (pieces, keep, cot_far)], axis=0)
-    rows = lax.all_gather(own, ("zh", "zl"), axis=0, tiled=True).reshape(
-        n_z, 2 * n_s, 2 * part, half
-    )
-    weights, tables = gather_weights(low, high, tables)
-    weights = [value for block in weights for value in block]
+    weights = [value for block in gather_weights(low, high) for value in block]
     down_far = swap(down_t)
 
     back = kernel_call(
         back_kernel,
         jax.ShapeDtypeStruct((n_x, n_z * part, hidden), bf16),
-        [anywhere, vmem, vmem],
-        [pltpu.VMEM((n_z, n_s, 2 * part, half), bf16), pltpu.SemaphoreType.DMA],
+        [anywhere] * 3,
+        [
+            pltpu.VMEM((2, n_z, n_s // 2, 2 * part, half), bf16),
+            pltpu.VMEM((feats, hidden), bf16),
+            pltpu.VMEM((feats, hidden), bf16),
+            pltpu.SemaphoreType.DMA((4,)),
+        ],
     )(rows, down_t, down_far)
     back = lax.all_to_all(back, "x", 0, 0, tiled=True)
     sums = kernel_call(
         products_kernel,
         jax.ShapeDtypeStruct((n_z * part, 2 * hidden), f32),
-        [smem] + [anywhere] * (1 + len(weights)),
+        [smem] * 2 + [anywhere] * (1 + len(weights)),
         [
             pltpu.VMEM((n_z, n_s, 2 * part, half), bf16),
             pltpu.VMEM((len(blocks_at), 2, 2, half, hidden), bf16),
             pltpu.SemaphoreType.DMA((len(weights) + 1,)),
         ],
-    )(place, rows, *weights)
+    )(x, core, rows, *weights)
+    result_shape = (n_s, window, 2, quarter // 2, n_z * part)
     result = kernel_call(
         result_kernel,
-        jax.ShapeDtypeStruct((n_s, window, 2, quarter // 2, n_z * part), bf16),
-        [smem, vmem, vmem] + [anywhere] * len(weights),
+        jax.ShapeDtypeStruct(result_shape, bf16),
+        [smem] * 2 + [anywhere] * (2 + len(weights)),
         [
+            pltpu.VMEM((n_z * part, 2 * hidden), f32),
+            pltpu.VMEM((n_x, n_z * part, hidden), bf16),
             pltpu.VMEM((len(blocks_at), 2, 2, half, hidden), bf16),
-            pltpu.SemaphoreType.DMA((len(weights),)),
+            pltpu.VMEM(result_shape, bf16),
+            pltpu.SemaphoreType.DMA((len(weights) + 2,)),
+            pltpu.SemaphoreType.DMA((len(blocks_at),)),
         ],
-    )(place, sums, back, *weights)
+        anywhere,
+    )(x, core, sums, back, *weights)
+    tables = lax.dynamic_index_in_dim(
+        rows.reshape(n_high, 2, groups, 2 * part, half)[:, :, groups - 1, :, :count],
+        lax.axis_index("zl"),
+        axis=1,
+        keepdims=False,
+    )
     shape = result.shape
     result = lax.all_to_all(
         result.reshape(n_s * window * 2, *shape[3:]), ("x", "c", "y", "zl"), 0, 0, tiled=True
     ).reshape(shape)
     dense = kernel_call(
-        combine_kernel, jax.ShapeDtypeStruct((n_high, quarter, count), bf16), [vmem] * 2
+        combine_kernel,
+        jax.ShapeDtypeStruct((n_high, quarter, count), bf16),
+        [vmem] * 2,
+        vmem_limit=small_vmem_bytes,
     )(tables, result)
     dense = lax.all_to_all(dense, "zh", 0, 0, tiled=True)
     return jnp.sum(dense.astype(f32), axis=0).astype(bf16).T

time: 208 us -> 206 us (level)
  waiting for transfers between devices: 24.7 us -> 53.7 us
  blocking collectives: 62.1 us -> 39.1 us
  Pallas kernels: 29.9 us -> 24.3 us
  starting transfers between devices: 73.3 us -> 70 us
    all_to_all x1 -> x0, blocking collectives: 31.1 us -> none  [per_device(): lax.all_to_all(result.reshape(n_s * window * 2, *shape[3:]), ('x', 'c', '...]
    all_to_all x1, waiting for transfers between devices: 7.94 us -> 22.8 us  [per_device(): lax.all_to_all(result.reshape(n_s * window * 2, *shape[3:]), ('x', 'c', '...]
    all_to_all x1, blocking collectives: 31 us -> 39.1 us  [per_device(): dense = lax.all_to_all(dense, 'zh', 0, 0, tiled=True)]
    ppermute x1, waiting for transfers between devices: 5.9 us -> 12.4 us  [gather_weights(): low_before = lax.ppermute(low, 'x', ahead)]
    all_to_all x1, starting transfers between devices: 10.5 us -> 5.27 us  [per_device(): lax.all_to_all(result.reshape(n_s * window * 2, *shape[3:]), ('x', 'c', '...]
    ppermute x1, waiting for transfers between devices: 0.01 us -> 4.29 us  [gather_weights(): low_across = lax.ppermute(low_before, 'x', ahead)]
    pallas_call x1, Pallas kernels: 2.95 us -> 0.76 us  [per_device(): kernel_call(combine_kernel, jax.ShapeDtypeStruct((n_high, quarter, count)...]
  transfers between devices with their start and end apart: 20 -> 20, of which waited for: 5 -> 8; matrix products, arithmetic and copies ran while one was open for 0% -> 0% of each run, Pallas kernels for 7% -> 6%
where the time goes in v8:
time: 206 us; the launch traced here: 205 us
  starting transfers between devices  70 us (34%)
  waiting for transfers between devices  53.7 us (26%)
  blocking collectives  39.1 us (19%)
  Pallas kernels  24.3 us (12%)
  between operations  13.7 us (7%)
  other arithmetic  2.2 us (1%)
    all_to_all x1, blocking collectives, per_device(): dense = lax.all_to_all(dense, 'zh', 0, 0, tiled=True)  39.1 us
    ppermute x10, starting transfers between devices, swap(): return lax.ppermute(value, 'c', [(0, 1), (1, 0)])  30.1 us
    all_to_all x1, waiting for transfers between devices, per_device(): lax.all_to_all(result.reshape(n_s * window * 2, *shape[3:]), ('x', 'c', '...  22.8 us
    ppermute x1, waiting for transfers between devices, gather_weights(): low_before = lax.ppermute(low, 'x', ahead)  12.4 us
    all_to_all x1, starting transfers between devices, per_device(): pieces = lax.all_to_all(pieces, ('x', 'c'), 0, 0, tiled=True)  10.1 us
    pallas_call x1, Pallas kernels, per_device(): kernel_call(result_kernel, jax.ShapeDtypeStruct(result_shape, bf16), [sme...  8.4 us
    pallas_call x1, Pallas kernels, per_device(): kernel_call(products_kernel, jax.ShapeDtypeStruct((n_z * part, 2 * hidden...  6.45 us
    ppermute x1, waiting for transfers between devices, gather_weights(): high_before = lax.ppermute(high_later, 'x', ahead)  6.41 us
  transfers between devices with their start and end apart: 20, of which 8 were waited for; matrix products, arithmetic and copies ran while one was open for 0% of the time, Pallas kernels for 6%

profile of v8, /device:TPU:1, one launch (start us, length us, event | category | flops | bytes accessed | tf_op | source)
XLA Modules:
  0.0 204.7 jit_solution(15660621737237807226)
XLA Ops:
  8.6 10.1 %all-to-all-start = ((bf16[8,16,384]{2,1,0:T(8,128)(2,1)}), bf16[8,16,384]{2,1,0:T(8,128)(2,1)S(1)}, u32[]{:S(2)}, u32[]{:S(2)}) async-start(bf16[8,16,384]{2,1,0:T(8,128)(2,1)} %get-tuple-element.20), calls=%async_computation | async-start | bytes 196608 | tf_op jit(solution)/shard_map/all_to_all | solution.py:324
  25.3 3.2 %shard_map.74 = (bf16[2,384,512]{2,1,0:T(8,128)(2,1)}, bf16[2,384,512]{2,1,0:T(8,128)(2,1)}, bf16[768,512]{1,0:T(8,128)(2,1)}) custom-call(bf16[768,512]{1,0:T(8,128)(2,1)} %bitcast.23, bf16[768,512]{1,0:T(8,128)(2,1)} %bitcast.24, bf16[512,768]{1,0:T(8,128)(2,1)} %bitcast.25), custom_call_target="tpu_custom_call" | custom-call | tf_op jit(solution)/shard_map/pallas_call | solution.py:331
  28.5 2.7 %collective-permute-start.1 = (bf16[2,384,512]{2,1,0:T(8,128)(2,1)}, bf16[2,384,512]{2,1,0:T(8,128)(2,1)S(1)}, u32[]{:S(2)}, u32[]{:S(2)}) collective-permute-start(bf16[2,384,512]{2,1,0:T(8,128)(2,1)} %get-tuple-element.33.refs_1_.refs_2_), channel_id=1, source_target_pairs={{0,4},{4,0},{1,5},{5,1},{2,6},{6,2},{3,7},{7,3},{8,12},{12,8},{9,1... | collective-permute-start | bytes 2359304 | tf_op jit(solution)/shard_map/ppermute | solution.py:276
  33.1 2.2 %collective-permute-start.3 = (bf16[2,384,512]{2,1,0:T(8,128)(2,1)}, bf16[2,384,512]{2,1,0:T(8,128)(2,1)S(1)}, u32[]{:S(2)}, u32[]{:S(2)}) collective-permute-start(bf16[2,384,512]{2,1,0:T(8,128)(2,1)} %get-tuple-element.33.refs_1_.refs_2_), channel_id=1, source_target_pairs={{0,8},{8,16},{16,24},{24,0},{1,9},{9,17},{17,25},{25,1},{2,10},{10... | collective-permute-start | bytes 2359304 | tf_op jit(solution)/shard_map/ppermute | solution.py:283
  35.3 4.3 %collective-permute-start.6 = (bf16[2,384,512]{2,1,0:T(8,128)(2,1)}, bf16[2,384,512]{2,1,0:T(8,128)(2,1)S(1)}, u32[]{:S(2)}, u32[]{:S(2)}) collective-permute-start(bf16[2,384,512]{2,1,0:T(8,128)(2,1)} %get-tuple-element.32.refs_2_.refs_3_), channel_id=1, source_target_pairs={{0,24},{8,0},{16,8},{24,16},{1,25},{9,1},{17,9},{25,17},{2,26},{10... | collective-permute-start | bytes 2359304 | tf_op jit(solution)/shard_map/ppermute | solution.py:284
  39.6 3.0 %collective-permute-start.15 = (bf16[768,512]{1,0:T(8,128)(2,1)}, bf16[768,512]{1,0:T(8,128)(2,1)S(1)}, u32[]{:S(2)}, u32[]{:S(2)}) collective-permute-start(bf16[768,512]{1,0:T(8,128)(2,1)} %get-tuple-element.34.near_hbm), channel_id=1, source_target_pairs={{0,4},{4,0},{1,5},{5,1},{2,6},{6,2},{3,7},{7,3},{8,12},{12,8},{9,1... | collective-permute-start | bytes 2359304 | tf_op jit(solution)/shard_map/ppermute | solution.py:276
  42.6 12.4 %collective-permute-done.3.refs_5_.refs_6_ = bf16[2,384,512]{2,1,0:T(8,128)(2,1)S(1)} collective-permute-done((bf16[2,384,512]{2,1,0:T(8,128)(2,1)}, bf16[2,384,512]{2,1,0:T(8,128)(2,1)S(1)}, u32[]{:S(2)}, u32[]{:S(2)}) %collective-permute-start.3) | collective-permute-done | bytes 786464 | tf_op jit(solution)/shard_map/ppermute | solution.py:283
  57.0 3.3 %collective-permute-start.7 = (bf16[2,384,512]{2,1,0:T(8,128)(2,1)S(1)}, bf16[2,384,512]{2,1,0:T(8,128)(2,1)S(1)}, u32[]{:S(2)}, u32[]{:S(2)}) collective-permute-start(bf16[2,384,512]{2,1,0:T(8,128)(2,1)S(1)} %collective-permute-done.3.refs_5_.refs_6_), channel_id=1, source_target_pairs={{0,4},{4,0},{1,5},{5,1},{2,6},{6,2},{3,7},{7,3},{8,12},{12,8},{9,1... | collective-permute-start | bytes 2359304 | tf_op jit(solution)/shard_map/ppermute | solution.py:276
  60.3 4.9 %collective-permute-start.12 = (bf16[2,384,512]{2,1,0:T(8,128)(2,1)S(1)}, bf16[2,384,512]{2,1,0:T(8,128)(2,1)}, u32[]{:S(2)}, u32[]{:S(2)}) collective-permute-start(bf16[2,384,512]{2,1,0:T(8,128)(2,1)S(1)} %collective-permute-done.6.refs_8_.refs_9_), channel_id=1, source_target_pairs={{0,24},{8,0},{16,8},{24,16},{1,25},{9,1},{17,9},{25,17},{2,26},{10... | collective-permute-start | bytes 2359304 | tf_op jit(solution)/shard_map/ppermute | solution.py:290
  67.1 4.6 %collective-permute-start.5 = (bf16[2,384,512]{2,1,0:T(8,128)(2,1)}, bf16[2,384,512]{2,1,0:T(8,128)(2,1)}, u32[]{:S(2)}, u32[]{:S(2)}) collective-permute-start(bf16[2,384,512]{2,1,0:T(8,128)(2,1)} %get-tuple-element.33.refs_1_.refs_2_), channel_id=1, source_target_pairs={{0,24},{8,0},{16,8},{24,16},{1,25},{9,1},{17,9},{25,17},{2,26},{10... | collective-permute-start | bytes 2359304 | tf_op jit(solution)/shard_map/ppermute | solution.py:288
  71.6 4.3 %collective-permute-done.11.refs_13_.refs_14_ = bf16[2,384,512]{2,1,0:T(8,128)(2,1)} collective-permute-done((bf16[2,384,512]{2,1,0:T(8,128)(2,1)S(1)}, bf16[2,384,512]{2,1,0:T(8,128)(2,1)}, u32[]{:S(2)}, u32[]{:S(2)}) %collective-permute-start.11) | collective-permute-done | bytes 786464 | tf_op jit(solution)/shard_map/ppermute | solution.py:289
  75.9 6.0 %collective-permute-start.10 = (bf16[2,384,512]{2,1,0:T(8,128)(2,1)S(1)}, bf16[2,384,512]{2,1,0:T(8,128)(2,1)}, u32[]{:S(2)}, u32[]{:S(2)}) collective-permute-start(bf16[2,384,512]{2,1,0:T(8,128)(2,1)S(1)} %collective-permute-done.6.refs_8_.refs_9_), channel_id=1, source_target_pairs={{0,4},{4,0},{1,5},{5,1},{2,6},{6,2},{3,7},{7,3},{8,12},{12,8},{9,1... | collective-permute-start | bytes 2359304 | tf_op jit(solution)/shard_map/ppermute | solution.py:276
  84.0 2.4 %collective-permute-start.14 = (bf16[2,384,512]{2,1,0:T(8,128)(2,1)}, bf16[2,384,512]{2,1,0:T(8,128)(2,1)}, u32[]{:S(2)}, u32[]{:S(2)}) collective-permute-start(bf16[2,384,512]{2,1,0:T(8,128)(2,1)} %collective-permute-done.12.refs_14_.refs_15_), channel_id=1, source_target_pairs={{0,4},{4,0},{1,5},{5,1},{2,6},{6,2},{3,7},{7,3},{8,12},{12,8},{9,1... | collective-permute-start | bytes 2359304 | tf_op jit(solution)/shard_map/ppermute | solution.py:276
  86.4 6.4 %collective-permute-done.4.refs_6_.refs_7_ = bf16[2,384,512]{2,1,0:T(8,128)(2,1)} collective-permute-done((bf16[2,384,512]{2,1,0:T(8,128)(2,1)}, bf16[2,384,512]{2,1,0:T(8,128)(2,1)}, u32[]{:S(2)}, u32[]{:S(2)}) %collective-permute-start.4) | collective-permute-done | bytes 786464 | tf_op jit(solution)/shard_map/ppermute | solution.py:287
  92.8 4.2 %collective-permute-start.8 = (bf16[2,384,512]{2,1,0:T(8,128)(2,1)}, bf16[2,384,512]{2,1,0:T(8,128)(2,1)}, u32[]{:S(2)}, u32[]{:S(2)}) collective-permute-start(bf16[2,384,512]{2,1,0:T(8,128)(2,1)} %collective-permute-done.4.refs_6_.refs_7_), channel_id=1, source_target_pairs={{0,4},{4,0},{1,5},{5,1},{2,6},{6,2},{3,7},{7,3},{8,12},{12,8},{9,1... | collective-permute-start | bytes 2359304 | tf_op jit(solution)/shard_map/ppermute | solution.py:276
  99.0 2.7 %collective-permute-start.9 = (bf16[2,384,512]{2,1,0:T(8,128)(2,1)}, bf16[2,384,512]{2,1,0:T(8,128)(2,1)}, u32[]{:S(2)}, u32[]{:S(2)}) collective-permute-start(bf16[2,384,512]{2,1,0:T(8,128)(2,1)} %collective-permute-done.5.refs_7_.refs_8_), channel_id=1, source_target_pairs={{0,4},{4,0},{1,5},{5,1},{2,6},{6,2},{3,7},{7,3},{8,12},{12,8},{9,1... | collective-permute-start | bytes 2359304 | tf_op jit(solution)/shard_map/ppermute | solution.py:276
  101.7 3.5 %shard_map.76 = bf16[4,128,512]{2,1,0:T(8,128)(2,1)} custom-call(bf16[16,17,16,384]{3,2,1,0:T(8,128)(2,1)} %bitcast.19, bf16[768,512]{1,0:T(8,128)(2,1)} %get-tuple-element.34.near_hbm, bf16[768,512]{1,0:T(8,128)(2,1)} %copy-done.6), custom_call_target="tpu_custom_call" | custom-call | tf_op jit(solution)/shard_map/pallas_call | solution.py:343
  105.3 4.7 %all-to-all-start.1 = ((bf16[4,128,512]{2,1,0:T(8,128)(2,1)}), bf16[4,128,512]{2,1,0:T(8,128)(2,1)S(1)}, u32[]{:S(2)}, u32[]{:S(2)}) async-start(bf16[4,128,512]{2,1,0:T(8,128)(2,1)} %shard_map.76), calls=%async_computation.1 | async-start | bytes 1048576 | tf_op jit(solution)/shard_map/all_to_all | solution.py:354
  110.0 6.4 %shard_map.75.refs_0_ = f32[128,1024]{1,0:T(8,128)} custom-call(s32[1]{0:T(128)} %bitcast.12.x_ref, s32[1]{0:T(128)} %bitcast.4.core_ref, bf16[16,17,16,384]{3,2,1,0:T(8,128)(2,1)} %bitcast.20, bf16[2,384,512]{2,1,0:T(8,128)(2,1)} %get-tuple-element.33.refs_1_.refs_2_, bf16[2,384,512]{2,1,0:T(8,128)(2,1)} %get-tuple-element.32.refs_2_.refs_3_, ...), custom_call_target="tpu_custom_call" | custom-call | tf_op jit(solution)/shard_map/pallas_call | solution.py:355
  116.5 2.8 %all-to-all-done.1.refs_1_ = bf16[4,128,512]{2,1,0:T(8,128)(2,1)S(1)} async-done(((bf16[4,128,512]{2,1,0:T(8,128)(2,1)}), bf16[4,128,512]{2,1,0:T(8,128)(2,1)S(1)}, u32[]{:S(2)}, u32[]{:S(2)}) %all-to-all-start.1) | async-done | bytes 524320 | tf_op jit(solution)/shard_map/all_to_all | solution.py:354
  120.1 8.4 %shard_map.77 = bf16[8,4,2,96,128]{4,3,2,1,0:T(8,128)(2,1)} custom-call(s32[1]{0:T(128)} %bitcast.12.x_ref, s32[1]{0:T(128)} %bitcast.4.core_ref, f32[128,1024]{1,0:T(8,128)} %shard_map.75.refs_0_, bf16[4,128,512]{2,1,0:T(8,128)(2,1)} %copy-done.5, bf16[2,384,512]{2,1,0:T(8,128)(2,1)} %get-tuple-element.33.refs_1_.refs_2_, ...), custom_call_target="tpu_custom_call" | custom-call | tf_op jit(solution)/shard_map/pallas_call | solution.py:366
  128.5 5.3 %all-to-all-start.2 = ((bf16[64,96,128]{2,1,0:T(8,128)(2,1)}), bf16[64,96,128]{2,1,0:T(8,128)(2,1)S(1)}, u32[]{:S(2)}, u32[]{:S(2)}) async-start(bf16[64,96,128]{2,1,0:T(8,128)(2,1)} %bitcast.22), calls=%async_computation.2 | async-start | bytes 3145728 | tf_op jit(solution)/shard_map/all_to_all | solution.py:387
  134.6 22.8 %all-to-all-done.2 = bf16[64,96,128]{2,1,0:T(8,128)(2,1)S(1)} async-done(((bf16[64,96,128]{2,1,0:T(8,128)(2,1)}), bf16[64,96,128]{2,1,0:T(8,128)(2,1)S(1)}, u32[]{:S(2)}, u32[]{:S(2)}) %all-to-all-start.2) | async-done | bytes 1572896 | tf_op jit(solution)/shard_map/all_to_all | solution.py:387
  158.1 39.1 %all_to_all.20 = bf16[8,192,128]{2,1,0:T(8,128)(2,1)S(1)} all-to-all(bf16[8,192,128]{2,1,0:T(8,128)(2,1)S(1)} %shard_map.78), channel_id=1, replica_groups=mesh['zh'=8,'zl'=2,'x'=4,'c'=2,'y'=4] {'zh'}, dimensions={0} | all-to-all | bytes 786432 | tf_op jit(solution)/shard_map/all_to_all | solution.py:396
  (42 shorter events, 21.4 us)
Async XLA Ops:
  8.6 15.1 %all-to-all-start = ((bf16[8,16,384]{2,1,0:T(8,128)(2,1)}), bf16[8,16,384]{2,1,0:T(8,128)(2,1)S(1)}, u32[]{:S(2)}, u32[]{:S(2)}) async-start(bf16[8,16,384]{2,1,0:T(8,128)(2,1)} %get-tuple-element.20), calls=%async_computation | async-start | bytes 196608 | tf_op jit(solution)/shard_map/all_to_all | solution.py:324
  18.7 83.0 %all-gather.2.cloned.1.call-start = ((), (), s32[]{:S(2)}) async-start(), calls=%async_computation.4 | async-start | bytes 3551232 | tf_op jit(solution)/shard_map/all_gather | solution.py:327
  18.7 3.3 %collective-permute-start = (bf16[2,32,384]{2,1,0:T(8,128)(2,1)}, bf16[2,32,384]{2,1,0:T(8,128)(2,1)S(1)}, u32[]{:S(2)}, u32[]{:S(2)}) collective-permute-start(bf16[2,32,384]{2,1,0:T(8,128)(2,1)} %get-tuple-element.22), channel_id=1, source_target_pairs={{0,4},{4,0},{1,5},{5,1},{2,6},{6,2},{3,7},{7,3},{8,12},{12,8},{9,1... | collective-permute-start | bytes 147464 | tf_op jit(solution)/shard_map/ppermute | solution.py:276
  28.5 14.1 %collective-permute-start.1 = (bf16[2,384,512]{2,1,0:T(8,128)(2,1)}, bf16[2,384,512]{2,1,0:T(8,128)(2,1)S(1)}, u32[]{:S(2)}, u32[]{:S(2)}) collective-permute-start(bf16[2,384,512]{2,1,0:T(8,128)(2,1)} %get-tuple-element.33.refs_1_.refs_2_), channel_id=1, source_target_pairs={{0,4},{4,0},{1,5},{5,1},{2,6},{6,2},{3,7},{7,3},{8,12},{12,8},{9,1... | collective-permute-start | bytes 2359304 | tf_op jit(solution)/shard_map/ppermute | solution.py:276
  31.2 11.4 %collective-permute-start.2 = (bf16[2,384,512]{2,1,0:T(8,128)(2,1)}, bf16[2,384,512]{2,1,0:T(8,128)(2,1)S(1)}, u32[]{:S(2)}, u32[]{:S(2)}) collective-permute-start(bf16[2,384,512]{2,1,0:T(8,128)(2,1)} %get-tuple-element.32.refs_2_.refs_3_), channel_id=1, source_target_pairs={{0,4},{4,0},{1,5},{5,1},{2,6},{6,2},{3,7},{7,3},{8,12},{12,8},{9,1... | collective-permute-start | bytes 2359304 | tf_op jit(solution)/shard_map/ppermute | solution.py:276
  33.1 21.9 %collective-permute-start.3 = (bf16[2,384,512]{2,1,0:T(8,128)(2,1)}, bf16[2,384,512]{2,1,0:T(8,128)(2,1)S(1)}, u32[]{:S(2)}, u32[]{:S(2)}) collective-permute-start(bf16[2,384,512]{2,1,0:T(8,128)(2,1)} %get-tuple-element.33.refs_1_.refs_2_), channel_id=1, source_target_pairs={{0,8},{8,16},{16,24},{24,0},{1,9},{9,17},{17,25},{25,1},{2,10},{10... | collective-permute-start | bytes 2359304 | tf_op jit(solution)/shard_map/ppermute | solution.py:283
  35.3 24.9 %collective-permute-start.6 = (bf16[2,384,512]{2,1,0:T(8,128)(2,1)}, bf16[2,384,512]{2,1,0:T(8,128)(2,1)S(1)}, u32[]{:S(2)}, u32[]{:S(2)}) collective-permute-start(bf16[2,384,512]{2,1,0:T(8,128)(2,1)} %get-tuple-element.32.refs_2_.refs_3_), channel_id=1, source_target_pairs={{0,24},{8,0},{16,8},{24,16},{1,25},{9,1},{17,9},{25,17},{2,26},{10... | collective-permute-start | bytes 2359304 | tf_op jit(solution)/shard_map/ppermute | solution.py:284
  39.6 27.4 %collective-permute-start.15 = (bf16[768,512]{1,0:T(8,128)(2,1)}, bf16[768,512]{1,0:T(8,128)(2,1)S(1)}, u32[]{:S(2)}, u32[]{:S(2)}) collective-permute-start(bf16[768,512]{1,0:T(8,128)(2,1)} %get-tuple-element.34.near_hbm), channel_id=1, source_target_pairs={{0,4},{4,0},{1,5},{5,1},{2,6},{6,2},{3,7},{7,3},{8,12},{12,8},{9,1... | collective-permute-start | bytes 2359304 | tf_op jit(solution)/shard_map/ppermute | solution.py:276
  42.6 62.6 %copy-start = (bf16[2,384,512]{2,1,0:T(8,128)(2,1)}, bf16[2,384,512]{2,1,0:T(8,128)(2,1)S(1)}, u32[]{:S(2)}) copy-start(bf16[2,384,512]{2,1,0:T(8,128)(2,1)S(1)} %collective-permute-done.1.refs_3_.refs_4_) | copy-start | bytes 2359300
  42.6 62.6 %copy-start.1 = (bf16[2,384,512]{2,1,0:T(8,128)(2,1)}, bf16[2,384,512]{2,1,0:T(8,128)(2,1)S(1)}, u32[]{:S(2)}) copy-start(bf16[2,384,512]{2,1,0:T(8,128)(2,1)S(1)} %collective-permute-done.2.refs_4_.refs_5_) | copy-start | bytes 2359300
  55.0 50.2 %copy-start.2 = (bf16[2,384,512]{2,1,0:T(8,128)(2,1)}, bf16[2,384,512]{2,1,0:T(8,128)(2,1)S(1)}, u32[]{:S(2)}) copy-start(bf16[2,384,512]{2,1,0:T(8,128)(2,1)S(1)} %collective-permute-done.3.refs_5_.refs_6_) | copy-start | bytes 2359300
  55.0 20.9 %collective-permute-start.11 = (bf16[2,384,512]{2,1,0:T(8,128)(2,1)S(1)}, bf16[2,384,512]{2,1,0:T(8,128)(2,1)}, u32[]{:S(2)}, u32[]{:S(2)}) collective-permute-start(bf16[2,384,512]{2,1,0:T(8,128)(2,1)S(1)} %collective-permute-done.3.refs_5_.refs_6_), channel_id=1, source_target_pairs={{0,8},{8,16},{16,24},{24,0},{1,9},{9,17},{17,25},{25,1},{2,10},{10... | collective-permute-start | bytes 2359304 | tf_op jit(solution)/shard_map/ppermute | solution.py:289
  57.0 25.0 %collective-permute-start.7 = (bf16[2,384,512]{2,1,0:T(8,128)(2,1)S(1)}, bf16[2,384,512]{2,1,0:T(8,128)(2,1)S(1)}, u32[]{:S(2)}, u32[]{:S(2)}) collective-permute-start(bf16[2,384,512]{2,1,0:T(8,128)(2,1)S(1)} %collective-permute-done.3.refs_5_.refs_6_), channel_id=1, source_target_pairs={{0,4},{4,0},{1,5},{5,1},{2,6},{6,2},{3,7},{7,3},{8,12},{12,8},{9,1... | collective-permute-start | bytes 2359304 | tf_op jit(solution)/shard_map/ppermute | solution.py:276
  60.2 45.0 %copy-start.3 = (bf16[2,384,512]{2,1,0:T(8,128)(2,1)}, bf16[2,384,512]{2,1,0:T(8,128)(2,1)S(1)}, u32[]{:S(2)}) copy-start(bf16[2,384,512]{2,1,0:T(8,128)(2,1)S(1)} %collective-permute-done.6.refs_8_.refs_9_) | copy-start | bytes 2359300
  60.3 23.7 %collective-permute-start.12 = (bf16[2,384,512]{2,1,0:T(8,128)(2,1)S(1)}, bf16[2,384,512]{2,1,0:T(8,128)(2,1)}, u32[]{:S(2)}, u32[]{:S(2)}) collective-permute-start(bf16[2,384,512]{2,1,0:T(8,128)(2,1)S(1)} %collective-permute-done.6.refs_8_.refs_9_), channel_id=1, source_target_pairs={{0,24},{8,0},{16,8},{24,16},{1,25},{9,1},{17,9},{25,17},{2,26},{10... | collective-permute-start | bytes 2359304 | tf_op jit(solution)/shard_map/ppermute | solution.py:290
  65.1 27.7 %collective-permute-start.4 = (bf16[2,384,512]{2,1,0:T(8,128)(2,1)}, bf16[2,384,512]{2,1,0:T(8,128)(2,1)}, u32[]{:S(2)}, u32[]{:S(2)}) collective-permute-start(bf16[2,384,512]{2,1,0:T(8,128)(2,1)} %get-tuple-element.32.refs_2_.refs_3_), channel_id=1, source_target_pairs={{0,8},{8,16},{16,24},{24,0},{1,9},{9,17},{17,25},{25,1},{2,10},{10... | collective-permute-start | bytes 2359304 | tf_op jit(solution)/shard_map/ppermute | solution.py:287
  67.1 31.9 %collective-permute-start.5 = (bf16[2,384,512]{2,1,0:T(8,128)(2,1)}, bf16[2,384,512]{2,1,0:T(8,128)(2,1)}, u32[]{:S(2)}, u32[]{:S(2)}) collective-permute-start(bf16[2,384,512]{2,1,0:T(8,128)(2,1)} %get-tuple-element.33.refs_1_.refs_2_), channel_id=1, source_target_pairs={{0,24},{8,0},{16,8},{24,16},{1,25},{9,1},{17,9},{25,17},{2,26},{10... | collective-permute-start | bytes 2359304 | tf_op jit(solution)/shard_map/ppermute | solution.py:288
  75.9 34.0 %collective-permute-start.10 = (bf16[2,384,512]{2,1,0:T(8,128)(2,1)S(1)}, bf16[2,384,512]{2,1,0:T(8,128)(2,1)}, u32[]{:S(2)}, u32[]{:S(2)}) collective-permute-start(bf16[2,384,512]{2,1,0:T(8,128)(2,1)S(1)} %collective-permute-done.6.refs_8_.refs_9_), channel_id=1, source_target_pairs={{0,4},{4,0},{1,5},{5,1},{2,6},{6,2},{3,7},{7,3},{8,12},{12,8},{9,1... | collective-permute-start | bytes 2359304 | tf_op jit(solution)/shard_map/ppermute | solution.py:276
  82.0 28.0 %collective-permute-start.13 = (bf16[2,384,512]{2,1,0:T(8,128)(2,1)}, bf16[2,384,512]{2,1,0:T(8,128)(2,1)}, u32[]{:S(2)}, u32[]{:S(2)}) collective-permute-start(bf16[2,384,512]{2,1,0:T(8,128)(2,1)} %collective-permute-done.11.refs_13_.refs_14_), channel_id=1, source_target_pairs={{0,4},{4,0},{1,5},{5,1},{2,6},{6,2},{3,7},{7,3},{8,12},{12,8},{9,1... | collective-permute-start | bytes 2359304 | tf_op jit(solution)/shard_map/ppermute | solution.py:276
  84.0 26.0 %collective-permute-start.14 = (bf16[2,384,512]{2,1,0:T(8,128)(2,1)}, bf16[2,384,512]{2,1,0:T(8,128)(2,1)}, u32[]{:S(2)}, u32[]{:S(2)}) collective-permute-start(bf16[2,384,512]{2,1,0:T(8,128)(2,1)} %collective-permute-done.12.refs_14_.refs_15_), channel_id=1, source_target_pairs={{0,4},{4,0},{1,5},{5,1},{2,6},{6,2},{3,7},{7,3},{8,12},{12,8},{9,1... | collective-permute-start | bytes 2359304 | tf_op jit(solution)/shard_map/ppermute | solution.py:276
  92.8 17.2 %collective-permute-start.8 = (bf16[2,384,512]{2,1,0:T(8,128)(2,1)}, bf16[2,384,512]{2,1,0:T(8,128)(2,1)}, u32[]{:S(2)}, u32[]{:S(2)}) collective-permute-start(bf16[2,384,512]{2,1,0:T(8,128)(2,1)} %collective-permute-done.4.refs_6_.refs_7_), channel_id=1, source_target_pairs={{0,4},{4,0},{1,5},{5,1},{2,6},{6,2},{3,7},{7,3},{8,12},{12,8},{9,1... | collective-permute-start | bytes 2359304 | tf_op jit(solution)/shard_map/ppermute | solution.py:276
  99.0 11.0 %collective-permute-start.9 = (bf16[2,384,512]{2,1,0:T(8,128)(2,1)}, bf16[2,384,512]{2,1,0:T(8,128)(2,1)}, u32[]{:S(2)}, u32[]{:S(2)}) collective-permute-start(bf16[2,384,512]{2,1,0:T(8,128)(2,1)} %collective-permute-done.5.refs_7_.refs_8_), channel_id=1, source_target_pairs={{0,4},{4,0},{1,5},{5,1},{2,6},{6,2},{3,7},{7,3},{8,12},{12,8},{9,1... | collective-permute-start | bytes 2359304 | tf_op jit(solution)/shard_map/ppermute | solution.py:276
  105.3 14.0 %all-to-all-start.1 = ((bf16[4,128,512]{2,1,0:T(8,128)(2,1)}), bf16[4,128,512]{2,1,0:T(8,128)(2,1)S(1)}, u32[]{:S(2)}, u32[]{:S(2)}) async-start(bf16[4,128,512]{2,1,0:T(8,128)(2,1)} %shard_map.76), calls=%async_computation.1 | async-start | bytes 1048576 | tf_op jit(solution)/shard_map/all_to_all | solution.py:354
  128.5 28.9 %all-to-all-start.2 = ((bf16[64,96,128]{2,1,0:T(8,128)(2,1)}), bf16[64,96,128]{2,1,0:T(8,128)(2,1)S(1)}, u32[]{:S(2)}, u32[]{:S(2)}) async-start(bf16[64,96,128]{2,1,0:T(8,128)(2,1)} %bitcast.22), calls=%async_computation.2 | async-start | bytes 3145728 | tf_op jit(solution)/shard_map/all_to_all | solution.py:387
  (3 other events, 22.1 us)
Sparse Core Ops, SparseCore 0:
  25.4 66.6 all-gather.1

commit v9 on v8

--- a/solution.py
+++ b/solution.py
@@ -88,6 +88,15 @@
     table_ref[...] = jnp.concatenate(
         [padded, jnp.zeros((table_rows, half - count), f32)], axis=1
     ).astype(bf16)
+
+
+def pack_kernel(tok_ref, keep_ref, far_ref, table_ref, out_ref):
+    n_dest, rows, half = tok_ref.shape
+    out_ref[:n_dest] = tok_ref[...]
+    for i, ref in enumerate((keep_ref, far_ref)):
+        begin = n_dest + i * n_dest // 2
+        out_ref[begin : begin + n_dest // 2] = ref[...].reshape(n_dest // 2, rows, half)
+    out_ref[2 * n_dest] = table_ref[...]
 
 
 def weights_kernel(gate_ref, up_ref, down_ref, low_ref, high_ref, flip_ref):
@@ -282,12 +291,14 @@
     behind = [(i, (i - 1) % n_x) for i in range(n_x)]
     low_before = lax.ppermute(low, "x", ahead)
     high_after = lax.ppermute(high, "x", behind)
-    far = (swap(low), swap(high))
-    low_later, high_later, far = lax.optimization_barrier((low, high, far))
-    high_before = lax.ppermute(high_later, "x", ahead)
-    low_after = lax.ppermute(low_later, "x", behind)
+    high_before = lax.ppermute(high, "x", ahead)
+    low_after = lax.ppermute(low, "x", behind)
+    low_before, high_after, high_before, low_after = lax.optimization_barrier(
+        (low_before, high_after, high_before, low_after)
+    )
     low_across = lax.ppermute(low_before, "x", ahead)
     high_across = lax.ppermute(high_after, "x", behind)
+    far = (swap(low), swap(high))
     near = [(low_before, high_before), (low_after, high_after), (low_across, high_across)]
     swapped = [(swap(a), swap(b)) for a, b in near]
     blocks = [(low, high), far, near[0], near[1], swapped[0], swapped[1], near[2], swapped[2]]
@@ -322,9 +333,14 @@
         [smem] * 2 + [vmem] * 4,
     )(expert_id, core, experts.T, route_weight.T, tokens, cotangent)
     pieces = lax.all_to_all(pieces, ("x", "c"), 0, 0, tiled=True)
-    own = jnp.concatenate([v.reshape(-1, half) for v in (pieces, keep, swap(send), table)], axis=0)
+    own = kernel_call(
+        pack_kernel,
+        jax.ShapeDtypeStruct((groups, 2 * part, half), bf16),
+        [vmem] * 4,
+        vmem_limit=small_vmem_bytes,
+    )(pieces, keep, swap(send), table)
     gate, up, down, own = lax.optimization_barrier((gate, up, down, own))
-    rows = lax.all_gather(own, ("zh", "zl"), axis=0, tiled=True).reshape(
+    rows = lax.all_gather(own.reshape(-1, half), ("zh", "zl"), axis=0, tiled=True).reshape(
         n_z, groups, 2 * part, half
     )
 

time: 206 us -> 205 us (level)
    ppermute x1, waiting for transfers between devices: 12.4 us -> 0.01 us  [gather_weights(): low_before = lax.ppermute(low, 'x', ahead)]
    ppermute x2, waiting for transfers between devices: 8.46 us -> 16.4 us  [the longest x1 11.6 us: gather_weights(): high_before = lax.ppermute(high, 'x', ahead)]
    ppermute x1, waiting for transfers between devices: 4.29 us -> 8.94 us  [gather_weights(): low_across = lax.ppermute(low_before, 'x', ahead)]
    all_to_all x1, starting transfers between devices: 5.27 us -> 8.48 us  [per_device(): lax.all_to_all(result.reshape(n_s * window * 2, *shape[3:]), ('x', 'c', '...]
  transfers between devices with their start and end apart: 20 -> 20, of which waited for: 8 -> 7; matrix products, arithmetic and copies ran while one was open for 0% -> 0% of each run, Pallas kernels for 6% -> 6%
where the time goes in v9:
time: 205 us; the launch traced here: 203 us
  starting transfers between devices  71 us (35%)
  waiting for transfers between devices  52.6 us (26%)
  blocking collectives  37.2 us (18%)
  Pallas kernels  25.1 us (12%)
  between operations  13.8 us (7%)
  local copies, waits for them, and re-layouts  3.19 us (2%)
    all_to_all x1, blocking collectives, per_device(): dense = lax.all_to_all(dense, 'zh', 0, 0, tiled=True)  37.2 us
    ppermute x10, starting transfers between devices, swap(): return lax.ppermute(value, 'c', [(0, 1), (1, 0)])  30.2 us
    all_to_all x1, waiting for transfers between devices, per_device(): lax.all_to_all(result.reshape(n_s * window * 2, *shape[3:]), ('x', 'c', '...  22.7 us
    ppermute x1, waiting for transfers between devices, gather_weights(): high_before = lax.ppermute(high, 'x', ahead)  11.6 us
    all_to_all x1, starting transfers between devices, per_device(): pieces = lax.all_to_all(pieces, ('x', 'c'), 0, 0, tiled=True)  10.1 us
    ppermute x1, waiting for transfers between devices, gather_weights(): low_across = lax.ppermute(low_before, 'x', ahead)  8.94 us
    all_to_all x1, starting transfers between devices, per_device(): lax.all_to_all(result.reshape(n_s * window * 2, *shape[3:]), ('x', 'c', '...  8.48 us
    pallas_call x1, Pallas kernels, per_device(): kernel_call(result_kernel, jax.ShapeDtypeStruct(result_shape, bf16), [sme...  8.37 us
  transfers between devices with their start and end apart: 20, of which 7 were waited for; matrix products, arithmetic and copies ran while one was open for 0% of the time, Pallas kernels for 6%

profile of v9, /device:TPU:1, one launch (start us, length us, event | category | flops | bytes accessed | tf_op | source)
XLA Modules:
  0.0 203.5 jit_solution(15980363549907939520)
XLA Ops:
  8.6 10.1 %all-to-all-start = ((bf16[8,16,384]{2,1,0:T(8,128)(2,1)}), bf16[8,16,384]{2,1,0:T(8,128)(2,1)S(1)}, u32[]{:S(2)}, u32[]{:S(2)}) async-start(bf16[8,16,384]{2,1,0:T(8,128)(2,1)} %get-tuple-element.20), calls=%async_computation | async-start | bytes 196608 | tf_op jit(solution)/shard_map/all_to_all | solution.py:335
  26.0 3.2 %shard_map.75 = (bf16[2,384,512]{2,1,0:T(8,128)(2,1)}, bf16[2,384,512]{2,1,0:T(8,128)(2,1)}, bf16[768,512]{1,0:T(8,128)(2,1)}) custom-call(bf16[768,512]{1,0:T(8,128)(2,1)} %bitcast.21, bf16[768,512]{1,0:T(8,128)(2,1)} %bitcast.22, bf16[512,768]{1,0:T(8,128)(2,1)} %bitcast.23), custom_call_target="tpu_custom_call" | custom-call | tf_op jit(solution)/shard_map/pallas_call | solution.py:347
  29.2 2.9 %collective-permute-start.6 = (bf16[2,384,512]{2,1,0:T(8,128)(2,1)}, bf16[2,384,512]{2,1,0:T(8,128)(2,1)S(1)}, u32[]{:S(2)}, u32[]{:S(2)}) collective-permute-start(bf16[2,384,512]{2,1,0:T(8,128)(2,1)} %get-tuple-element.28.refs_1_.refs_2_), channel_id=1, source_target_pairs={{0,24},{8,0},{16,8},{24,16},{1,25},{9,1},{17,9},{25,17},{2,26},{10... | collective-permute-start | bytes 2359304 | tf_op jit(solution)/shard_map/ppermute | solution.py:295
  32.1 2.4 %collective-permute-start.3 = (bf16[2,384,512]{2,1,0:T(8,128)(2,1)}, bf16[2,384,512]{2,1,0:T(8,128)(2,1)S(1)}, u32[]{:S(2)}, u32[]{:S(2)}) collective-permute-start(bf16[2,384,512]{2,1,0:T(8,128)(2,1)} %get-tuple-element.28.refs_1_.refs_2_), channel_id=1, source_target_pairs={{0,8},{8,16},{16,24},{24,0},{1,9},{9,17},{17,25},{25,1},{2,10},{10... | collective-permute-start | bytes 2359304 | tf_op jit(solution)/shard_map/ppermute | solution.py:292
  34.5 2.2 %collective-permute-start.5 = (bf16[2,384,512]{2,1,0:T(8,128)(2,1)}, bf16[2,384,512]{2,1,0:T(8,128)(2,1)S(1)}, u32[]{:S(2)}, u32[]{:S(2)}) collective-permute-start(bf16[2,384,512]{2,1,0:T(8,128)(2,1)} %get-tuple-element.29.refs_2_.refs_3_), channel_id=1, source_target_pairs={{0,8},{8,16},{16,24},{24,0},{1,9},{9,17},{17,25},{25,1},{2,10},{10... | collective-permute-start | bytes 2359304 | tf_op jit(solution)/shard_map/ppermute | solution.py:294
  36.7 4.3 %collective-permute-start.4 = (bf16[2,384,512]{2,1,0:T(8,128)(2,1)}, bf16[2,384,512]{2,1,0:T(8,128)(2,1)S(1)}, u32[]{:S(2)}, u32[]{:S(2)}) collective-permute-start(bf16[2,384,512]{2,1,0:T(8,128)(2,1)} %get-tuple-element.29.refs_2_.refs_3_), channel_id=1, source_target_pairs={{0,24},{8,0},{16,8},{24,16},{1,25},{9,1},{17,9},{25,17},{2,26},{10... | collective-permute-start | bytes 2359304 | tf_op jit(solution)/shard_map/ppermute | solution.py:293
  41.0 3.8 %collective-permute-start.15 = (bf16[768,512]{1,0:T(8,128)(2,1)}, bf16[768,512]{1,0:T(8,128)(2,1)S(1)}, u32[]{:S(2)}, u32[]{:S(2)}) collective-permute-start(bf16[768,512]{1,0:T(8,128)(2,1)} %get-tuple-element.34.near_hbm), channel_id=1, source_target_pairs={{0,4},{4,0},{1,5},{5,1},{2,6},{6,2},{3,7},{7,3},{8,12},{12,8},{9,1... | collective-permute-start | bytes 2359304 | tf_op jit(solution)/shard_map/ppermute | solution.py:285
  44.9 4.8 %collective-permute-done.6.refs_7_.refs_8_ = bf16[2,384,512]{2,1,0:T(8,128)(2,1)S(1)} collective-permute-done((bf16[2,384,512]{2,1,0:T(8,128)(2,1)}, bf16[2,384,512]{2,1,0:T(8,128)(2,1)S(1)}, u32[]{:S(2)}, u32[]{:S(2)}) %collective-permute-start.6) | collective-permute-done | bytes 786464 | tf_op jit(solution)/shard_map/ppermute | solution.py:295
  49.6 4.8 %collective-permute-start.1 = (bf16[2,384,512]{2,1,0:T(8,128)(2,1)}, bf16[2,384,512]{2,1,0:T(8,128)(2,1)S(1)}, u32[]{:S(2)}, u32[]{:S(2)}) collective-permute-start(bf16[2,384,512]{2,1,0:T(8,128)(2,1)} %get-tuple-element.28.refs_1_.refs_2_), channel_id=1, source_target_pairs={{0,4},{4,0},{1,5},{5,1},{2,6},{6,2},{3,7},{7,3},{8,12},{12,8},{9,1... | collective-permute-start | bytes 2359304 | tf_op jit(solution)/shard_map/ppermute | solution.py:285
  54.5 4.3 %collective-permute-start.2 = (bf16[2,384,512]{2,1,0:T(8,128)(2,1)}, bf16[2,384,512]{2,1,0:T(8,128)(2,1)S(1)}, u32[]{:S(2)}, u32[]{:S(2)}) collective-permute-start(bf16[2,384,512]{2,1,0:T(8,128)(2,1)} %get-tuple-element.29.refs_2_.refs_3_), channel_id=1, source_target_pairs={{0,4},{4,0},{1,5},{5,1},{2,6},{6,2},{3,7},{7,3},{8,12},{12,8},{9,1... | collective-permute-start | bytes 2359304 | tf_op jit(solution)/shard_map/ppermute | solution.py:285
  58.8 11.6 %collective-permute-done.5.refs_6_.refs_7_ = bf16[2,384,512]{2,1,0:T(8,128)(2,1)S(1)} collective-permute-done((bf16[2,384,512]{2,1,0:T(8,128)(2,1)}, bf16[2,384,512]{2,1,0:T(8,128)(2,1)S(1)}, u32[]{:S(2)}, u32[]{:S(2)}) %collective-permute-start.5) | collective-permute-done | bytes 786464 | tf_op jit(solution)/shard_map/ppermute | solution.py:294
  70.4 3.7 %collective-permute-start.8 = (bf16[2,384,512]{2,1,0:T(8,128)(2,1)S(1)}, bf16[2,384,512]{2,1,0:T(8,128)(2,1)S(1)}, u32[]{:S(2)}, u32[]{:S(2)}) collective-permute-start(bf16[2,384,512]{2,1,0:T(8,128)(2,1)S(1)} %collective-permute-done.5.refs_6_.refs_7_), channel_id=1, source_target_pairs={{0,4},{4,0},{1,5},{5,1},{2,6},{6,2},{3,7},{7,3},{8,12},{12,8},{9,1... | collective-permute-start | bytes 2359304 | tf_op jit(solution)/shard_map/ppermute | solution.py:285
  76.1 4.6 %collective-permute-start.12 = (bf16[2,384,512]{2,1,0:T(8,128)(2,1)S(1)}, bf16[2,384,512]{2,1,0:T(8,128)(2,1)}, u32[]{:S(2)}, u32[]{:S(2)}) collective-permute-start(bf16[2,384,512]{2,1,0:T(8,128)(2,1)S(1)} %collective-permute-done.4.refs_8_.refs_9_), channel_id=1, source_target_pairs={{0,24},{8,0},{16,8},{24,16},{1,25},{9,1},{17,9},{25,17},{2,26},{10... | collective-permute-start | bytes 2359304 | tf_op jit(solution)/shard_map/ppermute | solution.py:300
  80.7 2.5 %collective-permute-start.7 = (bf16[2,384,512]{2,1,0:T(8,128)(2,1)S(1)}, bf16[2,384,512]{2,1,0:T(8,128)(2,1)}, u32[]{:S(2)}, u32[]{:S(2)}) collective-permute-start(bf16[2,384,512]{2,1,0:T(8,128)(2,1)S(1)} %collective-permute-done.3.refs_5_.refs_6_), channel_id=1, source_target_pairs={{0,4},{4,0},{1,5},{5,1},{2,6},{6,2},{3,7},{7,3},{8,12},{12,8},{9,1... | collective-permute-start | bytes 2359304 | tf_op jit(solution)/shard_map/ppermute | solution.py:285
  85.1 2.4 %collective-permute-start.9 = (bf16[2,384,512]{2,1,0:T(8,128)(2,1)S(1)}, bf16[2,384,512]{2,1,0:T(8,128)(2,1)}, u32[]{:S(2)}, u32[]{:S(2)}) collective-permute-start(bf16[2,384,512]{2,1,0:T(8,128)(2,1)S(1)} %collective-permute-done.6.refs_7_.refs_8_), channel_id=1, source_target_pairs={{0,4},{4,0},{1,5},{5,1},{2,6},{6,2},{3,7},{7,3},{8,12},{12,8},{9,1... | collective-permute-start | bytes 2359304 | tf_op jit(solution)/shard_map/ppermute | solution.py:285
  87.5 8.9 %collective-permute-done.11.refs_13_.refs_14_ = bf16[2,384,512]{2,1,0:T(8,128)(2,1)} collective-permute-done((bf16[2,384,512]{2,1,0:T(8,128)(2,1)S(1)}, bf16[2,384,512]{2,1,0:T(8,128)(2,1)}, u32[]{:S(2)}, u32[]{:S(2)}) %collective-permute-start.11) | collective-permute-done | bytes 786464 | tf_op jit(solution)/shard_map/ppermute | solution.py:299
  96.5 2.7 %collective-permute-start.13 = (bf16[2,384,512]{2,1,0:T(8,128)(2,1)}, bf16[2,384,512]{2,1,0:T(8,128)(2,1)}, u32[]{:S(2)}, u32[]{:S(2)}) collective-permute-start(bf16[2,384,512]{2,1,0:T(8,128)(2,1)} %collective-permute-done.11.refs_13_.refs_14_), channel_id=1, source_target_pairs={{0,4},{4,0},{1,5},{5,1},{2,6},{6,2},{3,7},{7,3},{8,12},{12,8},{9,1... | collective-permute-start | bytes 2359304 | tf_op jit(solution)/shard_map/ppermute | solution.py:285
  101.2 3.5 %shard_map.77 = bf16[4,128,512]{2,1,0:T(8,128)(2,1)} custom-call(bf16[16,17,16,384]{3,2,1,0:T(8,128)(2,1)} %bitcast.17, bf16[768,512]{1,0:T(8,128)(2,1)} %get-tuple-element.34.near_hbm, bf16[768,512]{1,0:T(8,128)(2,1)} %copy-done.10), custom_call_target="tpu_custom_call" | custom-call | tf_op jit(solution)/shard_map/pallas_call | solution.py:359
  104.7 3.9 %all-to-all-start.1 = ((bf16[4,128,512]{2,1,0:T(8,128)(2,1)}), bf16[4,128,512]{2,1,0:T(8,128)(2,1)S(1)}, u32[]{:S(2)}, u32[]{:S(2)}) async-start(bf16[4,128,512]{2,1,0:T(8,128)(2,1)} %shard_map.77), calls=%async_computation.1 | async-start | bytes 1048576 | tf_op jit(solution)/shard_map/all_to_all | solution.py:370
  108.7 6.5 %shard_map.76.refs_0_ = f32[128,1024]{1,0:T(8,128)} custom-call(s32[1]{0:T(128)} %bitcast.10.x_ref, s32[1]{0:T(128)} %bitcast.4.core_ref, bf16[16,17,16,384]{3,2,1,0:T(8,128)(2,1)} %bitcast.18, bf16[2,384,512]{2,1,0:T(8,128)(2,1)} %get-tuple-element.28.refs_1_.refs_2_, bf16[2,384,512]{2,1,0:T(8,128)(2,1)} %get-tuple-element.29.refs_2_.refs_3_, ...), custom_call_target="tpu_custom_call" | custom-call | tf_op jit(solution)/shard_map/pallas_call | solution.py:371
  117.6 8.4 %shard_map.78 = bf16[8,4,2,96,128]{4,3,2,1,0:T(8,128)(2,1)} custom-call(s32[1]{0:T(128)} %bitcast.10.x_ref, s32[1]{0:T(128)} %bitcast.4.core_ref, f32[128,1024]{1,0:T(8,128)} %shard_map.76.refs_0_, bf16[4,128,512]{2,1,0:T(8,128)(2,1)} %copy-done.9, bf16[2,384,512]{2,1,0:T(8,128)(2,1)} %get-tuple-element.28.refs_1_.refs_2_, ...), custom_call_target="tpu_custom_call" | custom-call | tf_op jit(solution)/shard_map/pallas_call | solution.py:382
  125.9 8.5 %all-to-all-start.2 = ((bf16[64,96,128]{2,1,0:T(8,128)(2,1)}), bf16[64,96,128]{2,1,0:T(8,128)(2,1)S(1)}, u32[]{:S(2)}, u32[]{:S(2)}) async-start(bf16[64,96,128]{2,1,0:T(8,128)(2,1)} %bitcast.20), calls=%async_computation.2 | async-start | bytes 3145728 | tf_op jit(solution)/shard_map/all_to_all | solution.py:403
  135.3 22.7 %all-to-all-done.2 = bf16[64,96,128]{2,1,0:T(8,128)(2,1)S(1)} async-done(((bf16[64,96,128]{2,1,0:T(8,128)(2,1)}), bf16[64,96,128]{2,1,0:T(8,128)(2,1)S(1)}, u32[]{:S(2)}, u32[]{:S(2)}) %all-to-all-start.2) | async-done | bytes 1572896 | tf_op jit(solution)/shard_map/all_to_all | solution.py:403
  158.7 37.2 %all_to_all.20 = bf16[8,192,128]{2,1,0:T(8,128)(2,1)S(1)} all-to-all(bf16[8,192,128]{2,1,0:T(8,128)(2,1)S(1)} %shard_map.79), channel_id=1, replica_groups=mesh['zh'=8,'zl'=2,'x'=4,'c'=2,'y'=4] {'zh'}, dimensions={0} | all-to-all | bytes 786432 | tf_op jit(solution)/shard_map/all_to_all | solution.py:412
  (50 shorter events, 19.7 us)
Async XLA Ops:
  8.6 15.1 %all-to-all-start = ((bf16[8,16,384]{2,1,0:T(8,128)(2,1)}), bf16[8,16,384]{2,1,0:T(8,128)(2,1)S(1)}, u32[]{:S(2)}, u32[]{:S(2)}) async-start(bf16[8,16,384]{2,1,0:T(8,128)(2,1)} %get-tuple-element.20), calls=%async_computation | async-start | bytes 196608 | tf_op jit(solution)/shard_map/all_to_all | solution.py:335
  18.7 82.5 %all-gather.2.cloned.1.call-start = ((), (), s32[]{:S(2)}) async-start(), calls=%async_computation.4 | async-start | bytes 3551232 | tf_op jit(solution)/shard_map/all_gather | solution.py:343
  18.7 3.3 %collective-permute-start = (bf16[2,32,384]{2,1,0:T(8,128)(2,1)}, bf16[2,32,384]{2,1,0:T(8,128)(2,1)S(1)}, u32[]{:S(2)}, u32[]{:S(2)}) collective-permute-start(bf16[2,32,384]{2,1,0:T(8,128)(2,1)} %get-tuple-element.22), channel_id=1, source_target_pairs={{0,4},{4,0},{1,5},{5,1},{2,6},{6,2},{3,7},{7,3},{8,12},{12,8},{9,1... | collective-permute-start | bytes 147464 | tf_op jit(solution)/shard_map/ppermute | solution.py:285
  29.2 20.4 %collective-permute-start.6 = (bf16[2,384,512]{2,1,0:T(8,128)(2,1)}, bf16[2,384,512]{2,1,0:T(8,128)(2,1)S(1)}, u32[]{:S(2)}, u32[]{:S(2)}) collective-permute-start(bf16[2,384,512]{2,1,0:T(8,128)(2,1)} %get-tuple-element.28.refs_1_.refs_2_), channel_id=1, source_target_pairs={{0,24},{8,0},{16,8},{24,16},{1,25},{9,1},{17,9},{25,17},{2,26},{10... | collective-permute-start | bytes 2359304 | tf_op jit(solution)/shard_map/ppermute | solution.py:295
  32.1 22.4 %collective-permute-start.3 = (bf16[2,384,512]{2,1,0:T(8,128)(2,1)}, bf16[2,384,512]{2,1,0:T(8,128)(2,1)S(1)}, u32[]{:S(2)}, u32[]{:S(2)}) collective-permute-start(bf16[2,384,512]{2,1,0:T(8,128)(2,1)} %get-tuple-element.28.refs_1_.refs_2_), channel_id=1, source_target_pairs={{0,8},{8,16},{16,24},{24,0},{1,9},{9,17},{17,25},{25,1},{2,10},{10... | collective-permute-start | bytes 2359304 | tf_op jit(solution)/shard_map/ppermute | solution.py:292
  34.5 35.9 %collective-permute-start.5 = (bf16[2,384,512]{2,1,0:T(8,128)(2,1)}, bf16[2,384,512]{2,1,0:T(8,128)(2,1)S(1)}, u32[]{:S(2)}, u32[]{:S(2)}) collective-permute-start(bf16[2,384,512]{2,1,0:T(8,128)(2,1)} %get-tuple-element.29.refs_2_.refs_3_), channel_id=1, source_target_pairs={{0,8},{8,16},{16,24},{24,0},{1,9},{9,17},{17,25},{25,1},{2,10},{10... | collective-permute-start | bytes 2359304 | tf_op jit(solution)/shard_map/ppermute | solution.py:294
  36.7 33.7 %collective-permute-start.4 = (bf16[2,384,512]{2,1,0:T(8,128)(2,1)}, bf16[2,384,512]{2,1,0:T(8,128)(2,1)S(1)}, u32[]{:S(2)}, u32[]{:S(2)}) collective-permute-start(bf16[2,384,512]{2,1,0:T(8,128)(2,1)} %get-tuple-element.29.refs_2_.refs_3_), channel_id=1, source_target_pairs={{0,24},{8,0},{16,8},{24,16},{1,25},{9,1},{17,9},{25,17},{2,26},{10... | collective-permute-start | bytes 2359304 | tf_op jit(solution)/shard_map/ppermute | solution.py:293
  41.0 35.1 %collective-permute-start.15 = (bf16[768,512]{1,0:T(8,128)(2,1)}, bf16[768,512]{1,0:T(8,128)(2,1)S(1)}, u32[]{:S(2)}, u32[]{:S(2)}) collective-permute-start(bf16[768,512]{1,0:T(8,128)(2,1)} %get-tuple-element.34.near_hbm), channel_id=1, source_target_pairs={{0,4},{4,0},{1,5},{5,1},{2,6},{6,2},{3,7},{7,3},{8,12},{12,8},{9,1... | collective-permute-start | bytes 2359304 | tf_op jit(solution)/shard_map/ppermute | solution.py:285
  49.6 55.1 %copy-start.2 = (bf16[2,384,512]{2,1,0:T(8,128)(2,1)}, bf16[2,384,512]{2,1,0:T(8,128)(2,1)S(1)}, u32[]{:S(2)}) copy-start(bf16[2,384,512]{2,1,0:T(8,128)(2,1)S(1)} %collective-permute-done.6.refs_7_.refs_8_) | copy-start | bytes 2359300
  49.6 31.0 %collective-permute-start.1 = (bf16[2,384,512]{2,1,0:T(8,128)(2,1)}, bf16[2,384,512]{2,1,0:T(8,128)(2,1)S(1)}, u32[]{:S(2)}, u32[]{:S(2)}) collective-permute-start(bf16[2,384,512]{2,1,0:T(8,128)(2,1)} %get-tuple-element.28.refs_1_.refs_2_), channel_id=1, source_target_pairs={{0,4},{4,0},{1,5},{5,1},{2,6},{6,2},{3,7},{7,3},{8,12},{12,8},{9,1... | collective-permute-start | bytes 2359304 | tf_op jit(solution)/shard_map/ppermute | solution.py:285
  54.5 50.2 %copy-start.3 = (bf16[2,384,512]{2,1,0:T(8,128)(2,1)}, bf16[2,384,512]{2,1,0:T(8,128)(2,1)S(1)}, u32[]{:S(2)}) copy-start(bf16[2,384,512]{2,1,0:T(8,128)(2,1)S(1)} %collective-permute-done.3.refs_5_.refs_6_) | copy-start | bytes 2359300
  54.5 28.7 %collective-permute-start.2 = (bf16[2,384,512]{2,1,0:T(8,128)(2,1)}, bf16[2,384,512]{2,1,0:T(8,128)(2,1)S(1)}, u32[]{:S(2)}, u32[]{:S(2)}) collective-permute-start(bf16[2,384,512]{2,1,0:T(8,128)(2,1)} %get-tuple-element.29.refs_2_.refs_3_), channel_id=1, source_target_pairs={{0,4},{4,0},{1,5},{5,1},{2,6},{6,2},{3,7},{7,3},{8,12},{12,8},{9,1... | collective-permute-start | bytes 2359304 | tf_op jit(solution)/shard_map/ppermute | solution.py:285
  70.4 34.3 %copy-start.4 = (bf16[2,384,512]{2,1,0:T(8,128)(2,1)}, bf16[2,384,512]{2,1,0:T(8,128)(2,1)S(1)}, u32[]{:S(2)}) copy-start(bf16[2,384,512]{2,1,0:T(8,128)(2,1)S(1)} %collective-permute-done.5.refs_6_.refs_7_) | copy-start | bytes 2359300
  70.4 34.4 %copy-start.5 = (bf16[2,384,512]{2,1,0:T(8,128)(2,1)}, bf16[2,384,512]{2,1,0:T(8,128)(2,1)S(1)}, u32[]{:S(2)}) copy-start(bf16[2,384,512]{2,1,0:T(8,128)(2,1)S(1)} %collective-permute-done.4.refs_8_.refs_9_) | copy-start | bytes 2359300
  70.4 14.7 %collective-permute-start.8 = (bf16[2,384,512]{2,1,0:T(8,128)(2,1)S(1)}, bf16[2,384,512]{2,1,0:T(8,128)(2,1)S(1)}, u32[]{:S(2)}, u32[]{:S(2)}) collective-permute-start(bf16[2,384,512]{2,1,0:T(8,128)(2,1)S(1)} %collective-permute-done.5.refs_6_.refs_7_), channel_id=1, source_target_pairs={{0,4},{4,0},{1,5},{5,1},{2,6},{6,2},{3,7},{7,3},{8,12},{12,8},{9,1... | collective-permute-start | bytes 2359304 | tf_op jit(solution)/shard_map/ppermute | solution.py:285
  74.1 22.4 %collective-permute-start.11 = (bf16[2,384,512]{2,1,0:T(8,128)(2,1)S(1)}, bf16[2,384,512]{2,1,0:T(8,128)(2,1)}, u32[]{:S(2)}, u32[]{:S(2)}) collective-permute-start(bf16[2,384,512]{2,1,0:T(8,128)(2,1)S(1)} %collective-permute-done.3.refs_5_.refs_6_), channel_id=1, source_target_pairs={{0,8},{8,16},{16,24},{24,0},{1,9},{9,17},{17,25},{25,1},{2,10},{10... | collective-permute-start | bytes 2359304 | tf_op jit(solution)/shard_map/ppermute | solution.py:299
  76.1 23.1 %collective-permute-start.12 = (bf16[2,384,512]{2,1,0:T(8,128)(2,1)S(1)}, bf16[2,384,512]{2,1,0:T(8,128)(2,1)}, u32[]{:S(2)}, u32[]{:S(2)}) collective-permute-start(bf16[2,384,512]{2,1,0:T(8,128)(2,1)S(1)} %collective-permute-done.4.refs_8_.refs_9_), channel_id=1, source_target_pairs={{0,24},{8,0},{16,8},{24,16},{1,25},{9,1},{17,9},{25,17},{2,26},{10... | collective-permute-start | bytes 2359304 | tf_op jit(solution)/shard_map/ppermute | solution.py:300
  80.7 28.0 %collective-permute-start.7 = (bf16[2,384,512]{2,1,0:T(8,128)(2,1)S(1)}, bf16[2,384,512]{2,1,0:T(8,128)(2,1)}, u32[]{:S(2)}, u32[]{:S(2)}) collective-permute-start(bf16[2,384,512]{2,1,0:T(8,128)(2,1)S(1)} %collective-permute-done.3.refs_5_.refs_6_), channel_id=1, source_target_pairs={{0,4},{4,0},{1,5},{5,1},{2,6},{6,2},{3,7},{7,3},{8,12},{12,8},{9,1... | collective-permute-start | bytes 2359304 | tf_op jit(solution)/shard_map/ppermute | solution.py:285
  83.2 25.5 %collective-permute-start.10 = (bf16[2,384,512]{2,1,0:T(8,128)(2,1)S(1)}, bf16[2,384,512]{2,1,0:T(8,128)(2,1)}, u32[]{:S(2)}, u32[]{:S(2)}) collective-permute-start(bf16[2,384,512]{2,1,0:T(8,128)(2,1)S(1)} %collective-permute-done.4.refs_8_.refs_9_), channel_id=1, source_target_pairs={{0,4},{4,0},{1,5},{5,1},{2,6},{6,2},{3,7},{7,3},{8,12},{12,8},{9,1... | collective-permute-start | bytes 2359304 | tf_op jit(solution)/shard_map/ppermute | solution.py:285
  85.1 23.6 %collective-permute-start.9 = (bf16[2,384,512]{2,1,0:T(8,128)(2,1)S(1)}, bf16[2,384,512]{2,1,0:T(8,128)(2,1)}, u32[]{:S(2)}, u32[]{:S(2)}) collective-permute-start(bf16[2,384,512]{2,1,0:T(8,128)(2,1)S(1)} %collective-permute-done.6.refs_7_.refs_8_), channel_id=1, source_target_pairs={{0,4},{4,0},{1,5},{5,1},{2,6},{6,2},{3,7},{7,3},{8,12},{12,8},{9,1... | collective-permute-start | bytes 2359304 | tf_op jit(solution)/shard_map/ppermute | solution.py:285
  96.5 12.2 %collective-permute-start.13 = (bf16[2,384,512]{2,1,0:T(8,128)(2,1)}, bf16[2,384,512]{2,1,0:T(8,128)(2,1)}, u32[]{:S(2)}, u32[]{:S(2)}) collective-permute-start(bf16[2,384,512]{2,1,0:T(8,128)(2,1)} %collective-permute-done.11.refs_13_.refs_14_), channel_id=1, source_target_pairs={{0,4},{4,0},{1,5},{5,1},{2,6},{6,2},{3,7},{7,3},{8,12},{12,8},{9,1... | collective-permute-start | bytes 2359304 | tf_op jit(solution)/shard_map/ppermute | solution.py:285
  99.2 9.5 %collective-permute-start.14 = (bf16[2,384,512]{2,1,0:T(8,128)(2,1)}, bf16[2,384,512]{2,1,0:T(8,128)(2,1)}, u32[]{:S(2)}, u32[]{:S(2)}) collective-permute-start(bf16[2,384,512]{2,1,0:T(8,128)(2,1)} %collective-permute-done.12.refs_14_.refs_15_), channel_id=1, source_target_pairs={{0,4},{4,0},{1,5},{5,1},{2,6},{6,2},{3,7},{7,3},{8,12},{12,8},{9,1... | collective-permute-start | bytes 2359304 | tf_op jit(solution)/shard_map/ppermute | solution.py:285
  104.7 12.0 %all-to-all-start.1 = ((bf16[4,128,512]{2,1,0:T(8,128)(2,1)}), bf16[4,128,512]{2,1,0:T(8,128)(2,1)S(1)}, u32[]{:S(2)}, u32[]{:S(2)}) async-start(bf16[4,128,512]{2,1,0:T(8,128)(2,1)} %shard_map.77), calls=%async_computation.1 | async-start | bytes 1048576 | tf_op jit(solution)/shard_map/all_to_all | solution.py:370
  125.9 32.0 %all-to-all-start.2 = ((bf16[64,96,128]{2,1,0:T(8,128)(2,1)}), bf16[64,96,128]{2,1,0:T(8,128)(2,1)S(1)}, u32[]{:S(2)}, u32[]{:S(2)}) async-start(bf16[64,96,128]{2,1,0:T(8,128)(2,1)} %bitcast.20), calls=%async_computation.2 | async-start | bytes 3145728 | tf_op jit(solution)/shard_map/all_to_all | solution.py:403
  (7 other events, 74.2 us)
Sparse Core Ops, SparseCore 0:
  26.1 66.5 all-gather.1

commit v10 on v8

--- a/solution.py
+++ b/solution.py
@@ -82,12 +82,25 @@
     mine = jnp.where(core == 0, sets[0], sets[1]).astype(bf16)
     other = jnp.where(core == 0, sets[1], sets[0]).astype(bf16)
     for h in range(2):
-        keep_ref[h] = mine[:, h * half : (h + 1) * half]
-        send_ref[h] = other[:, h * half : (h + 1) * half]
+        for i in range(2):
+            span = slice(i * both, (i + 1) * both)
+            keep_ref[2 * h + i] = mine[span, h * half : (h + 1) * half]
+            send_ref[2 * h + i] = other[span, h * half : (h + 1) * half]
     padded = jnp.concatenate([table, jnp.zeros((table_rows - window, count), f32)], axis=0)
-    table_ref[...] = jnp.concatenate(
+    table_ref[0] = jnp.concatenate(
         [padded, jnp.zeros((table_rows, half - count), f32)], axis=1
     ).astype(bf16)
+
+
+def pack_kernel(tok_ref, keep_ref, far_ref, table_ref, out_ref, sems):
+    begin, copies = 0, []
+    for i, ref in enumerate((tok_ref, keep_ref, far_ref, table_ref)):
+        size = ref.shape[0]
+        copies.append(pltpu.make_async_copy(ref, out_ref.at[pl.ds(begin, size)], sems.at[i]))
+        copies[-1].start()
+        begin += size
+    for copy in copies:
+        copy.wait()
 
 
 def weights_kernel(gate_ref, up_ref, down_ref, low_ref, high_ref, flip_ref):
@@ -282,12 +295,14 @@
     behind = [(i, (i - 1) % n_x) for i in range(n_x)]
     low_before = lax.ppermute(low, "x", ahead)
     high_after = lax.ppermute(high, "x", behind)
-    far = (swap(low), swap(high))
-    low_later, high_later, far = lax.optimization_barrier((low, high, far))
-    high_before = lax.ppermute(high_later, "x", ahead)
-    low_after = lax.ppermute(low_later, "x", behind)
+    high_before = lax.ppermute(high, "x", ahead)
+    low_after = lax.ppermute(low, "x", behind)
+    low_before, high_after, high_before, low_after = lax.optimization_barrier(
+        (low_before, high_after, high_before, low_after)
+    )
     low_across = lax.ppermute(low_before, "x", ahead)
     high_across = lax.ppermute(high_after, "x", behind)
+    far = (swap(low), swap(high))
     near = [(low_before, high_before), (low_after, high_after), (low_across, high_across)]
     swapped = [(swap(a), swap(b)) for a, b in near]
     blocks = [(low, high), far, near[0], near[1], swapped[0], swapped[1], near[2], swapped[2]]
@@ -315,19 +330,14 @@
         prep_kernel,
         (
             jax.ShapeDtypeStruct((n_s, 2 * part, half), bf16),
-            jax.ShapeDtypeStruct((2, n_s * part // 2, half), bf16),
-            jax.ShapeDtypeStruct((2, n_s * part // 2, half), bf16),
-            jax.ShapeDtypeStruct((table_rows, half), bf16),
+            jax.ShapeDtypeStruct((n_s // 2, 2 * part, half), bf16),
+            jax.ShapeDtypeStruct((n_s // 2, 2 * part, half), bf16),
+            jax.ShapeDtypeStruct((1, table_rows, half), bf16),
         ),
         [smem] * 2 + [vmem] * 4,
     )(expert_id, core, experts.T, route_weight.T, tokens, cotangent)
+    gate, up, down, pieces = lax.optimization_barrier((gate, up, down, pieces))
     pieces = lax.all_to_all(pieces, ("x", "c"), 0, 0, tiled=True)
-    own = jnp.concatenate([v.reshape(-1, half) for v in (pieces, keep, swap(send), table)], axis=0)
-    gate, up, down, own = lax.optimization_barrier((gate, up, down, own))
-    rows = lax.all_gather(own, ("zh", "zl"), axis=0, tiled=True).reshape(
-        n_z, groups, 2 * part, half
-    )
-
     low, high, down_t = kernel_call(
         weights_kernel,
         (
@@ -337,6 +347,18 @@
         ),
         [vmem] * 3,
     )(gate, up, down)
+    pieces, low, high, down_t = lax.optimization_barrier((pieces, low, high, down_t))
+    own = kernel_call(
+        pack_kernel,
+        jax.ShapeDtypeStruct((groups, 2 * part, half), bf16),
+        [anywhere] * 4,
+        [pltpu.SemaphoreType.DMA((4,))],
+        anywhere,
+        small_vmem_bytes,
+    )(pieces, keep, swap(send), table)
+    rows = lax.all_gather(own.reshape(-1, half), ("zh", "zl"), axis=0, tiled=True).reshape(
+        n_z, groups, 2 * part, half
+    )
     weights = [value for block in gather_weights(low, high) for value in block]
     down_far = swap(down_t)
 

time: 206 us -> 202 us (0.981)
  blocking collectives: 39.1 us -> 34.5 us
  starting transfers between devices: 70 us -> 73.2 us
    ppermute x1, waiting for transfers between devices: 12.4 us -> 1.57 us  [gather_weights(): low_before = lax.ppermute(low, 'x', ahead)]
    ppermute x2, waiting for transfers between devices: 8.46 us -> 18.5 us  [the longest x1 12.8 us: gather_weights(): high_before = lax.ppermute(high, 'x', ahead)]
    all_to_all x1, starting transfers between devices: 5.27 us -> 12.4 us  [per_device(): lax.all_to_all(result.reshape(n_s * window * 2, *shape[3:]), ('x', 'c', '...]
    ppermute x1, waiting for transfers between devices: 4.29 us -> 8.94 us  [gather_weights(): low_across = lax.ppermute(low_before, 'x', ahead)]
    all_to_all x1, blocking collectives: 39.1 us -> 34.5 us  [per_device(): dense = lax.all_to_all(dense, 'zh', 0, 0, tiled=True)]
    ppermute x10, starting transfers between devices: 30.1 us -> 27 us  [swap(): return lax.ppermute(value, 'c', [(0, 1), (1, 0)])]
    all_to_all x1, waiting for transfers between devices: 2.83 us -> 0.42 us  [per_device(): back = lax.all_to_all(back, 'x', 0, 0, tiled=True)]
  transfers between devices with their start and end apart: 20 -> 20, of which waited for: 8 -> 6; matrix products, arithmetic and copies ran while one was open for 0% -> 0% of each run, Pallas kernels for 6% -> 7%
where the time goes in v10:
time: 202 us; the launch traced here: 201 us
  starting transfers between devices  73.2 us (36%)
  waiting for transfers between devices  52.2 us (26%)
  blocking collectives  34.5 us (17%)
  Pallas kernels  25.1 us (12%)
  between operations  13.8 us (7%)
    all_to_all x1, blocking collectives, per_device(): dense = lax.all_to_all(dense, 'zh', 0, 0, tiled=True)  34.5 us
    ppermute x10, starting transfers between devices, swap(): return lax.ppermute(value, 'c', [(0, 1), (1, 0)])  27 us
    all_to_all x1, waiting for transfers between devices, per_device(): lax.all_to_all(result.reshape(n_s * window * 2, *shape[3:]), ('x', 'c', '...  22.7 us
    ppermute x1, waiting for transfers between devices, gather_weights(): high_before = lax.ppermute(high, 'x', ahead)  12.8 us
    all_to_all x1, starting transfers between devices, per_device(): lax.all_to_all(result.reshape(n_s * window * 2, *shape[3:]), ('x', 'c', '...  12.4 us
    all_to_all x1, starting transfers between devices, per_device(): pieces = lax.all_to_all(pieces, ('x', 'c'), 0, 0, tiled=True)  10.3 us
    ppermute x1, waiting for transfers between devices, gather_weights(): low_across = lax.ppermute(low_before, 'x', ahead)  8.94 us
    pallas_call x1, Pallas kernels, per_device(): kernel_call(result_kernel, jax.ShapeDtypeStruct(result_shape, bf16), [sme...  8.37 us
  transfers between devices with their start and end apart: 20, of which 6 were waited for; matrix products, arithmetic and copies ran while one was open for 0% of the time, Pallas kernels for 7%

profile of v10, /device:TPU:1, one launch (start us, length us, event | category | flops | bytes accessed | tf_op | source)
XLA Modules:
  0.0 201.1 jit_solution(5615047474099345542)
XLA Ops:
  8.6 10.3 %all-to-all-start = ((bf16[8,16,384]{2,1,0:T(8,128)(2,1)}), bf16[8,16,384]{2,1,0:T(8,128)(2,1)S(1)}, u32[]{:S(2)}, u32[]{:S(2)}) async-start(bf16[8,16,384]{2,1,0:T(8,128)(2,1)} %get-tuple-element.25), calls=%async_computation | async-start | bytes 196608 | tf_op jit(solution)/shard_map/all_to_all | solution.py:340
  18.8 2.1 %collective-permute-start = (bf16[4,16,384]{2,1,0:T(8,128)(2,1)}, bf16[4,16,384]{2,1,0:T(8,128)(2,1)S(1)}, u32[]{:S(2)}, u32[]{:S(2)}) collective-permute-start(bf16[4,16,384]{2,1,0:T(8,128)(2,1)} %get-tuple-element.34), channel_id=1, source_target_pairs={{0,4},{4,0},{1,5},{5,1},{2,6},{6,2},{3,7},{7,3},{8,12},{12,8},{9,1... | collective-permute-start | bytes 147464 | tf_op jit(solution)/shard_map/ppermute | solution.py:289
  20.9 3.2 %shard_map.74 = (bf16[2,384,512]{2,1,0:T(8,128)(2,1)}, bf16[2,384,512]{2,1,0:T(8,128)(2,1)}, bf16[768,512]{1,0:T(8,128)(2,1)}) custom-call(bf16[768,512]{1,0:T(8,128)(2,1)} %bitcast.21, bf16[768,512]{1,0:T(8,128)(2,1)} %bitcast.22, bf16[512,768]{1,0:T(8,128)(2,1)} %bitcast.23), custom_call_target="tpu_custom_call" | custom-call | tf_op jit(solution)/shard_map/pallas_call | solution.py:341
  25.0 4.7 %collective-permute-start.6 = (bf16[2,384,512]{2,1,0:T(8,128)(2,1)}, bf16[2,384,512]{2,1,0:T(8,128)(2,1)S(1)}, u32[]{:S(2)}, u32[]{:S(2)}) collective-permute-start(bf16[2,384,512]{2,1,0:T(8,128)(2,1)} %get-tuple-element.36.refs_1_.refs_2_), channel_id=1, source_target_pairs={{0,24},{8,0},{16,8},{24,16},{1,25},{9,1},{17,9},{25,17},{2,26},{10... | collective-permute-start | bytes 2359304 | tf_op jit(solution)/shard_map/ppermute | solution.py:299
  31.6 2.1 %collective-permute-start.5 = (bf16[2,384,512]{2,1,0:T(8,128)(2,1)}, bf16[2,384,512]{2,1,0:T(8,128)(2,1)S(1)}, u32[]{:S(2)}, u32[]{:S(2)}) collective-permute-start(bf16[2,384,512]{2,1,0:T(8,128)(2,1)} %get-tuple-element.37.refs_2_.refs_3_), channel_id=1, source_target_pairs={{0,8},{8,16},{16,24},{24,0},{1,9},{9,17},{17,25},{25,1},{2,10},{10... | collective-permute-start | bytes 2359304 | tf_op jit(solution)/shard_map/ppermute | solution.py:298
  33.8 4.4 %collective-permute-start.4 = (bf16[2,384,512]{2,1,0:T(8,128)(2,1)}, bf16[2,384,512]{2,1,0:T(8,128)(2,1)S(1)}, u32[]{:S(2)}, u32[]{:S(2)}) collective-permute-start(bf16[2,384,512]{2,1,0:T(8,128)(2,1)} %get-tuple-element.37.refs_2_.refs_3_), channel_id=1, source_target_pairs={{0,24},{8,0},{16,8},{24,16},{1,25},{9,1},{17,9},{25,17},{2,26},{10... | collective-permute-start | bytes 2359304 | tf_op jit(solution)/shard_map/ppermute | solution.py:297
  38.1 2.9 %collective-permute-start.15 = (bf16[768,512]{1,0:T(8,128)(2,1)}, bf16[768,512]{1,0:T(8,128)(2,1)S(1)}, u32[]{:S(2)}, u32[]{:S(2)}) collective-permute-start(bf16[768,512]{1,0:T(8,128)(2,1)} %get-tuple-element.42.near_hbm), channel_id=1, source_target_pairs={{0,4},{4,0},{1,5},{5,1},{2,6},{6,2},{3,7},{7,3},{8,12},{12,8},{9,1... | collective-permute-start | bytes 2359304 | tf_op jit(solution)/shard_map/ppermute | solution.py:289
  41.1 5.7 %collective-permute-done.6.refs_7_.refs_8_ = bf16[2,384,512]{2,1,0:T(8,128)(2,1)S(1)} collective-permute-done((bf16[2,384,512]{2,1,0:T(8,128)(2,1)}, bf16[2,384,512]{2,1,0:T(8,128)(2,1)S(1)}, u32[]{:S(2)}, u32[]{:S(2)}) %collective-permute-start.6) | collective-permute-done | bytes 786464 | tf_op jit(solution)/shard_map/ppermute | solution.py:299
  46.8 3.4 %collective-permute-start.1 = (bf16[2,384,512]{2,1,0:T(8,128)(2,1)}, bf16[2,384,512]{2,1,0:T(8,128)(2,1)S(1)}, u32[]{:S(2)}, u32[]{:S(2)}) collective-permute-start(bf16[2,384,512]{2,1,0:T(8,128)(2,1)} %get-tuple-element.36.refs_1_.refs_2_), channel_id=1, source_target_pairs={{0,4},{4,0},{1,5},{5,1},{2,6},{6,2},{3,7},{7,3},{8,12},{12,8},{9,1... | collective-permute-start | bytes 2359304 | tf_op jit(solution)/shard_map/ppermute | solution.py:289
  51.8 4.0 %collective-permute-start.2 = (bf16[2,384,512]{2,1,0:T(8,128)(2,1)}, bf16[2,384,512]{2,1,0:T(8,128)(2,1)S(1)}, u32[]{:S(2)}, u32[]{:S(2)}) collective-permute-start(bf16[2,384,512]{2,1,0:T(8,128)(2,1)} %get-tuple-element.37.refs_2_.refs_3_), channel_id=1, source_target_pairs={{0,4},{4,0},{1,5},{5,1},{2,6},{6,2},{3,7},{7,3},{8,12},{12,8},{9,1... | collective-permute-start | bytes 2359304 | tf_op jit(solution)/shard_map/ppermute | solution.py:289
  55.8 12.8 %collective-permute-done.5.refs_6_.refs_7_ = bf16[2,384,512]{2,1,0:T(8,128)(2,1)S(1)} collective-permute-done((bf16[2,384,512]{2,1,0:T(8,128)(2,1)}, bf16[2,384,512]{2,1,0:T(8,128)(2,1)S(1)}, u32[]{:S(2)}, u32[]{:S(2)}) %collective-permute-start.5) | collective-permute-done | bytes 786464 | tf_op jit(solution)/shard_map/ppermute | solution.py:298
  68.5 3.2 %collective-permute-start.8 = (bf16[2,384,512]{2,1,0:T(8,128)(2,1)S(1)}, bf16[2,384,512]{2,1,0:T(8,128)(2,1)S(1)}, u32[]{:S(2)}, u32[]{:S(2)}) collective-permute-start(bf16[2,384,512]{2,1,0:T(8,128)(2,1)S(1)} %collective-permute-done.5.refs_6_.refs_7_), channel_id=1, source_target_pairs={{0,4},{4,0},{1,5},{5,1},{2,6},{6,2},{3,7},{7,3},{8,12},{12,8},{9,1... | collective-permute-start | bytes 2359304 | tf_op jit(solution)/shard_map/ppermute | solution.py:289
  73.7 4.6 %collective-permute-start.12 = (bf16[2,384,512]{2,1,0:T(8,128)(2,1)S(1)}, bf16[2,384,512]{2,1,0:T(8,128)(2,1)}, u32[]{:S(2)}, u32[]{:S(2)}) collective-permute-start(bf16[2,384,512]{2,1,0:T(8,128)(2,1)S(1)} %collective-permute-done.4.refs_8_.refs_9_), channel_id=1, source_target_pairs={{0,24},{8,0},{16,8},{24,16},{1,25},{9,1},{17,9},{25,17},{2,26},{10... | collective-permute-start | bytes 2359304 | tf_op jit(solution)/shard_map/ppermute | solution.py:304
  78.3 2.5 %collective-permute-start.7 = (bf16[2,384,512]{2,1,0:T(8,128)(2,1)S(1)}, bf16[2,384,512]{2,1,0:T(8,128)(2,1)}, u32[]{:S(2)}, u32[]{:S(2)}) collective-permute-start(bf16[2,384,512]{2,1,0:T(8,128)(2,1)S(1)} %collective-permute-done.3.refs_5_.refs_6_), channel_id=1, source_target_pairs={{0,4},{4,0},{1,5},{5,1},{2,6},{6,2},{3,7},{7,3},{8,12},{12,8},{9,1... | collective-permute-start | bytes 2359304 | tf_op jit(solution)/shard_map/ppermute | solution.py:289
  82.8 2.4 %collective-permute-start.9 = (bf16[2,384,512]{2,1,0:T(8,128)(2,1)S(1)}, bf16[2,384,512]{2,1,0:T(8,128)(2,1)}, u32[]{:S(2)}, u32[]{:S(2)}) collective-permute-start(bf16[2,384,512]{2,1,0:T(8,128)(2,1)S(1)} %collective-permute-done.6.refs_7_.refs_8_), channel_id=1, source_target_pairs={{0,4},{4,0},{1,5},{5,1},{2,6},{6,2},{3,7},{7,3},{8,12},{12,8},{9,1... | collective-permute-start | bytes 2359304 | tf_op jit(solution)/shard_map/ppermute | solution.py:289
  85.2 8.9 %collective-permute-done.11.refs_13_.refs_14_ = bf16[2,384,512]{2,1,0:T(8,128)(2,1)} collective-permute-done((bf16[2,384,512]{2,1,0:T(8,128)(2,1)S(1)}, bf16[2,384,512]{2,1,0:T(8,128)(2,1)}, u32[]{:S(2)}, u32[]{:S(2)}) %collective-permute-start.11) | collective-permute-done | bytes 786464 | tf_op jit(solution)/shard_map/ppermute | solution.py:303
  94.1 2.7 %collective-permute-start.13 = (bf16[2,384,512]{2,1,0:T(8,128)(2,1)}, bf16[2,384,512]{2,1,0:T(8,128)(2,1)}, u32[]{:S(2)}, u32[]{:S(2)}) collective-permute-start(bf16[2,384,512]{2,1,0:T(8,128)(2,1)} %collective-permute-done.11.refs_13_.refs_14_), channel_id=1, source_target_pairs={{0,4},{4,0},{1,5},{5,1},{2,6},{6,2},{3,7},{7,3},{8,12},{12,8},{9,1... | collective-permute-start | bytes 2359304 | tf_op jit(solution)/shard_map/ppermute | solution.py:289
  98.8 3.5 %shard_map.77 = bf16[4,128,512]{2,1,0:T(8,128)(2,1)} custom-call(bf16[16,17,16,384]{3,2,1,0:T(8,128)(2,1)} %bitcast.17, bf16[768,512]{1,0:T(8,128)(2,1)} %get-tuple-element.42.near_hbm, bf16[768,512]{1,0:T(8,128)(2,1)} %copy-done.10), custom_call_target="tpu_custom_call" | custom-call | tf_op jit(solution)/shard_map/pallas_call | solution.py:365
  102.4 3.9 %all-to-all-start.1 = ((bf16[4,128,512]{2,1,0:T(8,128)(2,1)}), bf16[4,128,512]{2,1,0:T(8,128)(2,1)S(1)}, u32[]{:S(2)}, u32[]{:S(2)}) async-start(bf16[4,128,512]{2,1,0:T(8,128)(2,1)} %shard_map.77), calls=%async_computation.1 | async-start | bytes 1048576 | tf_op jit(solution)/shard_map/all_to_all | solution.py:376
  106.4 6.5 %shard_map.76.refs_0_ = f32[128,1024]{1,0:T(8,128)} custom-call(s32[1]{0:T(128)} %bitcast.10.x_ref, s32[1]{0:T(128)} %bitcast.4.core_ref, bf16[16,17,16,384]{3,2,1,0:T(8,128)(2,1)} %bitcast.18, bf16[2,384,512]{2,1,0:T(8,128)(2,1)} %get-tuple-element.36.refs_1_.refs_2_, bf16[2,384,512]{2,1,0:T(8,128)(2,1)} %get-tuple-element.37.refs_2_.refs_3_, ...), custom_call_target="tpu_custom_call" | custom-call | tf_op jit(solution)/shard_map/pallas_call | solution.py:377
  114.0 8.4 %shard_map.78 = bf16[8,4,2,96,128]{4,3,2,1,0:T(8,128)(2,1)} custom-call(s32[1]{0:T(128)} %bitcast.10.x_ref, s32[1]{0:T(128)} %bitcast.4.core_ref, f32[128,1024]{1,0:T(8,128)} %shard_map.76.refs_0_, bf16[4,128,512]{2,1,0:T(8,128)(2,1)} %copy-done.9, bf16[2,384,512]{2,1,0:T(8,128)(2,1)} %get-tuple-element.36.refs_1_.refs_2_, ...), custom_call_target="tpu_custom_call" | custom-call | tf_op jit(solution)/shard_map/pallas_call | solution.py:388
  122.4 12.4 %all-to-all-start.2 = ((bf16[64,96,128]{2,1,0:T(8,128)(2,1)}), bf16[64,96,128]{2,1,0:T(8,128)(2,1)S(1)}, u32[]{:S(2)}, u32[]{:S(2)}) async-start(bf16[64,96,128]{2,1,0:T(8,128)(2,1)} %bitcast.20), calls=%async_computation.2 | async-start | bytes 3145728 | tf_op jit(solution)/shard_map/all_to_all | solution.py:409
  135.7 22.7 %all-to-all-done.2 = bf16[64,96,128]{2,1,0:T(8,128)(2,1)S(1)} async-done(((bf16[64,96,128]{2,1,0:T(8,128)(2,1)}), bf16[64,96,128]{2,1,0:T(8,128)(2,1)S(1)}, u32[]{:S(2)}, u32[]{:S(2)}) %all-to-all-start.2) | async-done | bytes 1572896 | tf_op jit(solution)/shard_map/all_to_all | solution.py:409
  159.1 34.5 %all_to_all.20 = bf16[8,192,128]{2,1,0:T(8,128)(2,1)S(1)} all-to-all(bf16[8,192,128]{2,1,0:T(8,128)(2,1)S(1)} %shard_map.79), channel_id=1, replica_groups=mesh['zh'=8,'zl'=2,'x'=4,'c'=2,'y'=4] {'zh'}, dimensions={0} | all-to-all | bytes 786432 | tf_op jit(solution)/shard_map/all_to_all | solution.py:418
  (50 shorter events, 15.6 us)
Async XLA Ops:
  8.6 15.6 %all-to-all-start = ((bf16[8,16,384]{2,1,0:T(8,128)(2,1)}), bf16[8,16,384]{2,1,0:T(8,128)(2,1)S(1)}, u32[]{:S(2)}, u32[]{:S(2)}) async-start(bf16[8,16,384]{2,1,0:T(8,128)(2,1)} %get-tuple-element.25), calls=%async_computation | async-start | bytes 196608 | tf_op jit(solution)/shard_map/all_to_all | solution.py:340
  18.8 80.0 %all-gather.2.cloned.1.call-start = ((), (), s32[]{:S(2)}) async-start(), calls=%async_computation.4 | async-start | bytes 3551232 | tf_op jit(solution)/shard_map/all_gather | solution.py:359
  18.8 5.3 %collective-permute-start = (bf16[4,16,384]{2,1,0:T(8,128)(2,1)}, bf16[4,16,384]{2,1,0:T(8,128)(2,1)S(1)}, u32[]{:S(2)}, u32[]{:S(2)}) collective-permute-start(bf16[4,16,384]{2,1,0:T(8,128)(2,1)} %get-tuple-element.34), channel_id=1, source_target_pairs={{0,4},{4,0},{1,5},{5,1},{2,6},{6,2},{3,7},{7,3},{8,12},{12,8},{9,1... | collective-permute-start | bytes 147464 | tf_op jit(solution)/shard_map/ppermute | solution.py:289
  25.0 21.8 %collective-permute-start.6 = (bf16[2,384,512]{2,1,0:T(8,128)(2,1)}, bf16[2,384,512]{2,1,0:T(8,128)(2,1)S(1)}, u32[]{:S(2)}, u32[]{:S(2)}) collective-permute-start(bf16[2,384,512]{2,1,0:T(8,128)(2,1)} %get-tuple-element.36.refs_1_.refs_2_), channel_id=1, source_target_pairs={{0,24},{8,0},{16,8},{24,16},{1,25},{9,1},{17,9},{25,17},{2,26},{10... | collective-permute-start | bytes 2359304 | tf_op jit(solution)/shard_map/ppermute | solution.py:299
  29.7 22.1 %collective-permute-start.3 = (bf16[2,384,512]{2,1,0:T(8,128)(2,1)}, bf16[2,384,512]{2,1,0:T(8,128)(2,1)S(1)}, u32[]{:S(2)}, u32[]{:S(2)}) collective-permute-start(bf16[2,384,512]{2,1,0:T(8,128)(2,1)} %get-tuple-element.36.refs_1_.refs_2_), channel_id=1, source_target_pairs={{0,8},{8,16},{16,24},{24,0},{1,9},{9,17},{17,25},{25,1},{2,10},{10... | collective-permute-start | bytes 2359304 | tf_op jit(solution)/shard_map/ppermute | solution.py:296
  31.6 36.9 %collective-permute-start.5 = (bf16[2,384,512]{2,1,0:T(8,128)(2,1)}, bf16[2,384,512]{2,1,0:T(8,128)(2,1)S(1)}, u32[]{:S(2)}, u32[]{:S(2)}) collective-permute-start(bf16[2,384,512]{2,1,0:T(8,128)(2,1)} %get-tuple-element.37.refs_2_.refs_3_), channel_id=1, source_target_pairs={{0,8},{8,16},{16,24},{24,0},{1,9},{9,17},{17,25},{25,1},{2,10},{10... | collective-permute-start | bytes 2359304 | tf_op jit(solution)/shard_map/ppermute | solution.py:298
  33.8 34.8 %collective-permute-start.4 = (bf16[2,384,512]{2,1,0:T(8,128)(2,1)}, bf16[2,384,512]{2,1,0:T(8,128)(2,1)S(1)}, u32[]{:S(2)}, u32[]{:S(2)}) collective-permute-start(bf16[2,384,512]{2,1,0:T(8,128)(2,1)} %get-tuple-element.37.refs_2_.refs_3_), channel_id=1, source_target_pairs={{0,24},{8,0},{16,8},{24,16},{1,25},{9,1},{17,9},{25,17},{2,26},{10... | collective-permute-start | bytes 2359304 | tf_op jit(solution)/shard_map/ppermute | solution.py:297
  38.1 35.5 %collective-permute-start.15 = (bf16[768,512]{1,0:T(8,128)(2,1)}, bf16[768,512]{1,0:T(8,128)(2,1)S(1)}, u32[]{:S(2)}, u32[]{:S(2)}) collective-permute-start(bf16[768,512]{1,0:T(8,128)(2,1)} %get-tuple-element.42.near_hbm), channel_id=1, source_target_pairs={{0,4},{4,0},{1,5},{5,1},{2,6},{6,2},{3,7},{7,3},{8,12},{12,8},{9,1... | collective-permute-start | bytes 2359304 | tf_op jit(solution)/shard_map/ppermute | solution.py:289
  46.8 55.5 %copy-start.2 = (bf16[2,384,512]{2,1,0:T(8,128)(2,1)}, bf16[2,384,512]{2,1,0:T(8,128)(2,1)S(1)}, u32[]{:S(2)}) copy-start(bf16[2,384,512]{2,1,0:T(8,128)(2,1)S(1)} %collective-permute-done.6.refs_7_.refs_8_) | copy-start | bytes 2359300
  46.8 31.5 %collective-permute-start.1 = (bf16[2,384,512]{2,1,0:T(8,128)(2,1)}, bf16[2,384,512]{2,1,0:T(8,128)(2,1)S(1)}, u32[]{:S(2)}, u32[]{:S(2)}) collective-permute-start(bf16[2,384,512]{2,1,0:T(8,128)(2,1)} %get-tuple-element.36.refs_1_.refs_2_), channel_id=1, source_target_pairs={{0,4},{4,0},{1,5},{5,1},{2,6},{6,2},{3,7},{7,3},{8,12},{12,8},{9,1... | collective-permute-start | bytes 2359304 | tf_op jit(solution)/shard_map/ppermute | solution.py:289
  51.8 50.5 %copy-start.3 = (bf16[2,384,512]{2,1,0:T(8,128)(2,1)}, bf16[2,384,512]{2,1,0:T(8,128)(2,1)S(1)}, u32[]{:S(2)}) copy-start(bf16[2,384,512]{2,1,0:T(8,128)(2,1)S(1)} %collective-permute-done.3.refs_5_.refs_6_) | copy-start | bytes 2359300
  51.8 29.0 %collective-permute-start.2 = (bf16[2,384,512]{2,1,0:T(8,128)(2,1)}, bf16[2,384,512]{2,1,0:T(8,128)(2,1)S(1)}, u32[]{:S(2)}, u32[]{:S(2)}) collective-permute-start(bf16[2,384,512]{2,1,0:T(8,128)(2,1)} %get-tuple-element.37.refs_2_.refs_3_), channel_id=1, source_target_pairs={{0,4},{4,0},{1,5},{5,1},{2,6},{6,2},{3,7},{7,3},{8,12},{12,8},{9,1... | collective-permute-start | bytes 2359304 | tf_op jit(solution)/shard_map/ppermute | solution.py:289
  68.5 33.8 %copy-start.4 = (bf16[2,384,512]{2,1,0:T(8,128)(2,1)}, bf16[2,384,512]{2,1,0:T(8,128)(2,1)S(1)}, u32[]{:S(2)}) copy-start(bf16[2,384,512]{2,1,0:T(8,128)(2,1)S(1)} %collective-permute-done.5.refs_6_.refs_7_) | copy-start | bytes 2359300
  68.5 33.8 %copy-start.5 = (bf16[2,384,512]{2,1,0:T(8,128)(2,1)}, bf16[2,384,512]{2,1,0:T(8,128)(2,1)S(1)}, u32[]{:S(2)}) copy-start(bf16[2,384,512]{2,1,0:T(8,128)(2,1)S(1)} %collective-permute-done.4.refs_8_.refs_9_) | copy-start | bytes 2359300
  68.5 14.2 %collective-permute-start.8 = (bf16[2,384,512]{2,1,0:T(8,128)(2,1)S(1)}, bf16[2,384,512]{2,1,0:T(8,128)(2,1)S(1)}, u32[]{:S(2)}, u32[]{:S(2)}) collective-permute-start(bf16[2,384,512]{2,1,0:T(8,128)(2,1)S(1)} %collective-permute-done.5.refs_6_.refs_7_), channel_id=1, source_target_pairs={{0,4},{4,0},{1,5},{5,1},{2,6},{6,2},{3,7},{7,3},{8,12},{12,8},{9,1... | collective-permute-start | bytes 2359304 | tf_op jit(solution)/shard_map/ppermute | solution.py:289
  71.7 22.4 %collective-permute-start.11 = (bf16[2,384,512]{2,1,0:T(8,128)(2,1)S(1)}, bf16[2,384,512]{2,1,0:T(8,128)(2,1)}, u32[]{:S(2)}, u32[]{:S(2)}) collective-permute-start(bf16[2,384,512]{2,1,0:T(8,128)(2,1)S(1)} %collective-permute-done.3.refs_5_.refs_6_), channel_id=1, source_target_pairs={{0,8},{8,16},{16,24},{24,0},{1,9},{9,17},{17,25},{25,1},{2,10},{10... | collective-permute-start | bytes 2359304 | tf_op jit(solution)/shard_map/ppermute | solution.py:303
  73.7 23.1 %collective-permute-start.12 = (bf16[2,384,512]{2,1,0:T(8,128)(2,1)S(1)}, bf16[2,384,512]{2,1,0:T(8,128)(2,1)}, u32[]{:S(2)}, u32[]{:S(2)}) collective-permute-start(bf16[2,384,512]{2,1,0:T(8,128)(2,1)S(1)} %collective-permute-done.4.refs_8_.refs_9_), channel_id=1, source_target_pairs={{0,24},{8,0},{16,8},{24,16},{1,25},{9,1},{17,9},{25,17},{2,26},{10... | collective-permute-start | bytes 2359304 | tf_op jit(solution)/shard_map/ppermute | solution.py:304
  78.3 28.0 %collective-permute-start.7 = (bf16[2,384,512]{2,1,0:T(8,128)(2,1)S(1)}, bf16[2,384,512]{2,1,0:T(8,128)(2,1)}, u32[]{:S(2)}, u32[]{:S(2)}) collective-permute-start(bf16[2,384,512]{2,1,0:T(8,128)(2,1)S(1)} %collective-permute-done.3.refs_5_.refs_6_), channel_id=1, source_target_pairs={{0,4},{4,0},{1,5},{5,1},{2,6},{6,2},{3,7},{7,3},{8,12},{12,8},{9,1... | collective-permute-start | bytes 2359304 | tf_op jit(solution)/shard_map/ppermute | solution.py:289
  80.8 25.5 %collective-permute-start.10 = (bf16[2,384,512]{2,1,0:T(8,128)(2,1)S(1)}, bf16[2,384,512]{2,1,0:T(8,128)(2,1)}, u32[]{:S(2)}, u32[]{:S(2)}) collective-permute-start(bf16[2,384,512]{2,1,0:T(8,128)(2,1)S(1)} %collective-permute-done.4.refs_8_.refs_9_), channel_id=1, source_target_pairs={{0,4},{4,0},{1,5},{5,1},{2,6},{6,2},{3,7},{7,3},{8,12},{12,8},{9,1... | collective-permute-start | bytes 2359304 | tf_op jit(solution)/shard_map/ppermute | solution.py:289
  82.8 23.6 %collective-permute-start.9 = (bf16[2,384,512]{2,1,0:T(8,128)(2,1)S(1)}, bf16[2,384,512]{2,1,0:T(8,128)(2,1)}, u32[]{:S(2)}, u32[]{:S(2)}) collective-permute-start(bf16[2,384,512]{2,1,0:T(8,128)(2,1)S(1)} %collective-permute-done.6.refs_7_.refs_8_), channel_id=1, source_target_pairs={{0,4},{4,0},{1,5},{5,1},{2,6},{6,2},{3,7},{7,3},{8,12},{12,8},{9,1... | collective-permute-start | bytes 2359304 | tf_op jit(solution)/shard_map/ppermute | solution.py:289
  94.1 12.2 %collective-permute-start.13 = (bf16[2,384,512]{2,1,0:T(8,128)(2,1)}, bf16[2,384,512]{2,1,0:T(8,128)(2,1)}, u32[]{:S(2)}, u32[]{:S(2)}) collective-permute-start(bf16[2,384,512]{2,1,0:T(8,128)(2,1)} %collective-permute-done.11.refs_13_.refs_14_), channel_id=1, source_target_pairs={{0,4},{4,0},{1,5},{5,1},{2,6},{6,2},{3,7},{7,3},{8,12},{12,8},{9,1... | collective-permute-start | bytes 2359304 | tf_op jit(solution)/shard_map/ppermute | solution.py:289
  96.9 9.5 %collective-permute-start.14 = (bf16[2,384,512]{2,1,0:T(8,128)(2,1)}, bf16[2,384,512]{2,1,0:T(8,128)(2,1)}, u32[]{:S(2)}, u32[]{:S(2)}) collective-permute-start(bf16[2,384,512]{2,1,0:T(8,128)(2,1)} %collective-permute-done.12.refs_14_.refs_15_), channel_id=1, source_target_pairs={{0,4},{4,0},{1,5},{5,1},{2,6},{6,2},{3,7},{7,3},{8,12},{12,8},{9,1... | collective-permute-start | bytes 2359304 | tf_op jit(solution)/shard_map/ppermute | solution.py:289
  102.4 10.9 %all-to-all-start.1 = ((bf16[4,128,512]{2,1,0:T(8,128)(2,1)}), bf16[4,128,512]{2,1,0:T(8,128)(2,1)S(1)}, u32[]{:S(2)}, u32[]{:S(2)}) async-start(bf16[4,128,512]{2,1,0:T(8,128)(2,1)} %shard_map.77), calls=%async_computation.1 | async-start | bytes 1048576 | tf_op jit(solution)/shard_map/all_to_all | solution.py:376
  122.4 35.9 %all-to-all-start.2 = ((bf16[64,96,128]{2,1,0:T(8,128)(2,1)}), bf16[64,96,128]{2,1,0:T(8,128)(2,1)S(1)}, u32[]{:S(2)}, u32[]{:S(2)}) async-start(bf16[64,96,128]{2,1,0:T(8,128)(2,1)} %bitcast.20), calls=%async_computation.2 | async-start | bytes 3145728 | tf_op jit(solution)/shard_map/all_to_all | solution.py:409
  (7 other events, 103.9 us)
Sparse Core Ops, SparseCore 0:
  25.1 68.1 all-gather.1

commit v11 on v10

--- a/solution.py
+++ b/solution.py
@@ -14,6 +14,7 @@
 contract_last = (((1,), (1,)), ((), ()))
 contract_first = (((0,), (0,)), ((), ()))
 vmem_bytes = 56 * 1024 * 1024
+late_vmem_bytes = 52 * 1024 * 1024
 small_vmem_bytes = 16 * 1024 * 1024
 blocks_at = ((0, 0), (0, 1), (-1, 0), (1, 0), (-1, 1), (1, 1), (2, 0), (2, 1))
 
@@ -188,18 +189,12 @@
 
 def result_kernel(x_ref, core_ref, *refs):
     n_w = 2 * len(blocks_at)
-    sums_hbm, back_hbm, weights_hbm = refs[0], refs[1], refs[2 : 2 + n_w]
-    out_hbm, sums_ref, back_ref, weights_ref, out_ref, sems, out_sems = refs[2 + n_w :]
+    sums_ref, back_ref, weights_hbm = refs[0], refs[1], refs[2 : 2 + n_w]
+    out_hbm, weights_ref, out_ref, sems, out_sems = refs[2 + n_w :]
     n_x, slots, hidden = back_ref.shape
     half = weights_ref.shape[3]
     n_z = slots // 8
-    sums_copy = pltpu.make_async_copy(sums_hbm, sums_ref, sems.at[n_w])
-    back_copy = pltpu.make_async_copy(back_hbm, back_ref, sems.at[n_w + 1])
-    sums_copy.start()
-    back_copy.start()
     copies = start_weights(weights_hbm, weights_ref, sems)
-    sums_copy.wait()
-    back_copy.wait()
 
     back = sum(back_ref[i].astype(f32) for i in range(n_x))
     gate_sum, up_sum, back_sum = (
@@ -224,14 +219,18 @@
         s = source(x_ref, core_ref, n_x, dx, dc)
         copies[2 * b].wait()
         copies[2 * b + 1].wait()
+        wide = [
+            lax.dot_general(
+                grad_gate, weights_ref[b, side, 0], contract_last, preferred_element_type=f32
+            )
+            + lax.dot_general(
+                grad_up, weights_ref[b, side, 1], contract_last, preferred_element_type=f32
+            )
+            for side in range(2)
+        ]
         for y in range(window):
             side, begin = y * quarter // half, y * quarter % half
-            span = slice(begin, begin + quarter)
-            rows = lax.dot_general(
-                grad_gate, weights_ref[b, side, 0, span], contract_last, preferred_element_type=f32
-            ) + lax.dot_general(
-                grad_up, weights_ref[b, side, 1, span], contract_last, preferred_element_type=f32
-            )
+            rows = wide[side][:, begin : begin + quarter]
             for pair in range(2):
                 mine = rows[pair * slots // 2 : (pair + 1) * slots // 2]
                 out_ref[s, y, pair, : slots // 2, :] = mine[:, :128].astype(bf16)
@@ -383,21 +382,21 @@
             pltpu.VMEM((len(blocks_at), 2, 2, half, hidden), bf16),
             pltpu.SemaphoreType.DMA((len(weights) + 1,)),
         ],
+        vmem_limit=late_vmem_bytes,
     )(x, core, rows, *weights)
     result_shape = (n_s, window, 2, quarter // 2, n_z * part)
     result = kernel_call(
         result_kernel,
         jax.ShapeDtypeStruct(result_shape, bf16),
-        [smem] * 2 + [anywhere] * (2 + len(weights)),
+        [smem] * 2 + [vmem] * 2 + [anywhere] * len(weights),
         [
-            pltpu.VMEM((n_z * part, 2 * hidden), f32),
-            pltpu.VMEM((n_x, n_z * part, hidden), bf16),
             pltpu.VMEM((len(blocks_at), 2, 2, half, hidden), bf16),
             pltpu.VMEM(result_shape, bf16),
-            pltpu.SemaphoreType.DMA((len(weights) + 2,)),
+            pltpu.SemaphoreType.DMA((len(weights),)),
             pltpu.SemaphoreType.DMA((len(blocks_at),)),
         ],
         anywhere,
+        late_vmem_bytes,
     )(x, core, sums, back, *weights)
     tables = lax.dynamic_index_in_dim(
         rows.reshape(n_high, 2, groups, 2 * part, half)[:, :, groups - 1, :, :count],

time: 202 us -> 201 us (level)
  transfers between devices with their start and end apart: 20 -> 20, of which waited for: 6 -> 6; matrix products, arithmetic and copies ran while one was open for 0% -> 0% of each run, Pallas kernels for 7% -> 6%
where the time goes in v11:
time: 201 us; the launch traced here: 200 us
  starting transfers between devices  72.3 us (36%)
  waiting for transfers between devices  53.3 us (27%)
  blocking collectives  35.7 us (18%)
  Pallas kernels  23.2 us (12%)
  between operations  13.8 us (7%)
    all_to_all x1, blocking collectives, per_device(): dense = lax.all_to_all(dense, 'zh', 0, 0, tiled=True)  35.7 us
    ppermute x10, starting transfers between devices, swap(): return lax.ppermute(value, 'c', [(0, 1), (1, 0)])  27 us
    all_to_all x1, waiting for transfers between devices, per_device(): lax.all_to_all(result.reshape(n_s * window * 2, *shape[3:]), ('x', 'c', '...  22.7 us
    ppermute x1, waiting for transfers between devices, gather_weights(): high_before = lax.ppermute(high, 'x', ahead)  12.8 us
    all_to_all x1, starting transfers between devices, per_device(): lax.all_to_all(result.reshape(n_s * window * 2, *shape[3:]), ('x', 'c', '...  11.2 us
    all_to_all x1, starting transfers between devices, per_device(): pieces = lax.all_to_all(pieces, ('x', 'c'), 0, 0, tiled=True)  10.3 us
    ppermute x1, waiting for transfers between devices, gather_weights(): low_across = lax.ppermute(low_before, 'x', ahead)  8.94 us
    pallas_call x1, Pallas kernels, per_device(): kernel_call(result_kernel, jax.ShapeDtypeStruct(result_shape, bf16), [sme...  7.47 us
  transfers between devices with their start and end apart: 20, of which 6 were waited for; matrix products, arithmetic and copies ran while one was open for 0% of the time, Pallas kernels for 6%

profile of v11, /device:TPU:1, one launch (start us, length us, event | category | flops | bytes accessed | tf_op | source)
XLA Modules:
  0.0 199.7 jit_solution(463547409123877258)
XLA Ops:
  8.6 10.3 %all-to-all-start = ((bf16[8,16,384]{2,1,0:T(8,128)(2,1)}), bf16[8,16,384]{2,1,0:T(8,128)(2,1)S(1)}, u32[]{:S(2)}, u32[]{:S(2)}) async-start(bf16[8,16,384]{2,1,0:T(8,128)(2,1)} %get-tuple-element.25), calls=%async_computation | async-start | bytes 196608 | tf_op jit(solution)/shard_map/all_to_all | solution.py:339
  18.8 2.1 %collective-permute-start = (bf16[4,16,384]{2,1,0:T(8,128)(2,1)}, bf16[4,16,384]{2,1,0:T(8,128)(2,1)S(1)}, u32[]{:S(2)}, u32[]{:S(2)}) collective-permute-start(bf16[4,16,384]{2,1,0:T(8,128)(2,1)} %get-tuple-element.34), channel_id=1, source_target_pairs={{0,4},{4,0},{1,5},{5,1},{2,6},{6,2},{3,7},{7,3},{8,12},{12,8},{9,1... | collective-permute-start | bytes 147464 | tf_op jit(solution)/shard_map/ppermute | solution.py:288
  20.9 3.3 %shard_map.74 = (bf16[2,384,512]{2,1,0:T(8,128)(2,1)}, bf16[2,384,512]{2,1,0:T(8,128)(2,1)}, bf16[768,512]{1,0:T(8,128)(2,1)}) custom-call(bf16[768,512]{1,0:T(8,128)(2,1)} %bitcast.21, bf16[768,512]{1,0:T(8,128)(2,1)} %bitcast.22, bf16[512,768]{1,0:T(8,128)(2,1)} %bitcast.23), custom_call_target="tpu_custom_call" | custom-call | tf_op jit(solution)/shard_map/pallas_call | solution.py:340
  25.0 4.7 %collective-permute-start.6 = (bf16[2,384,512]{2,1,0:T(8,128)(2,1)}, bf16[2,384,512]{2,1,0:T(8,128)(2,1)S(1)}, u32[]{:S(2)}, u32[]{:S(2)}) collective-permute-start(bf16[2,384,512]{2,1,0:T(8,128)(2,1)} %get-tuple-element.36.refs_1_.refs_2_), channel_id=1, source_target_pairs={{0,24},{8,0},{16,8},{24,16},{1,25},{9,1},{17,9},{25,17},{2,26},{10... | collective-permute-start | bytes 2359304 | tf_op jit(solution)/shard_map/ppermute | solution.py:298
  31.6 2.1 %collective-permute-start.5 = (bf16[2,384,512]{2,1,0:T(8,128)(2,1)}, bf16[2,384,512]{2,1,0:T(8,128)(2,1)S(1)}, u32[]{:S(2)}, u32[]{:S(2)}) collective-permute-start(bf16[2,384,512]{2,1,0:T(8,128)(2,1)} %get-tuple-element.37.refs_2_.refs_3_), channel_id=1, source_target_pairs={{0,8},{8,16},{16,24},{24,0},{1,9},{9,17},{17,25},{25,1},{2,10},{10... | collective-permute-start | bytes 2359304 | tf_op jit(solution)/shard_map/ppermute | solution.py:297
  33.8 4.4 %collective-permute-start.4 = (bf16[2,384,512]{2,1,0:T(8,128)(2,1)}, bf16[2,384,512]{2,1,0:T(8,128)(2,1)}, u32[]{:S(2)}, u32[]{:S(2)}) collective-permute-start(bf16[2,384,512]{2,1,0:T(8,128)(2,1)} %get-tuple-element.37.refs_2_.refs_3_), channel_id=1, source_target_pairs={{0,24},{8,0},{16,8},{24,16},{1,25},{9,1},{17,9},{25,17},{2,26},{10... | collective-permute-start | bytes 2359304 | tf_op jit(solution)/shard_map/ppermute | solution.py:296
  38.1 2.9 %collective-permute-start.15 = (bf16[768,512]{1,0:T(8,128)(2,1)}, bf16[768,512]{1,0:T(8,128)(2,1)S(1)}, u32[]{:S(2)}, u32[]{:S(2)}) collective-permute-start(bf16[768,512]{1,0:T(8,128)(2,1)} %get-tuple-element.42.near_hbm), channel_id=1, source_target_pairs={{0,4},{4,0},{1,5},{5,1},{2,6},{6,2},{3,7},{7,3},{8,12},{12,8},{9,1... | collective-permute-start | bytes 2359304 | tf_op jit(solution)/shard_map/ppermute | solution.py:288
  41.1 5.7 %collective-permute-done.6.refs_7_.refs_8_ = bf16[2,384,512]{2,1,0:T(8,128)(2,1)S(1)} collective-permute-done((bf16[2,384,512]{2,1,0:T(8,128)(2,1)}, bf16[2,384,512]{2,1,0:T(8,128)(2,1)S(1)}, u32[]{:S(2)}, u32[]{:S(2)}) %collective-permute-start.6) | collective-permute-done | bytes 786464 | tf_op jit(solution)/shard_map/ppermute | solution.py:298
  46.8 3.4 %collective-permute-start.1 = (bf16[2,384,512]{2,1,0:T(8,128)(2,1)}, bf16[2,384,512]{2,1,0:T(8,128)(2,1)S(1)}, u32[]{:S(2)}, u32[]{:S(2)}) collective-permute-start(bf16[2,384,512]{2,1,0:T(8,128)(2,1)} %get-tuple-element.36.refs_1_.refs_2_), channel_id=1, source_target_pairs={{0,4},{4,0},{1,5},{5,1},{2,6},{6,2},{3,7},{7,3},{8,12},{12,8},{9,1... | collective-permute-start | bytes 2359304 | tf_op jit(solution)/shard_map/ppermute | solution.py:288
  51.8 4.0 %collective-permute-start.2 = (bf16[2,384,512]{2,1,0:T(8,128)(2,1)}, bf16[2,384,512]{2,1,0:T(8,128)(2,1)S(1)}, u32[]{:S(2)}, u32[]{:S(2)}) collective-permute-start(bf16[2,384,512]{2,1,0:T(8,128)(2,1)} %get-tuple-element.37.refs_2_.refs_3_), channel_id=1, source_target_pairs={{0,4},{4,0},{1,5},{5,1},{2,6},{6,2},{3,7},{7,3},{8,12},{12,8},{9,1... | collective-permute-start | bytes 2359304 | tf_op jit(solution)/shard_map/ppermute | solution.py:288
  55.8 12.8 %collective-permute-done.5.refs_6_.refs_7_ = bf16[2,384,512]{2,1,0:T(8,128)(2,1)S(1)} collective-permute-done((bf16[2,384,512]{2,1,0:T(8,128)(2,1)}, bf16[2,384,512]{2,1,0:T(8,128)(2,1)S(1)}, u32[]{:S(2)}, u32[]{:S(2)}) %collective-permute-start.5) | collective-permute-done | bytes 786464 | tf_op jit(solution)/shard_map/ppermute | solution.py:297
  68.6 3.2 %collective-permute-start.8 = (bf16[2,384,512]{2,1,0:T(8,128)(2,1)S(1)}, bf16[2,384,512]{2,1,0:T(8,128)(2,1)S(1)}, u32[]{:S(2)}, u32[]{:S(2)}) collective-permute-start(bf16[2,384,512]{2,1,0:T(8,128)(2,1)S(1)} %collective-permute-done.5.refs_6_.refs_7_), channel_id=1, source_target_pairs={{0,4},{4,0},{1,5},{5,1},{2,6},{6,2},{3,7},{7,3},{8,12},{12,8},{9,1... | collective-permute-start | bytes 2359304 | tf_op jit(solution)/shard_map/ppermute | solution.py:288
  73.7 4.6 %collective-permute-start.12 = (bf16[2,384,512]{2,1,0:T(8,128)(2,1)}, bf16[2,384,512]{2,1,0:T(8,128)(2,1)}, u32[]{:S(2)}, u32[]{:S(2)}) collective-permute-start(bf16[2,384,512]{2,1,0:T(8,128)(2,1)} %collective-permute-done.4.refs_8_.refs_9_), channel_id=1, source_target_pairs={{0,24},{8,0},{16,8},{24,16},{1,25},{9,1},{17,9},{25,17},{2,26},{10... | collective-permute-start | bytes 2359304 | tf_op jit(solution)/shard_map/ppermute | solution.py:303
  78.3 2.5 %collective-permute-start.7 = (bf16[2,384,512]{2,1,0:T(8,128)(2,1)S(1)}, bf16[2,384,512]{2,1,0:T(8,128)(2,1)}, u32[]{:S(2)}, u32[]{:S(2)}) collective-permute-start(bf16[2,384,512]{2,1,0:T(8,128)(2,1)S(1)} %collective-permute-done.3.refs_5_.refs_6_), channel_id=1, source_target_pairs={{0,4},{4,0},{1,5},{5,1},{2,6},{6,2},{3,7},{7,3},{8,12},{12,8},{9,1... | collective-permute-start | bytes 2359304 | tf_op jit(solution)/shard_map/ppermute | solution.py:288
  82.8 2.4 %collective-permute-start.9 = (bf16[2,384,512]{2,1,0:T(8,128)(2,1)S(1)}, bf16[2,384,512]{2,1,0:T(8,128)(2,1)}, u32[]{:S(2)}, u32[]{:S(2)}) collective-permute-start(bf16[2,384,512]{2,1,0:T(8,128)(2,1)S(1)} %collective-permute-done.6.refs_7_.refs_8_), channel_id=1, source_target_pairs={{0,4},{4,0},{1,5},{5,1},{2,6},{6,2},{3,7},{7,3},{8,12},{12,8},{9,1... | collective-permute-start | bytes 2359304 | tf_op jit(solution)/shard_map/ppermute | solution.py:288
  85.2 8.9 %collective-permute-done.11.refs_13_.refs_14_ = bf16[2,384,512]{2,1,0:T(8,128)(2,1)} collective-permute-done((bf16[2,384,512]{2,1,0:T(8,128)(2,1)S(1)}, bf16[2,384,512]{2,1,0:T(8,128)(2,1)}, u32[]{:S(2)}, u32[]{:S(2)}) %collective-permute-start.11) | collective-permute-done | bytes 786464 | tf_op jit(solution)/shard_map/ppermute | solution.py:302
  94.1 2.7 %collective-permute-start.13 = (bf16[2,384,512]{2,1,0:T(8,128)(2,1)}, bf16[2,384,512]{2,1,0:T(8,128)(2,1)}, u32[]{:S(2)}, u32[]{:S(2)}) collective-permute-start(bf16[2,384,512]{2,1,0:T(8,128)(2,1)} %collective-permute-done.11.refs_13_.refs_14_), channel_id=1, source_target_pairs={{0,4},{4,0},{1,5},{5,1},{2,6},{6,2},{3,7},{7,3},{8,12},{12,8},{9,1... | collective-permute-start | bytes 2359304 | tf_op jit(solution)/shard_map/ppermute | solution.py:288
  98.8 3.5 %shard_map.77 = bf16[4,128,512]{2,1,0:T(8,128)(2,1)} custom-call(bf16[16,17,16,384]{3,2,1,0:T(8,128)(2,1)} %bitcast.17, bf16[768,512]{1,0:T(8,128)(2,1)} %get-tuple-element.42.near_hbm, bf16[768,512]{1,0:T(8,128)(2,1)} %copy-done.9), custom_call_target="tpu_custom_call" | custom-call | tf_op jit(solution)/shard_map/pallas_call | solution.py:364
  102.4 4.3 %all-to-all-start.1 = ((bf16[4,128,512]{2,1,0:T(8,128)(2,1)}), bf16[4,128,512]{2,1,0:T(8,128)(2,1)S(1)}, u32[]{:S(2)}, u32[]{:S(2)}) async-start(bf16[4,128,512]{2,1,0:T(8,128)(2,1)} %shard_map.77), calls=%async_computation.1 | async-start | bytes 1048576 | tf_op jit(solution)/shard_map/all_to_all | solution.py:375
  106.7 5.4 %shard_map.76.refs_0_ = f32[128,1024]{1,0:T(8,128)S(1)} custom-call(s32[1]{0:T(128)} %bitcast.10.x_ref, s32[1]{0:T(128)} %bitcast.4.core_ref, bf16[16,17,16,384]{3,2,1,0:T(8,128)(2,1)} %bitcast.18, bf16[2,384,512]{2,1,0:T(8,128)(2,1)S(1)} %copy-done, bf16[2,384,512]{2,1,0:T(8,128)(2,1)} %get-tuple-element.37.refs_2_.refs_3_, bf16[2,384,512]{2,1,0:T(8,128)(2,1)} %copy-done.6, ...), custom_call_target="tpu_custom_call" | custom-call | tf_op jit(solution)/shard_map/pallas_call | solution.py:376
  113.6 7.5 %shard_map.78 = bf16[8,4,2,96,128]{4,3,2,1,0:T(8,128)(2,1)} custom-call(s32[1]{0:T(128)} %bitcast.10.x_ref, s32[1]{0:T(128)} %bitcast.4.core_ref, f32[128,1024]{1,0:T(8,128)S(1)} %shard_map.76.refs_0_, bf16[4,128,512]{2,1,0:T(8,128)(2,1)S(1)} %all-to-all-done.1.refs_1_, bf16[2,384,512]{2,1,0:T(8,128)(2,1)S(1)} %copy-done, ...), custom_call_target="tpu_custom_call" | custom-call | tf_op jit(solution)/shard_map/pallas_call | solution.py:388
  121.1 11.2 %all-to-all-start.2 = ((bf16[64,96,128]{2,1,0:T(8,128)(2,1)}), bf16[64,96,128]{2,1,0:T(8,128)(2,1)S(1)}, u32[]{:S(2)}, u32[]{:S(2)}) async-start(bf16[64,96,128]{2,1,0:T(8,128)(2,1)} %bitcast.20), calls=%async_computation.2 | async-start | bytes 3145728 | tf_op jit(solution)/shard_map/all_to_all | solution.py:408
  133.1 22.7 %all-to-all-done.2 = bf16[64,96,128]{2,1,0:T(8,128)(2,1)S(1)} async-done(((bf16[64,96,128]{2,1,0:T(8,128)(2,1)}), bf16[64,96,128]{2,1,0:T(8,128)(2,1)S(1)}, u32[]{:S(2)}, u32[]{:S(2)}) %all-to-all-start.2) | async-done | bytes 1572896 | tf_op jit(solution)/shard_map/all_to_all | solution.py:408
  156.6 35.7 %all_to_all.20 = bf16[8,192,128]{2,1,0:T(8,128)(2,1)S(1)} all-to-all(bf16[8,192,128]{2,1,0:T(8,128)(2,1)S(1)} %shard_map.79), channel_id=1, replica_groups=mesh['zh'=8,'zl'=2,'x'=4,'c'=2,'y'=4] {'zh'}, dimensions={0} | all-to-all | bytes 786432 | tf_op jit(solution)/shard_map/all_to_all | solution.py:417
  (48 shorter events, 15.9 us)
Async XLA Ops:
  8.6 15.6 %all-to-all-start = ((bf16[8,16,384]{2,1,0:T(8,128)(2,1)}), bf16[8,16,384]{2,1,0:T(8,128)(2,1)S(1)}, u32[]{:S(2)}, u32[]{:S(2)}) async-start(bf16[8,16,384]{2,1,0:T(8,128)(2,1)} %get-tuple-element.25), calls=%async_computation | async-start | bytes 196608 | tf_op jit(solution)/shard_map/all_to_all | solution.py:339
  18.8 80.0 %all-gather.2.cloned.1.call-start = ((), (), s32[]{:S(2)}) async-start(), calls=%async_computation.4 | async-start | bytes 3551232 | tf_op jit(solution)/shard_map/all_gather | solution.py:358
  18.8 5.3 %collective-permute-start = (bf16[4,16,384]{2,1,0:T(8,128)(2,1)}, bf16[4,16,384]{2,1,0:T(8,128)(2,1)S(1)}, u32[]{:S(2)}, u32[]{:S(2)}) collective-permute-start(bf16[4,16,384]{2,1,0:T(8,128)(2,1)} %get-tuple-element.34), channel_id=1, source_target_pairs={{0,4},{4,0},{1,5},{5,1},{2,6},{6,2},{3,7},{7,3},{8,12},{12,8},{9,1... | collective-permute-start | bytes 147464 | tf_op jit(solution)/shard_map/ppermute | solution.py:288
  25.0 21.8 %collective-permute-start.6 = (bf16[2,384,512]{2,1,0:T(8,128)(2,1)}, bf16[2,384,512]{2,1,0:T(8,128)(2,1)S(1)}, u32[]{:S(2)}, u32[]{:S(2)}) collective-permute-start(bf16[2,384,512]{2,1,0:T(8,128)(2,1)} %get-tuple-element.36.refs_1_.refs_2_), channel_id=1, source_target_pairs={{0,24},{8,0},{16,8},{24,16},{1,25},{9,1},{17,9},{25,17},{2,26},{10... | collective-permute-start | bytes 2359304 | tf_op jit(solution)/shard_map/ppermute | solution.py:298
  29.7 22.1 %collective-permute-start.3 = (bf16[2,384,512]{2,1,0:T(8,128)(2,1)}, bf16[2,384,512]{2,1,0:T(8,128)(2,1)S(1)}, u32[]{:S(2)}, u32[]{:S(2)}) collective-permute-start(bf16[2,384,512]{2,1,0:T(8,128)(2,1)} %get-tuple-element.36.refs_1_.refs_2_), channel_id=1, source_target_pairs={{0,8},{8,16},{16,24},{24,0},{1,9},{9,17},{17,25},{25,1},{2,10},{10... | collective-permute-start | bytes 2359304 | tf_op jit(solution)/shard_map/ppermute | solution.py:295
  31.6 36.9 %collective-permute-start.5 = (bf16[2,384,512]{2,1,0:T(8,128)(2,1)}, bf16[2,384,512]{2,1,0:T(8,128)(2,1)S(1)}, u32[]{:S(2)}, u32[]{:S(2)}) collective-permute-start(bf16[2,384,512]{2,1,0:T(8,128)(2,1)} %get-tuple-element.37.refs_2_.refs_3_), channel_id=1, source_target_pairs={{0,8},{8,16},{16,24},{24,0},{1,9},{9,17},{17,25},{25,1},{2,10},{10... | collective-permute-start | bytes 2359304 | tf_op jit(solution)/shard_map/ppermute | solution.py:297
  33.8 34.8 %collective-permute-start.4 = (bf16[2,384,512]{2,1,0:T(8,128)(2,1)}, bf16[2,384,512]{2,1,0:T(8,128)(2,1)}, u32[]{:S(2)}, u32[]{:S(2)}) collective-permute-start(bf16[2,384,512]{2,1,0:T(8,128)(2,1)} %get-tuple-element.37.refs_2_.refs_3_), channel_id=1, source_target_pairs={{0,24},{8,0},{16,8},{24,16},{1,25},{9,1},{17,9},{25,17},{2,26},{10... | collective-permute-start | bytes 2359304 | tf_op jit(solution)/shard_map/ppermute | solution.py:296
  38.1 35.5 %collective-permute-start.15 = (bf16[768,512]{1,0:T(8,128)(2,1)}, bf16[768,512]{1,0:T(8,128)(2,1)S(1)}, u32[]{:S(2)}, u32[]{:S(2)}) collective-permute-start(bf16[768,512]{1,0:T(8,128)(2,1)} %get-tuple-element.42.near_hbm), channel_id=1, source_target_pairs={{0,4},{4,0},{1,5},{5,1},{2,6},{6,2},{3,7},{7,3},{8,12},{12,8},{9,1... | collective-permute-start | bytes 2359304 | tf_op jit(solution)/shard_map/ppermute | solution.py:288
  46.8 55.6 %copy-start.3 = (bf16[2,384,512]{2,1,0:T(8,128)(2,1)}, bf16[2,384,512]{2,1,0:T(8,128)(2,1)S(1)}, u32[]{:S(2)}) copy-start(bf16[2,384,512]{2,1,0:T(8,128)(2,1)S(1)} %collective-permute-done.6.refs_7_.refs_8_) | copy-start | bytes 2359300
  46.8 31.5 %collective-permute-start.1 = (bf16[2,384,512]{2,1,0:T(8,128)(2,1)}, bf16[2,384,512]{2,1,0:T(8,128)(2,1)S(1)}, u32[]{:S(2)}, u32[]{:S(2)}) collective-permute-start(bf16[2,384,512]{2,1,0:T(8,128)(2,1)} %get-tuple-element.36.refs_1_.refs_2_), channel_id=1, source_target_pairs={{0,4},{4,0},{1,5},{5,1},{2,6},{6,2},{3,7},{7,3},{8,12},{12,8},{9,1... | collective-permute-start | bytes 2359304 | tf_op jit(solution)/shard_map/ppermute | solution.py:288
  51.8 50.6 %copy-start.4 = (bf16[2,384,512]{2,1,0:T(8,128)(2,1)}, bf16[2,384,512]{2,1,0:T(8,128)(2,1)S(1)}, u32[]{:S(2)}) copy-start(bf16[2,384,512]{2,1,0:T(8,128)(2,1)S(1)} %collective-permute-done.3.refs_5_.refs_6_) | copy-start | bytes 2359300
  51.8 29.0 %collective-permute-start.2 = (bf16[2,384,512]{2,1,0:T(8,128)(2,1)}, bf16[2,384,512]{2,1,0:T(8,128)(2,1)S(1)}, u32[]{:S(2)}, u32[]{:S(2)}) collective-permute-start(bf16[2,384,512]{2,1,0:T(8,128)(2,1)} %get-tuple-element.37.refs_2_.refs_3_), channel_id=1, source_target_pairs={{0,4},{4,0},{1,5},{5,1},{2,6},{6,2},{3,7},{7,3},{8,12},{12,8},{9,1... | collective-permute-start | bytes 2359304 | tf_op jit(solution)/shard_map/ppermute | solution.py:288
  68.5 25.6 %copy-start.5 = (bf16[2,384,512]{2,1,0:T(8,128)(2,1)}, bf16[2,384,512]{2,1,0:T(8,128)(2,1)S(1)}, u32[]{:S(2)}) copy-start(bf16[2,384,512]{2,1,0:T(8,128)(2,1)S(1)} %collective-permute-done.5.refs_6_.refs_7_) | copy-start | bytes 2359300
  68.6 14.2 %collective-permute-start.8 = (bf16[2,384,512]{2,1,0:T(8,128)(2,1)S(1)}, bf16[2,384,512]{2,1,0:T(8,128)(2,1)S(1)}, u32[]{:S(2)}, u32[]{:S(2)}) collective-permute-start(bf16[2,384,512]{2,1,0:T(8,128)(2,1)S(1)} %collective-permute-done.5.refs_6_.refs_7_), channel_id=1, source_target_pairs={{0,4},{4,0},{1,5},{5,1},{2,6},{6,2},{3,7},{7,3},{8,12},{12,8},{9,1... | collective-permute-start | bytes 2359304 | tf_op jit(solution)/shard_map/ppermute | solution.py:288
  71.7 22.4 %collective-permute-start.11 = (bf16[2,384,512]{2,1,0:T(8,128)(2,1)S(1)}, bf16[2,384,512]{2,1,0:T(8,128)(2,1)}, u32[]{:S(2)}, u32[]{:S(2)}) collective-permute-start(bf16[2,384,512]{2,1,0:T(8,128)(2,1)S(1)} %collective-permute-done.3.refs_5_.refs_6_), channel_id=1, source_target_pairs={{0,8},{8,16},{16,24},{24,0},{1,9},{9,17},{17,25},{25,1},{2,10},{10... | collective-permute-start | bytes 2359304 | tf_op jit(solution)/shard_map/ppermute | solution.py:302
  73.7 25.1 %copy-start.9 = (bf16[768,512]{1,0:T(8,128)(2,1)}, bf16[768,512]{1,0:T(8,128)(2,1)S(1)}, u32[]{:S(2)}) copy-start(bf16[768,512]{1,0:T(8,128)(2,1)S(1)} %collective-permute-done.15.far_hbm) | copy-start | bytes 2359300
  73.7 23.1 %collective-permute-start.12 = (bf16[2,384,512]{2,1,0:T(8,128)(2,1)}, bf16[2,384,512]{2,1,0:T(8,128)(2,1)}, u32[]{:S(2)}, u32[]{:S(2)}) collective-permute-start(bf16[2,384,512]{2,1,0:T(8,128)(2,1)} %collective-permute-done.4.refs_8_.refs_9_), channel_id=1, source_target_pairs={{0,24},{8,0},{16,8},{24,16},{1,25},{9,1},{17,9},{25,17},{2,26},{10... | collective-permute-start | bytes 2359304 | tf_op jit(solution)/shard_map/ppermute | solution.py:303
  78.3 28.4 %collective-permute-start.7 = (bf16[2,384,512]{2,1,0:T(8,128)(2,1)S(1)}, bf16[2,384,512]{2,1,0:T(8,128)(2,1)}, u32[]{:S(2)}, u32[]{:S(2)}) collective-permute-start(bf16[2,384,512]{2,1,0:T(8,128)(2,1)S(1)} %collective-permute-done.3.refs_5_.refs_6_), channel_id=1, source_target_pairs={{0,4},{4,0},{1,5},{5,1},{2,6},{6,2},{3,7},{7,3},{8,12},{12,8},{9,1... | collective-permute-start | bytes 2359304 | tf_op jit(solution)/shard_map/ppermute | solution.py:288
  80.8 25.9 %collective-permute-start.10 = (bf16[2,384,512]{2,1,0:T(8,128)(2,1)}, bf16[2,384,512]{2,1,0:T(8,128)(2,1)}, u32[]{:S(2)}, u32[]{:S(2)}) collective-permute-start(bf16[2,384,512]{2,1,0:T(8,128)(2,1)} %collective-permute-done.4.refs_8_.refs_9_), channel_id=1, source_target_pairs={{0,4},{4,0},{1,5},{5,1},{2,6},{6,2},{3,7},{7,3},{8,12},{12,8},{9,1... | collective-permute-start | bytes 2359304 | tf_op jit(solution)/shard_map/ppermute | solution.py:288
  82.8 23.9 %collective-permute-start.9 = (bf16[2,384,512]{2,1,0:T(8,128)(2,1)S(1)}, bf16[2,384,512]{2,1,0:T(8,128)(2,1)}, u32[]{:S(2)}, u32[]{:S(2)}) collective-permute-start(bf16[2,384,512]{2,1,0:T(8,128)(2,1)S(1)} %collective-permute-done.6.refs_7_.refs_8_), channel_id=1, source_target_pairs={{0,4},{4,0},{1,5},{5,1},{2,6},{6,2},{3,7},{7,3},{8,12},{12,8},{9,1... | collective-permute-start | bytes 2359304 | tf_op jit(solution)/shard_map/ppermute | solution.py:288
  94.1 12.6 %collective-permute-start.13 = (bf16[2,384,512]{2,1,0:T(8,128)(2,1)}, bf16[2,384,512]{2,1,0:T(8,128)(2,1)}, u32[]{:S(2)}, u32[]{:S(2)}) collective-permute-start(bf16[2,384,512]{2,1,0:T(8,128)(2,1)} %collective-permute-done.11.refs_13_.refs_14_), channel_id=1, source_target_pairs={{0,4},{4,0},{1,5},{5,1},{2,6},{6,2},{3,7},{7,3},{8,12},{12,8},{9,1... | collective-permute-start | bytes 2359304 | tf_op jit(solution)/shard_map/ppermute | solution.py:288
  96.9 9.8 %collective-permute-start.14 = (bf16[2,384,512]{2,1,0:T(8,128)(2,1)}, bf16[2,384,512]{2,1,0:T(8,128)(2,1)}, u32[]{:S(2)}, u32[]{:S(2)}) collective-permute-start(bf16[2,384,512]{2,1,0:T(8,128)(2,1)} %collective-permute-done.12.refs_14_.refs_15_), channel_id=1, source_target_pairs={{0,4},{4,0},{1,5},{5,1},{2,6},{6,2},{3,7},{7,3},{8,12},{12,8},{9,1... | collective-permute-start | bytes 2359304 | tf_op jit(solution)/shard_map/ppermute | solution.py:288
  102.4 11.2 %all-to-all-start.1 = ((bf16[4,128,512]{2,1,0:T(8,128)(2,1)}), bf16[4,128,512]{2,1,0:T(8,128)(2,1)S(1)}, u32[]{:S(2)}, u32[]{:S(2)}) async-start(bf16[4,128,512]{2,1,0:T(8,128)(2,1)} %shard_map.77), calls=%async_computation.1 | async-start | bytes 1048576 | tf_op jit(solution)/shard_map/all_to_all | solution.py:375
  121.1 34.7 %all-to-all-start.2 = ((bf16[64,96,128]{2,1,0:T(8,128)(2,1)}), bf16[64,96,128]{2,1,0:T(8,128)(2,1)S(1)}, u32[]{:S(2)}, u32[]{:S(2)}) async-start(bf16[64,96,128]{2,1,0:T(8,128)(2,1)} %bitcast.20), calls=%async_computation.2 | async-start | bytes 3145728 | tf_op jit(solution)/shard_map/all_to_all | solution.py:408
  (6 other events, 84.3 us)
Sparse Core Ops, SparseCore 0:
  25.1 68.2 all-gather.1

commit v12 on v11

--- a/solution.py
+++ b/solution.py
@@ -104,13 +104,8 @@
         copy.wait()
 
 
-def weights_kernel(gate_ref, up_ref, down_ref, low_ref, high_ref, flip_ref):
-    half = low_ref.shape[1]
-    for i, ref in enumerate((low_ref, high_ref)):
-        span = slice(i * half, (i + 1) * half)
-        ref[0] = gate_ref[span, :]
-        ref[1] = up_ref[span, :]
-        flip_ref[span, :] = down_ref[:, span].T
+def flip_kernel(in_ref, out_ref):
+    out_ref[...] = in_ref[...].T
 
 
 def source(x_ref, core_ref, n_x, dx, dc):
@@ -179,8 +174,8 @@
         )
         for m in range(2):
             span = slice(m * hidden, (m + 1) * hidden)
-            term = jnp.dot(low, weights_ref[b, 0, m], preferred_element_type=f32)
-            term += jnp.dot(high, weights_ref[b, 1, m], preferred_element_type=f32)
+            term = jnp.dot(low, weights_ref[b, m, :half], preferred_element_type=f32)
+            term += jnp.dot(high, weights_ref[b, m, half:], preferred_element_type=f32)
             if b == 0:
                 total_ref[:, span] = term
             else:
@@ -192,7 +187,7 @@
     sums_ref, back_ref, weights_hbm = refs[0], refs[1], refs[2 : 2 + n_w]
     out_hbm, weights_ref, out_ref, sems, out_sems = refs[2 + n_w :]
     n_x, slots, hidden = back_ref.shape
-    half = weights_ref.shape[3]
+    feats = weights_ref.shape[2]
     n_z = slots // 8
     copies = start_weights(weights_hbm, weights_ref, sems)
 
@@ -213,24 +208,19 @@
         back_sum * up_sum * sigmoid_gate * (1.0 + gate_sum * (1.0 - sigmoid_gate))
     ).astype(bf16)
 
-    quarter = 2 * half // window
+    quarter = feats // window
     sent = []
     for b, (dx, dc) in enumerate(blocks_at):
         s = source(x_ref, core_ref, n_x, dx, dc)
         copies[2 * b].wait()
         copies[2 * b + 1].wait()
-        wide = [
-            lax.dot_general(
-                grad_gate, weights_ref[b, side, 0], contract_last, preferred_element_type=f32
-            )
-            + lax.dot_general(
-                grad_up, weights_ref[b, side, 1], contract_last, preferred_element_type=f32
-            )
-            for side in range(2)
-        ]
+        wide = lax.dot_general(
+            grad_gate, weights_ref[b, 0], contract_last, preferred_element_type=f32
+        ) + lax.dot_general(
+            grad_up, weights_ref[b, 1], contract_last, preferred_element_type=f32
+        )
         for y in range(window):
-            side, begin = y * quarter // half, y * quarter % half
-            rows = wide[side][:, begin : begin + quarter]
+            rows = wide[:, y * quarter : (y + 1) * quarter]
             for pair in range(2):
                 mine = rows[pair * slots // 2 : (pair + 1) * slots // 2]
                 out_ref[s, y, pair, : slots // 2, :] = mine[:, :128].astype(bf16)
@@ -288,24 +278,23 @@
     return lax.ppermute(value, "c", [(0, 1), (1, 0)])
 
 
-def gather_weights(low, high):
+def gather_weights(gate, up):
     n_x = lax.axis_size("x")
     ahead = [(i, (i + 1) % n_x) for i in range(n_x)]
     behind = [(i, (i - 1) % n_x) for i in range(n_x)]
-    low_before = lax.ppermute(low, "x", ahead)
-    high_after = lax.ppermute(high, "x", behind)
-    high_before = lax.ppermute(high, "x", ahead)
-    low_after = lax.ppermute(low, "x", behind)
-    low_before, high_after, high_before, low_after = lax.optimization_barrier(
-        (low_before, high_after, high_before, low_after)
-    )
-    low_across = lax.ppermute(low_before, "x", ahead)
-    high_across = lax.ppermute(high_after, "x", behind)
-    far = (swap(low), swap(high))
-    near = [(low_before, high_before), (low_after, high_after), (low_across, high_across)]
+    gate_before = lax.ppermute(gate, "x", ahead)
+    up_after = lax.ppermute(up, "x", behind)
+    up_before = lax.ppermute(up, "x", ahead)
+    gate_after = lax.ppermute(gate, "x", behind)
+    gate_before, up_after, up_before, gate_after = lax.optimization_barrier(
+        (gate_before, up_after, up_before, gate_after)
+    )
+    gate_across = lax.ppermute(gate_before, "x", ahead)
+    up_across = lax.ppermute(up_after, "x", behind)
+    far = (swap(gate), swap(up))
+    near = [(gate_before, up_before), (gate_after, up_after), (gate_across, up_across)]
     swapped = [(swap(a), swap(b)) for a, b in near]
-    blocks = [(low, high), far, near[0], near[1], swapped[0], swapped[1], near[2], swapped[2]]
-    return blocks
+    return [(gate, up), far, near[0], near[1], swapped[0], swapped[1], near[2], swapped[2]]
 
 
 def per_device(tokens, cotangent, experts, route_weight, gate_weight, up_weight, down_weight):
@@ -335,18 +324,10 @@
         ),
         [smem] * 2 + [vmem] * 4,
     )(expert_id, core, experts.T, route_weight.T, tokens, cotangent)
-    gate, up, down, pieces = lax.optimization_barrier((gate, up, down, pieces))
+    down, pieces = lax.optimization_barrier((down, pieces))
     pieces = lax.all_to_all(pieces, ("x", "c"), 0, 0, tiled=True)
-    low, high, down_t = kernel_call(
-        weights_kernel,
-        (
-            jax.ShapeDtypeStruct((2, half, hidden), bf16),
-            jax.ShapeDtypeStruct((2, half, hidden), bf16),
-            jax.ShapeDtypeStruct((feats, hidden), bf16),
-        ),
-        [vmem] * 3,
-    )(gate, up, down)
-    pieces, low, high, down_t = lax.optimization_barrier((pieces, low, high, down_t))
+    down_t = kernel_call(flip_kernel, jax.ShapeDtypeStruct((feats, hidden), bf16), [vmem])(down)
+    pieces, down_t = lax.optimization_barrier((pieces, down_t))
     own = kernel_call(
         pack_kernel,
         jax.ShapeDtypeStruct((groups, 2 * part, half), bf16),
@@ -355,10 +336,11 @@
         anywhere,
         small_vmem_bytes,
     )(pieces, keep, swap(send), table)
+    gate, up, own = lax.optimization_barrier((gate, up, own))
     rows = lax.all_gather(own.reshape(-1, half), ("zh", "zl"), axis=0, tiled=True).reshape(
         n_z, groups, 2 * part, half
     )
-    weights = [value for block in gather_weights(low, high) for value in block]
+    weights = [value for block in gather_weights(gate, up) for value in block]
     down_far = swap(down_t)
 
     back = kernel_call(
@@ -379,7 +361,7 @@
         [smem] * 2 + [anywhere] * (1 + len(weights)),
         [
             pltpu.VMEM((n_z, n_s, 2 * part, half), bf16),
-            pltpu.VMEM((len(blocks_at), 2, 2, half, hidden), bf16),
+            pltpu.VMEM((len(blocks_at), 2, feats, hidden), bf16),
             pltpu.SemaphoreType.DMA((len(weights) + 1,)),
         ],
         vmem_limit=late_vmem_bytes,
@@ -390,7 +372,7 @@
         jax.ShapeDtypeStruct(result_shape, bf16),
         [smem] * 2 + [vmem] * 2 + [anywhere] * len(weights),
         [
-            pltpu.VMEM((len(blocks_at), 2, 2, half, hidden), bf16),
+            pltpu.VMEM((len(blocks_at), 2, feats, hidden), bf16),
             pltpu.VMEM(result_shape, bf16),
             pltpu.SemaphoreType.DMA((len(weights),)),
             pltpu.SemaphoreType.DMA((len(blocks_at),)),

time: 201 us -> 199 us (0.990)
  waiting for transfers between devices: 53.3 us -> 47 us
  starting transfers between devices: 72.3 us -> 77.4 us
  blocking collectives: 35.7 us -> 33.3 us
    ppermute x6, waiting for transfers between devices: 29 us -> 23.1 us  [the longest x1 10.1 us: gather_weights(): up_before = lax.ppermute(up, 'x', ahead)]
    all_to_all x1, starting transfers between devices: 11.2 us -> 15 us  [per_device(): lax.all_to_all(result.reshape(n_s * window * 2, *shape[3:]), ('x', 'c', '...]
    all_to_all x1, blocking collectives: 35.7 us -> 33.3 us  [per_device(): dense = lax.all_to_all(dense, 'zh', 0, 0, tiled=True)]
    ppermute x10, starting transfers between devices: 27 us -> 29.2 us  [swap(): return lax.ppermute(value, 'c', [(0, 1), (1, 0)])]
  transfers between devices with their start and end apart: 20 -> 20, of which waited for: 6 -> 7; matrix products, arithmetic and copies ran while one was open for 0% -> 0% of each run, Pallas kernels for 6% -> 6%
where the time goes in v12:
time: 199 us; the launch traced here: 198 us
  starting transfers between devices  77.4 us (39%)
  waiting for transfers between devices  47 us (24%)
  blocking collectives  33.3 us (17%)
  Pallas kernels  23.6 us (12%)
  between operations  13.8 us (7%)
  local copies, waits for them, and re-layouts  2.68 us (1%)
    all_to_all x1, blocking collectives, per_device(): dense = lax.all_to_all(dense, 'zh', 0, 0, tiled=True)  33.3 us
    ppermute x10, starting transfers between devices, swap(): return lax.ppermute(value, 'c', [(0, 1), (1, 0)])  29.2 us
    all_to_all x1, waiting for transfers between devices, per_device(): lax.all_to_all(result.reshape(n_s * window * 2, *shape[3:]), ('x', 'c', '...  22.7 us
    all_to_all x1, starting transfers between devices, per_device(): lax.all_to_all(result.reshape(n_s * window * 2, *shape[3:]), ('x', 'c', '...  15 us
    all_to_all x1, starting transfers between devices, per_device(): pieces = lax.all_to_all(pieces, ('x', 'c'), 0, 0, tiled=True)  10.3 us
    ppermute x1, waiting for transfers between devices, gather_weights(): up_before = lax.ppermute(up, 'x', ahead)  10.1 us
    pallas_call x1, Pallas kernels, per_device(): kernel_call(result_kernel, jax.ShapeDtypeStruct(result_shape, bf16), [sme...  8.7 us
    ppermute x1, waiting for transfers between devices, gather_weights(): gate_across = lax.ppermute(gate_before, 'x', ahead)  6.29 us
  transfers between devices with their start and end apart: 20, of which 7 were waited for; matrix products, arithmetic and copies ran while one was open for 0% of the time, Pallas kernels for 6%

profile of v12, /device:TPU:1, one launch (start us, length us, event | category | flops | bytes accessed | tf_op | source)
XLA Modules:
  0.0 198.4 jit_solution(8036146970406942419)
XLA Ops:
  6.5 2.1 %shard_map.73 = (bf16[8,16,384]{2,1,0:T(8,128)(2,1)}, bf16[4,16,384]{2,1,0:T(8,128)(2,1)}, bf16[4,16,384]{2,1,0:T(8,128)(2,1)}, bf16[1,16,384]{2,1,0:T(8,128)(2,1)}) custom-call(s32[1]{0:T(128)} %bitcast.3.expert_ref, s32[1]{0:T(128)} %bitcast.4.core_ref, s32[2,128]{1,0:T(2,128)} %bitcast.32, s32[2,128]{1,0:T(2,128)} %bitcast.33, bf16[128,768]{1,0:T(8,128)(2,1)} %tok_ref.1, ...), custom_call_target="tpu_custom_call" | custom-call | tf_op jit(solution)/shard_map/pallas_call | solution.py:317
  8.7 10.3 %all-to-all-start = ((bf16[8,16,384]{2,1,0:T(8,128)(2,1)}), bf16[8,16,384]{2,1,0:T(8,128)(2,1)S(1)}, u32[]{:S(2)}, u32[]{:S(2)}) async-start(bf16[8,16,384]{2,1,0:T(8,128)(2,1)} %get-tuple-element.21), calls=%async_computation | async-start | bytes 196608 | tf_op jit(solution)/shard_map/all_to_all | solution.py:328
  21.0 2.3 %shard_map.74.near_hbm = bf16[768,512]{1,0:T(8,128)(2,1)} custom-call(bf16[512,768]{1,0:T(8,128)(2,1)} %bitcast.31), custom_call_target="tpu_custom_call" | custom-call | tf_op jit(solution)/shard_map/pallas_call | solution.py:329
  24.8 2.9 %collective-permute-start.3 = (bf16[768,512]{1,0:T(8,128)(2,1)S(1)}, bf16[768,512]{1,0:T(8,128)(2,1)S(1)}, u32[]{:S(2)}, u32[]{:S(2)}) collective-permute-start(bf16[768,512]{1,0:T(8,128)(2,1)S(1)} %bitcast.17), channel_id=1, source_target_pairs={{0,8},{8,16},{16,24},{24,0},{1,9},{9,17},{17,25},{25,1},{2,10},{10... | collective-permute-start | bytes 2359304 | tf_op jit(solution)/shard_map/ppermute | solution.py:285
  27.7 3.6 %collective-permute-start.4 = (bf16[768,512]{1,0:T(8,128)(2,1)S(1)}, bf16[768,512]{1,0:T(8,128)(2,1)S(1)}, u32[]{:S(2)}, u32[]{:S(2)}) collective-permute-start(bf16[768,512]{1,0:T(8,128)(2,1)S(1)} %bitcast.28), channel_id=1, source_target_pairs={{0,24},{8,0},{16,8},{24,16},{1,25},{9,1},{17,9},{25,17},{2,26},{10... | collective-permute-start | bytes 2359304 | tf_op jit(solution)/shard_map/ppermute | solution.py:286
  33.2 4.6 %collective-permute-start.6 = (bf16[768,512]{1,0:T(8,128)(2,1)S(1)}, bf16[768,512]{1,0:T(8,128)(2,1)}, u32[]{:S(2)}, u32[]{:S(2)}) collective-permute-start(bf16[768,512]{1,0:T(8,128)(2,1)S(1)} %bitcast.18), channel_id=1, source_target_pairs={{0,24},{8,0},{16,8},{24,16},{1,25},{9,1},{17,9},{25,17},{2,26},{10... | collective-permute-start | bytes 2359304 | tf_op jit(solution)/shard_map/ppermute | solution.py:288
  37.8 3.8 %collective-permute-start.1 = (bf16[768,512]{1,0:T(8,128)(2,1)S(1)}, bf16[768,512]{1,0:T(8,128)(2,1)S(1)}, u32[]{:S(2)}, u32[]{:S(2)}) collective-permute-start(bf16[768,512]{1,0:T(8,128)(2,1)S(1)} %bitcast.19), channel_id=1, source_target_pairs={{0,4},{4,0},{1,5},{5,1},{2,6},{6,2},{3,7},{7,3},{8,12},{12,8},{9,1... | collective-permute-start | bytes 2359304 | tf_op jit(solution)/shard_map/ppermute | solution.py:278
  41.6 4.6 %collective-permute-done.3.refs_5_.refs_6_ = bf16[768,512]{1,0:T(8,128)(2,1)S(1)} collective-permute-done((bf16[768,512]{1,0:T(8,128)(2,1)S(1)}, bf16[768,512]{1,0:T(8,128)(2,1)S(1)}, u32[]{:S(2)}, u32[]{:S(2)}) %collective-permute-start.3) | collective-permute-done | bytes 786464 | tf_op jit(solution)/shard_map/ppermute | solution.py:285
  46.2 4.8 %collective-permute-start.2 = (bf16[768,512]{1,0:T(8,128)(2,1)S(1)}, bf16[768,512]{1,0:T(8,128)(2,1)S(1)}, u32[]{:S(2)}, u32[]{:S(2)}) collective-permute-start(bf16[768,512]{1,0:T(8,128)(2,1)S(1)} %bitcast.30), channel_id=1, source_target_pairs={{0,4},{4,0},{1,5},{5,1},{2,6},{6,2},{3,7},{7,3},{8,12},{12,8},{9,1... | collective-permute-start | bytes 2359304 | tf_op jit(solution)/shard_map/ppermute | solution.py:278
  53.0 10.1 %collective-permute-done.5.refs_6_.refs_7_ = bf16[768,512]{1,0:T(8,128)(2,1)} collective-permute-done((bf16[768,512]{1,0:T(8,128)(2,1)S(1)}, bf16[768,512]{1,0:T(8,128)(2,1)}, u32[]{:S(2)}, u32[]{:S(2)}) %collective-permute-start.5) | collective-permute-done | bytes 786464 | tf_op jit(solution)/shard_map/ppermute | solution.py:287
  65.2 3.1 %collective-permute-start.11 = (bf16[768,512]{1,0:T(8,128)(2,1)S(1)}, bf16[768,512]{1,0:T(8,128)(2,1)}, u32[]{:S(2)}, u32[]{:S(2)}) collective-permute-start(bf16[768,512]{1,0:T(8,128)(2,1)S(1)} %collective-permute-done.3.refs_5_.refs_6_), channel_id=1, source_target_pairs={{0,8},{8,16},{16,24},{24,0},{1,9},{9,17},{17,25},{25,1},{2,10},{10... | collective-permute-start | bytes 2359304 | tf_op jit(solution)/shard_map/ppermute | solution.py:292
  68.3 3.4 %collective-permute-start.12 = (bf16[768,512]{1,0:T(8,128)(2,1)S(1)}, bf16[768,512]{1,0:T(8,128)(2,1)}, u32[]{:S(2)}, u32[]{:S(2)}) collective-permute-start(bf16[768,512]{1,0:T(8,128)(2,1)S(1)} %collective-permute-done.4.refs_8_.refs_9_), channel_id=1, source_target_pairs={{0,24},{8,0},{16,8},{24,16},{1,25},{9,1},{17,9},{25,17},{2,26},{10... | collective-permute-start | bytes 2359304 | tf_op jit(solution)/shard_map/ppermute | solution.py:293
  71.7 3.8 %collective-permute-start.10 = (bf16[768,512]{1,0:T(8,128)(2,1)S(1)}, bf16[768,512]{1,0:T(8,128)(2,1)S(1)}, u32[]{:S(2)}, u32[]{:S(2)}) collective-permute-start(bf16[768,512]{1,0:T(8,128)(2,1)S(1)} %collective-permute-done.4.refs_8_.refs_9_), channel_id=1, source_target_pairs={{0,4},{4,0},{1,5},{5,1},{2,6},{6,2},{3,7},{7,3},{8,12},{12,8},{9,1... | collective-permute-start | bytes 2359304 | tf_op jit(solution)/shard_map/ppermute | solution.py:278
  77.4 2.4 %collective-permute-start.8 = (bf16[768,512]{1,0:T(8,128)(2,1)}, bf16[768,512]{1,0:T(8,128)(2,1)}, u32[]{:S(2)}, u32[]{:S(2)}) collective-permute-start(bf16[768,512]{1,0:T(8,128)(2,1)} %collective-permute-done.5.refs_6_.refs_7_), channel_id=1, source_target_pairs={{0,4},{4,0},{1,5},{5,1},{2,6},{6,2},{3,7},{7,3},{8,12},{12,8},{9,1... | collective-permute-start | bytes 2359304 | tf_op jit(solution)/shard_map/ppermute | solution.py:278
  79.8 6.3 %collective-permute-done.11.refs_13_.refs_14_ = bf16[768,512]{1,0:T(8,128)(2,1)} collective-permute-done((bf16[768,512]{1,0:T(8,128)(2,1)S(1)}, bf16[768,512]{1,0:T(8,128)(2,1)}, u32[]{:S(2)}, u32[]{:S(2)}) %collective-permute-start.11) | collective-permute-done | bytes 786464 | tf_op jit(solution)/shard_map/ppermute | solution.py:292
  86.1 4.1 %collective-permute-start.9 = (bf16[768,512]{1,0:T(8,128)(2,1)}, bf16[768,512]{1,0:T(8,128)(2,1)}, u32[]{:S(2)}, u32[]{:S(2)}) collective-permute-start(bf16[768,512]{1,0:T(8,128)(2,1)} %collective-permute-done.6.refs_7_.refs_8_), channel_id=1, source_target_pairs={{0,4},{4,0},{1,5},{5,1},{2,6},{6,2},{3,7},{7,3},{8,12},{12,8},{9,1... | collective-permute-start | bytes 2359304 | tf_op jit(solution)/shard_map/ppermute | solution.py:278
  93.1 2.4 %collective-permute-start.14 = (bf16[768,512]{1,0:T(8,128)(2,1)}, bf16[768,512]{1,0:T(8,128)(2,1)}, u32[]{:S(2)}, u32[]{:S(2)}) collective-permute-start(bf16[768,512]{1,0:T(8,128)(2,1)} %collective-permute-done.12.refs_14_.refs_15_), channel_id=1, source_target_pairs={{0,4},{4,0},{1,5},{5,1},{2,6},{6,2},{3,7},{7,3},{8,12},{12,8},{9,1... | collective-permute-start | bytes 2359304 | tf_op jit(solution)/shard_map/ppermute | solution.py:278
  95.6 3.5 %shard_map.77 = bf16[4,128,512]{2,1,0:T(8,128)(2,1)} custom-call(bf16[16,17,16,384]{3,2,1,0:T(8,128)(2,1)} %bitcast.22, bf16[768,512]{1,0:T(8,128)(2,1)} %shard_map.74.near_hbm, bf16[768,512]{1,0:T(8,128)(2,1)} %copy-done.10), custom_call_target="tpu_custom_call" | custom-call | tf_op jit(solution)/shard_map/pallas_call | solution.py:346
  99.1 3.5 %all-to-all-start.1 = ((bf16[4,128,512]{2,1,0:T(8,128)(2,1)}), bf16[4,128,512]{2,1,0:T(8,128)(2,1)S(1)}, u32[]{:S(2)}, u32[]{:S(2)}) async-start(bf16[4,128,512]{2,1,0:T(8,128)(2,1)} %shard_map.77), calls=%async_computation.1 | async-start | bytes 1048576 | tf_op jit(solution)/shard_map/all_to_all | solution.py:357
  103.6 5.4 %shard_map.76.refs_0_ = f32[128,1024]{1,0:T(8,128)S(1)} custom-call(s32[1]{0:T(128)} %bitcast.10.x_ref, s32[1]{0:T(128)} %bitcast.4.core_ref, bf16[16,17,16,384]{3,2,1,0:T(8,128)(2,1)} %bitcast.23, bf16[768,512]{1,0:T(8,128)(2,1)S(1)} %bitcast.20, bf16[768,512]{1,0:T(8,128)(2,1)} %bitcast.26, bf16[768,512]{1,0:T(8,128)(2,1)} %copy-done.6, ...), custom_call_target="tpu_custom_call" | custom-call | tf_op jit(solution)/shard_map/pallas_call | solution.py:358
  109.5 8.7 %shard_map.78 = bf16[8,4,2,96,128]{4,3,2,1,0:T(8,128)(2,1)} custom-call(s32[1]{0:T(128)} %bitcast.10.x_ref, s32[1]{0:T(128)} %bitcast.4.core_ref, f32[128,1024]{1,0:T(8,128)S(1)} %shard_map.76.refs_0_, bf16[4,128,512]{2,1,0:T(8,128)(2,1)S(1)} %all-to-all-done.1.refs_1_, bf16[768,512]{1,0:T(8,128)(2,1)S(1)} %bitcast.21, bf16[768,512]{1,0:T(8,128)(2,1)} %bitcast.27, ...), custom_call_target="tpu_custom_call" | custom-call | tf_op jit(solution)/shard_map/pallas_call | solution.py:370
  118.2 15.0 %all-to-all-start.2 = ((bf16[64,96,128]{2,1,0:T(8,128)(2,1)}), bf16[64,96,128]{2,1,0:T(8,128)(2,1)S(1)}, u32[]{:S(2)}, u32[]{:S(2)}) async-start(bf16[64,96,128]{2,1,0:T(8,128)(2,1)} %bitcast.25), calls=%async_computation.2 | async-start | bytes 3145728 | tf_op jit(solution)/shard_map/all_to_all | solution.py:390
  134.1 22.7 %all-to-all-done.2 = bf16[64,96,128]{2,1,0:T(8,128)(2,1)S(1)} async-done(((bf16[64,96,128]{2,1,0:T(8,128)(2,1)}), bf16[64,96,128]{2,1,0:T(8,128)(2,1)S(1)}, u32[]{:S(2)}, u32[]{:S(2)}) %all-to-all-start.2) | async-done | bytes 1572896 | tf_op jit(solution)/shard_map/all_to_all | solution.py:390
  157.5 33.3 %all_to_all.20 = bf16[8,192,128]{2,1,0:T(8,128)(2,1)S(1)} all-to-all(bf16[8,192,128]{2,1,0:T(8,128)(2,1)S(1)} %shard_map.79), channel_id=1, replica_groups=mesh['zh'=8,'zl'=2,'x'=4,'c'=2,'y'=4] {'zh'}, dimensions={0} | all-to-all | bytes 786432 | tf_op jit(solution)/shard_map/all_to_all | solution.py:399
  (50 shorter events, 17.9 us)
Async XLA Ops:
  6.5 21.1 %copy-start.3 = (bf16[1,768,512]{2,1,0:T(8,128)(2,1)S(1)}, bf16[1,768,512]{2,1,0:T(8,128)(2,1)}, u32[]{:S(2)}) copy-start(bf16[1,768,512]{2,1,0:T(8,128)(2,1)} %param.12) | copy-start | bytes 2359300
  8.7 15.3 %all-to-all-start = ((bf16[8,16,384]{2,1,0:T(8,128)(2,1)}), bf16[8,16,384]{2,1,0:T(8,128)(2,1)S(1)}, u32[]{:S(2)}, u32[]{:S(2)}) async-start(bf16[8,16,384]{2,1,0:T(8,128)(2,1)} %get-tuple-element.21), calls=%async_computation | async-start | bytes 196608 | tf_op jit(solution)/shard_map/all_to_all | solution.py:328
  19.0 76.6 %all-gather.2.cloned.1.call-start = ((), (), s32[]{:S(2)}) async-start(), calls=%async_computation.4 | async-start | bytes 3551232 | tf_op jit(solution)/shard_map/all_gather | solution.py:340
  19.0 5.0 %collective-permute-start = (bf16[4,16,384]{2,1,0:T(8,128)(2,1)}, bf16[4,16,384]{2,1,0:T(8,128)(2,1)S(1)}, u32[]{:S(2)}, u32[]{:S(2)}) collective-permute-start(bf16[4,16,384]{2,1,0:T(8,128)(2,1)} %get-tuple-element.25), channel_id=1, source_target_pairs={{0,4},{4,0},{1,5},{5,1},{2,6},{6,2},{3,7},{7,3},{8,12},{12,8},{9,1... | collective-permute-start | bytes 147464 | tf_op jit(solution)/shard_map/ppermute | solution.py:278
  24.8 21.4 %collective-permute-start.3 = (bf16[768,512]{1,0:T(8,128)(2,1)S(1)}, bf16[768,512]{1,0:T(8,128)(2,1)S(1)}, u32[]{:S(2)}, u32[]{:S(2)}) collective-permute-start(bf16[768,512]{1,0:T(8,128)(2,1)S(1)} %bitcast.17), channel_id=1, source_target_pairs={{0,8},{8,16},{16,24},{24,0},{1,9},{9,17},{17,25},{25,1},{2,10},{10... | collective-permute-start | bytes 2359304 | tf_op jit(solution)/shard_map/ppermute | solution.py:285
  27.7 23.4 %collective-permute-start.4 = (bf16[768,512]{1,0:T(8,128)(2,1)S(1)}, bf16[768,512]{1,0:T(8,128)(2,1)S(1)}, u32[]{:S(2)}, u32[]{:S(2)}) collective-permute-start(bf16[768,512]{1,0:T(8,128)(2,1)S(1)} %bitcast.28), channel_id=1, source_target_pairs={{0,24},{8,0},{16,8},{24,16},{1,25},{9,1},{17,9},{25,17},{2,26},{10... | collective-permute-start | bytes 2359304 | tf_op jit(solution)/shard_map/ppermute | solution.py:286
  31.3 31.8 %collective-permute-start.5 = (bf16[768,512]{1,0:T(8,128)(2,1)S(1)}, bf16[768,512]{1,0:T(8,128)(2,1)}, u32[]{:S(2)}, u32[]{:S(2)}) collective-permute-start(bf16[768,512]{1,0:T(8,128)(2,1)S(1)} %bitcast.29), channel_id=1, source_target_pairs={{0,8},{8,16},{16,24},{24,0},{1,9},{9,17},{17,25},{25,1},{2,10},{10... | collective-permute-start | bytes 2359304 | tf_op jit(solution)/shard_map/ppermute | solution.py:287
  33.2 32.0 %collective-permute-start.6 = (bf16[768,512]{1,0:T(8,128)(2,1)S(1)}, bf16[768,512]{1,0:T(8,128)(2,1)}, u32[]{:S(2)}, u32[]{:S(2)}) collective-permute-start(bf16[768,512]{1,0:T(8,128)(2,1)S(1)} %bitcast.18), channel_id=1, source_target_pairs={{0,24},{8,0},{16,8},{24,16},{1,25},{9,1},{17,9},{25,17},{2,26},{10... | collective-permute-start | bytes 2359304 | tf_op jit(solution)/shard_map/ppermute | solution.py:288
  37.8 33.9 %collective-permute-start.1 = (bf16[768,512]{1,0:T(8,128)(2,1)S(1)}, bf16[768,512]{1,0:T(8,128)(2,1)S(1)}, u32[]{:S(2)}, u32[]{:S(2)}) collective-permute-start(bf16[768,512]{1,0:T(8,128)(2,1)S(1)} %bitcast.19), channel_id=1, source_target_pairs={{0,4},{4,0},{1,5},{5,1},{2,6},{6,2},{3,7},{7,3},{8,12},{12,8},{9,1... | collective-permute-start | bytes 2359304 | tf_op jit(solution)/shard_map/ppermute | solution.py:278
  46.2 52.9 %copy-start.4 = (bf16[768,512]{1,0:T(8,128)(2,1)}, bf16[768,512]{1,0:T(8,128)(2,1)S(1)}, u32[]{:S(2)}) copy-start(bf16[768,512]{1,0:T(8,128)(2,1)S(1)} %collective-permute-done.3.refs_5_.refs_6_) | copy-start | bytes 2359300
  46.2 29.3 %collective-permute-start.2 = (bf16[768,512]{1,0:T(8,128)(2,1)S(1)}, bf16[768,512]{1,0:T(8,128)(2,1)S(1)}, u32[]{:S(2)}, u32[]{:S(2)}) collective-permute-start(bf16[768,512]{1,0:T(8,128)(2,1)S(1)} %bitcast.30), channel_id=1, source_target_pairs={{0,4},{4,0},{1,5},{5,1},{2,6},{6,2},{3,7},{7,3},{8,12},{12,8},{9,1... | collective-permute-start | bytes 2359304 | tf_op jit(solution)/shard_map/ppermute | solution.py:278
  51.0 35.1 %copy-start.5 = (bf16[768,512]{1,0:T(8,128)(2,1)}, bf16[768,512]{1,0:T(8,128)(2,1)S(1)}, u32[]{:S(2)}) copy-start(bf16[768,512]{1,0:T(8,128)(2,1)S(1)} %collective-permute-done.4.refs_8_.refs_9_) | copy-start | bytes 2359300
  51.1 26.4 %collective-permute-start.15 = (bf16[768,512]{1,0:T(8,128)(2,1)}, bf16[768,512]{1,0:T(8,128)(2,1)S(1)}, u32[]{:S(2)}, u32[]{:S(2)}) collective-permute-start(bf16[768,512]{1,0:T(8,128)(2,1)} %shard_map.74.near_hbm), channel_id=1, source_target_pairs={{0,4},{4,0},{1,5},{5,1},{2,6},{6,2},{3,7},{7,3},{8,12},{12,8},{9,1... | collective-permute-start | bytes 2359304 | tf_op jit(solution)/shard_map/ppermute | solution.py:278
  65.2 21.0 %collective-permute-start.11 = (bf16[768,512]{1,0:T(8,128)(2,1)S(1)}, bf16[768,512]{1,0:T(8,128)(2,1)}, u32[]{:S(2)}, u32[]{:S(2)}) collective-permute-start(bf16[768,512]{1,0:T(8,128)(2,1)S(1)} %collective-permute-done.3.refs_5_.refs_6_), channel_id=1, source_target_pairs={{0,8},{8,16},{16,24},{24,0},{1,9},{9,17},{17,25},{25,1},{2,10},{10... | collective-permute-start | bytes 2359304 | tf_op jit(solution)/shard_map/ppermute | solution.py:292
  68.3 22.0 %collective-permute-start.12 = (bf16[768,512]{1,0:T(8,128)(2,1)S(1)}, bf16[768,512]{1,0:T(8,128)(2,1)}, u32[]{:S(2)}, u32[]{:S(2)}) collective-permute-start(bf16[768,512]{1,0:T(8,128)(2,1)S(1)} %collective-permute-done.4.refs_8_.refs_9_), channel_id=1, source_target_pairs={{0,24},{8,0},{16,8},{24,16},{1,25},{9,1},{17,9},{25,17},{2,26},{10... | collective-permute-start | bytes 2359304 | tf_op jit(solution)/shard_map/ppermute | solution.py:293
  71.7 20.5 %copy-start.6 = (bf16[768,512]{1,0:T(8,128)(2,1)}, bf16[768,512]{1,0:T(8,128)(2,1)S(1)}, u32[]{:S(2)}) copy-start(bf16[768,512]{1,0:T(8,128)(2,1)S(1)} %collective-permute-done.1.refs_3_.refs_4_) | copy-start | bytes 2359300
  71.7 20.5 %collective-permute-start.10 = (bf16[768,512]{1,0:T(8,128)(2,1)S(1)}, bf16[768,512]{1,0:T(8,128)(2,1)S(1)}, u32[]{:S(2)}, u32[]{:S(2)}) collective-permute-start(bf16[768,512]{1,0:T(8,128)(2,1)S(1)} %collective-permute-done.4.refs_8_.refs_9_), channel_id=1, source_target_pairs={{0,4},{4,0},{1,5},{5,1},{2,6},{6,2},{3,7},{7,3},{8,12},{12,8},{9,1... | collective-permute-start | bytes 2359304 | tf_op jit(solution)/shard_map/ppermute | solution.py:278
  75.5 27.1 %collective-permute-start.7 = (bf16[768,512]{1,0:T(8,128)(2,1)S(1)}, bf16[768,512]{1,0:T(8,128)(2,1)S(1)}, u32[]{:S(2)}, u32[]{:S(2)}) collective-permute-start(bf16[768,512]{1,0:T(8,128)(2,1)S(1)} %collective-permute-done.3.refs_5_.refs_6_), channel_id=1, source_target_pairs={{0,4},{4,0},{1,5},{5,1},{2,6},{6,2},{3,7},{7,3},{8,12},{12,8},{9,1... | collective-permute-start | bytes 2359304 | tf_op jit(solution)/shard_map/ppermute | solution.py:278
  77.4 25.2 %collective-permute-start.8 = (bf16[768,512]{1,0:T(8,128)(2,1)}, bf16[768,512]{1,0:T(8,128)(2,1)}, u32[]{:S(2)}, u32[]{:S(2)}) collective-permute-start(bf16[768,512]{1,0:T(8,128)(2,1)} %collective-permute-done.5.refs_6_.refs_7_), channel_id=1, source_target_pairs={{0,4},{4,0},{1,5},{5,1},{2,6},{6,2},{3,7},{7,3},{8,12},{12,8},{9,1... | collective-permute-start | bytes 2359304 | tf_op jit(solution)/shard_map/ppermute | solution.py:278
  86.1 16.5 %collective-permute-start.9 = (bf16[768,512]{1,0:T(8,128)(2,1)}, bf16[768,512]{1,0:T(8,128)(2,1)}, u32[]{:S(2)}, u32[]{:S(2)}) collective-permute-start(bf16[768,512]{1,0:T(8,128)(2,1)} %collective-permute-done.6.refs_7_.refs_8_), channel_id=1, source_target_pairs={{0,4},{4,0},{1,5},{5,1},{2,6},{6,2},{3,7},{7,3},{8,12},{12,8},{9,1... | collective-permute-start | bytes 2359304 | tf_op jit(solution)/shard_map/ppermute | solution.py:278
  90.3 12.4 %collective-permute-start.13 = (bf16[768,512]{1,0:T(8,128)(2,1)}, bf16[768,512]{1,0:T(8,128)(2,1)}, u32[]{:S(2)}, u32[]{:S(2)}) collective-permute-start(bf16[768,512]{1,0:T(8,128)(2,1)} %collective-permute-done.11.refs_13_.refs_14_), channel_id=1, source_target_pairs={{0,4},{4,0},{1,5},{5,1},{2,6},{6,2},{3,7},{7,3},{8,12},{12,8},{9,1... | collective-permute-start | bytes 2359304 | tf_op jit(solution)/shard_map/ppermute | solution.py:278
  93.1 9.5 %collective-permute-start.14 = (bf16[768,512]{1,0:T(8,128)(2,1)}, bf16[768,512]{1,0:T(8,128)(2,1)}, u32[]{:S(2)}, u32[]{:S(2)}) collective-permute-start(bf16[768,512]{1,0:T(8,128)(2,1)} %collective-permute-done.12.refs_14_.refs_15_), channel_id=1, source_target_pairs={{0,4},{4,0},{1,5},{5,1},{2,6},{6,2},{3,7},{7,3},{8,12},{12,8},{9,1... | collective-permute-start | bytes 2359304 | tf_op jit(solution)/shard_map/ppermute | solution.py:278
  99.1 10.4 %all-to-all-start.1 = ((bf16[4,128,512]{2,1,0:T(8,128)(2,1)}), bf16[4,128,512]{2,1,0:T(8,128)(2,1)S(1)}, u32[]{:S(2)}, u32[]{:S(2)}) async-start(bf16[4,128,512]{2,1,0:T(8,128)(2,1)} %shard_map.77), calls=%async_computation.1 | async-start | bytes 1048576 | tf_op jit(solution)/shard_map/all_to_all | solution.py:357
  118.2 38.5 %all-to-all-start.2 = ((bf16[64,96,128]{2,1,0:T(8,128)(2,1)}), bf16[64,96,128]{2,1,0:T(8,128)(2,1)S(1)}, u32[]{:S(2)}, u32[]{:S(2)}) async-start(bf16[64,96,128]{2,1,0:T(8,128)(2,1)} %bitcast.25), calls=%async_computation.2 | async-start | bytes 3145728 | tf_op jit(solution)/shard_map/all_to_all | solution.py:390
  (7 other events, 85.5 us)
Sparse Core Ops, SparseCore 0:
  24.9 67.5 all-gather.1

commit v13 on v12

--- a/solution.py
+++ b/solution.py
@@ -188,6 +188,7 @@
     out_hbm, weights_ref, out_ref, sems, out_sems = refs[2 + n_w :]
     n_x, slots, hidden = back_ref.shape
     feats = weights_ref.shape[2]
+    half = feats // 2
     n_z = slots // 8
     copies = start_weights(weights_hbm, weights_ref, sems)
 
@@ -214,13 +215,18 @@
         s = source(x_ref, core_ref, n_x, dx, dc)
         copies[2 * b].wait()
         copies[2 * b + 1].wait()
-        wide = lax.dot_general(
-            grad_gate, weights_ref[b, 0], contract_last, preferred_element_type=f32
-        ) + lax.dot_general(
-            grad_up, weights_ref[b, 1], contract_last, preferred_element_type=f32
-        )
+        wide = [
+            lax.dot_general(
+                grad_gate, weights_ref[b, 0, span], contract_last, preferred_element_type=f32
+            )
+            + lax.dot_general(
+                grad_up, weights_ref[b, 1, span], contract_last, preferred_element_type=f32
+            )
+            for span in (slice(0, half), slice(half, feats))
+        ]
         for y in range(window):
-            rows = wide[:, y * quarter : (y + 1) * quarter]
+            begin = y * quarter % half
+            rows = wide[y * quarter // half][:, begin : begin + quarter]
             for pair in range(2):
                 mine = rows[pair * slots // 2 : (pair + 1) * slots // 2]
                 out_ref[s, y, pair, : slots // 2, :] = mine[:, :128].astype(bf16)

time: 199 us -> 198 us (level)
  no operation moved by 1% of the time
where the time goes in v13:
time: 198 us; the launch traced here: 197 us
  starting transfers between devices  77.4 us (39%)
  waiting for transfers between devices  47 us (24%)
  blocking collectives  33.3 us (17%)
  Pallas kernels  22.3 us (11%)
  between operations  13.8 us (7%)
  local copies, waits for them, and re-layouts  2.68 us (1%)
    all_to_all x1, blocking collectives, per_device(): dense = lax.all_to_all(dense, 'zh', 0, 0, tiled=True)  33.3 us
    ppermute x10, starting transfers between devices, swap(): return lax.ppermute(value, 'c', [(0, 1), (1, 0)])  29.2 us
    all_to_all x1, waiting for transfers between devices, per_device(): lax.all_to_all(result.reshape(n_s * window * 2, *shape[3:]), ('x', 'c', '...  22.7 us
    all_to_all x1, starting transfers between devices, per_device(): lax.all_to_all(result.reshape(n_s * window * 2, *shape[3:]), ('x', 'c', '...  15 us
    all_to_all x1, starting transfers between devices, per_device(): pieces = lax.all_to_all(pieces, ('x', 'c'), 0, 0, tiled=True)  10.3 us
    ppermute x1, waiting for transfers between devices, gather_weights(): up_before = lax.ppermute(up, 'x', ahead)  10.1 us
    pallas_call x1, Pallas kernels, per_device(): kernel_call(result_kernel, jax.ShapeDtypeStruct(result_shape, bf16), [sme...  7.45 us
    ppermute x1, waiting for transfers between devices, gather_weights(): gate_across = lax.ppermute(gate_before, 'x', ahead)  6.29 us
  transfers between devices with their start and end apart: 20, of which 7 were waited for; matrix products, arithmetic and copies ran while one was open for 0% of the time, Pallas kernels for 6%

profile of v13, /device:TPU:1, one launch (start us, length us, event | category | flops | bytes accessed | tf_op | source)
XLA Modules:
  0.0 197.1 jit_solution(1656208317619657561)
XLA Ops:
  6.5 2.1 %shard_map.73 = (bf16[8,16,384]{2,1,0:T(8,128)(2,1)}, bf16[4,16,384]{2,1,0:T(8,128)(2,1)}, bf16[4,16,384]{2,1,0:T(8,128)(2,1)}, bf16[1,16,384]{2,1,0:T(8,128)(2,1)}) custom-call(s32[1]{0:T(128)} %bitcast.3.expert_ref, s32[1]{0:T(128)} %bitcast.4.core_ref, s32[2,128]{1,0:T(2,128)} %bitcast.32, s32[2,128]{1,0:T(2,128)} %bitcast.33, bf16[128,768]{1,0:T(8,128)(2,1)} %tok_ref.1, ...), custom_call_target="tpu_custom_call" | custom-call | tf_op jit(solution)/shard_map/pallas_call | solution.py:323
  8.7 10.3 %all-to-all-start = ((bf16[8,16,384]{2,1,0:T(8,128)(2,1)}), bf16[8,16,384]{2,1,0:T(8,128)(2,1)S(1)}, u32[]{:S(2)}, u32[]{:S(2)}) async-start(bf16[8,16,384]{2,1,0:T(8,128)(2,1)} %get-tuple-element.21), calls=%async_computation | async-start | bytes 196608 | tf_op jit(solution)/shard_map/all_to_all | solution.py:334
  21.0 2.3 %shard_map.74.near_hbm = bf16[768,512]{1,0:T(8,128)(2,1)} custom-call(bf16[512,768]{1,0:T(8,128)(2,1)} %bitcast.31), custom_call_target="tpu_custom_call" | custom-call | tf_op jit(solution)/shard_map/pallas_call | solution.py:335
  24.8 2.9 %collective-permute-start.3 = (bf16[768,512]{1,0:T(8,128)(2,1)S(1)}, bf16[768,512]{1,0:T(8,128)(2,1)S(1)}, u32[]{:S(2)}, u32[]{:S(2)}) collective-permute-start(bf16[768,512]{1,0:T(8,128)(2,1)S(1)} %bitcast.17), channel_id=1, source_target_pairs={{0,8},{8,16},{16,24},{24,0},{1,9},{9,17},{17,25},{25,1},{2,10},{10... | collective-permute-start | bytes 2359304 | tf_op jit(solution)/shard_map/ppermute | solution.py:291
  27.7 3.6 %collective-permute-start.4 = (bf16[768,512]{1,0:T(8,128)(2,1)S(1)}, bf16[768,512]{1,0:T(8,128)(2,1)S(1)}, u32[]{:S(2)}, u32[]{:S(2)}) collective-permute-start(bf16[768,512]{1,0:T(8,128)(2,1)S(1)} %bitcast.28), channel_id=1, source_target_pairs={{0,24},{8,0},{16,8},{24,16},{1,25},{9,1},{17,9},{25,17},{2,26},{10... | collective-permute-start | bytes 2359304 | tf_op jit(solution)/shard_map/ppermute | solution.py:292
  33.2 4.6 %collective-permute-start.6 = (bf16[768,512]{1,0:T(8,128)(2,1)S(1)}, bf16[768,512]{1,0:T(8,128)(2,1)}, u32[]{:S(2)}, u32[]{:S(2)}) collective-permute-start(bf16[768,512]{1,0:T(8,128)(2,1)S(1)} %bitcast.18), channel_id=1, source_target_pairs={{0,24},{8,0},{16,8},{24,16},{1,25},{9,1},{17,9},{25,17},{2,26},{10... | collective-permute-start | bytes 2359304 | tf_op jit(solution)/shard_map/ppermute | solution.py:294
  37.8 3.8 %collective-permute-start.1 = (bf16[768,512]{1,0:T(8,128)(2,1)S(1)}, bf16[768,512]{1,0:T(8,128)(2,1)S(1)}, u32[]{:S(2)}, u32[]{:S(2)}) collective-permute-start(bf16[768,512]{1,0:T(8,128)(2,1)S(1)} %bitcast.19), channel_id=1, source_target_pairs={{0,4},{4,0},{1,5},{5,1},{2,6},{6,2},{3,7},{7,3},{8,12},{12,8},{9,1... | collective-permute-start | bytes 2359304 | tf_op jit(solution)/shard_map/ppermute | solution.py:284
  41.6 4.6 %collective-permute-done.3.refs_5_.refs_6_ = bf16[768,512]{1,0:T(8,128)(2,1)S(1)} collective-permute-done((bf16[768,512]{1,0:T(8,128)(2,1)S(1)}, bf16[768,512]{1,0:T(8,128)(2,1)S(1)}, u32[]{:S(2)}, u32[]{:S(2)}) %collective-permute-start.3) | collective-permute-done | bytes 786464 | tf_op jit(solution)/shard_map/ppermute | solution.py:291
  46.2 4.8 %collective-permute-start.2 = (bf16[768,512]{1,0:T(8,128)(2,1)S(1)}, bf16[768,512]{1,0:T(8,128)(2,1)S(1)}, u32[]{:S(2)}, u32[]{:S(2)}) collective-permute-start(bf16[768,512]{1,0:T(8,128)(2,1)S(1)} %bitcast.30), channel_id=1, source_target_pairs={{0,4},{4,0},{1,5},{5,1},{2,6},{6,2},{3,7},{7,3},{8,12},{12,8},{9,1... | collective-permute-start | bytes 2359304 | tf_op jit(solution)/shard_map/ppermute | solution.py:284
  53.0 10.1 %collective-permute-done.5.refs_6_.refs_7_ = bf16[768,512]{1,0:T(8,128)(2,1)} collective-permute-done((bf16[768,512]{1,0:T(8,128)(2,1)S(1)}, bf16[768,512]{1,0:T(8,128)(2,1)}, u32[]{:S(2)}, u32[]{:S(2)}) %collective-permute-start.5) | collective-permute-done | bytes 786464 | tf_op jit(solution)/shard_map/ppermute | solution.py:293
  65.2 3.1 %collective-permute-start.11 = (bf16[768,512]{1,0:T(8,128)(2,1)S(1)}, bf16[768,512]{1,0:T(8,128)(2,1)}, u32[]{:S(2)}, u32[]{:S(2)}) collective-permute-start(bf16[768,512]{1,0:T(8,128)(2,1)S(1)} %collective-permute-done.3.refs_5_.refs_6_), channel_id=1, source_target_pairs={{0,8},{8,16},{16,24},{24,0},{1,9},{9,17},{17,25},{25,1},{2,10},{10... | collective-permute-start | bytes 2359304 | tf_op jit(solution)/shard_map/ppermute | solution.py:298
  68.3 3.4 %collective-permute-start.12 = (bf16[768,512]{1,0:T(8,128)(2,1)S(1)}, bf16[768,512]{1,0:T(8,128)(2,1)}, u32[]{:S(2)}, u32[]{:S(2)}) collective-permute-start(bf16[768,512]{1,0:T(8,128)(2,1)S(1)} %collective-permute-done.4.refs_8_.refs_9_), channel_id=1, source_target_pairs={{0,24},{8,0},{16,8},{24,16},{1,25},{9,1},{17,9},{25,17},{2,26},{10... | collective-permute-start | bytes 2359304 | tf_op jit(solution)/shard_map/ppermute | solution.py:299
  71.7 3.8 %collective-permute-start.10 = (bf16[768,512]{1,0:T(8,128)(2,1)S(1)}, bf16[768,512]{1,0:T(8,128)(2,1)S(1)}, u32[]{:S(2)}, u32[]{:S(2)}) collective-permute-start(bf16[768,512]{1,0:T(8,128)(2,1)S(1)} %collective-permute-done.4.refs_8_.refs_9_), channel_id=1, source_target_pairs={{0,4},{4,0},{1,5},{5,1},{2,6},{6,2},{3,7},{7,3},{8,12},{12,8},{9,1... | collective-permute-start | bytes 2359304 | tf_op jit(solution)/shard_map/ppermute | solution.py:284
  77.4 2.4 %collective-permute-start.8 = (bf16[768,512]{1,0:T(8,128)(2,1)}, bf16[768,512]{1,0:T(8,128)(2,1)}, u32[]{:S(2)}, u32[]{:S(2)}) collective-permute-start(bf16[768,512]{1,0:T(8,128)(2,1)} %collective-permute-done.5.refs_6_.refs_7_), channel_id=1, source_target_pairs={{0,4},{4,0},{1,5},{5,1},{2,6},{6,2},{3,7},{7,3},{8,12},{12,8},{9,1... | collective-permute-start | bytes 2359304 | tf_op jit(solution)/shard_map/ppermute | solution.py:284
  79.8 6.3 %collective-permute-done.11.refs_13_.refs_14_ = bf16[768,512]{1,0:T(8,128)(2,1)} collective-permute-done((bf16[768,512]{1,0:T(8,128)(2,1)S(1)}, bf16[768,512]{1,0:T(8,128)(2,1)}, u32[]{:S(2)}, u32[]{:S(2)}) %collective-permute-start.11) | collective-permute-done | bytes 786464 | tf_op jit(solution)/shard_map/ppermute | solution.py:298
  86.1 4.1 %collective-permute-start.9 = (bf16[768,512]{1,0:T(8,128)(2,1)}, bf16[768,512]{1,0:T(8,128)(2,1)}, u32[]{:S(2)}, u32[]{:S(2)}) collective-permute-start(bf16[768,512]{1,0:T(8,128)(2,1)} %collective-permute-done.6.refs_7_.refs_8_), channel_id=1, source_target_pairs={{0,4},{4,0},{1,5},{5,1},{2,6},{6,2},{3,7},{7,3},{8,12},{12,8},{9,1... | collective-permute-start | bytes 2359304 | tf_op jit(solution)/shard_map/ppermute | solution.py:284
  93.1 2.4 %collective-permute-start.14 = (bf16[768,512]{1,0:T(8,128)(2,1)}, bf16[768,512]{1,0:T(8,128)(2,1)}, u32[]{:S(2)}, u32[]{:S(2)}) collective-permute-start(bf16[768,512]{1,0:T(8,128)(2,1)} %collective-permute-done.12.refs_14_.refs_15_), channel_id=1, source_target_pairs={{0,4},{4,0},{1,5},{5,1},{2,6},{6,2},{3,7},{7,3},{8,12},{12,8},{9,1... | collective-permute-start | bytes 2359304 | tf_op jit(solution)/shard_map/ppermute | solution.py:284
  95.6 3.5 %shard_map.77 = bf16[4,128,512]{2,1,0:T(8,128)(2,1)} custom-call(bf16[16,17,16,384]{3,2,1,0:T(8,128)(2,1)} %bitcast.22, bf16[768,512]{1,0:T(8,128)(2,1)} %shard_map.74.near_hbm, bf16[768,512]{1,0:T(8,128)(2,1)} %copy-done.10), custom_call_target="tpu_custom_call" | custom-call | tf_op jit(solution)/shard_map/pallas_call | solution.py:352
  99.1 3.5 %all-to-all-start.1 = ((bf16[4,128,512]{2,1,0:T(8,128)(2,1)}), bf16[4,128,512]{2,1,0:T(8,128)(2,1)S(1)}, u32[]{:S(2)}, u32[]{:S(2)}) async-start(bf16[4,128,512]{2,1,0:T(8,128)(2,1)} %shard_map.77), calls=%async_computation.1 | async-start | bytes 1048576 | tf_op jit(solution)/shard_map/all_to_all | solution.py:363
  103.6 5.4 %shard_map.76.refs_0_ = f32[128,1024]{1,0:T(8,128)S(1)} custom-call(s32[1]{0:T(128)} %bitcast.10.x_ref, s32[1]{0:T(128)} %bitcast.4.core_ref, bf16[16,17,16,384]{3,2,1,0:T(8,128)(2,1)} %bitcast.23, bf16[768,512]{1,0:T(8,128)(2,1)S(1)} %bitcast.20, bf16[768,512]{1,0:T(8,128)(2,1)} %bitcast.26, bf16[768,512]{1,0:T(8,128)(2,1)} %copy-done.6, ...), custom_call_target="tpu_custom_call" | custom-call | tf_op jit(solution)/shard_map/pallas_call | solution.py:364
  109.5 7.5 %shard_map.78 = bf16[8,4,2,96,128]{4,3,2,1,0:T(8,128)(2,1)} custom-call(s32[1]{0:T(128)} %bitcast.10.x_ref, s32[1]{0:T(128)} %bitcast.4.core_ref, f32[128,1024]{1,0:T(8,128)S(1)} %shard_map.76.refs_0_, bf16[4,128,512]{2,1,0:T(8,128)(2,1)S(1)} %all-to-all-done.1.refs_1_, bf16[768,512]{1,0:T(8,128)(2,1)S(1)} %bitcast.21, bf16[768,512]{1,0:T(8,128)(2,1)} %bitcast.27, ...), custom_call_target="tpu_custom_call" | custom-call | tf_op jit(solution)/shard_map/pallas_call | solution.py:376
  117.0 15.0 %all-to-all-start.2 = ((bf16[64,96,128]{2,1,0:T(8,128)(2,1)}), bf16[64,96,128]{2,1,0:T(8,128)(2,1)S(1)}, u32[]{:S(2)}, u32[]{:S(2)}) async-start(bf16[64,96,128]{2,1,0:T(8,128)(2,1)} %bitcast.25), calls=%async_computation.2 | async-start | bytes 3145728 | tf_op jit(solution)/shard_map/all_to_all | solution.py:396
  132.8 22.7 %all-to-all-done.2 = bf16[64,96,128]{2,1,0:T(8,128)(2,1)S(1)} async-done(((bf16[64,96,128]{2,1,0:T(8,128)(2,1)}), bf16[64,96,128]{2,1,0:T(8,128)(2,1)S(1)}, u32[]{:S(2)}, u32[]{:S(2)}) %all-to-all-start.2) | async-done | bytes 1572896 | tf_op jit(solution)/shard_map/all_to_all | solution.py:396
  156.3 33.3 %all_to_all.20 = bf16[8,192,128]{2,1,0:T(8,128)(2,1)S(1)} all-to-all(bf16[8,192,128]{2,1,0:T(8,128)(2,1)S(1)} %shard_map.79), channel_id=1, replica_groups=mesh['zh'=8,'zl'=2,'x'=4,'c'=2,'y'=4] {'zh'}, dimensions={0} | all-to-all | bytes 786432 | tf_op jit(solution)/shard_map/all_to_all | solution.py:405
  (50 shorter events, 18.0 us)
Async XLA Ops:
  6.5 21.1 %copy-start.3 = (bf16[1,768,512]{2,1,0:T(8,128)(2,1)S(1)}, bf16[1,768,512]{2,1,0:T(8,128)(2,1)}, u32[]{:S(2)}) copy-start(bf16[1,768,512]{2,1,0:T(8,128)(2,1)} %param.12) | copy-start | bytes 2359300
  8.7 15.3 %all-to-all-start = ((bf16[8,16,384]{2,1,0:T(8,128)(2,1)}), bf16[8,16,384]{2,1,0:T(8,128)(2,1)S(1)}, u32[]{:S(2)}, u32[]{:S(2)}) async-start(bf16[8,16,384]{2,1,0:T(8,128)(2,1)} %get-tuple-element.21), calls=%async_computation | async-start | bytes 196608 | tf_op jit(solution)/shard_map/all_to_all | solution.py:334
  19.0 76.6 %all-gather.2.cloned.1.call-start = ((), (), s32[]{:S(2)}) async-start(), calls=%async_computation.4 | async-start | bytes 3551232 | tf_op jit(solution)/shard_map/all_gather | solution.py:346
  19.0 5.0 %collective-permute-start = (bf16[4,16,384]{2,1,0:T(8,128)(2,1)}, bf16[4,16,384]{2,1,0:T(8,128)(2,1)S(1)}, u32[]{:S(2)}, u32[]{:S(2)}) collective-permute-start(bf16[4,16,384]{2,1,0:T(8,128)(2,1)} %get-tuple-element.25), channel_id=1, source_target_pairs={{0,4},{4,0},{1,5},{5,1},{2,6},{6,2},{3,7},{7,3},{8,12},{12,8},{9,1... | collective-permute-start | bytes 147464 | tf_op jit(solution)/shard_map/ppermute | solution.py:284
  24.8 21.4 %collective-permute-start.3 = (bf16[768,512]{1,0:T(8,128)(2,1)S(1)}, bf16[768,512]{1,0:T(8,128)(2,1)S(1)}, u32[]{:S(2)}, u32[]{:S(2)}) collective-permute-start(bf16[768,512]{1,0:T(8,128)(2,1)S(1)} %bitcast.17), channel_id=1, source_target_pairs={{0,8},{8,16},{16,24},{24,0},{1,9},{9,17},{17,25},{25,1},{2,10},{10... | collective-permute-start | bytes 2359304 | tf_op jit(solution)/shard_map/ppermute | solution.py:291
  27.7 23.4 %collective-permute-start.4 = (bf16[768,512]{1,0:T(8,128)(2,1)S(1)}, bf16[768,512]{1,0:T(8,128)(2,1)S(1)}, u32[]{:S(2)}, u32[]{:S(2)}) collective-permute-start(bf16[768,512]{1,0:T(8,128)(2,1)S(1)} %bitcast.28), channel_id=1, source_target_pairs={{0,24},{8,0},{16,8},{24,16},{1,25},{9,1},{17,9},{25,17},{2,26},{10... | collective-permute-start | bytes 2359304 | tf_op jit(solution)/shard_map/ppermute | solution.py:292
  31.3 31.8 %collective-permute-start.5 = (bf16[768,512]{1,0:T(8,128)(2,1)S(1)}, bf16[768,512]{1,0:T(8,128)(2,1)}, u32[]{:S(2)}, u32[]{:S(2)}) collective-permute-start(bf16[768,512]{1,0:T(8,128)(2,1)S(1)} %bitcast.29), channel_id=1, source_target_pairs={{0,8},{8,16},{16,24},{24,0},{1,9},{9,17},{17,25},{25,1},{2,10},{10... | collective-permute-start | bytes 2359304 | tf_op jit(solution)/shard_map/ppermute | solution.py:293
  33.2 32.0 %collective-permute-start.6 = (bf16[768,512]{1,0:T(8,128)(2,1)S(1)}, bf16[768,512]{1,0:T(8,128)(2,1)}, u32[]{:S(2)}, u32[]{:S(2)}) collective-permute-start(bf16[768,512]{1,0:T(8,128)(2,1)S(1)} %bitcast.18), channel_id=1, source_target_pairs={{0,24},{8,0},{16,8},{24,16},{1,25},{9,1},{17,9},{25,17},{2,26},{10... | collective-permute-start | bytes 2359304 | tf_op jit(solution)/shard_map/ppermute | solution.py:294
  37.8 33.9 %collective-permute-start.1 = (bf16[768,512]{1,0:T(8,128)(2,1)S(1)}, bf16[768,512]{1,0:T(8,128)(2,1)S(1)}, u32[]{:S(2)}, u32[]{:S(2)}) collective-permute-start(bf16[768,512]{1,0:T(8,128)(2,1)S(1)} %bitcast.19), channel_id=1, source_target_pairs={{0,4},{4,0},{1,5},{5,1},{2,6},{6,2},{3,7},{7,3},{8,12},{12,8},{9,1... | collective-permute-start | bytes 2359304 | tf_op jit(solution)/shard_map/ppermute | solution.py:284
  46.2 52.9 %copy-start.4 = (bf16[768,512]{1,0:T(8,128)(2,1)}, bf16[768,512]{1,0:T(8,128)(2,1)S(1)}, u32[]{:S(2)}) copy-start(bf16[768,512]{1,0:T(8,128)(2,1)S(1)} %collective-permute-done.3.refs_5_.refs_6_) | copy-start | bytes 2359300
  46.2 29.3 %collective-permute-start.2 = (bf16[768,512]{1,0:T(8,128)(2,1)S(1)}, bf16[768,512]{1,0:T(8,128)(2,1)S(1)}, u32[]{:S(2)}, u32[]{:S(2)}) collective-permute-start(bf16[768,512]{1,0:T(8,128)(2,1)S(1)} %bitcast.30), channel_id=1, source_target_pairs={{0,4},{4,0},{1,5},{5,1},{2,6},{6,2},{3,7},{7,3},{8,12},{12,8},{9,1... | collective-permute-start | bytes 2359304 | tf_op jit(solution)/shard_map/ppermute | solution.py:284
  51.0 35.1 %copy-start.5 = (bf16[768,512]{1,0:T(8,128)(2,1)}, bf16[768,512]{1,0:T(8,128)(2,1)S(1)}, u32[]{:S(2)}) copy-start(bf16[768,512]{1,0:T(8,128)(2,1)S(1)} %collective-permute-done.4.refs_8_.refs_9_) | copy-start | bytes 2359300
  51.1 26.4 %collective-permute-start.15 = (bf16[768,512]{1,0:T(8,128)(2,1)}, bf16[768,512]{1,0:T(8,128)(2,1)S(1)}, u32[]{:S(2)}, u32[]{:S(2)}) collective-permute-start(bf16[768,512]{1,0:T(8,128)(2,1)} %shard_map.74.near_hbm), channel_id=1, source_target_pairs={{0,4},{4,0},{1,5},{5,1},{2,6},{6,2},{3,7},{7,3},{8,12},{12,8},{9,1... | collective-permute-start | bytes 2359304 | tf_op jit(solution)/shard_map/ppermute | solution.py:284
  65.2 21.0 %collective-permute-start.11 = (bf16[768,512]{1,0:T(8,128)(2,1)S(1)}, bf16[768,512]{1,0:T(8,128)(2,1)}, u32[]{:S(2)}, u32[]{:S(2)}) collective-permute-start(bf16[768,512]{1,0:T(8,128)(2,1)S(1)} %collective-permute-done.3.refs_5_.refs_6_), channel_id=1, source_target_pairs={{0,8},{8,16},{16,24},{24,0},{1,9},{9,17},{17,25},{25,1},{2,10},{10... | collective-permute-start | bytes 2359304 | tf_op jit(solution)/shard_map/ppermute | solution.py:298
  68.3 22.0 %collective-permute-start.12 = (bf16[768,512]{1,0:T(8,128)(2,1)S(1)}, bf16[768,512]{1,0:T(8,128)(2,1)}, u32[]{:S(2)}, u32[]{:S(2)}) collective-permute-start(bf16[768,512]{1,0:T(8,128)(2,1)S(1)} %collective-permute-done.4.refs_8_.refs_9_), channel_id=1, source_target_pairs={{0,24},{8,0},{16,8},{24,16},{1,25},{9,1},{17,9},{25,17},{2,26},{10... | collective-permute-start | bytes 2359304 | tf_op jit(solution)/shard_map/ppermute | solution.py:299
  71.7 20.5 %copy-start.6 = (bf16[768,512]{1,0:T(8,128)(2,1)}, bf16[768,512]{1,0:T(8,128)(2,1)S(1)}, u32[]{:S(2)}) copy-start(bf16[768,512]{1,0:T(8,128)(2,1)S(1)} %collective-permute-done.1.refs_3_.refs_4_) | copy-start | bytes 2359300
  71.7 20.5 %collective-permute-start.10 = (bf16[768,512]{1,0:T(8,128)(2,1)S(1)}, bf16[768,512]{1,0:T(8,128)(2,1)S(1)}, u32[]{:S(2)}, u32[]{:S(2)}) collective-permute-start(bf16[768,512]{1,0:T(8,128)(2,1)S(1)} %collective-permute-done.4.refs_8_.refs_9_), channel_id=1, source_target_pairs={{0,4},{4,0},{1,5},{5,1},{2,6},{6,2},{3,7},{7,3},{8,12},{12,8},{9,1... | collective-permute-start | bytes 2359304 | tf_op jit(solution)/shard_map/ppermute | solution.py:284
  75.5 27.1 %collective-permute-start.7 = (bf16[768,512]{1,0:T(8,128)(2,1)S(1)}, bf16[768,512]{1,0:T(8,128)(2,1)S(1)}, u32[]{:S(2)}, u32[]{:S(2)}) collective-permute-start(bf16[768,512]{1,0:T(8,128)(2,1)S(1)} %collective-permute-done.3.refs_5_.refs_6_), channel_id=1, source_target_pairs={{0,4},{4,0},{1,5},{5,1},{2,6},{6,2},{3,7},{7,3},{8,12},{12,8},{9,1... | collective-permute-start | bytes 2359304 | tf_op jit(solution)/shard_map/ppermute | solution.py:284
  77.4 25.2 %collective-permute-start.8 = (bf16[768,512]{1,0:T(8,128)(2,1)}, bf16[768,512]{1,0:T(8,128)(2,1)}, u32[]{:S(2)}, u32[]{:S(2)}) collective-permute-start(bf16[768,512]{1,0:T(8,128)(2,1)} %collective-permute-done.5.refs_6_.refs_7_), channel_id=1, source_target_pairs={{0,4},{4,0},{1,5},{5,1},{2,6},{6,2},{3,7},{7,3},{8,12},{12,8},{9,1... | collective-permute-start | bytes 2359304 | tf_op jit(solution)/shard_map/ppermute | solution.py:284
  86.1 16.5 %collective-permute-start.9 = (bf16[768,512]{1,0:T(8,128)(2,1)}, bf16[768,512]{1,0:T(8,128)(2,1)}, u32[]{:S(2)}, u32[]{:S(2)}) collective-permute-start(bf16[768,512]{1,0:T(8,128)(2,1)} %collective-permute-done.6.refs_7_.refs_8_), channel_id=1, source_target_pairs={{0,4},{4,0},{1,5},{5,1},{2,6},{6,2},{3,7},{7,3},{8,12},{12,8},{9,1... | collective-permute-start | bytes 2359304 | tf_op jit(solution)/shard_map/ppermute | solution.py:284
  90.3 12.4 %collective-permute-start.13 = (bf16[768,512]{1,0:T(8,128)(2,1)}, bf16[768,512]{1,0:T(8,128)(2,1)}, u32[]{:S(2)}, u32[]{:S(2)}) collective-permute-start(bf16[768,512]{1,0:T(8,128)(2,1)} %collective-permute-done.11.refs_13_.refs_14_), channel_id=1, source_target_pairs={{0,4},{4,0},{1,5},{5,1},{2,6},{6,2},{3,7},{7,3},{8,12},{12,8},{9,1... | collective-permute-start | bytes 2359304 | tf_op jit(solution)/shard_map/ppermute | solution.py:284
  93.1 9.5 %collective-permute-start.14 = (bf16[768,512]{1,0:T(8,128)(2,1)}, bf16[768,512]{1,0:T(8,128)(2,1)}, u32[]{:S(2)}, u32[]{:S(2)}) collective-permute-start(bf16[768,512]{1,0:T(8,128)(2,1)} %collective-permute-done.12.refs_14_.refs_15_), channel_id=1, source_target_pairs={{0,4},{4,0},{1,5},{5,1},{2,6},{6,2},{3,7},{7,3},{8,12},{12,8},{9,1... | collective-permute-start | bytes 2359304 | tf_op jit(solution)/shard_map/ppermute | solution.py:284
  99.1 10.4 %all-to-all-start.1 = ((bf16[4,128,512]{2,1,0:T(8,128)(2,1)}), bf16[4,128,512]{2,1,0:T(8,128)(2,1)S(1)}, u32[]{:S(2)}, u32[]{:S(2)}) async-start(bf16[4,128,512]{2,1,0:T(8,128)(2,1)} %shard_map.77), calls=%async_computation.1 | async-start | bytes 1048576 | tf_op jit(solution)/shard_map/all_to_all | solution.py:363
  117.0 38.5 %all-to-all-start.2 = ((bf16[64,96,128]{2,1,0:T(8,128)(2,1)}), bf16[64,96,128]{2,1,0:T(8,128)(2,1)S(1)}, u32[]{:S(2)}, u32[]{:S(2)}) async-start(bf16[64,96,128]{2,1,0:T(8,128)(2,1)} %bitcast.25), calls=%async_computation.2 | async-start | bytes 3145728 | tf_op jit(solution)/shard_map/all_to_all | solution.py:396
  (7 other events, 85.5 us)
Sparse Core Ops, SparseCore 0:
  24.9 67.5 all-gather.1

commit v14 on v13

--- a/solution.py
+++ b/solution.py
@@ -15,6 +15,7 @@
 contract_first = (((0,), (0,)), ((), ()))
 vmem_bytes = 56 * 1024 * 1024
 late_vmem_bytes = 52 * 1024 * 1024
+result_vmem_bytes = 50 * 1024 * 1024
 small_vmem_bytes = 16 * 1024 * 1024
 blocks_at = ((0, 0), (0, 1), (-1, 0), (1, 0), (-1, 1), (1, 1), (2, 0), (2, 1))
 
@@ -384,7 +385,7 @@
             pltpu.SemaphoreType.DMA((len(blocks_at),)),
         ],
         anywhere,
-        late_vmem_bytes,
+        result_vmem_bytes,
     )(x, core, sums, back, *weights)
     tables = lax.dynamic_index_in_dim(
         rows.reshape(n_high, 2, groups, 2 * part, half)[:, :, groups - 1, :, :count],

time: 198 us -> 197 us (level)
  no operation moved by 1% of the time
where the time goes in v14:
time: 197 us; the launch traced here: 196 us
  starting transfers between devices  76.9 us (39%)
  waiting for transfers between devices  47.6 us (24%)
  blocking collectives  33.3 us (17%)
  Pallas kernels  21.8 us (11%)
  between operations  13.8 us (7%)
    all_to_all x1, blocking collectives, per_device(): dense = lax.all_to_all(dense, 'zh', 0, 0, tiled=True)  33.3 us
    ppermute x10, starting transfers between devices, swap(): return lax.ppermute(value, 'c', [(0, 1), (1, 0)])  29.2 us
    all_to_all x1, waiting for transfers between devices, per_device(): lax.all_to_all(result.reshape(n_s * window * 2, *shape[3:]), ('x', 'c', '...  22.7 us
    all_to_all x1, starting transfers between devices, per_device(): lax.all_to_all(result.reshape(n_s * window * 2, *shape[3:]), ('x', 'c', '...  14.4 us
    all_to_all x1, starting transfers between devices, per_device(): pieces = lax.all_to_all(pieces, ('x', 'c'), 0, 0, tiled=True)  10.3 us
    ppermute x1, waiting for transfers between devices, gather_weights(): up_before = lax.ppermute(up, 'x', ahead)  10.1 us
    pallas_call x1, Pallas kernels, per_device(): kernel_call(result_kernel, jax.ShapeDtypeStruct(result_shape, bf16), [sme...  6.89 us
    ppermute x1, waiting for transfers between devices, gather_weights(): gate_across = lax.ppermute(gate_before, 'x', ahead)  6.23 us
  transfers between devices with their start and end apart: 20, of which 7 were waited for; matrix products, arithmetic and copies ran while one was open for 0% of the time, Pallas kernels for 6%

profile of v14, /device:TPU:1, one launch (start us, length us, event | category | flops | bytes accessed | tf_op | source)
XLA Modules:
  0.0 195.8 jit_solution(16817387650792050923)
XLA Ops:
  6.5 2.1 %shard_map.73 = (bf16[8,16,384]{2,1,0:T(8,128)(2,1)}, bf16[4,16,384]{2,1,0:T(8,128)(2,1)}, bf16[4,16,384]{2,1,0:T(8,128)(2,1)}, bf16[1,16,384]{2,1,0:T(8,128)(2,1)}) custom-call(s32[1]{0:T(128)} %bitcast.3.expert_ref, s32[1]{0:T(128)} %bitcast.4.core_ref, s32[2,128]{1,0:T(2,128)} %bitcast.32, s32[2,128]{1,0:T(2,128)} %bitcast.33, bf16[128,768]{1,0:T(8,128)(2,1)} %tok_ref.1, ...), custom_call_target="tpu_custom_call" | custom-call | tf_op jit(solution)/shard_map/pallas_call | solution.py:324
  8.7 10.3 %all-to-all-start = ((bf16[8,16,384]{2,1,0:T(8,128)(2,1)}), bf16[8,16,384]{2,1,0:T(8,128)(2,1)S(1)}, u32[]{:S(2)}, u32[]{:S(2)}) async-start(bf16[8,16,384]{2,1,0:T(8,128)(2,1)} %get-tuple-element.21), calls=%async_computation | async-start | bytes 196608 | tf_op jit(solution)/shard_map/all_to_all | solution.py:335
  21.0 2.3 %shard_map.74.near_hbm = bf16[768,512]{1,0:T(8,128)(2,1)} custom-call(bf16[512,768]{1,0:T(8,128)(2,1)} %bitcast.31), custom_call_target="tpu_custom_call" | custom-call | tf_op jit(solution)/shard_map/pallas_call | solution.py:336
  24.7 2.8 %collective-permute-start.3 = (bf16[768,512]{1,0:T(8,128)(2,1)S(1)}, bf16[768,512]{1,0:T(8,128)(2,1)S(1)}, u32[]{:S(2)}, u32[]{:S(2)}) collective-permute-start(bf16[768,512]{1,0:T(8,128)(2,1)S(1)} %bitcast.17), channel_id=1, source_target_pairs={{0,8},{8,16},{16,24},{24,0},{1,9},{9,17},{17,25},{25,1},{2,10},{10... | collective-permute-start | bytes 2359304 | tf_op jit(solution)/shard_map/ppermute | solution.py:292
  27.6 3.6 %collective-permute-start.4 = (bf16[768,512]{1,0:T(8,128)(2,1)S(1)}, bf16[768,512]{1,0:T(8,128)(2,1)S(1)}, u32[]{:S(2)}, u32[]{:S(2)}) collective-permute-start(bf16[768,512]{1,0:T(8,128)(2,1)S(1)} %bitcast.23), channel_id=1, source_target_pairs={{0,24},{8,0},{16,8},{24,16},{1,25},{9,1},{17,9},{25,17},{2,26},{10... | collective-permute-start | bytes 2359304 | tf_op jit(solution)/shard_map/ppermute | solution.py:293
  33.2 4.6 %collective-permute-start.6 = (bf16[768,512]{1,0:T(8,128)(2,1)S(1)}, bf16[768,512]{1,0:T(8,128)(2,1)}, u32[]{:S(2)}, u32[]{:S(2)}) collective-permute-start(bf16[768,512]{1,0:T(8,128)(2,1)S(1)} %bitcast.18), channel_id=1, source_target_pairs={{0,24},{8,0},{16,8},{24,16},{1,25},{9,1},{17,9},{25,17},{2,26},{10... | collective-permute-start | bytes 2359304 | tf_op jit(solution)/shard_map/ppermute | solution.py:295
  37.8 3.8 %collective-permute-start.1 = (bf16[768,512]{1,0:T(8,128)(2,1)S(1)}, bf16[768,512]{1,0:T(8,128)(2,1)S(1)}, u32[]{:S(2)}, u32[]{:S(2)}) collective-permute-start(bf16[768,512]{1,0:T(8,128)(2,1)S(1)} %bitcast.19), channel_id=1, source_target_pairs={{0,4},{4,0},{1,5},{5,1},{2,6},{6,2},{3,7},{7,3},{8,12},{12,8},{9,1... | collective-permute-start | bytes 2359304 | tf_op jit(solution)/shard_map/ppermute | solution.py:285
  41.6 4.5 %collective-permute-done.3.refs_5_.refs_6_ = bf16[768,512]{1,0:T(8,128)(2,1)S(1)} collective-permute-done((bf16[768,512]{1,0:T(8,128)(2,1)S(1)}, bf16[768,512]{1,0:T(8,128)(2,1)S(1)}, u32[]{:S(2)}, u32[]{:S(2)}) %collective-permute-start.3) | collective-permute-done | bytes 786464 | tf_op jit(solution)/shard_map/ppermute | solution.py:292
  46.2 4.9 %collective-permute-start.2 = (bf16[768,512]{1,0:T(8,128)(2,1)S(1)}, bf16[768,512]{1,0:T(8,128)(2,1)S(1)}, u32[]{:S(2)}, u32[]{:S(2)}) collective-permute-start(bf16[768,512]{1,0:T(8,128)(2,1)S(1)} %bitcast.25), channel_id=1, source_target_pairs={{0,4},{4,0},{1,5},{5,1},{2,6},{6,2},{3,7},{7,3},{8,12},{12,8},{9,1... | collective-permute-start | bytes 2359304 | tf_op jit(solution)/shard_map/ppermute | solution.py:285
  53.0 10.1 %collective-permute-done.5.refs_6_.refs_7_ = bf16[768,512]{1,0:T(8,128)(2,1)} collective-permute-done((bf16[768,512]{1,0:T(8,128)(2,1)S(1)}, bf16[768,512]{1,0:T(8,128)(2,1)}, u32[]{:S(2)}, u32[]{:S(2)}) %collective-permute-start.5) | collective-permute-done | bytes 786464 | tf_op jit(solution)/shard_map/ppermute | solution.py:294
  65.1 3.1 %collective-permute-start.11 = (bf16[768,512]{1,0:T(8,128)(2,1)S(1)}, bf16[768,512]{1,0:T(8,128)(2,1)}, u32[]{:S(2)}, u32[]{:S(2)}) collective-permute-start(bf16[768,512]{1,0:T(8,128)(2,1)S(1)} %collective-permute-done.3.refs_5_.refs_6_), channel_id=1, source_target_pairs={{0,8},{8,16},{16,24},{24,0},{1,9},{9,17},{17,25},{25,1},{2,10},{10... | collective-permute-start | bytes 2359304 | tf_op jit(solution)/shard_map/ppermute | solution.py:299
  68.2 3.4 %collective-permute-start.12 = (bf16[768,512]{1,0:T(8,128)(2,1)S(1)}, bf16[768,512]{1,0:T(8,128)(2,1)}, u32[]{:S(2)}, u32[]{:S(2)}) collective-permute-start(bf16[768,512]{1,0:T(8,128)(2,1)S(1)} %collective-permute-done.4.refs_8_.refs_9_), channel_id=1, source_target_pairs={{0,24},{8,0},{16,8},{24,16},{1,25},{9,1},{17,9},{25,17},{2,26},{10... | collective-permute-start | bytes 2359304 | tf_op jit(solution)/shard_map/ppermute | solution.py:300
  71.6 3.8 %collective-permute-start.10 = (bf16[768,512]{1,0:T(8,128)(2,1)S(1)}, bf16[768,512]{1,0:T(8,128)(2,1)S(1)}, u32[]{:S(2)}, u32[]{:S(2)}) collective-permute-start(bf16[768,512]{1,0:T(8,128)(2,1)S(1)} %collective-permute-done.4.refs_8_.refs_9_), channel_id=1, source_target_pairs={{0,4},{4,0},{1,5},{5,1},{2,6},{6,2},{3,7},{7,3},{8,12},{12,8},{9,1... | collective-permute-start | bytes 2359304 | tf_op jit(solution)/shard_map/ppermute | solution.py:285
  77.4 2.4 %collective-permute-start.8 = (bf16[768,512]{1,0:T(8,128)(2,1)}, bf16[768,512]{1,0:T(8,128)(2,1)}, u32[]{:S(2)}, u32[]{:S(2)}) collective-permute-start(bf16[768,512]{1,0:T(8,128)(2,1)} %collective-permute-done.5.refs_6_.refs_7_), channel_id=1, source_target_pairs={{0,4},{4,0},{1,5},{5,1},{2,6},{6,2},{3,7},{7,3},{8,12},{12,8},{9,1... | collective-permute-start | bytes 2359304 | tf_op jit(solution)/shard_map/ppermute | solution.py:285
  79.8 6.2 %collective-permute-done.11.refs_13_.refs_14_ = bf16[768,512]{1,0:T(8,128)(2,1)} collective-permute-done((bf16[768,512]{1,0:T(8,128)(2,1)S(1)}, bf16[768,512]{1,0:T(8,128)(2,1)}, u32[]{:S(2)}, u32[]{:S(2)}) %collective-permute-start.11) | collective-permute-done | bytes 786464 | tf_op jit(solution)/shard_map/ppermute | solution.py:299
  86.0 4.1 %collective-permute-start.9 = (bf16[768,512]{1,0:T(8,128)(2,1)}, bf16[768,512]{1,0:T(8,128)(2,1)}, u32[]{:S(2)}, u32[]{:S(2)}) collective-permute-start(bf16[768,512]{1,0:T(8,128)(2,1)} %collective-permute-done.6.refs_7_.refs_8_), channel_id=1, source_target_pairs={{0,4},{4,0},{1,5},{5,1},{2,6},{6,2},{3,7},{7,3},{8,12},{12,8},{9,1... | collective-permute-start | bytes 2359304 | tf_op jit(solution)/shard_map/ppermute | solution.py:285
  93.0 2.4 %collective-permute-start.14 = (bf16[768,512]{1,0:T(8,128)(2,1)}, bf16[768,512]{1,0:T(8,128)(2,1)}, u32[]{:S(2)}, u32[]{:S(2)}) collective-permute-start(bf16[768,512]{1,0:T(8,128)(2,1)} %collective-permute-done.12.refs_14_.refs_15_), channel_id=1, source_target_pairs={{0,4},{4,0},{1,5},{5,1},{2,6},{6,2},{3,7},{7,3},{8,12},{12,8},{9,1... | collective-permute-start | bytes 2359304 | tf_op jit(solution)/shard_map/ppermute | solution.py:285
  95.5 3.5 %shard_map.77 = bf16[4,128,512]{2,1,0:T(8,128)(2,1)} custom-call(bf16[16,17,16,384]{3,2,1,0:T(8,128)(2,1)} %bitcast.27, bf16[768,512]{1,0:T(8,128)(2,1)} %shard_map.74.near_hbm, bf16[768,512]{1,0:T(8,128)(2,1)} %copy-done.11), custom_call_target="tpu_custom_call" | custom-call | tf_op jit(solution)/shard_map/pallas_call | solution.py:353
  99.0 3.5 %all-to-all-start.1 = ((bf16[4,128,512]{2,1,0:T(8,128)(2,1)}), bf16[4,128,512]{2,1,0:T(8,128)(2,1)S(1)}, u32[]{:S(2)}, u32[]{:S(2)}) async-start(bf16[4,128,512]{2,1,0:T(8,128)(2,1)} %shard_map.77), calls=%async_computation.1 | async-start | bytes 1048576 | tf_op jit(solution)/shard_map/all_to_all | solution.py:364
  102.6 5.5 %shard_map.76.refs_0_ = f32[128,1024]{1,0:T(8,128)S(1)} custom-call(s32[1]{0:T(128)} %bitcast.10.x_ref, s32[1]{0:T(128)} %bitcast.4.core_ref, bf16[16,17,16,384]{3,2,1,0:T(8,128)(2,1)} %bitcast.28, bf16[768,512]{1,0:T(8,128)(2,1)S(1)} %bitcast.20, bf16[768,512]{1,0:T(8,128)(2,1)} %bitcast.22, bf16[768,512]{1,0:T(8,128)(2,1)} %copy-done.3, ...), custom_call_target="tpu_custom_call" | custom-call | tf_op jit(solution)/shard_map/pallas_call | solution.py:365
  109.4 6.9 %shard_map.78 = bf16[8,4,2,96,128]{4,3,2,1,0:T(8,128)(2,1)} custom-call(s32[1]{0:T(128)} %bitcast.10.x_ref, s32[1]{0:T(128)} %bitcast.4.core_ref, f32[128,1024]{1,0:T(8,128)S(1)} %shard_map.76.refs_0_, bf16[4,128,512]{2,1,0:T(8,128)(2,1)S(1)} %all-to-all-done.1.refs_1_, bf16[768,512]{1,0:T(8,128)(2,1)S(1)} %bitcast.21, bf16[768,512]{1,0:T(8,128)(2,1)S(1)} %bitcast.26, ...), custom_call_target="tpu_custom_call" | custom-call | tf_op jit(solution)/shard_map/pallas_call | solution.py:377
  116.3 14.4 %all-to-all-start.2 = ((bf16[64,96,128]{2,1,0:T(8,128)(2,1)}), bf16[64,96,128]{2,1,0:T(8,128)(2,1)S(1)}, u32[]{:S(2)}, u32[]{:S(2)}) async-start(bf16[64,96,128]{2,1,0:T(8,128)(2,1)} %bitcast.30), calls=%async_computation.2 | async-start | bytes 3145728 | tf_op jit(solution)/shard_map/all_to_all | solution.py:397
  131.5 22.7 %all-to-all-done.2 = bf16[64,96,128]{2,1,0:T(8,128)(2,1)S(1)} async-done(((bf16[64,96,128]{2,1,0:T(8,128)(2,1)}), bf16[64,96,128]{2,1,0:T(8,128)(2,1)S(1)}, u32[]{:S(2)}, u32[]{:S(2)}) %all-to-all-start.2) | async-done | bytes 1572896 | tf_op jit(solution)/shard_map/all_to_all | solution.py:397
  155.0 33.3 %all_to_all.20 = bf16[8,192,128]{2,1,0:T(8,128)(2,1)S(1)} all-to-all(bf16[8,192,128]{2,1,0:T(8,128)(2,1)S(1)} %shard_map.79), channel_id=1, replica_groups=mesh['zh'=8,'zl'=2,'x'=4,'c'=2,'y'=4] {'zh'}, dimensions={0} | all-to-all | bytes 786432 | tf_op jit(solution)/shard_map/all_to_all | solution.py:406
  (52 shorter events, 17.8 us)
Async XLA Ops:
  6.5 21.1 %copy-start.1 = (bf16[1,768,512]{2,1,0:T(8,128)(2,1)S(1)}, bf16[1,768,512]{2,1,0:T(8,128)(2,1)}, u32[]{:S(2)}) copy-start(bf16[1,768,512]{2,1,0:T(8,128)(2,1)} %param.12) | copy-start | bytes 2359300
  8.7 15.3 %all-to-all-start = ((bf16[8,16,384]{2,1,0:T(8,128)(2,1)}), bf16[8,16,384]{2,1,0:T(8,128)(2,1)S(1)}, u32[]{:S(2)}, u32[]{:S(2)}) async-start(bf16[8,16,384]{2,1,0:T(8,128)(2,1)} %get-tuple-element.21), calls=%async_computation | async-start | bytes 196608 | tf_op jit(solution)/shard_map/all_to_all | solution.py:335
  19.0 76.5 %all-gather.2.cloned.1.call-start = ((), (), s32[]{:S(2)}) async-start(), calls=%async_computation.4 | async-start | bytes 3551232 | tf_op jit(solution)/shard_map/all_gather | solution.py:347
  19.0 5.0 %collective-permute-start = (bf16[4,16,384]{2,1,0:T(8,128)(2,1)}, bf16[4,16,384]{2,1,0:T(8,128)(2,1)S(1)}, u32[]{:S(2)}, u32[]{:S(2)}) collective-permute-start(bf16[4,16,384]{2,1,0:T(8,128)(2,1)} %get-tuple-element.25), channel_id=1, source_target_pairs={{0,4},{4,0},{1,5},{5,1},{2,6},{6,2},{3,7},{7,3},{8,12},{12,8},{9,1... | collective-permute-start | bytes 147464 | tf_op jit(solution)/shard_map/ppermute | solution.py:285
  24.7 21.4 %collective-permute-start.3 = (bf16[768,512]{1,0:T(8,128)(2,1)S(1)}, bf16[768,512]{1,0:T(8,128)(2,1)S(1)}, u32[]{:S(2)}, u32[]{:S(2)}) collective-permute-start(bf16[768,512]{1,0:T(8,128)(2,1)S(1)} %bitcast.17), channel_id=1, source_target_pairs={{0,8},{8,16},{16,24},{24,0},{1,9},{9,17},{17,25},{25,1},{2,10},{10... | collective-permute-start | bytes 2359304 | tf_op jit(solution)/shard_map/ppermute | solution.py:292
  27.6 23.4 %collective-permute-start.4 = (bf16[768,512]{1,0:T(8,128)(2,1)S(1)}, bf16[768,512]{1,0:T(8,128)(2,1)S(1)}, u32[]{:S(2)}, u32[]{:S(2)}) collective-permute-start(bf16[768,512]{1,0:T(8,128)(2,1)S(1)} %bitcast.23), channel_id=1, source_target_pairs={{0,24},{8,0},{16,8},{24,16},{1,25},{9,1},{17,9},{25,17},{2,26},{10... | collective-permute-start | bytes 2359304 | tf_op jit(solution)/shard_map/ppermute | solution.py:293
  31.3 31.8 %collective-permute-start.5 = (bf16[768,512]{1,0:T(8,128)(2,1)S(1)}, bf16[768,512]{1,0:T(8,128)(2,1)}, u32[]{:S(2)}, u32[]{:S(2)}) collective-permute-start(bf16[768,512]{1,0:T(8,128)(2,1)S(1)} %bitcast.24), channel_id=1, source_target_pairs={{0,8},{8,16},{16,24},{24,0},{1,9},{9,17},{17,25},{25,1},{2,10},{10... | collective-permute-start | bytes 2359304 | tf_op jit(solution)/shard_map/ppermute | solution.py:294
  33.2 31.9 %collective-permute-start.6 = (bf16[768,512]{1,0:T(8,128)(2,1)S(1)}, bf16[768,512]{1,0:T(8,128)(2,1)}, u32[]{:S(2)}, u32[]{:S(2)}) collective-permute-start(bf16[768,512]{1,0:T(8,128)(2,1)S(1)} %bitcast.18), channel_id=1, source_target_pairs={{0,24},{8,0},{16,8},{24,16},{1,25},{9,1},{17,9},{25,17},{2,26},{10... | collective-permute-start | bytes 2359304 | tf_op jit(solution)/shard_map/ppermute | solution.py:295
  37.8 33.8 %collective-permute-start.1 = (bf16[768,512]{1,0:T(8,128)(2,1)S(1)}, bf16[768,512]{1,0:T(8,128)(2,1)S(1)}, u32[]{:S(2)}, u32[]{:S(2)}) collective-permute-start(bf16[768,512]{1,0:T(8,128)(2,1)S(1)} %bitcast.19), channel_id=1, source_target_pairs={{0,4},{4,0},{1,5},{5,1},{2,6},{6,2},{3,7},{7,3},{8,12},{12,8},{9,1... | collective-permute-start | bytes 2359304 | tf_op jit(solution)/shard_map/ppermute | solution.py:285
  46.2 52.8 %copy-start.7 = (bf16[768,512]{1,0:T(8,128)(2,1)}, bf16[768,512]{1,0:T(8,128)(2,1)S(1)}, u32[]{:S(2)}) copy-start(bf16[768,512]{1,0:T(8,128)(2,1)S(1)} %collective-permute-done.3.refs_5_.refs_6_) | copy-start | bytes 2359300
  46.2 29.3 %collective-permute-start.2 = (bf16[768,512]{1,0:T(8,128)(2,1)S(1)}, bf16[768,512]{1,0:T(8,128)(2,1)S(1)}, u32[]{:S(2)}, u32[]{:S(2)}) collective-permute-start(bf16[768,512]{1,0:T(8,128)(2,1)S(1)} %bitcast.25), channel_id=1, source_target_pairs={{0,4},{4,0},{1,5},{5,1},{2,6},{6,2},{3,7},{7,3},{8,12},{12,8},{9,1... | collective-permute-start | bytes 2359304 | tf_op jit(solution)/shard_map/ppermute | solution.py:285
  51.0 35.0 %copy-start.8 = (bf16[768,512]{1,0:T(8,128)(2,1)}, bf16[768,512]{1,0:T(8,128)(2,1)S(1)}, u32[]{:S(2)}) copy-start(bf16[768,512]{1,0:T(8,128)(2,1)S(1)} %collective-permute-done.4.refs_8_.refs_9_) | copy-start | bytes 2359300
  51.0 26.3 %collective-permute-start.15 = (bf16[768,512]{1,0:T(8,128)(2,1)}, bf16[768,512]{1,0:T(8,128)(2,1)S(1)}, u32[]{:S(2)}, u32[]{:S(2)}) collective-permute-start(bf16[768,512]{1,0:T(8,128)(2,1)} %shard_map.74.near_hbm), channel_id=1, source_target_pairs={{0,4},{4,0},{1,5},{5,1},{2,6},{6,2},{3,7},{7,3},{8,12},{12,8},{9,1... | collective-permute-start | bytes 2359304 | tf_op jit(solution)/shard_map/ppermute | solution.py:285
  65.1 20.9 %collective-permute-start.11 = (bf16[768,512]{1,0:T(8,128)(2,1)S(1)}, bf16[768,512]{1,0:T(8,128)(2,1)}, u32[]{:S(2)}, u32[]{:S(2)}) collective-permute-start(bf16[768,512]{1,0:T(8,128)(2,1)S(1)} %collective-permute-done.3.refs_5_.refs_6_), channel_id=1, source_target_pairs={{0,8},{8,16},{16,24},{24,0},{1,9},{9,17},{17,25},{25,1},{2,10},{10... | collective-permute-start | bytes 2359304 | tf_op jit(solution)/shard_map/ppermute | solution.py:299
  68.2 21.9 %collective-permute-start.12 = (bf16[768,512]{1,0:T(8,128)(2,1)S(1)}, bf16[768,512]{1,0:T(8,128)(2,1)}, u32[]{:S(2)}, u32[]{:S(2)}) collective-permute-start(bf16[768,512]{1,0:T(8,128)(2,1)S(1)} %collective-permute-done.4.refs_8_.refs_9_), channel_id=1, source_target_pairs={{0,24},{8,0},{16,8},{24,16},{1,25},{9,1},{17,9},{25,17},{2,26},{10... | collective-permute-start | bytes 2359304 | tf_op jit(solution)/shard_map/ppermute | solution.py:300
  71.6 27.4 %copy-start.3 = (bf16[768,512]{1,0:T(8,128)(2,1)}, bf16[768,512]{1,0:T(8,128)(2,1)S(1)}, u32[]{:S(2)}) copy-start(bf16[768,512]{1,0:T(8,128)(2,1)S(1)} %collective-permute-done.1.refs_3_.refs_4_) | copy-start | bytes 2359300
  71.6 20.5 %collective-permute-start.10 = (bf16[768,512]{1,0:T(8,128)(2,1)S(1)}, bf16[768,512]{1,0:T(8,128)(2,1)S(1)}, u32[]{:S(2)}, u32[]{:S(2)}) collective-permute-start(bf16[768,512]{1,0:T(8,128)(2,1)S(1)} %collective-permute-done.4.refs_8_.refs_9_), channel_id=1, source_target_pairs={{0,4},{4,0},{1,5},{5,1},{2,6},{6,2},{3,7},{7,3},{8,12},{12,8},{9,1... | collective-permute-start | bytes 2359304 | tf_op jit(solution)/shard_map/ppermute | solution.py:285
  75.4 27.1 %collective-permute-start.7 = (bf16[768,512]{1,0:T(8,128)(2,1)S(1)}, bf16[768,512]{1,0:T(8,128)(2,1)}, u32[]{:S(2)}, u32[]{:S(2)}) collective-permute-start(bf16[768,512]{1,0:T(8,128)(2,1)S(1)} %collective-permute-done.3.refs_5_.refs_6_), channel_id=1, source_target_pairs={{0,4},{4,0},{1,5},{5,1},{2,6},{6,2},{3,7},{7,3},{8,12},{12,8},{9,1... | collective-permute-start | bytes 2359304 | tf_op jit(solution)/shard_map/ppermute | solution.py:285
  77.4 25.1 %collective-permute-start.8 = (bf16[768,512]{1,0:T(8,128)(2,1)}, bf16[768,512]{1,0:T(8,128)(2,1)}, u32[]{:S(2)}, u32[]{:S(2)}) collective-permute-start(bf16[768,512]{1,0:T(8,128)(2,1)} %collective-permute-done.5.refs_6_.refs_7_), channel_id=1, source_target_pairs={{0,4},{4,0},{1,5},{5,1},{2,6},{6,2},{3,7},{7,3},{8,12},{12,8},{9,1... | collective-permute-start | bytes 2359304 | tf_op jit(solution)/shard_map/ppermute | solution.py:285
  86.0 16.5 %collective-permute-start.9 = (bf16[768,512]{1,0:T(8,128)(2,1)}, bf16[768,512]{1,0:T(8,128)(2,1)}, u32[]{:S(2)}, u32[]{:S(2)}) collective-permute-start(bf16[768,512]{1,0:T(8,128)(2,1)} %collective-permute-done.6.refs_7_.refs_8_), channel_id=1, source_target_pairs={{0,4},{4,0},{1,5},{5,1},{2,6},{6,2},{3,7},{7,3},{8,12},{12,8},{9,1... | collective-permute-start | bytes 2359304 | tf_op jit(solution)/shard_map/ppermute | solution.py:285
  90.2 12.3 %collective-permute-start.13 = (bf16[768,512]{1,0:T(8,128)(2,1)}, bf16[768,512]{1,0:T(8,128)(2,1)}, u32[]{:S(2)}, u32[]{:S(2)}) collective-permute-start(bf16[768,512]{1,0:T(8,128)(2,1)} %collective-permute-done.11.refs_13_.refs_14_), channel_id=1, source_target_pairs={{0,4},{4,0},{1,5},{5,1},{2,6},{6,2},{3,7},{7,3},{8,12},{12,8},{9,1... | collective-permute-start | bytes 2359304 | tf_op jit(solution)/shard_map/ppermute | solution.py:285
  93.0 9.5 %collective-permute-start.14 = (bf16[768,512]{1,0:T(8,128)(2,1)}, bf16[768,512]{1,0:T(8,128)(2,1)}, u32[]{:S(2)}, u32[]{:S(2)}) collective-permute-start(bf16[768,512]{1,0:T(8,128)(2,1)} %collective-permute-done.12.refs_14_.refs_15_), channel_id=1, source_target_pairs={{0,4},{4,0},{1,5},{5,1},{2,6},{6,2},{3,7},{7,3},{8,12},{12,8},{9,1... | collective-permute-start | bytes 2359304 | tf_op jit(solution)/shard_map/ppermute | solution.py:285
  99.0 10.4 %all-to-all-start.1 = ((bf16[4,128,512]{2,1,0:T(8,128)(2,1)}), bf16[4,128,512]{2,1,0:T(8,128)(2,1)S(1)}, u32[]{:S(2)}, u32[]{:S(2)}) async-start(bf16[4,128,512]{2,1,0:T(8,128)(2,1)} %shard_map.77), calls=%async_computation.1 | async-start | bytes 1048576 | tf_op jit(solution)/shard_map/all_to_all | solution.py:364
  116.3 38.0 %all-to-all-start.2 = ((bf16[64,96,128]{2,1,0:T(8,128)(2,1)}), bf16[64,96,128]{2,1,0:T(8,128)(2,1)S(1)}, u32[]{:S(2)}, u32[]{:S(2)}) async-start(bf16[64,96,128]{2,1,0:T(8,128)(2,1)} %bitcast.30), calls=%async_computation.2 | async-start | bytes 3145728 | tf_op jit(solution)/shard_map/all_to_all | solution.py:397
  (8 other events, 94.8 us)
Sparse Core Ops, SparseCore 0:
  24.8 67.5 all-gather.1

commit v15 on v14

--- a/solution.py
+++ b/solution.py
@@ -38,13 +38,20 @@
     core_ref,
     experts_ref,
     weight_ref,
-    tok_ref,
-    cot_ref,
+    tok_hbm,
+    cot_hbm,
     tok_out_ref,
     keep_ref,
     send_ref,
     table_ref,
+    tok_ref,
+    cot_ref,
+    sems,
 ):
+    tok_copy = pltpu.make_async_copy(tok_hbm, tok_ref, sems.at[0])
+    cot_copy = pltpu.make_async_copy(cot_hbm, cot_ref, sems.at[1])
+    tok_copy.start()
+    cot_copy.start()
     expert_id, core = expert_ref[0], core_ref[0]
     n_dest, both, half = tok_out_ref.shape
     part = both // 2
@@ -70,6 +77,8 @@
     hit = own == slot
     select = jnp.where(hit, 1.0, 0.0).astype(bf16)
     slot_share = jnp.sum(jnp.where(hit, share, 0.0), axis=1, keepdims=True)
+    tok_copy.wait()
+    cot_copy.wait()
     tok = jnp.dot(select, tok_ref[...], preferred_element_type=f32)
     cot = slot_share * jnp.dot(select, cot_ref[...], preferred_element_type=f32)
     for d in range(n_dest):
@@ -329,7 +338,12 @@
             jax.ShapeDtypeStruct((n_s // 2, 2 * part, half), bf16),
             jax.ShapeDtypeStruct((1, table_rows, half), bf16),
         ),
-        [smem] * 2 + [vmem] * 4,
+        [smem] * 2 + [vmem] * 2 + [anywhere] * 2,
+        [
+            pltpu.VMEM((count, feats), bf16),
+            pltpu.VMEM((count, feats), bf16),
+            pltpu.SemaphoreType.DMA((2,)),
+        ],
     )(expert_id, core, experts.T, route_weight.T, tokens, cotangent)
     down, pieces = lax.optimization_barrier((down, pieces))
     pieces = lax.all_to_all(pieces, ("x", "c"), 0, 0, tiled=True)

time: 197 us -> 197 us (level)
  no operation moved by 1% of the time
where the time goes in v15:
time: 197 us; the launch traced here: 196 us
  starting transfers between devices  76.9 us (39%)
  waiting for transfers between devices  47.6 us (24%)
  blocking collectives  33.3 us (17%)
  Pallas kernels  22.3 us (11%)
  between operations  13.8 us (7%)
    all_to_all x1, blocking collectives, per_device(): dense = lax.all_to_all(dense, 'zh', 0, 0, tiled=True)  33.3 us
    ppermute x10, starting transfers between devices, swap(): return lax.ppermute(value, 'c', [(0, 1), (1, 0)])  29.2 us
    all_to_all x1, waiting for transfers between devices, per_device(): lax.all_to_all(result.reshape(n_s * window * 2, *shape[3:]), ('x', 'c', '...  22.7 us
    all_to_all x1, starting transfers between devices, per_device(): lax.all_to_all(result.reshape(n_s * window * 2, *shape[3:]), ('x', 'c', '...  14.4 us
    all_to_all x1, starting transfers between devices, per_device(): pieces = lax.all_to_all(pieces, ('x', 'c'), 0, 0, tiled=True)  10.3 us
    ppermute x1, waiting for transfers between devices, gather_weights(): up_before = lax.ppermute(up, 'x', ahead)  10.1 us
    pallas_call x1, Pallas kernels, per_device(): kernel_call(result_kernel, jax.ShapeDtypeStruct(result_shape, bf16), [sme...  6.89 us
    ppermute x1, waiting for transfers between devices, gather_weights(): gate_across = lax.ppermute(gate_before, 'x', ahead)  6.23 us
  transfers between devices with their start and end apart: 20, of which 7 were waited for; matrix products, arithmetic and copies ran while one was open for 0% of the time, Pallas kernels for 6%

profile of v15, /device:TPU:1, one launch (start us, length us, event | category | flops | bytes accessed | tf_op | source)
XLA Modules:
  0.0 196.4 jit_solution(2074673477841627627)
XLA Ops:
  6.5 2.7 %shard_map.73 = (bf16[8,16,384]{2,1,0:T(8,128)(2,1)}, bf16[4,16,384]{2,1,0:T(8,128)(2,1)}, bf16[4,16,384]{2,1,0:T(8,128)(2,1)}, bf16[1,16,384]{2,1,0:T(8,128)(2,1)}) custom-call(s32[1]{0:T(128)} %bitcast.3.expert_ref, s32[1]{0:T(128)} %bitcast.4.core_ref, s32[2,128]{1,0:T(2,128)} %bitcast.32, s32[2,128]{1,0:T(2,128)} %bitcast.33, bf16[128,768]{1,0:T(8,128)(2,1)} %tok_hbm.1, ...), custom_call_target="tpu_custom_call" | custom-call | tf_op jit(solution)/shard_map/pallas_call | solution.py:333
  9.3 10.3 %all-to-all-start = ((bf16[8,16,384]{2,1,0:T(8,128)(2,1)}), bf16[8,16,384]{2,1,0:T(8,128)(2,1)S(1)}, u32[]{:S(2)}, u32[]{:S(2)}) async-start(bf16[8,16,384]{2,1,0:T(8,128)(2,1)} %get-tuple-element.21), calls=%async_computation | async-start | bytes 196608 | tf_op jit(solution)/shard_map/all_to_all | solution.py:349
  21.6 2.3 %shard_map.74.near_hbm = bf16[768,512]{1,0:T(8,128)(2,1)} custom-call(bf16[512,768]{1,0:T(8,128)(2,1)} %bitcast.31), custom_call_target="tpu_custom_call" | custom-call | tf_op jit(solution)/shard_map/pallas_call | solution.py:350
  25.3 2.8 %collective-permute-start.3 = (bf16[768,512]{1,0:T(8,128)(2,1)S(1)}, bf16[768,512]{1,0:T(8,128)(2,1)S(1)}, u32[]{:S(2)}, u32[]{:S(2)}) collective-permute-start(bf16[768,512]{1,0:T(8,128)(2,1)S(1)} %bitcast.17), channel_id=1, source_target_pairs={{0,8},{8,16},{16,24},{24,0},{1,9},{9,17},{17,25},{25,1},{2,10},{10... | collective-permute-start | bytes 2359304 | tf_op jit(solution)/shard_map/ppermute | solution.py:301
  28.2 3.6 %collective-permute-start.4 = (bf16[768,512]{1,0:T(8,128)(2,1)S(1)}, bf16[768,512]{1,0:T(8,128)(2,1)S(1)}, u32[]{:S(2)}, u32[]{:S(2)}) collective-permute-start(bf16[768,512]{1,0:T(8,128)(2,1)S(1)} %bitcast.23), channel_id=1, source_target_pairs={{0,24},{8,0},{16,8},{24,16},{1,25},{9,1},{17,9},{25,17},{2,26},{10... | collective-permute-start | bytes 2359304 | tf_op jit(solution)/shard_map/ppermute | solution.py:302
  33.8 4.6 %collective-permute-start.6 = (bf16[768,512]{1,0:T(8,128)(2,1)S(1)}, bf16[768,512]{1,0:T(8,128)(2,1)}, u32[]{:S(2)}, u32[]{:S(2)}) collective-permute-start(bf16[768,512]{1,0:T(8,128)(2,1)S(1)} %bitcast.18), channel_id=1, source_target_pairs={{0,24},{8,0},{16,8},{24,16},{1,25},{9,1},{17,9},{25,17},{2,26},{10... | collective-permute-start | bytes 2359304 | tf_op jit(solution)/shard_map/ppermute | solution.py:304
  38.4 3.8 %collective-permute-start.1 = (bf16[768,512]{1,0:T(8,128)(2,1)S(1)}, bf16[768,512]{1,0:T(8,128)(2,1)S(1)}, u32[]{:S(2)}, u32[]{:S(2)}) collective-permute-start(bf16[768,512]{1,0:T(8,128)(2,1)S(1)} %bitcast.19), channel_id=1, source_target_pairs={{0,4},{4,0},{1,5},{5,1},{2,6},{6,2},{3,7},{7,3},{8,12},{12,8},{9,1... | collective-permute-start | bytes 2359304 | tf_op jit(solution)/shard_map/ppermute | solution.py:294
  42.2 4.5 %collective-permute-done.3.refs_5_.refs_6_ = bf16[768,512]{1,0:T(8,128)(2,1)S(1)} collective-permute-done((bf16[768,512]{1,0:T(8,128)(2,1)S(1)}, bf16[768,512]{1,0:T(8,128)(2,1)S(1)}, u32[]{:S(2)}, u32[]{:S(2)}) %collective-permute-start.3) | collective-permute-done | bytes 786464 | tf_op jit(solution)/shard_map/ppermute | solution.py:301
  46.7 4.9 %collective-permute-start.2 = (bf16[768,512]{1,0:T(8,128)(2,1)S(1)}, bf16[768,512]{1,0:T(8,128)(2,1)S(1)}, u32[]{:S(2)}, u32[]{:S(2)}) collective-permute-start(bf16[768,512]{1,0:T(8,128)(2,1)S(1)} %bitcast.25), channel_id=1, source_target_pairs={{0,4},{4,0},{1,5},{5,1},{2,6},{6,2},{3,7},{7,3},{8,12},{12,8},{9,1... | collective-permute-start | bytes 2359304 | tf_op jit(solution)/shard_map/ppermute | solution.py:294
  53.6 10.1 %collective-permute-done.5.refs_6_.refs_7_ = bf16[768,512]{1,0:T(8,128)(2,1)} collective-permute-done((bf16[768,512]{1,0:T(8,128)(2,1)S(1)}, bf16[768,512]{1,0:T(8,128)(2,1)}, u32[]{:S(2)}, u32[]{:S(2)}) %collective-permute-start.5) | collective-permute-done | bytes 786464 | tf_op jit(solution)/shard_map/ppermute | solution.py:303
  65.7 3.1 %collective-permute-start.11 = (bf16[768,512]{1,0:T(8,128)(2,1)S(1)}, bf16[768,512]{1,0:T(8,128)(2,1)}, u32[]{:S(2)}, u32[]{:S(2)}) collective-permute-start(bf16[768,512]{1,0:T(8,128)(2,1)S(1)} %collective-permute-done.3.refs_5_.refs_6_), channel_id=1, source_target_pairs={{0,8},{8,16},{16,24},{24,0},{1,9},{9,17},{17,25},{25,1},{2,10},{10... | collective-permute-start | bytes 2359304 | tf_op jit(solution)/shard_map/ppermute | solution.py:308
  68.8 3.4 %collective-permute-start.12 = (bf16[768,512]{1,0:T(8,128)(2,1)S(1)}, bf16[768,512]{1,0:T(8,128)(2,1)}, u32[]{:S(2)}, u32[]{:S(2)}) collective-permute-start(bf16[768,512]{1,0:T(8,128)(2,1)S(1)} %collective-permute-done.4.refs_8_.refs_9_), channel_id=1, source_target_pairs={{0,24},{8,0},{16,8},{24,16},{1,25},{9,1},{17,9},{25,17},{2,26},{10... | collective-permute-start | bytes 2359304 | tf_op jit(solution)/shard_map/ppermute | solution.py:309
  72.2 3.8 %collective-permute-start.10 = (bf16[768,512]{1,0:T(8,128)(2,1)S(1)}, bf16[768,512]{1,0:T(8,128)(2,1)S(1)}, u32[]{:S(2)}, u32[]{:S(2)}) collective-permute-start(bf16[768,512]{1,0:T(8,128)(2,1)S(1)} %collective-permute-done.4.refs_8_.refs_9_), channel_id=1, source_target_pairs={{0,4},{4,0},{1,5},{5,1},{2,6},{6,2},{3,7},{7,3},{8,12},{12,8},{9,1... | collective-permute-start | bytes 2359304 | tf_op jit(solution)/shard_map/ppermute | solution.py:294
  78.0 2.4 %collective-permute-start.8 = (bf16[768,512]{1,0:T(8,128)(2,1)}, bf16[768,512]{1,0:T(8,128)(2,1)}, u32[]{:S(2)}, u32[]{:S(2)}) collective-permute-start(bf16[768,512]{1,0:T(8,128)(2,1)} %collective-permute-done.5.refs_6_.refs_7_), channel_id=1, source_target_pairs={{0,4},{4,0},{1,5},{5,1},{2,6},{6,2},{3,7},{7,3},{8,12},{12,8},{9,1... | collective-permute-start | bytes 2359304 | tf_op jit(solution)/shard_map/ppermute | solution.py:294
  80.4 6.2 %collective-permute-done.11.refs_13_.refs_14_ = bf16[768,512]{1,0:T(8,128)(2,1)} collective-permute-done((bf16[768,512]{1,0:T(8,128)(2,1)S(1)}, bf16[768,512]{1,0:T(8,128)(2,1)}, u32[]{:S(2)}, u32[]{:S(2)}) %collective-permute-start.11) | collective-permute-done | bytes 786464 | tf_op jit(solution)/shard_map/ppermute | solution.py:308
  86.6 4.1 %collective-permute-start.9 = (bf16[768,512]{1,0:T(8,128)(2,1)}, bf16[768,512]{1,0:T(8,128)(2,1)}, u32[]{:S(2)}, u32[]{:S(2)}) collective-permute-start(bf16[768,512]{1,0:T(8,128)(2,1)} %collective-permute-done.6.refs_7_.refs_8_), channel_id=1, source_target_pairs={{0,4},{4,0},{1,5},{5,1},{2,6},{6,2},{3,7},{7,3},{8,12},{12,8},{9,1... | collective-permute-start | bytes 2359304 | tf_op jit(solution)/shard_map/ppermute | solution.py:294
  93.6 2.4 %collective-permute-start.14 = (bf16[768,512]{1,0:T(8,128)(2,1)}, bf16[768,512]{1,0:T(8,128)(2,1)}, u32[]{:S(2)}, u32[]{:S(2)}) collective-permute-start(bf16[768,512]{1,0:T(8,128)(2,1)} %collective-permute-done.12.refs_14_.refs_15_), channel_id=1, source_target_pairs={{0,4},{4,0},{1,5},{5,1},{2,6},{6,2},{3,7},{7,3},{8,12},{12,8},{9,1... | collective-permute-start | bytes 2359304 | tf_op jit(solution)/shard_map/ppermute | solution.py:294
  96.0 3.5 %shard_map.77 = bf16[4,128,512]{2,1,0:T(8,128)(2,1)} custom-call(bf16[16,17,16,384]{3,2,1,0:T(8,128)(2,1)} %bitcast.27, bf16[768,512]{1,0:T(8,128)(2,1)} %shard_map.74.near_hbm, bf16[768,512]{1,0:T(8,128)(2,1)} %copy-done.11), custom_call_target="tpu_custom_call" | custom-call | tf_op jit(solution)/shard_map/pallas_call | solution.py:367
  99.6 3.5 %all-to-all-start.1 = ((bf16[4,128,512]{2,1,0:T(8,128)(2,1)}), bf16[4,128,512]{2,1,0:T(8,128)(2,1)S(1)}, u32[]{:S(2)}, u32[]{:S(2)}) async-start(bf16[4,128,512]{2,1,0:T(8,128)(2,1)} %shard_map.77), calls=%async_computation.1 | async-start | bytes 1048576 | tf_op jit(solution)/shard_map/all_to_all | solution.py:378
  103.1 5.5 %shard_map.76.refs_0_ = f32[128,1024]{1,0:T(8,128)S(1)} custom-call(s32[1]{0:T(128)} %bitcast.10.x_ref, s32[1]{0:T(128)} %bitcast.4.core_ref, bf16[16,17,16,384]{3,2,1,0:T(8,128)(2,1)} %bitcast.28, bf16[768,512]{1,0:T(8,128)(2,1)S(1)} %bitcast.20, bf16[768,512]{1,0:T(8,128)(2,1)} %bitcast.22, bf16[768,512]{1,0:T(8,128)(2,1)} %copy-done.3, ...), custom_call_target="tpu_custom_call" | custom-call | tf_op jit(solution)/shard_map/pallas_call | solution.py:379
  110.0 6.9 %shard_map.78 = bf16[8,4,2,96,128]{4,3,2,1,0:T(8,128)(2,1)} custom-call(s32[1]{0:T(128)} %bitcast.10.x_ref, s32[1]{0:T(128)} %bitcast.4.core_ref, f32[128,1024]{1,0:T(8,128)S(1)} %shard_map.76.refs_0_, bf16[4,128,512]{2,1,0:T(8,128)(2,1)S(1)} %all-to-all-done.1.refs_1_, bf16[768,512]{1,0:T(8,128)(2,1)S(1)} %bitcast.21, bf16[768,512]{1,0:T(8,128)(2,1)S(1)} %bitcast.26, ...), custom_call_target="tpu_custom_call" | custom-call | tf_op jit(solution)/shard_map/pallas_call | solution.py:391
  116.9 14.4 %all-to-all-start.2 = ((bf16[64,96,128]{2,1,0:T(8,128)(2,1)}), bf16[64,96,128]{2,1,0:T(8,128)(2,1)S(1)}, u32[]{:S(2)}, u32[]{:S(2)}) async-start(bf16[64,96,128]{2,1,0:T(8,128)(2,1)} %bitcast.30), calls=%async_computation.2 | async-start | bytes 3145728 | tf_op jit(solution)/shard_map/all_to_all | solution.py:411
  132.1 22.7 %all-to-all-done.2 = bf16[64,96,128]{2,1,0:T(8,128)(2,1)S(1)} async-done(((bf16[64,96,128]{2,1,0:T(8,128)(2,1)}), bf16[64,96,128]{2,1,0:T(8,128)(2,1)S(1)}, u32[]{:S(2)}, u32[]{:S(2)}) %all-to-all-start.2) | async-done | bytes 1572896 | tf_op jit(solution)/shard_map/all_to_all | solution.py:411
  155.6 33.3 %all_to_all.20 = bf16[8,192,128]{2,1,0:T(8,128)(2,1)S(1)} all-to-all(bf16[8,192,128]{2,1,0:T(8,128)(2,1)S(1)} %shard_map.79), channel_id=1, replica_groups=mesh['zh'=8,'zl'=2,'x'=4,'c'=2,'y'=4] {'zh'}, dimensions={0} | all-to-all | bytes 786432 | tf_op jit(solution)/shard_map/all_to_all | solution.py:420
  (52 shorter events, 17.8 us)
Async XLA Ops:
  6.5 21.6 %copy-start.1 = (bf16[1,768,512]{2,1,0:T(8,128)(2,1)S(1)}, bf16[1,768,512]{2,1,0:T(8,128)(2,1)}, u32[]{:S(2)}) copy-start(bf16[1,768,512]{2,1,0:T(8,128)(2,1)} %param.12) | copy-start | bytes 2359300
  9.3 15.3 %all-to-all-start = ((bf16[8,16,384]{2,1,0:T(8,128)(2,1)}), bf16[8,16,384]{2,1,0:T(8,128)(2,1)S(1)}, u32[]{:S(2)}, u32[]{:S(2)}) async-start(bf16[8,16,384]{2,1,0:T(8,128)(2,1)} %get-tuple-element.21), calls=%async_computation | async-start | bytes 196608 | tf_op jit(solution)/shard_map/all_to_all | solution.py:349
  19.5 76.5 %all-gather.2.cloned.1.call-start = ((), (), s32[]{:S(2)}) async-start(), calls=%async_computation.4 | async-start | bytes 3551232 | tf_op jit(solution)/shard_map/all_gather | solution.py:361
  19.6 5.0 %collective-permute-start = (bf16[4,16,384]{2,1,0:T(8,128)(2,1)}, bf16[4,16,384]{2,1,0:T(8,128)(2,1)S(1)}, u32[]{:S(2)}, u32[]{:S(2)}) collective-permute-start(bf16[4,16,384]{2,1,0:T(8,128)(2,1)} %get-tuple-element.25), channel_id=1, source_target_pairs={{0,4},{4,0},{1,5},{5,1},{2,6},{6,2},{3,7},{7,3},{8,12},{12,8},{9,1... | collective-permute-start | bytes 147464 | tf_op jit(solution)/shard_map/ppermute | solution.py:294
  25.3 21.4 %collective-permute-start.3 = (bf16[768,512]{1,0:T(8,128)(2,1)S(1)}, bf16[768,512]{1,0:T(8,128)(2,1)S(1)}, u32[]{:S(2)}, u32[]{:S(2)}) collective-permute-start(bf16[768,512]{1,0:T(8,128)(2,1)S(1)} %bitcast.17), channel_id=1, source_target_pairs={{0,8},{8,16},{16,24},{24,0},{1,9},{9,17},{17,25},{25,1},{2,10},{10... | collective-permute-start | bytes 2359304 | tf_op jit(solution)/shard_map/ppermute | solution.py:301
  28.2 23.4 %collective-permute-start.4 = (bf16[768,512]{1,0:T(8,128)(2,1)S(1)}, bf16[768,512]{1,0:T(8,128)(2,1)S(1)}, u32[]{:S(2)}, u32[]{:S(2)}) collective-permute-start(bf16[768,512]{1,0:T(8,128)(2,1)S(1)} %bitcast.23), channel_id=1, source_target_pairs={{0,24},{8,0},{16,8},{24,16},{1,25},{9,1},{17,9},{25,17},{2,26},{10... | collective-permute-start | bytes 2359304 | tf_op jit(solution)/shard_map/ppermute | solution.py:302
  31.8 31.8 %collective-permute-start.5 = (bf16[768,512]{1,0:T(8,128)(2,1)S(1)}, bf16[768,512]{1,0:T(8,128)(2,1)}, u32[]{:S(2)}, u32[]{:S(2)}) collective-permute-start(bf16[768,512]{1,0:T(8,128)(2,1)S(1)} %bitcast.24), channel_id=1, source_target_pairs={{0,8},{8,16},{16,24},{24,0},{1,9},{9,17},{17,25},{25,1},{2,10},{10... | collective-permute-start | bytes 2359304 | tf_op jit(solution)/shard_map/ppermute | solution.py:303
  33.8 31.9 %collective-permute-start.6 = (bf16[768,512]{1,0:T(8,128)(2,1)S(1)}, bf16[768,512]{1,0:T(8,128)(2,1)}, u32[]{:S(2)}, u32[]{:S(2)}) collective-permute-start(bf16[768,512]{1,0:T(8,128)(2,1)S(1)} %bitcast.18), channel_id=1, source_target_pairs={{0,24},{8,0},{16,8},{24,16},{1,25},{9,1},{17,9},{25,17},{2,26},{10... | collective-permute-start | bytes 2359304 | tf_op jit(solution)/shard_map/ppermute | solution.py:304
  38.4 33.8 %collective-permute-start.1 = (bf16[768,512]{1,0:T(8,128)(2,1)S(1)}, bf16[768,512]{1,0:T(8,128)(2,1)S(1)}, u32[]{:S(2)}, u32[]{:S(2)}) collective-permute-start(bf16[768,512]{1,0:T(8,128)(2,1)S(1)} %bitcast.19), channel_id=1, source_target_pairs={{0,4},{4,0},{1,5},{5,1},{2,6},{6,2},{3,7},{7,3},{8,12},{12,8},{9,1... | collective-permute-start | bytes 2359304 | tf_op jit(solution)/shard_map/ppermute | solution.py:294
  46.7 52.8 %copy-start.7 = (bf16[768,512]{1,0:T(8,128)(2,1)}, bf16[768,512]{1,0:T(8,128)(2,1)S(1)}, u32[]{:S(2)}) copy-start(bf16[768,512]{1,0:T(8,128)(2,1)S(1)} %collective-permute-done.3.refs_5_.refs_6_) | copy-start | bytes 2359300
  46.7 29.3 %collective-permute-start.2 = (bf16[768,512]{1,0:T(8,128)(2,1)S(1)}, bf16[768,512]{1,0:T(8,128)(2,1)S(1)}, u32[]{:S(2)}, u32[]{:S(2)}) collective-permute-start(bf16[768,512]{1,0:T(8,128)(2,1)S(1)} %bitcast.25), channel_id=1, source_target_pairs={{0,4},{4,0},{1,5},{5,1},{2,6},{6,2},{3,7},{7,3},{8,12},{12,8},{9,1... | collective-permute-start | bytes 2359304 | tf_op jit(solution)/shard_map/ppermute | solution.py:294
  51.6 35.0 %copy-start.8 = (bf16[768,512]{1,0:T(8,128)(2,1)}, bf16[768,512]{1,0:T(8,128)(2,1)S(1)}, u32[]{:S(2)}) copy-start(bf16[768,512]{1,0:T(8,128)(2,1)S(1)} %collective-permute-done.4.refs_8_.refs_9_) | copy-start | bytes 2359300
  51.6 26.3 %collective-permute-start.15 = (bf16[768,512]{1,0:T(8,128)(2,1)}, bf16[768,512]{1,0:T(8,128)(2,1)S(1)}, u32[]{:S(2)}, u32[]{:S(2)}) collective-permute-start(bf16[768,512]{1,0:T(8,128)(2,1)} %shard_map.74.near_hbm), channel_id=1, source_target_pairs={{0,4},{4,0},{1,5},{5,1},{2,6},{6,2},{3,7},{7,3},{8,12},{12,8},{9,1... | collective-permute-start | bytes 2359304 | tf_op jit(solution)/shard_map/ppermute | solution.py:294
  65.7 20.9 %collective-permute-start.11 = (bf16[768,512]{1,0:T(8,128)(2,1)S(1)}, bf16[768,512]{1,0:T(8,128)(2,1)}, u32[]{:S(2)}, u32[]{:S(2)}) collective-permute-start(bf16[768,512]{1,0:T(8,128)(2,1)S(1)} %collective-permute-done.3.refs_5_.refs_6_), channel_id=1, source_target_pairs={{0,8},{8,16},{16,24},{24,0},{1,9},{9,17},{17,25},{25,1},{2,10},{10... | collective-permute-start | bytes 2359304 | tf_op jit(solution)/shard_map/ppermute | solution.py:308
  68.8 21.9 %collective-permute-start.12 = (bf16[768,512]{1,0:T(8,128)(2,1)S(1)}, bf16[768,512]{1,0:T(8,128)(2,1)}, u32[]{:S(2)}, u32[]{:S(2)}) collective-permute-start(bf16[768,512]{1,0:T(8,128)(2,1)S(1)} %collective-permute-done.4.refs_8_.refs_9_), channel_id=1, source_target_pairs={{0,24},{8,0},{16,8},{24,16},{1,25},{9,1},{17,9},{25,17},{2,26},{10... | collective-permute-start | bytes 2359304 | tf_op jit(solution)/shard_map/ppermute | solution.py:309
  72.2 27.4 %copy-start.3 = (bf16[768,512]{1,0:T(8,128)(2,1)}, bf16[768,512]{1,0:T(8,128)(2,1)S(1)}, u32[]{:S(2)}) copy-start(bf16[768,512]{1,0:T(8,128)(2,1)S(1)} %collective-permute-done.1.refs_3_.refs_4_) | copy-start | bytes 2359300
  72.2 20.5 %collective-permute-start.10 = (bf16[768,512]{1,0:T(8,128)(2,1)S(1)}, bf16[768,512]{1,0:T(8,128)(2,1)S(1)}, u32[]{:S(2)}, u32[]{:S(2)}) collective-permute-start(bf16[768,512]{1,0:T(8,128)(2,1)S(1)} %collective-permute-done.4.refs_8_.refs_9_), channel_id=1, source_target_pairs={{0,4},{4,0},{1,5},{5,1},{2,6},{6,2},{3,7},{7,3},{8,12},{12,8},{9,1... | collective-permute-start | bytes 2359304 | tf_op jit(solution)/shard_map/ppermute | solution.py:294
  76.0 27.1 %collective-permute-start.7 = (bf16[768,512]{1,0:T(8,128)(2,1)S(1)}, bf16[768,512]{1,0:T(8,128)(2,1)}, u32[]{:S(2)}, u32[]{:S(2)}) collective-permute-start(bf16[768,512]{1,0:T(8,128)(2,1)S(1)} %collective-permute-done.3.refs_5_.refs_6_), channel_id=1, source_target_pairs={{0,4},{4,0},{1,5},{5,1},{2,6},{6,2},{3,7},{7,3},{8,12},{12,8},{9,1... | collective-permute-start | bytes 2359304 | tf_op jit(solution)/shard_map/ppermute | solution.py:294
  78.0 25.1 %collective-permute-start.8 = (bf16[768,512]{1,0:T(8,128)(2,1)}, bf16[768,512]{1,0:T(8,128)(2,1)}, u32[]{:S(2)}, u32[]{:S(2)}) collective-permute-start(bf16[768,512]{1,0:T(8,128)(2,1)} %collective-permute-done.5.refs_6_.refs_7_), channel_id=1, source_target_pairs={{0,4},{4,0},{1,5},{5,1},{2,6},{6,2},{3,7},{7,3},{8,12},{12,8},{9,1... | collective-permute-start | bytes 2359304 | tf_op jit(solution)/shard_map/ppermute | solution.py:294
  86.6 16.5 %collective-permute-start.9 = (bf16[768,512]{1,0:T(8,128)(2,1)}, bf16[768,512]{1,0:T(8,128)(2,1)}, u32[]{:S(2)}, u32[]{:S(2)}) collective-permute-start(bf16[768,512]{1,0:T(8,128)(2,1)} %collective-permute-done.6.refs_7_.refs_8_), channel_id=1, source_target_pairs={{0,4},{4,0},{1,5},{5,1},{2,6},{6,2},{3,7},{7,3},{8,12},{12,8},{9,1... | collective-permute-start | bytes 2359304 | tf_op jit(solution)/shard_map/ppermute | solution.py:294
  90.8 12.3 %collective-permute-start.13 = (bf16[768,512]{1,0:T(8,128)(2,1)}, bf16[768,512]{1,0:T(8,128)(2,1)}, u32[]{:S(2)}, u32[]{:S(2)}) collective-permute-start(bf16[768,512]{1,0:T(8,128)(2,1)} %collective-permute-done.11.refs_13_.refs_14_), channel_id=1, source_target_pairs={{0,4},{4,0},{1,5},{5,1},{2,6},{6,2},{3,7},{7,3},{8,12},{12,8},{9,1... | collective-permute-start | bytes 2359304 | tf_op jit(solution)/shard_map/ppermute | solution.py:294
  93.6 9.5 %collective-permute-start.14 = (bf16[768,512]{1,0:T(8,128)(2,1)}, bf16[768,512]{1,0:T(8,128)(2,1)}, u32[]{:S(2)}, u32[]{:S(2)}) collective-permute-start(bf16[768,512]{1,0:T(8,128)(2,1)} %collective-permute-done.12.refs_14_.refs_15_), channel_id=1, source_target_pairs={{0,4},{4,0},{1,5},{5,1},{2,6},{6,2},{3,7},{7,3},{8,12},{12,8},{9,1... | collective-permute-start | bytes 2359304 | tf_op jit(solution)/shard_map/ppermute | solution.py:294
  99.6 10.4 %all-to-all-start.1 = ((bf16[4,128,512]{2,1,0:T(8,128)(2,1)}), bf16[4,128,512]{2,1,0:T(8,128)(2,1)S(1)}, u32[]{:S(2)}, u32[]{:S(2)}) async-start(bf16[4,128,512]{2,1,0:T(8,128)(2,1)} %shard_map.77), calls=%async_computation.1 | async-start | bytes 1048576 | tf_op jit(solution)/shard_map/all_to_all | solution.py:378
  116.9 38.0 %all-to-all-start.2 = ((bf16[64,96,128]{2,1,0:T(8,128)(2,1)}), bf16[64,96,128]{2,1,0:T(8,128)(2,1)S(1)}, u32[]{:S(2)}, u32[]{:S(2)}) async-start(bf16[64,96,128]{2,1,0:T(8,128)(2,1)} %bitcast.30), calls=%async_computation.2 | async-start | bytes 3145728 | tf_op jit(solution)/shard_map/all_to_all | solution.py:411
  (8 other events, 95.4 us)
Sparse Core Ops, SparseCore 0:
  25.4 67.4 all-gather.1
